TPU v7x, 32 devices: a whole 2x2x4 slice. The times are simulated.
32 devices in a mesh: dp: 8 (over y, x, core), inner: 4 (over z).
Axes of the slice: x: 2, y: 2, z: 4, core: 2. Of those that a mesh axis runs over, the one named last changes fastest.
Arguments:
- image: bfloat16 [4096, 1152], P(('dp', 'inner')), may hold values from -0.059814453 to 0.059814453
- text: bfloat16 [4096, 1152], P(('dp', 'inner')), may hold values from -0.059814453 to 0.059814453
- logarithm_scale: float32 [1], replicated, may hold values from 1.8 to 2.6
- bias: float32 [1], replicated, may hold values from -4 to -2
Outputs:
- image_gradient: float32 [4096, 1152], P(('dp', 'inner'))
- text_gradient: float32 [4096, 1152], P(('dp', 'inner'))
- image_loss: float32 [4096], P(('dp', 'inner'))
All inputs are finite; a program needn't handle non-finite values.
Results may differ from a plain program's by a relative error of at most 0.0044.
Values may be sent and summed in bfloat16 or wider, within the bound.
No kernel may reach another device: no remote copies, remote signals or barrier semaphores. Data moves between devices by JAX's collectives and lax.ppermute only.
A program may use at most 64 MiB of HBM per device.

v0:
```python
import jax
import jax.numpy as jnp
from jax import lax
from jax.sharding import PartitionSpec as P

epsilon = 1e-06


def passed_along(value, axis, steps):
    count = lax.axis_size(axis)
    pairs = [(source, (source + steps) % count) for source in range(count)]
    return lax.ppermute(value, axis, pairs)


def normalize(values):
    wide = values.astype(jnp.float32)
    inverse = lax.rsqrt(jnp.sum(wide * wide, axis=-1, keepdims=True) + epsilon)
    return (wide * inverse, inverse)


def norm_backward_step(unit_rows, unit_grad, inverse):
    return (
        unit_grad - unit_rows * jnp.sum(unit_rows * unit_grad, axis=-1, keepdims=True)
    ) * inverse


def body(image, text, logarithm_scale, bias):
    rows = image.shape[0]
    logit_scale = jnp.exp(logarithm_scale[0])
    logit_bias = bias[0]
    normalized_image, image_inverse_norm = normalize(image)
    normalized_text, text_inverse_norm = normalize(text)
    image_emb = normalized_image.astype(jnp.bfloat16)
    text_embedding = normalized_text.astype(jnp.bfloat16)
    images = lax.all_gather(image_emb, "inner", axis=0, tiled=True)
    dp_count = lax.axis_size("dp")
    inner_count = lax.axis_size("inner")
    dp_index = lax.axis_index("dp")
    inner_index = lax.axis_index("inner")
    image_ids = dp_index * inner_count * rows + jnp.arange(images.shape[0], dtype=jnp.int32)

    def block_terms(block, text_ids):
        pair_logits = (
            logit_scale
            * lax.dot_general(
                images, block, (((1,), (1,)), ((), ())), preferred_element_type=jnp.float32
            )
            + logit_bias
        )
        match = (image_ids[:, None] == text_ids[None, :]).astype(jnp.float32)
        loss_part = jnp.sum(jax.nn.softplus(pair_logits) - match * pair_logits, axis=1)
        slopes = (jax.nn.sigmoid(pair_logits) - match).astype(jnp.bfloat16)
        image_part = jnp.dot(slopes, block, preferred_element_type=jnp.float32)
        text_part = lax.dot_general(
            slopes, images, (((0,), (0,)), ((), ())), preferred_element_type=jnp.float32
        )
        return (image_part, text_part, loss_part)

    def anchor_ids(source, count):
        return (source * inner_count + inner_index) * rows + jnp.arange(count, dtype=jnp.int32)

    image_part, text_part, loss_part = block_terms(text_embedding, anchor_ids(dp_index, rows))

    def advance(turn, state):
        block, carried, image_total, loss_total = state
        block = passed_along(block, "dp", 1)
        carried = passed_along(carried, "dp", 1)
        source = (dp_index - turn) % dp_count
        image_step, text_step, loss_step = block_terms(block, anchor_ids(source, rows))
        return (block, carried + text_step, image_total + image_step, loss_total + loss_step)

    block, carried, image_total, loss_total = lax.fori_loop(
        1, dp_count, advance, (text_embedding, text_part, image_part, loss_part)
    )
    caption_total = passed_along(carried, "dp", 1)
    picture_portion, loss_share = (
        lax.psum_scatter(image_total, "inner", scatter_dimension=0, tiled=True),
        lax.psum_scatter(loss_total, "inner", scatter_dimension=0, tiled=True),
    )
    batch_total = rows * dp_count * inner_count
    image_gradient = norm_backward_step(
        normalized_image, logit_scale * picture_portion, image_inverse_norm
    )
    text_gradient = norm_backward_step(
        normalized_text, logit_scale * caption_total, text_inverse_norm
    )
    image_loss = loss_share / batch_total
    return (image_gradient, text_gradient, image_loss)


def solution(mesh):
    return jax.shard_map(
        body,
        mesh=mesh,
        in_specs=(P(("dp", "inner"), None), P(("dp", "inner"), None), P(), P()),
        out_specs=(P(("dp", "inner"), None), P(("dp", "inner"), None), P(("dp", "inner"))),
        check_vma=False,
    )
```

profile of v0, /device:TPU:0, one launch (start us, length us, event | category | flops | bytes accessed | tf_op | source)
XLA Modules:
  0.0 209.1 jit_solution(5625660299623741446)
XLA Ops:
  12.6 30.9 %all-gather.2.cloned.1.call-done = bf16[512,1152]{1,0:T(8,128)(2,1)} async-done(((bf16[128,1152]{1,0:T(8,128)(2,1)}), bf16[512,1152]{1,0:T(8,128)(2,1)}) %all-gather.2.cloned.1.call-update) | async-done | bytes 1179664 | tf_op jit(solution)/shard_map/all_gather | solution.py:35
  48.4 103.7 %while.22 = (s32[]{:T(128)}, bf16[128,1152]{1,0:T(8,128)(2,1)}, f32[128,1152]{1,0:T(8,128)}, f32[512,1152]{1,0:T(8,128)S(1)}, f32[512]{0:T(512)S(1)}, /*index=5*...) while((s32[]{:T(128)}, bf16[128,1152]{1,0:T(8,128)(2,1)}, ...), condition=%wide.region_5.6_spmd.clone, body=%wide.region_3.5_spmd.clone.sunk | while | flops 455426688 | bytes 18500020 | solution.py:72
  50.0 5.7 %collective-permute-done = bf16[128,1152]{1,0:T(8,128)(2,1)S(1)} collective-permute-done((bf16[128,1152]{1,0:T(8,128)(2,1)}, bf16[128,1152]{1,0:T(8,128)(2,1)S(1)}, u32[]{:S(2)}, u32[]{:S(2)}) %collective-permute-start) | collective-permute-done | bytes 294944 | tf_op jit(solution)/shard_map/while/body/eval_jaxpr/ppermute | solution.py:12
  55.6 2.6 %fusion.53 = (f32[512]{0:T(512)S(1)}, f32[512,128]{0,1:T(8,128)S(1)}) fusion(s32[512]{0:T(512)S(1)} %iota_add_fusion.6, s32[128]{0:T(128)S(1)} %iota_add_fusion.7, f32[]{:T(128)} %get-tuple-element.436, bf16[512,1152]{1,0:T(8,128)(2,1)} %get-tuple-element.435, bf16[128,1152]{1,0:T(8,128)(2,1)S(1)} %collective-permute-done, f32[]{:T(128)} %get-tuple-element.434), kind=kOutput, calls=%fused_computation.11.clone.1 | convolution fusion | flops 151780864 | bytes 1741320 | tf_op jit(solution)/shard_map/while/body/eval_jaxpr/dot_general | solution.py:45
  63.9 6.6 %collective-permute-done = bf16[128,1152]{1,0:T(8,128)(2,1)S(1)} collective-permute-done((bf16[128,1152]{1,0:T(8,128)(2,1)}, bf16[128,1152]{1,0:T(8,128)(2,1)S(1)}, u32[]{:S(2)}, u32[]{:S(2)}) %collective-permute-start) | collective-permute-done | bytes 294944 | tf_op jit(solution)/shard_map/while/body/eval_jaxpr/ppermute | solution.py:12
  70.4 2.6 %fusion.53 = (f32[512]{0:T(512)S(1)}, f32[512,128]{0,1:T(8,128)S(1)}) fusion(s32[512]{0:T(512)S(1)} %iota_add_fusion.6, s32[128]{0:T(128)S(1)} %iota_add_fusion.7, f32[]{:T(128)} %get-tuple-element.436, bf16[512,1152]{1,0:T(8,128)(2,1)} %get-tuple-element.435, bf16[128,1152]{1,0:T(8,128)(2,1)S(1)} %collective-permute-done, f32[]{:T(128)} %get-tuple-element.434), kind=kOutput, calls=%fused_computation.11.clone.1 | convolution fusion | flops 151780864 | bytes 1741320 | tf_op jit(solution)/shard_map/while/body/eval_jaxpr/dot_general | solution.py:45
  74.5 2.3 %collective-permute-done.1 = f32[128,1152]{1,0:T(8,128)S(1)} collective-permute-done((f32[128,1152]{1,0:T(8,128)}, f32[128,1152]{1,0:T(8,128)S(1)}, u32[]{:S(2)}, u32[]{:S(2)}) %collective-permute-start.1) | collective-permute-done | bytes 589856 | tf_op jit(solution)/shard_map/while/body/eval_jaxpr/ppermute | solution.py:12
  78.0 7.2 %collective-permute-done = bf16[128,1152]{1,0:T(8,128)(2,1)S(1)} collective-permute-done((bf16[128,1152]{1,0:T(8,128)(2,1)}, bf16[128,1152]{1,0:T(8,128)(2,1)S(1)}, u32[]{:S(2)}, u32[]{:S(2)}) %collective-permute-start) | collective-permute-done | bytes 294944 | tf_op jit(solution)/shard_map/while/body/eval_jaxpr/ppermute | solution.py:12
  85.2 2.6 %fusion.53 = (f32[512]{0:T(512)S(1)}, f32[512,128]{0,1:T(8,128)S(1)}) fusion(s32[512]{0:T(512)S(1)} %iota_add_fusion.6, s32[128]{0:T(128)S(1)} %iota_add_fusion.7, f32[]{:T(128)} %get-tuple-element.436, bf16[512,1152]{1,0:T(8,128)(2,1)} %get-tuple-element.435, bf16[128,1152]{1,0:T(8,128)(2,1)S(1)} %collective-permute-done, f32[]{:T(128)} %get-tuple-element.434), kind=kOutput, calls=%fused_computation.11.clone.1 | convolution fusion | flops 151780864 | bytes 1741320 | tf_op jit(solution)/shard_map/while/body/eval_jaxpr/dot_general | solution.py:45
  89.3 2.3 %collective-permute-done.1 = f32[128,1152]{1,0:T(8,128)S(1)} collective-permute-done((f32[128,1152]{1,0:T(8,128)}, f32[128,1152]{1,0:T(8,128)S(1)}, u32[]{:S(2)}, u32[]{:S(2)}) %collective-permute-start.1) | collective-permute-done | bytes 589856 | tf_op jit(solution)/shard_map/while/body/eval_jaxpr/ppermute | solution.py:12
  92.8 7.2 %collective-permute-done = bf16[128,1152]{1,0:T(8,128)(2,1)S(1)} collective-permute-done((bf16[128,1152]{1,0:T(8,128)(2,1)}, bf16[128,1152]{1,0:T(8,128)(2,1)S(1)}, u32[]{:S(2)}, u32[]{:S(2)}) %collective-permute-start) | collective-permute-done | bytes 294944 | tf_op jit(solution)/shard_map/while/body/eval_jaxpr/ppermute | solution.py:12
  100.1 2.6 %fusion.53 = (f32[512]{0:T(512)S(1)}, f32[512,128]{0,1:T(8,128)S(1)}) fusion(s32[512]{0:T(512)S(1)} %iota_add_fusion.6, s32[128]{0:T(128)S(1)} %iota_add_fusion.7, f32[]{:T(128)} %get-tuple-element.436, bf16[512,1152]{1,0:T(8,128)(2,1)} %get-tuple-element.435, bf16[128,1152]{1,0:T(8,128)(2,1)S(1)} %collective-permute-done, f32[]{:T(128)} %get-tuple-element.434), kind=kOutput, calls=%fused_computation.11.clone.1 | convolution fusion | flops 151780864 | bytes 1741320 | tf_op jit(solution)/shard_map/while/body/eval_jaxpr/dot_general | solution.py:45
  104.1 2.3 %collective-permute-done.1 = f32[128,1152]{1,0:T(8,128)S(1)} collective-permute-done((f32[128,1152]{1,0:T(8,128)}, f32[128,1152]{1,0:T(8,128)S(1)}, u32[]{:S(2)}, u32[]{:S(2)}) %collective-permute-start.1) | collective-permute-done | bytes 589856 | tf_op jit(solution)/shard_map/while/body/eval_jaxpr/ppermute | solution.py:12
  107.6 7.2 %collective-permute-done = bf16[128,1152]{1,0:T(8,128)(2,1)S(1)} collective-permute-done((bf16[128,1152]{1,0:T(8,128)(2,1)}, bf16[128,1152]{1,0:T(8,128)(2,1)S(1)}, u32[]{:S(2)}, u32[]{:S(2)}) %collective-permute-start) | collective-permute-done | bytes 294944 | tf_op jit(solution)/shard_map/while/body/eval_jaxpr/ppermute | solution.py:12
  114.9 2.6 %fusion.53 = (f32[512]{0:T(512)S(1)}, f32[512,128]{0,1:T(8,128)S(1)}) fusion(s32[512]{0:T(512)S(1)} %iota_add_fusion.6, s32[128]{0:T(128)S(1)} %iota_add_fusion.7, f32[]{:T(128)} %get-tuple-element.436, bf16[512,1152]{1,0:T(8,128)(2,1)} %get-tuple-element.435, bf16[128,1152]{1,0:T(8,128)(2,1)S(1)} %collective-permute-done, f32[]{:T(128)} %get-tuple-element.434), kind=kOutput, calls=%fused_computation.11.clone.1 | convolution fusion | flops 151780864 | bytes 1741320 | tf_op jit(solution)/shard_map/while/body/eval_jaxpr/dot_general | solution.py:45
  118.9 2.3 %collective-permute-done.1 = f32[128,1152]{1,0:T(8,128)S(1)} collective-permute-done((f32[128,1152]{1,0:T(8,128)}, f32[128,1152]{1,0:T(8,128)S(1)}, u32[]{:S(2)}, u32[]{:S(2)}) %collective-permute-start.1) | collective-permute-done | bytes 589856 | tf_op jit(solution)/shard_map/while/body/eval_jaxpr/ppermute | solution.py:12
  122.4 7.2 %collective-permute-done = bf16[128,1152]{1,0:T(8,128)(2,1)S(1)} collective-permute-done((bf16[128,1152]{1,0:T(8,128)(2,1)}, bf16[128,1152]{1,0:T(8,128)(2,1)S(1)}, u32[]{:S(2)}, u32[]{:S(2)}) %collective-permute-start) | collective-permute-done | bytes 294944 | tf_op jit(solution)/shard_map/while/body/eval_jaxpr/ppermute | solution.py:12
  129.7 2.6 %fusion.53 = (f32[512]{0:T(512)S(1)}, f32[512,128]{0,1:T(8,128)S(1)}) fusion(s32[512]{0:T(512)S(1)} %iota_add_fusion.6, s32[128]{0:T(128)S(1)} %iota_add_fusion.7, f32[]{:T(128)} %get-tuple-element.436, bf16[512,1152]{1,0:T(8,128)(2,1)} %get-tuple-element.435, bf16[128,1152]{1,0:T(8,128)(2,1)S(1)} %collective-permute-done, f32[]{:T(128)} %get-tuple-element.434), kind=kOutput, calls=%fused_computation.11.clone.1 | convolution fusion | flops 151780864 | bytes 1741320 | tf_op jit(solution)/shard_map/while/body/eval_jaxpr/dot_general | solution.py:45
  133.7 2.3 %collective-permute-done.1 = f32[128,1152]{1,0:T(8,128)S(1)} collective-permute-done((f32[128,1152]{1,0:T(8,128)}, f32[128,1152]{1,0:T(8,128)S(1)}, u32[]{:S(2)}, u32[]{:S(2)}) %collective-permute-start.1) | collective-permute-done | bytes 589856 | tf_op jit(solution)/shard_map/while/body/eval_jaxpr/ppermute | solution.py:12
  137.3 7.2 %collective-permute-done = bf16[128,1152]{1,0:T(8,128)(2,1)S(1)} collective-permute-done((bf16[128,1152]{1,0:T(8,128)(2,1)}, bf16[128,1152]{1,0:T(8,128)(2,1)S(1)}, u32[]{:S(2)}, u32[]{:S(2)}) %collective-permute-start) | collective-permute-done | bytes 294944 | tf_op jit(solution)/shard_map/while/body/eval_jaxpr/ppermute | solution.py:12
  144.5 2.6 %fusion.53 = (f32[512]{0:T(512)S(1)}, f32[512,128]{0,1:T(8,128)S(1)}) fusion(s32[512]{0:T(512)S(1)} %iota_add_fusion.6, s32[128]{0:T(128)S(1)} %iota_add_fusion.7, f32[]{:T(128)} %get-tuple-element.436, bf16[512,1152]{1,0:T(8,128)(2,1)} %get-tuple-element.435, bf16[128,1152]{1,0:T(8,128)(2,1)S(1)} %collective-permute-done, f32[]{:T(128)} %get-tuple-element.434), kind=kOutput, calls=%fused_computation.11.clone.1 | convolution fusion | flops 151780864 | bytes 1741320 | tf_op jit(solution)/shard_map/while/body/eval_jaxpr/dot_general | solution.py:45
  148.5 2.3 %collective-permute-done.1 = f32[128,1152]{1,0:T(8,128)S(1)} collective-permute-done((f32[128,1152]{1,0:T(8,128)}, f32[128,1152]{1,0:T(8,128)S(1)}, u32[]{:S(2)}, u32[]{:S(2)}) %collective-permute-start.1) | collective-permute-done | bytes 589856 | tf_op jit(solution)/shard_map/while/body/eval_jaxpr/ppermute | solution.py:12
  154.8 10.1 %all-reduce = f32[512]{0:T(512)S(1)} all-reduce(f32[512]{0:T(512)S(1)} %get-tuple-element.272), channel_id=3, replica_groups=mesh['dp'=8,'inner'=4] {'inner'}, use_global_device_ids=true, to_apply=%region_9.10.clone | all-reduce | flops 512 | bytes 4096
  166.8 33.0 %reduce-scatter.2.cloned.1.call-done = f32[128,1152]{1,0:T(8,128)} async-done(((f32[512,1152]{1,0:T(8,128)}), f32[128,1152]{1,0:T(8,128)}) %reduce-scatter.2.cloned.1.call-update) | async-done | bytes 589840 | tf_op jit(solution)/shard_map/reduce_scatter | solution.py:77
  (108 shorter events, 38.6 us)
Async XLA Ops:
  7.2 4.4 %copy-start.3 = (bf16[128,1152]{1,0:T(8,128)(2,1)S(1)}, bf16[128,1152]{1,0:T(8,128)(2,1)}, u32[]{:S(2)}) copy-start(bf16[128,1152]{1,0:T(8,128)(2,1)} %param.7) | copy-start | bytes 884740
  7.2 36.3 %all-gather.2.cloned.1.call-start = ((), (), s32[]{:S(2)}) async-start(), calls=%async_computation.1 | async-start | bytes 1474560 | tf_op jit(solution)/shard_map/all_gather | solution.py:35
  10.2 189.7 %reduce-scatter.2.cloned.1.call-start = ((), (), s32[]{:S(2)}) async-start(), calls=%async_computation.2 | async-start | bytes 2949120 | tf_op jit(solution)/shard_map/reduce_scatter | solution.py:77
  48.4 7.3 %collective-permute-start = (bf16[128,1152]{1,0:T(8,128)(2,1)}, bf16[128,1152]{1,0:T(8,128)(2,1)S(1)}, u32[]{:S(2)}, u32[]{:S(2)}) collective-permute-start(bf16[128,1152]{1,0:T(8,128)(2,1)} %get-tuple-element.413), channel_id=1, source_target_pairs={{0,4},{4,8},{8,12},{12,16},{16,20},{20,24},{24,28},{28,0},{1,5},{5... | collective-permute-start | bytes 884744 | tf_op jit(solution)/shard_map/while/body/eval_jaxpr/ppermute | solution.py:12
  48.4 13.6 %collective-permute-start.1 = (f32[128,1152]{1,0:T(8,128)}, f32[128,1152]{1,0:T(8,128)S(1)}, u32[]{:S(2)}, u32[]{:S(2)}) collective-permute-start(f32[128,1152]{1,0:T(8,128)} %get-tuple-element.414), channel_id=1, source_target_pairs={{0,4},{4,8},{8,12},{12,16},{16,20},{20,24},{24,28},{28,0},{1,5},{5... | collective-permute-start | bytes 1769480 | tf_op jit(solution)/shard_map/while/body/eval_jaxpr/ppermute | solution.py:12
  63.2 7.3 %collective-permute-start = (bf16[128,1152]{1,0:T(8,128)(2,1)}, bf16[128,1152]{1,0:T(8,128)(2,1)S(1)}, u32[]{:S(2)}, u32[]{:S(2)}) collective-permute-start(bf16[128,1152]{1,0:T(8,128)(2,1)} %get-tuple-element.413), channel_id=1, source_target_pairs={{0,4},{4,8},{8,12},{12,16},{16,20},{20,24},{24,28},{28,0},{1,5},{5... | collective-permute-start | bytes 884744 | tf_op jit(solution)/shard_map/while/body/eval_jaxpr/ppermute | solution.py:12
  63.2 13.6 %collective-permute-start.1 = (f32[128,1152]{1,0:T(8,128)}, f32[128,1152]{1,0:T(8,128)S(1)}, u32[]{:S(2)}, u32[]{:S(2)}) collective-permute-start(f32[128,1152]{1,0:T(8,128)} %get-tuple-element.414), channel_id=1, source_target_pairs={{0,4},{4,8},{8,12},{12,16},{16,20},{20,24},{24,28},{28,0},{1,5},{5... | collective-permute-start | bytes 1769480 | tf_op jit(solution)/shard_map/while/body/eval_jaxpr/ppermute | solution.py:12
  78.0 7.3 %collective-permute-start = (bf16[128,1152]{1,0:T(8,128)(2,1)}, bf16[128,1152]{1,0:T(8,128)(2,1)S(1)}, u32[]{:S(2)}, u32[]{:S(2)}) collective-permute-start(bf16[128,1152]{1,0:T(8,128)(2,1)} %get-tuple-element.413), channel_id=1, source_target_pairs={{0,4},{4,8},{8,12},{12,16},{16,20},{20,24},{24,28},{28,0},{1,5},{5... | collective-permute-start | bytes 884744 | tf_op jit(solution)/shard_map/while/body/eval_jaxpr/ppermute | solution.py:12
  78.0 13.6 %collective-permute-start.1 = (f32[128,1152]{1,0:T(8,128)}, f32[128,1152]{1,0:T(8,128)S(1)}, u32[]{:S(2)}, u32[]{:S(2)}) collective-permute-start(f32[128,1152]{1,0:T(8,128)} %get-tuple-element.414), channel_id=1, source_target_pairs={{0,4},{4,8},{8,12},{12,16},{16,20},{20,24},{24,28},{28,0},{1,5},{5... | collective-permute-start | bytes 1769480 | tf_op jit(solution)/shard_map/while/body/eval_jaxpr/ppermute | solution.py:12
  88.6 3.0 %copy-start.2 = (bf16[512,1152]{1,0:T(8,128)(2,1)S(1)}, bf16[512,1152]{1,0:T(8,128)(2,1)}, u32[]{:S(2)}) copy-start(bf16[512,1152]{1,0:T(8,128)(2,1)} %get-tuple-element.435) | copy-start | bytes 3538948 | tf_op jit(solution)/shard_map/while
  92.8 7.3 %collective-permute-start = (bf16[128,1152]{1,0:T(8,128)(2,1)}, bf16[128,1152]{1,0:T(8,128)(2,1)S(1)}, u32[]{:S(2)}, u32[]{:S(2)}) collective-permute-start(bf16[128,1152]{1,0:T(8,128)(2,1)} %get-tuple-element.413), channel_id=1, source_target_pairs={{0,4},{4,8},{8,12},{12,16},{16,20},{20,24},{24,28},{28,0},{1,5},{5... | collective-permute-start | bytes 884744 | tf_op jit(solution)/shard_map/while/body/eval_jaxpr/ppermute | solution.py:12
  92.8 13.6 %collective-permute-start.1 = (f32[128,1152]{1,0:T(8,128)}, f32[128,1152]{1,0:T(8,128)S(1)}, u32[]{:S(2)}, u32[]{:S(2)}) collective-permute-start(f32[128,1152]{1,0:T(8,128)} %get-tuple-element.414), channel_id=1, source_target_pairs={{0,4},{4,8},{8,12},{12,16},{16,20},{20,24},{24,28},{28,0},{1,5},{5... | collective-permute-start | bytes 1769480 | tf_op jit(solution)/shard_map/while/body/eval_jaxpr/ppermute | solution.py:12
  103.4 3.0 %copy-start.2 = (bf16[512,1152]{1,0:T(8,128)(2,1)S(1)}, bf16[512,1152]{1,0:T(8,128)(2,1)}, u32[]{:S(2)}) copy-start(bf16[512,1152]{1,0:T(8,128)(2,1)} %get-tuple-element.435) | copy-start | bytes 3538948 | tf_op jit(solution)/shard_map/while
  107.6 7.3 %collective-permute-start = (bf16[128,1152]{1,0:T(8,128)(2,1)}, bf16[128,1152]{1,0:T(8,128)(2,1)S(1)}, u32[]{:S(2)}, u32[]{:S(2)}) collective-permute-start(bf16[128,1152]{1,0:T(8,128)(2,1)} %get-tuple-element.413), channel_id=1, source_target_pairs={{0,4},{4,8},{8,12},{12,16},{16,20},{20,24},{24,28},{28,0},{1,5},{5... | collective-permute-start | bytes 884744 | tf_op jit(solution)/shard_map/while/body/eval_jaxpr/ppermute | solution.py:12
  107.6 13.6 %collective-permute-start.1 = (f32[128,1152]{1,0:T(8,128)}, f32[128,1152]{1,0:T(8,128)S(1)}, u32[]{:S(2)}, u32[]{:S(2)}) collective-permute-start(f32[128,1152]{1,0:T(8,128)} %get-tuple-element.414), channel_id=1, source_target_pairs={{0,4},{4,8},{8,12},{12,16},{16,20},{20,24},{24,28},{28,0},{1,5},{5... | collective-permute-start | bytes 1769480 | tf_op jit(solution)/shard_map/while/body/eval_jaxpr/ppermute | solution.py:12
  118.2 3.0 %copy-start.2 = (bf16[512,1152]{1,0:T(8,128)(2,1)S(1)}, bf16[512,1152]{1,0:T(8,128)(2,1)}, u32[]{:S(2)}) copy-start(bf16[512,1152]{1,0:T(8,128)(2,1)} %get-tuple-element.435) | copy-start | bytes 3538948 | tf_op jit(solution)/shard_map/while
  122.4 7.3 %collective-permute-start = (bf16[128,1152]{1,0:T(8,128)(2,1)}, bf16[128,1152]{1,0:T(8,128)(2,1)S(1)}, u32[]{:S(2)}, u32[]{:S(2)}) collective-permute-start(bf16[128,1152]{1,0:T(8,128)(2,1)} %get-tuple-element.413), channel_id=1, source_target_pairs={{0,4},{4,8},{8,12},{12,16},{16,20},{20,24},{24,28},{28,0},{1,5},{5... | collective-permute-start | bytes 884744 | tf_op jit(solution)/shard_map/while/body/eval_jaxpr/ppermute | solution.py:12
  122.4 13.6 %collective-permute-start.1 = (f32[128,1152]{1,0:T(8,128)}, f32[128,1152]{1,0:T(8,128)S(1)}, u32[]{:S(2)}, u32[]{:S(2)}) collective-permute-start(f32[128,1152]{1,0:T(8,128)} %get-tuple-element.414), channel_id=1, source_target_pairs={{0,4},{4,8},{8,12},{12,16},{16,20},{20,24},{24,28},{28,0},{1,5},{5... | collective-permute-start | bytes 1769480 | tf_op jit(solution)/shard_map/while/body/eval_jaxpr/ppermute | solution.py:12
  133.0 3.0 %copy-start.2 = (bf16[512,1152]{1,0:T(8,128)(2,1)S(1)}, bf16[512,1152]{1,0:T(8,128)(2,1)}, u32[]{:S(2)}) copy-start(bf16[512,1152]{1,0:T(8,128)(2,1)} %get-tuple-element.435) | copy-start | bytes 3538948 | tf_op jit(solution)/shard_map/while
  137.2 7.3 %collective-permute-start = (bf16[128,1152]{1,0:T(8,128)(2,1)}, bf16[128,1152]{1,0:T(8,128)(2,1)S(1)}, u32[]{:S(2)}, u32[]{:S(2)}) collective-permute-start(bf16[128,1152]{1,0:T(8,128)(2,1)} %get-tuple-element.413), channel_id=1, source_target_pairs={{0,4},{4,8},{8,12},{12,16},{16,20},{20,24},{24,28},{28,0},{1,5},{5... | collective-permute-start | bytes 884744 | tf_op jit(solution)/shard_map/while/body/eval_jaxpr/ppermute | solution.py:12
  137.2 13.6 %collective-permute-start.1 = (f32[128,1152]{1,0:T(8,128)}, f32[128,1152]{1,0:T(8,128)S(1)}, u32[]{:S(2)}, u32[]{:S(2)}) collective-permute-start(f32[128,1152]{1,0:T(8,128)} %get-tuple-element.414), channel_id=1, source_target_pairs={{0,4},{4,8},{8,12},{12,16},{16,20},{20,24},{24,28},{28,0},{1,5},{5... | collective-permute-start | bytes 1769480 | tf_op jit(solution)/shard_map/while/body/eval_jaxpr/ppermute | solution.py:12
  147.8 3.0 %copy-start.2 = (bf16[512,1152]{1,0:T(8,128)(2,1)S(1)}, bf16[512,1152]{1,0:T(8,128)(2,1)}, u32[]{:S(2)}) copy-start(bf16[512,1152]{1,0:T(8,128)(2,1)} %get-tuple-element.435) | copy-start | bytes 3538948 | tf_op jit(solution)/shard_map/while
  153.5 12.0 %collective-permute-start.2 = (f32[128,1152]{1,0:T(8,128)S(1)}, f32[128,1152]{1,0:T(8,128)S(1)}, u32[]{:S(2)}, u32[]{:S(2)}) collective-permute-start(f32[128,1152]{1,0:T(8,128)S(1)} %copy-done.6), channel_id=1, source_target_pairs={{0,4},{4,8},{8,12},{12,16},{16,20},{20,24},{24,28},{28,0},{1,5},{5... | collective-permute-start | bytes 1769480 | tf_op jit(solution)/shard_map/ppermute | solution.py:12
  165.5 34.3 %copy-start.4 = (bf16[128,1152]{1,0:T(8,128)(2,1)S(1)}, bf16[128,1152]{1,0:T(8,128)(2,1)}, u32[]{:S(2)}) copy-start(bf16[128,1152]{1,0:T(8,128)(2,1)} %param.6) | copy-start | bytes 884740
  (7 other events, 13.4 us)
Sparse Core Ops, SparseCore 0:
  10.3 33.1 all-gather.1
  153.6 46.2 reduce-scatter.1
where the time goes:
time: 210 us; the launch traced here: 209 us
  waiting for transfers between devices  128 us (61%)
  matrix products  36.6 us (17%)
  between operations  16.1 us (8%)
  blocking collectives  10.1 us (5%)
  other arithmetic  8.34 us (4%)
  local copies, waits for them, and re-layouts  7.09 us (3%)
  starting transfers between devices  2.42 us (1%)
    ppermute x15, waiting for transfers between devices, passed_along(): return lax.ppermute(value, axis, pairs)  64.3 us
    reduce_scatter x1, waiting for transfers between devices, body(): lax.psum_scatter(image_total, 'inner', scatter_dimension=0, tiled=True)  33 us
    all_gather x1, waiting for transfers between devices, body(): images = lax.all_gather(image_emb, 'inner', axis=0, tiled=True)  30.9 us
    dot_general x8, matrix products, block_terms(): lax.dot_general(images, block, (((1,), (1,)), ((), ())), preferred_elemen...  20.2 us
    unnamed x1, blocking collectives  10.1 us
    dot_general x8, matrix products, block_terms(): lax.dot_general(slopes, images, (((0,), (0,)), ((), ())), preferred_eleme...  9.84 us
    dot_general x8, matrix products, block_terms(): image_part = jnp.dot(slopes, block, preferred_element_type=jnp.float32)  6.57 us
    while x21, local copies, waits for them, and re-layouts  5.04 us
  transfers between devices with their start and end apart: 17, of which 16 were waited for; matrix products, arithmetic and copies ran while one was open for 15% of the time, Pallas kernels for 0%

commit v1 on v0

v1 whole, which is shorter than its diff:
```python
import functools

import jax
import jax.numpy as jnp
from jax import lax
from jax.experimental import pallas as pl
from jax.experimental.pallas import tpu as pltpu
from jax.sharding import PartitionSpec as P

epsilon = 1e-06
f32, bf16 = jnp.float32, jnp.bfloat16
lanes = 128
extra = 16
VMEM = pl.BlockSpec(memory_space=pltpu.VMEM)
SMEM = pl.BlockSpec(memory_space=pltpu.SMEM)


def swapped(value, axis, step):
    return lax.ppermute(value, axis, [(place, place ^ step) for place in range(lax.axis_size(axis))])


def call(kernel, out_shape, *operands, flops=0, in_specs=None):
    moved = sum(o.size * o.dtype.itemsize for o in operands)
    moved += sum(o.size * o.dtype.itemsize for o in jax.tree.leaves(out_shape))
    return pl.pallas_call(
        kernel,
        out_shape=out_shape,
        in_specs=in_specs or [VMEM] * len(operands),
        out_specs=jax.tree.map(lambda _: VMEM, out_shape),
        compiler_params=pltpu.CompilerParams(vmem_limit_bytes=40 * 1024 * 1024),
        cost_estimate=pl.CostEstimate(flops=flops, bytes_accessed=moved, transcendentals=0),
    )(*operands)


def shape(dims, kind):
    return jax.ShapeDtypeStruct(dims, kind)


def unit_of(rows):
    wide = rows.astype(f32)
    inverse = lax.rsqrt(jnp.sum(wide * wide, axis=-1, keepdims=True) + epsilon)
    return wide * inverse, inverse


def pair_terms(scale, offset, texts, image_emb, slopes_ref, own):
    rows = image_emb.shape[0]
    total = jnp.zeros((1, rows), f32)
    step = 256
    for start in range(0, texts.shape[0], step):
        logits = (
            scale
            * lax.dot_general(
                texts[start : start + step, :],
                image_emb,
                (((1,), (1,)), ((), ())),
                preferred_element_type=f32,
            )
            + offset
        )
        shrunk = jnp.exp(-jnp.abs(logits))
        softplus = jnp.maximum(logits, 0.0) + jnp.log1p(shrunk)
        sigmoid = jnp.where(logits >= 0.0, 1.0, shrunk) / (1.0 + shrunk)
        if own and start == 0:
            text_ids = lax.broadcasted_iota(jnp.int32, logits.shape, 0)
            image_ids = lax.broadcasted_iota(jnp.int32, logits.shape, 1)
            match = (text_ids == image_ids).astype(f32)
            softplus = softplus - match * logits
            sigmoid = sigmoid - match
        slopes_ref[start : start + step, :] = sigmoid.astype(bf16)
        total = total + jnp.sum(softplus, axis=0, keepdims=True)
    return total


def image_sums(slopes_ref, texts_ref):
    return lax.dot_general(
        slopes_ref[...], texts_ref[...], (((0,), (0,)), ((), ())), preferred_element_type=f32
    )


def own_kernel(count, scale_ref, bias_ref, image_ref, *refs):
    raw_refs = refs[:count]
    texts_ref, slopes_ref, emb_ref, grad_ref, loss_ref = refs[count:]
    rows = image_ref.shape[0]
    for place, raw in enumerate(raw_refs):
        texts_ref[place * rows : (place + 1) * rows, :] = unit_of(raw[...])[0].astype(bf16)
    emb_ref[...] = unit_of(image_ref[...])[0].astype(bf16)
    loss_ref[...] = pair_terms(
        scale_ref[0], bias_ref[0], texts_ref, emb_ref[...], slopes_ref, True
    )
    grad_ref[...] = image_sums(slopes_ref, texts_ref)


def peer_kernel(scale_ref, bias_ref, image_ref, texts_ref, slopes_ref, emb_ref, sent_ref):
    rows, width = image_ref.shape
    emb_ref[...] = unit_of(image_ref[...])[0].astype(bf16)
    loss = pair_terms(scale_ref[0], bias_ref[0], texts_ref, emb_ref[...], slopes_ref, False)
    sums = image_sums(slopes_ref, texts_ref)
    for panel in range(width // lanes):
        sent_ref[panel * rows : (panel + 1) * rows, :] = sums[
            :, panel * lanes : (panel + 1) * lanes
        ].astype(bf16)
    high = loss.astype(bf16).astype(f32)
    which = lax.broadcasted_iota(jnp.int32, (extra, rows), 0)
    sent_ref[width // lanes * rows :, :] = jnp.where(which == 0, high, loss - high).astype(bf16)


def text_sums(slopes, embs, place, rows):
    left = jnp.concatenate([s[place * rows : (place + 1) * rows, :] for s in slopes], axis=1)
    return jnp.dot(left, embs, preferred_element_type=f32)


def other_core_kernel(count, *refs):
    slopes, emb_refs, sent_ref = refs[:count], refs[count : 2 * count], refs[2 * count]
    rows = emb_refs[0].shape[0]
    embs = jnp.concatenate([e[...] for e in emb_refs], axis=0)
    for k in range(slopes[0].shape[0] // rows // 2):
        sent_ref[k * rows : (k + 1) * rows, :] = text_sums(slopes, embs, 2 * k + 1, rows).astype(bf16)


def own_core_kernel(count, received_ref, *refs):
    slopes, emb_refs = refs[:count], refs[count : 2 * count]
    own_ref, sent_refs = refs[2 * count], refs[2 * count + 1 :]
    rows = emb_refs[0].shape[0]
    embs = jnp.concatenate([e[...] for e in emb_refs], axis=0)
    for k, out in enumerate((own_ref, *sent_refs)):
        sums = text_sums(slopes, embs, 2 * k, rows) + received_ref[k * rows : (k + 1) * rows, :].astype(f32)
        out[...] = sums.astype(out.dtype)


def row_gradient(rows, sums, scale, out_ref):
    unit_rows, inverse = unit_of(rows)
    unit_grad = scale * sums
    out_ref[...] = (
        unit_grad - unit_rows * jnp.sum(unit_rows * unit_grad, axis=-1, keepdims=True)
    ) * inverse


def image_end_kernel(batch, scale_ref, image_ref, grad_ref, loss_ref, *refs):
    received, out_ref, out_loss_ref, sums_ref = refs[:-3], refs[-3], refs[-2], refs[-1]
    rows, width = image_ref.shape
    for panel in range(width // lanes):
        cut = slice(panel * lanes, (panel + 1) * lanes)
        sums = grad_ref[:, cut]
        for r in received:
            sums = sums + r[panel * rows : (panel + 1) * rows, :].astype(f32)
        sums_ref[:, cut] = sums
    loss = loss_ref[...]
    for r in received:
        tail = r[width // lanes * rows :, :].astype(f32)
        loss = loss + (tail[0:1, :] + tail[1:2, :])
    row_gradient(image_ref[...], sums_ref[...], scale_ref[0], out_ref)
    out_loss_ref[...] = loss / batch


def text_end_kernel(scale_ref, text_ref, grad_ref, *refs):
    received, out_ref = refs[:-1], refs[-1]
    sums = grad_ref[...]
    for r in received:
        sums = sums + r[...].astype(f32)
    row_gradient(text_ref[...], sums, scale_ref[0], out_ref)


def body(image, text, logarithm_scale, bias):
    rows, width = image.shape
    dp_count, inner_count = lax.axis_size("dp"), lax.axis_size("inner")
    batch = rows * dp_count * inner_count
    texts_held = rows * dp_count
    scale = jnp.exp(logarithm_scale)
    block = shape((rows, width), bf16)
    block_flops = 2 * rows * texts_held * width

    images = {r: swapped(image, "inner", r) for r in reversed(range(1, inner_count))}
    texts = [text, swapped(text, "dp", 1)]
    for s in range(2, dp_count, 2):
        fetched = swapped(text, "dp", s)
        texts += [fetched, swapped(fetched, "dp", 1)]

    text_embs, slopes, emb, image_grad, loss = call(
        functools.partial(own_kernel, dp_count),
        (
            shape((texts_held, width), bf16),
            shape((texts_held, rows), bf16),
            block,
            shape((rows, width), f32),
            shape((1, rows), f32),
        ),
        scale,
        bias,
        image,
        *texts,
        flops=2 * block_flops,
        in_specs=[SMEM, SMEM] + [VMEM] * (1 + dp_count),
    )
    all_slopes, embs, image_parts = [slopes], [emb], []
    for r, peer_image in images.items():
        slopes, emb, sent = call(
            peer_kernel,
            (
                shape((texts_held, rows), bf16),
                block,
                shape((width // lanes * rows + extra, lanes), bf16),
            ),
            scale,
            bias,
            peer_image,
            text_embs,
            flops=2 * block_flops,
            in_specs=[SMEM, SMEM, VMEM, VMEM],
        )
        all_slopes.append(slopes)
        embs.append(emb)
        image_parts.append(swapped(sent, "inner", r))

    crossing = call(
        functools.partial(other_core_kernel, inner_count),
        shape((texts_held // 2, width), bf16),
        *all_slopes,
        *embs,
        flops=inner_count * block_flops // 2,
    )
    crossed = swapped(crossing, "dp", 1)
    text_grad, *text_sent = call(
        functools.partial(own_core_kernel, inner_count),
        (shape((rows, width), f32),) + (block,) * (dp_count // 2 - 1),
        crossed,
        *all_slopes,
        *embs,
        flops=inner_count * block_flops // 2,
    )
    text_parts = [swapped(part, "dp", 2 * k + 2) for k, part in enumerate(text_sent)]

    image_gradient, image_loss = pl.pallas_call(
        functools.partial(image_end_kernel, batch),
        out_shape=(shape((rows, width), f32), shape((1, rows), f32)),
        in_specs=[SMEM] + [VMEM] * (3 + len(image_parts)),
        out_specs=(VMEM, VMEM),
        scratch_shapes=[pltpu.VMEM((rows, width), f32)],
        compiler_params=pltpu.CompilerParams(vmem_limit_bytes=40 * 1024 * 1024),
    )(scale, image, image_grad, loss, *image_parts)
    text_gradient = call(
        text_end_kernel,
        shape((rows, width), f32),
        scale,
        text,
        text_grad,
        *text_parts,
        in_specs=[SMEM] + [VMEM] * (2 + len(text_parts)),
    )
    return (image_gradient, text_gradient, image_loss.reshape(rows))


def solution(mesh):
    return jax.shard_map(
        body,
        mesh=mesh,
        in_specs=(P(("dp", "inner"), None), P(("dp", "inner"), None), P(), P()),
        out_specs=(P(("dp", "inner"), None), P(("dp", "inner"), None), P(("dp", "inner"))),
        check_vma=False,
    )
```

time: 210 us -> 80.4 us (0.38)
  the two profiles are of different devices: /device:TPU:0 before, /device:TPU:9 now
where the time goes in v1:
time: 80.4 us; the launch traced here: 80.2 us
  waiting for transfers between devices  42.6 us (53%)
  starting transfers between devices  22.6 us (28%)
  Pallas kernels  11 us (14%)
  between operations  2.07 us (3%)
  local copies, waits for them, and re-layouts  1.93 us (2%)
    ppermute x17, waiting for transfers between devices, swapped(): lax.ppermute(value, axis, [(place, place ^ step) for place in range(lax.a...  42.6 us
    ppermute x17, starting transfers between devices, swapped(): lax.ppermute(value, axis, [(place, place ^ step) for place in range(lax.a...  22.6 us
    pallas_call x7, Pallas kernels, call(): pl.pallas_call(kernel, out_shape=out_shape, in_specs=in_specs or [VMEM] *...  9.78 us
    unnamed x8, local copies, waits for them, and re-layouts  1.93 us
  transfers between devices with their start and end apart: 17, of which 6 were waited for; matrix products, arithmetic and copies ran while one was open for 0% of the time, Pallas kernels for 9%

profile of v1, /device:TPU:9, one launch (start us, length us, event | category | flops | bytes accessed | tf_op | source)
XLA Modules:
  0.0 80.2 jit_solution(13310952890514156568)
XLA Ops:
  0.6 1.3 %collective-permute-start.1 = (bf16[128,1152]{1,0:T(8,128)(2,1)}, bf16[128,1152]{1,0:T(8,128)(2,1)S(1)}, u32[]{:S(2)}, u32[]{:S(2)}) collective-permute-start(bf16[128,1152]{1,0:T(8,128)(2,1)} %text_ref.1), channel_id=1, source_target_pairs={{0,8},{4,12},{8,0},{12,4},{16,24},{20,28},{24,16},{28,20},{1,9},{5... | collective-permute-start | bytes 884744 | tf_op jit(solution)/shard_map/ppermute | solution.py:19
  1.9 1.2 %collective-permute-start.3 = (bf16[128,1152]{1,0:T(8,128)(2,1)}, bf16[128,1152]{1,0:T(8,128)(2,1)S(1)}, u32[]{:S(2)}, u32[]{:S(2)}) collective-permute-start(bf16[128,1152]{1,0:T(8,128)(2,1)} %text_ref.1), channel_id=1, source_target_pairs={{0,16},{4,20},{8,24},{12,28},{16,0},{20,4},{24,8},{28,12},{1,17},{... | collective-permute-start | bytes 884744 | tf_op jit(solution)/shard_map/ppermute | solution.py:19
  3.3 1.5 %collective-permute-start = (bf16[128,1152]{1,0:T(8,128)(2,1)}, bf16[128,1152]{1,0:T(8,128)(2,1)S(1)}, u32[]{:S(2)}, u32[]{:S(2)}) collective-permute-start(bf16[128,1152]{1,0:T(8,128)(2,1)} %text_ref.1), channel_id=1, source_target_pairs={{0,4},{4,0},{8,12},{12,8},{16,20},{20,16},{24,28},{28,24},{1,5},{5... | collective-permute-start | bytes 884744 | tf_op jit(solution)/shard_map/ppermute | solution.py:19
  4.9 3.9 %collective-permute-done.1.refs_2_ = bf16[128,1152]{1,0:T(8,128)(2,1)S(1)} collective-permute-done((bf16[128,1152]{1,0:T(8,128)(2,1)}, bf16[128,1152]{1,0:T(8,128)(2,1)S(1)}, u32[]{:S(2)}, u32[]{:S(2)}) %collective-permute-start.1) | collective-permute-done | bytes 294944 | tf_op jit(solution)/shard_map/ppermute | solution.py:19
  8.8 2.7 %collective-permute-start.2 = (bf16[128,1152]{1,0:T(8,128)(2,1)S(1)}, bf16[128,1152]{1,0:T(8,128)(2,1)S(1)}, u32[]{:S(2)}, u32[]{:S(2)}) collective-permute-start(bf16[128,1152]{1,0:T(8,128)(2,1)S(1)} %collective-permute-done.1.refs_2_), channel_id=1, source_target_pairs={{0,4},{4,0},{8,12},{12,8},{16,20},{20,16},{24,28},{28,24},{1,5},{5... | collective-permute-start | bytes 884744 | tf_op jit(solution)/shard_map/ppermute | solution.py:19
  11.5 6.4 %collective-permute-start.4 = (bf16[128,1152]{1,0:T(8,128)(2,1)S(1)}, bf16[128,1152]{1,0:T(8,128)(2,1)S(1)}, u32[]{:S(2)}, u32[]{:S(2)}) collective-permute-start(bf16[128,1152]{1,0:T(8,128)(2,1)S(1)} %collective-permute-done.3.refs_4_), channel_id=1, source_target_pairs={{0,4},{4,0},{8,12},{12,8},{16,20},{20,16},{24,28},{28,24},{1,5},{5... | collective-permute-start | bytes 884744 | tf_op jit(solution)/shard_map/ppermute | solution.py:19
  17.9 2.3 %collective-permute-start.9 = (bf16[128,1152]{1,0:T(8,128)(2,1)}, bf16[128,1152]{1,0:T(8,128)(2,1)S(1)}, u32[]{:S(2)}, u32[]{:S(2)}) collective-permute-start(bf16[128,1152]{1,0:T(8,128)(2,1)} %image_ref.3), channel_id=1, source_target_pairs={{0,2},{1,3},{2,0},{3,1},{4,6},{5,7},{6,4},{7,5},{8,10},{9,11},{10,... | collective-permute-start | bytes 884744 | tf_op jit(solution)/shard_map/ppermute | solution.py:19
  21.9 1.0 %copy-done = bf16[128,1152]{1,0:T(8,128)(2,1)S(1)} copy-done((bf16[128,1152]{1,0:T(8,128)(2,1)S(1)}, bf16[128,1152]{1,0:T(8,128)(2,1)}, u32[]{:S(2)}) %copy-start) | copy-done | bytes 294936
  22.9 1.0 %copy-done.2 = bf16[128,1152]{1,0:T(8,128)(2,1)S(1)} copy-done((bf16[128,1152]{1,0:T(8,128)(2,1)S(1)}, bf16[128,1152]{1,0:T(8,128)(2,1)}, u32[]{:S(2)}) %copy-start.2) | copy-done | bytes 294936
  23.8 2.1 %shard_map.67 = (bf16[1024,1152]{1,0:T(8,128)(2,1)S(1)}, bf16[1024,128]{1,0:T(8,128)(2,1)S(1)}, bf16[128,1152]{1,0:T(8,128)(2,1)S(1)}, f32[128,1152]{1,0:T(8,128)S(1)}, f32[1,128]{1,0:T(1,128)S(1)}) custom-call(f32[1]{0:T(128)S(6)} %exp.3.scale_ref, f32[1]{0:T(128)S(6)} %copy.8.bias_ref, bf16[128,1152]{1,0:T(8,128)(2,1)S(1)} %copy-done.2, ...), custom_call_target="tpu_custom_call" | custom-call | flops 603979776 | bytes 6160904 | tf_op jit(solution)/shard_map/pallas_call | solution.py:25
  26.0 7.8 %collective-permute-done.9.image_ref = bf16[128,1152]{1,0:T(8,128)(2,1)S(1)} collective-permute-done((bf16[128,1152]{1,0:T(8,128)(2,1)}, bf16[128,1152]{1,0:T(8,128)(2,1)S(1)}, u32[]{:S(2)}, u32[]{:S(2)}) %collective-permute-start.9) | collective-permute-done | bytes 294944 | tf_op jit(solution)/shard_map/ppermute | solution.py:19
  33.8 1.6 %shard_map.69 = (bf16[1024,128]{1,0:T(8,128)(2,1)S(1)}, bf16[128,1152]{1,0:T(8,128)(2,1)S(1)}, bf16[1168,128]{1,0:T(8,128)(2,1)S(1)}) custom-call(f32[1]{0:T(128)S(6)} %exp.3.scale_ref, f32[1]{0:T(128)S(6)} %copy.8.bias_ref, bf16[128,1152]{1,0:T(8,128)(2,1)S(1)} %collective-permute-done.9.image_ref, bf16[1024,1152]{1,0:T(8,128)(2,1)S(1)} %get-tuple-element.25.texts_ref), custom_call_target="tpu_custom_call" | custom-call | flops 603979776 | bytes 3510280 | tf_op jit(solution)/shard_map/pallas_call | solution.py:25
  35.4 1.6 %shard_map.70 = (bf16[1024,128]{1,0:T(8,128)(2,1)S(1)}, bf16[128,1152]{1,0:T(8,128)(2,1)S(1)}, bf16[1168,128]{1,0:T(8,128)(2,1)S(1)}) custom-call(f32[1]{0:T(128)S(6)} %exp.3.scale_ref, f32[1]{0:T(128)S(6)} %copy.8.bias_ref, bf16[128,1152]{1,0:T(8,128)(2,1)S(1)} %collective-permute-done.11.image_ref, bf16[1024,1152]{1,0:T(8,128)(2,1)S(1)} %get-tuple-element.25.texts_ref), custom_call_target="tpu_custom_call" | custom-call | flops 603979776 | bytes 3510280 | tf_op jit(solution)/shard_map/pallas_call | solution.py:25
  36.9 9.1 %collective-permute-done.7.image_ref = bf16[128,1152]{1,0:T(8,128)(2,1)S(1)} collective-permute-done((bf16[128,1152]{1,0:T(8,128)(2,1)}, bf16[128,1152]{1,0:T(8,128)(2,1)S(1)}, u32[]{:S(2)}, u32[]{:S(2)}) %collective-permute-start.7) | collective-permute-done | bytes 294944 | tf_op jit(solution)/shard_map/ppermute | solution.py:19
  46.1 1.6 %shard_map.68 = (bf16[1024,128]{1,0:T(8,128)(2,1)S(1)}, bf16[128,1152]{1,0:T(8,128)(2,1)S(1)}, bf16[1168,128]{1,0:T(8,128)(2,1)S(1)}) custom-call(f32[1]{0:T(128)S(6)} %exp.3.scale_ref, f32[1]{0:T(128)S(6)} %copy.8.bias_ref, bf16[128,1152]{1,0:T(8,128)(2,1)S(1)} %collective-permute-done.7.image_ref, bf16[1024,1152]{1,0:T(8,128)(2,1)S(1)} %get-tuple-element.25.texts_ref), custom_call_target="tpu_custom_call" | custom-call | flops 603979776 | bytes 3510280 | tf_op jit(solution)/shard_map/pallas_call | solution.py:25
  49.1 3.3 %collective-permute-start.12 = (bf16[1168,128]{1,0:T(8,128)(2,1)S(1)}, bf16[1168,128]{1,0:T(8,128)(2,1)S(1)}, u32[]{:S(2)}, u32[]{:S(2)}) collective-permute-start(bf16[1168,128]{1,0:T(8,128)(2,1)S(1)} %get-tuple-element.28), channel_id=1, source_target_pairs={{0,1},{1,0},{2,3},{3,2},{4,5},{5,4},{6,7},{7,6},{8,9},{9,8},{10,11... | collective-permute-start | bytes 897032 | tf_op jit(solution)/shard_map/ppermute | solution.py:19
  52.4 0.9 %shard_map.73 = (f32[128,1152]{1,0:T(8,128)S(1)}, bf16[128,1152]{1,0:T(8,128)(2,1)S(1)}, bf16[128,1152]{1,0:T(8,128)(2,1)S(1)}, bf16[128,1152]{1,0:T(8,128)(2,1)S(1)}) custom-call(bf16[512,1152]{1,0:T(8,128)(2,1)S(1)} %collective-permute-done.13.received_ref, bf16[1024,128]{1,0:T(8,128)(2,1)S(1)} %get-tuple-element.30.refs_0_, ...), custom_call_target="tpu_custom_call" | custom-call | flops 603979776 | bytes 4882432 | tf_op jit(solution)/shard_map/pallas_call | solution.py:25
  53.3 1.0 %collective-permute-start.14 = (bf16[128,1152]{1,0:T(8,128)(2,1)S(1)}, bf16[128,1152]{1,0:T(8,128)(2,1)S(1)}, u32[]{:S(2)}, u32[]{:S(2)}) collective-permute-start(bf16[128,1152]{1,0:T(8,128)(2,1)S(1)} %get-tuple-element.39), channel_id=1, source_target_pairs={{0,8},{4,12},{8,0},{12,4},{16,24},{20,28},{24,16},{28,20},{1,9},{5... | collective-permute-start | bytes 884744 | tf_op jit(solution)/shard_map/ppermute | solution.py:19
  54.9 7.3 %collective-permute-done.10.refs_1_ = bf16[1168,128]{1,0:T(8,128)(2,1)S(1)} collective-permute-done((bf16[1168,128]{1,0:T(8,128)(2,1)S(1)}, bf16[1168,128]{1,0:T(8,128)(2,1)S(1)}, u32[]{:S(2)}, u32[]{:S(2)}) %collective-permute-start.10) | collective-permute-done | bytes 299040 | tf_op jit(solution)/shard_map/ppermute | solution.py:19
  62.2 1.2 %collective-permute-start.16 = (bf16[128,1152]{1,0:T(8,128)(2,1)S(1)}, bf16[128,1152]{1,0:T(8,128)(2,1)S(1)}, u32[]{:S(2)}, u32[]{:S(2)}) collective-permute-start(bf16[128,1152]{1,0:T(8,128)(2,1)S(1)} %get-tuple-element.41), channel_id=1, source_target_pairs={{0,24},{4,28},{8,16},{12,20},{16,8},{20,12},{24,0},{28,4},{1,25},{... | collective-permute-start | bytes 884744 | tf_op jit(solution)/shard_map/ppermute | solution.py:19
  63.4 2.7 %collective-permute-done.12.refs_2_ = bf16[1168,128]{1,0:T(8,128)(2,1)S(1)} collective-permute-done((bf16[1168,128]{1,0:T(8,128)(2,1)S(1)}, bf16[1168,128]{1,0:T(8,128)(2,1)S(1)}, u32[]{:S(2)}, u32[]{:S(2)}) %collective-permute-start.12) | collective-permute-done | bytes 299040 | tf_op jit(solution)/shard_map/ppermute | solution.py:19
  66.0 11.8 %collective-permute-done.8.refs_0_ = bf16[1168,128]{1,0:T(8,128)(2,1)S(1)} collective-permute-done((bf16[1168,128]{1,0:T(8,128)(2,1)S(1)}, bf16[1168,128]{1,0:T(8,128)(2,1)S(1)}, u32[]{:S(2)}, u32[]{:S(2)}) %collective-permute-start.8) | collective-permute-done | bytes 299040 | tf_op jit(solution)/shard_map/ppermute | solution.py:19
  77.8 1.2 %shard_map.71 = (f32[128,1152]{1,0:T(8,128)}, f32[1,128]{1,0:T(1,128)}) custom-call(f32[1]{0:T(128)S(6)} %exp.3.scale_ref, bf16[128,1152]{1,0:T(8,128)(2,1)S(1)} %copy-done.3, f32[128,1152]{1,0:T(8,128)S(1)} %get-tuple-element.23.grad_ref, f32[1,128]{1,0:T(1,128)S(1)} %get-tuple-element.24.loss_ref, bf16[1168,128]{1,0:T(8,128)(2,1)S(1)} %collective-permute-done.8.refs_0_, ...), custom_call_target="tpu_custom_call" | custom-call | tf_op jit(solution)/shard_map/pallas_call | solution.py:232
  79.1 1.2 %shard_map.74 = f32[128,1152]{1,0:T(8,128)} custom-call(f32[1]{0:T(128)S(6)} %exp.3.scale_ref, bf16[128,1152]{1,0:T(8,128)(2,1)S(1)} %copy-done.1, f32[128,1152]{1,0:T(8,128)S(1)} %get-tuple-element.38.grad_ref, bf16[128,1152]{1,0:T(8,128)(2,1)S(1)} %collective-permute-done.14.refs_0_, bf16[128,1152]{1,0:T(8,128)(2,1)S(1)} %collective-permute-done.15.refs_1_, ...), custom_call_target="tpu_custom_call" | custom-call | bytes 2359300 | tf_op jit(solution)/shard_map/pallas_call | solution.py:25
  (26 shorter events, 2.6 us)
Async XLA Ops:
  0.6 8.2 %collective-permute-start.1 = (bf16[128,1152]{1,0:T(8,128)(2,1)}, bf16[128,1152]{1,0:T(8,128)(2,1)S(1)}, u32[]{:S(2)}, u32[]{:S(2)}) collective-permute-start(bf16[128,1152]{1,0:T(8,128)(2,1)} %text_ref.1), channel_id=1, source_target_pairs={{0,8},{4,12},{8,0},{12,4},{16,24},{20,28},{24,16},{28,20},{1,9},{5... | collective-permute-start | bytes 884744 | tf_op jit(solution)/shard_map/ppermute | solution.py:19
  1.9 9.6 %collective-permute-start.3 = (bf16[128,1152]{1,0:T(8,128)(2,1)}, bf16[128,1152]{1,0:T(8,128)(2,1)S(1)}, u32[]{:S(2)}, u32[]{:S(2)}) collective-permute-start(bf16[128,1152]{1,0:T(8,128)(2,1)} %text_ref.1), channel_id=1, source_target_pairs={{0,16},{4,20},{8,24},{12,28},{16,0},{20,4},{24,8},{28,12},{1,17},{... | collective-permute-start | bytes 884744 | tf_op jit(solution)/shard_map/ppermute | solution.py:19
  3.1 14.7 %collective-permute-start.5 = (bf16[128,1152]{1,0:T(8,128)(2,1)}, bf16[128,1152]{1,0:T(8,128)(2,1)S(1)}, u32[]{:S(2)}, u32[]{:S(2)}) collective-permute-start(bf16[128,1152]{1,0:T(8,128)(2,1)} %text_ref.1), channel_id=1, source_target_pairs={{0,24},{4,28},{8,16},{12,20},{16,8},{20,12},{24,0},{28,4},{1,25},{... | collective-permute-start | bytes 884744 | tf_op jit(solution)/shard_map/ppermute | solution.py:19
  3.3 16.8 %collective-permute-start = (bf16[128,1152]{1,0:T(8,128)(2,1)}, bf16[128,1152]{1,0:T(8,128)(2,1)S(1)}, u32[]{:S(2)}, u32[]{:S(2)}) collective-permute-start(bf16[128,1152]{1,0:T(8,128)(2,1)} %text_ref.1), channel_id=1, source_target_pairs={{0,4},{4,0},{8,12},{12,8},{16,20},{20,16},{24,28},{28,24},{1,5},{5... | collective-permute-start | bytes 884744 | tf_op jit(solution)/shard_map/ppermute | solution.py:19
  8.8 11.6 %collective-permute-start.2 = (bf16[128,1152]{1,0:T(8,128)(2,1)S(1)}, bf16[128,1152]{1,0:T(8,128)(2,1)S(1)}, u32[]{:S(2)}, u32[]{:S(2)}) collective-permute-start(bf16[128,1152]{1,0:T(8,128)(2,1)S(1)} %collective-permute-done.1.refs_2_), channel_id=1, source_target_pairs={{0,4},{4,0},{8,12},{12,8},{16,20},{20,16},{24,28},{28,24},{1,5},{5... | collective-permute-start | bytes 884744 | tf_op jit(solution)/shard_map/ppermute | solution.py:19
  11.5 10.4 %collective-permute-start.4 = (bf16[128,1152]{1,0:T(8,128)(2,1)S(1)}, bf16[128,1152]{1,0:T(8,128)(2,1)S(1)}, u32[]{:S(2)}, u32[]{:S(2)}) collective-permute-start(bf16[128,1152]{1,0:T(8,128)(2,1)S(1)} %collective-permute-done.3.refs_4_), channel_id=1, source_target_pairs={{0,4},{4,0},{8,12},{12,8},{16,20},{20,16},{24,28},{28,24},{1,5},{5... | collective-permute-start | bytes 884744 | tf_op jit(solution)/shard_map/ppermute | solution.py:19
  17.9 4.0 %collective-permute-start.6 = (bf16[128,1152]{1,0:T(8,128)(2,1)S(1)}, bf16[128,1152]{1,0:T(8,128)(2,1)S(1)}, u32[]{:S(2)}, u32[]{:S(2)}) collective-permute-start(bf16[128,1152]{1,0:T(8,128)(2,1)S(1)} %collective-permute-done.5.refs_6_), channel_id=1, source_target_pairs={{0,4},{4,0},{8,12},{12,8},{16,20},{20,16},{24,28},{28,24},{1,5},{5... | collective-permute-start | bytes 884744 | tf_op jit(solution)/shard_map/ppermute | solution.py:19
  17.9 15.9 %collective-permute-start.9 = (bf16[128,1152]{1,0:T(8,128)(2,1)}, bf16[128,1152]{1,0:T(8,128)(2,1)S(1)}, u32[]{:S(2)}, u32[]{:S(2)}) collective-permute-start(bf16[128,1152]{1,0:T(8,128)(2,1)} %image_ref.3), channel_id=1, source_target_pairs={{0,2},{1,3},{2,0},{3,1},{4,6},{5,7},{6,4},{7,5},{8,10},{9,11},{10,... | collective-permute-start | bytes 884744 | tf_op jit(solution)/shard_map/ppermute | solution.py:19
  20.2 15.2 %collective-permute-start.11 = (bf16[128,1152]{1,0:T(8,128)(2,1)}, bf16[128,1152]{1,0:T(8,128)(2,1)S(1)}, u32[]{:S(2)}, u32[]{:S(2)}) collective-permute-start(bf16[128,1152]{1,0:T(8,128)(2,1)} %image_ref.3), channel_id=1, source_target_pairs={{0,1},{1,0},{2,3},{3,2},{4,5},{5,4},{6,7},{7,6},{8,9},{9,8},{10,11... | collective-permute-start | bytes 884744 | tf_op jit(solution)/shard_map/ppermute | solution.py:19
  20.4 25.7 %collective-permute-start.7 = (bf16[128,1152]{1,0:T(8,128)(2,1)}, bf16[128,1152]{1,0:T(8,128)(2,1)S(1)}, u32[]{:S(2)}, u32[]{:S(2)}) collective-permute-start(bf16[128,1152]{1,0:T(8,128)(2,1)} %image_ref.3), channel_id=1, source_target_pairs={{0,3},{1,2},{2,1},{3,0},{4,7},{5,6},{6,5},{7,4},{8,11},{9,10},{10,... | collective-permute-start | bytes 884744 | tf_op jit(solution)/shard_map/ppermute | solution.py:19
  21.9 1.0 %copy-start = (bf16[128,1152]{1,0:T(8,128)(2,1)S(1)}, bf16[128,1152]{1,0:T(8,128)(2,1)}, u32[]{:S(2)}) copy-start(bf16[128,1152]{1,0:T(8,128)(2,1)} %text_ref.1) | copy-start | bytes 884740
  22.9 1.0 %copy-start.2 = (bf16[128,1152]{1,0:T(8,128)(2,1)S(1)}, bf16[128,1152]{1,0:T(8,128)(2,1)}, u32[]{:S(2)}) copy-start(bf16[128,1152]{1,0:T(8,128)(2,1)} %image_ref.3) | copy-start | bytes 884740
  48.5 3.9 %collective-permute-start.13 = (bf16[512,1152]{1,0:T(8,128)(2,1)S(1)}, bf16[512,1152]{1,0:T(8,128)(2,1)S(1)}, u32[]{:S(2)}, u32[]{:S(2)}) collective-permute-start(bf16[512,1152]{1,0:T(8,128)(2,1)S(1)} %shard_map.72), channel_id=1, source_target_pairs={{0,4},{4,0},{8,12},{12,8},{16,20},{20,16},{24,28},{28,24},{1,5},{5... | collective-permute-start | bytes 3538952 | tf_op jit(solution)/shard_map/ppermute | solution.py:19
  49.1 13.1 %collective-permute-start.10 = (bf16[1168,128]{1,0:T(8,128)(2,1)S(1)}, bf16[1168,128]{1,0:T(8,128)(2,1)S(1)}, u32[]{:S(2)}, u32[]{:S(2)}) collective-permute-start(bf16[1168,128]{1,0:T(8,128)(2,1)S(1)} %get-tuple-element.27), channel_id=1, source_target_pairs={{0,2},{1,3},{2,0},{3,1},{4,6},{5,7},{6,4},{7,5},{8,10},{9,11},{10,... | collective-permute-start | bytes 897032 | tf_op jit(solution)/shard_map/ppermute | solution.py:19
  49.1 16.9 %collective-permute-start.12 = (bf16[1168,128]{1,0:T(8,128)(2,1)S(1)}, bf16[1168,128]{1,0:T(8,128)(2,1)S(1)}, u32[]{:S(2)}, u32[]{:S(2)}) collective-permute-start(bf16[1168,128]{1,0:T(8,128)(2,1)S(1)} %get-tuple-element.28), channel_id=1, source_target_pairs={{0,1},{1,0},{2,3},{3,2},{4,5},{5,4},{6,7},{7,6},{8,9},{9,8},{10,11... | collective-permute-start | bytes 897032 | tf_op jit(solution)/shard_map/ppermute | solution.py:19
  52.4 25.5 %copy-start.3 = (bf16[128,1152]{1,0:T(8,128)(2,1)S(1)}, bf16[128,1152]{1,0:T(8,128)(2,1)}, u32[]{:S(2)}) copy-start(bf16[128,1152]{1,0:T(8,128)(2,1)} %image_ref.3) | copy-start | bytes 884740
  52.4 25.5 %collective-permute-start.8 = (bf16[1168,128]{1,0:T(8,128)(2,1)S(1)}, bf16[1168,128]{1,0:T(8,128)(2,1)S(1)}, u32[]{:S(2)}, u32[]{:S(2)}) collective-permute-start(bf16[1168,128]{1,0:T(8,128)(2,1)S(1)} %get-tuple-element.26), channel_id=1, source_target_pairs={{0,3},{1,2},{2,1},{3,0},{4,7},{5,6},{6,5},{7,4},{8,11},{9,10},{10,... | collective-permute-start | bytes 897032 | tf_op jit(solution)/shard_map/ppermute | solution.py:19
  53.3 25.8 %copy-start.1 = (bf16[128,1152]{1,0:T(8,128)(2,1)S(1)}, bf16[128,1152]{1,0:T(8,128)(2,1)}, u32[]{:S(2)}) copy-start(bf16[128,1152]{1,0:T(8,128)(2,1)} %text_ref.1) | copy-start | bytes 884740
  53.3 25.7 %collective-permute-start.14 = (bf16[128,1152]{1,0:T(8,128)(2,1)S(1)}, bf16[128,1152]{1,0:T(8,128)(2,1)S(1)}, u32[]{:S(2)}, u32[]{:S(2)}) collective-permute-start(bf16[128,1152]{1,0:T(8,128)(2,1)S(1)} %get-tuple-element.39), channel_id=1, source_target_pairs={{0,8},{4,12},{8,0},{12,4},{16,24},{20,28},{24,16},{28,20},{1,9},{5... | collective-permute-start | bytes 884744 | tf_op jit(solution)/shard_map/ppermute | solution.py:19
  54.3 24.7 %collective-permute-start.15 = (bf16[128,1152]{1,0:T(8,128)(2,1)S(1)}, bf16[128,1152]{1,0:T(8,128)(2,1)S(1)}, u32[]{:S(2)}, u32[]{:S(2)}) collective-permute-start(bf16[128,1152]{1,0:T(8,128)(2,1)S(1)} %get-tuple-element.40), channel_id=1, source_target_pairs={{0,16},{4,20},{8,24},{12,28},{16,0},{20,4},{24,8},{28,12},{1,17},{... | collective-permute-start | bytes 884744 | tf_op jit(solution)/shard_map/ppermute | solution.py:19
  62.2 16.9 %collective-permute-start.16 = (bf16[128,1152]{1,0:T(8,128)(2,1)S(1)}, bf16[128,1152]{1,0:T(8,128)(2,1)S(1)}, u32[]{:S(2)}, u32[]{:S(2)}) collective-permute-start(bf16[128,1152]{1,0:T(8,128)(2,1)S(1)} %get-tuple-element.41), channel_id=1, source_target_pairs={{0,24},{4,28},{8,16},{12,20},{16,8},{20,12},{24,0},{28,4},{1,25},{... | collective-permute-start | bytes 884744 | tf_op jit(solution)/shard_map/ppermute | solution.py:19

commit v2 on v1

v2 whole, which is shorter than its diff:
```python
import functools

import jax
import jax.numpy as jnp
from jax import lax
from jax.experimental import pallas as pl
from jax.experimental.pallas import tpu as pltpu
from jax.sharding import PartitionSpec as P

epsilon = 1e-06
f32, bf16 = jnp.float32, jnp.bfloat16
lanes = 128
extra = 16
direct_panels = 5
VMEM = pl.BlockSpec(memory_space=pltpu.VMEM)
SMEM = pl.BlockSpec(memory_space=pltpu.SMEM)


def swapped(value, axis, step):
    return lax.ppermute(value, axis, [(place, place ^ step) for place in range(lax.axis_size(axis))])


def swapped_both(value, dp_step, inner_step):
    dp_count, inner_count = lax.axis_size("dp"), lax.axis_size("inner")
    pairs = [
        (d * inner_count + i, (d ^ dp_step) * inner_count + (i ^ inner_step))
        for d in range(dp_count)
        for i in range(inner_count)
    ]
    return lax.ppermute(value, ("dp", "inner"), pairs)


def call(kernel, out_shape, *operands, flops=0, scalars=0, scratch=()):
    moved = sum(o.size * o.dtype.itemsize for o in operands)
    moved += sum(o.size * o.dtype.itemsize for o in jax.tree.leaves(out_shape))
    return pl.pallas_call(
        kernel,
        out_shape=out_shape,
        in_specs=[SMEM] * scalars + [VMEM] * (len(operands) - scalars),
        out_specs=jax.tree.map(lambda _: VMEM, out_shape),
        scratch_shapes=scratch,
        compiler_params=pltpu.CompilerParams(vmem_limit_bytes=40 * 1024 * 1024),
        cost_estimate=pl.CostEstimate(flops=flops, bytes_accessed=moved, transcendentals=0),
    )(*operands)


def shape(dims, kind):
    return jax.ShapeDtypeStruct(dims, kind)


def unit_of(rows):
    wide = rows.astype(f32)
    inverse = lax.rsqrt(jnp.sum(wide * wide, axis=-1, keepdims=True) + epsilon)
    return wide * inverse, inverse


def pair_terms(scale, offset, texts, image_emb, slopes_ref, own):
    rows = image_emb.shape[0]
    total = jnp.zeros((1, rows), f32)
    step = 256
    for start in range(0, texts.shape[0], step):
        logits = (
            scale
            * lax.dot_general(
                texts[start : start + step, :],
                image_emb,
                (((1,), (1,)), ((), ())),
                preferred_element_type=f32,
            )
            + offset
        )
        shrunk = jnp.exp(-jnp.abs(logits))
        softplus = jnp.maximum(logits, 0.0) + jnp.log1p(shrunk)
        sigmoid = jnp.where(logits >= 0.0, 1.0, shrunk) / (1.0 + shrunk)
        if own and start == 0:
            text_ids = lax.broadcasted_iota(jnp.int32, logits.shape, 0)
            image_ids = lax.broadcasted_iota(jnp.int32, logits.shape, 1)
            match = (text_ids == image_ids).astype(f32)
            softplus = softplus - match * logits
            sigmoid = sigmoid - match
        slopes_ref[start : start + step, :] = sigmoid.astype(bf16)
        total = total + jnp.sum(softplus, axis=0, keepdims=True)
    return total


def image_sums(slopes_ref, texts_ref):
    return lax.dot_general(
        slopes_ref[...], texts_ref[...], (((0,), (0,)), ((), ())), preferred_element_type=f32
    )


def texts_kernel(*refs):
    out_ref, rows = refs[-1], refs[0].shape[0]
    for place, raw in enumerate(refs[:-1]):
        out_ref[place * rows : (place + 1) * rows, :] = unit_of(raw[...])[0].astype(bf16)


def own_kernel(scale_ref, bias_ref, image_ref, texts_ref, slopes_ref, emb_ref, grad_ref, loss_ref):
    emb_ref[...] = unit_of(image_ref[...])[0].astype(bf16)
    loss_ref[...] = pair_terms(
        scale_ref[0], bias_ref[0], texts_ref, emb_ref[...], slopes_ref, True
    )
    grad_ref[...] = image_sums(slopes_ref, texts_ref)


def peer_kernel(scale_ref, bias_ref, image_ref, texts_ref, slopes_ref, emb_ref, head_ref, tail_ref):
    rows = image_ref.shape[0]
    panels = (head_ref.shape[0] - extra) // rows
    emb_ref[...] = unit_of(image_ref[...])[0].astype(bf16)
    loss = pair_terms(scale_ref[0], bias_ref[0], texts_ref, emb_ref[...], slopes_ref, False)
    sums = image_sums(slopes_ref, texts_ref)
    for panel in range(panels):
        head_ref[panel * rows : (panel + 1) * rows, :] = sums[
            :, panel * lanes : (panel + 1) * lanes
        ].astype(bf16)
    tail_ref[...] = sums[:, panels * lanes :].astype(tail_ref.dtype)
    high = loss.astype(bf16).astype(f32)
    which = lax.broadcasted_iota(jnp.int32, (extra, rows), 0)
    head_ref[panels * rows :, :] = jnp.where(which == 0, high, loss - high).astype(bf16)


def text_sums(slopes, embs, place, rows):
    left = jnp.concatenate([s[place * rows : (place + 1) * rows, :] for s in slopes], axis=1)
    return jnp.dot(left, embs, preferred_element_type=f32)


def other_core_kernel(count, *refs):
    slopes, emb_refs, sent_ref = refs[:count], refs[count : 2 * count], refs[2 * count]
    rows = emb_refs[0].shape[0]
    embs = jnp.concatenate([e[...] for e in emb_refs], axis=0)
    for k in range(slopes[0].shape[0] // rows // 2):
        sent_ref[k * rows : (k + 1) * rows, :] = text_sums(slopes, embs, 2 * k + 1, rows).astype(bf16)


def own_core_kernel(count, received_ref, *refs):
    slopes, emb_refs = refs[:count], refs[count : 2 * count]
    rows = emb_refs[0].shape[0]
    embs = jnp.concatenate([e[...] for e in emb_refs], axis=0)
    for k, out in enumerate(refs[2 * count :]):
        sums = text_sums(slopes, embs, 2 * k, rows) + received_ref[k * rows : (k + 1) * rows, :].astype(f32)
        out[...] = sums.astype(out.dtype)


def add_kernel(*refs):
    total = refs[0][...].astype(f32)
    for part in refs[1:-1]:
        total = total + part[...].astype(f32)
    refs[-1][...] = total.astype(refs[-1].dtype)


def row_gradient(rows, sums, scale, out_ref):
    unit_rows, inverse = unit_of(rows)
    unit_grad = scale * sums
    out_ref[...] = (
        unit_grad - unit_rows * jnp.sum(unit_rows * unit_grad, axis=-1, keepdims=True)
    ) * inverse


def image_end_kernel(batch, heads, scale_ref, image_ref, grad_ref, loss_ref, *refs):
    out_ref, out_loss_ref, sums_ref = refs[-3:]
    head_refs, tail_refs = refs[:heads], refs[heads:-3]
    rows = image_ref.shape[0]
    panels = (head_refs[0].shape[0] - extra) // rows
    loss = loss_ref[...]
    for panel in range(panels):
        cut = slice(panel * lanes, (panel + 1) * lanes)
        sums = grad_ref[:, cut]
        for r in head_refs:
            sums = sums + r[panel * rows : (panel + 1) * rows, :].astype(f32)
        sums_ref[:, cut] = sums
    for r in head_refs:
        last = r[panels * rows :, :].astype(f32)
        loss = loss + (last[0:1, :] + last[1:2, :])
    sums = grad_ref[:, panels * lanes :]
    for r in tail_refs:
        sums = sums + r[...].astype(f32)
    sums_ref[:, panels * lanes :] = sums
    row_gradient(image_ref[...], sums_ref[...], scale_ref[0], out_ref)
    out_loss_ref[...] = loss / batch


def text_end_kernel(scale_ref, text_ref, grad_ref, *refs):
    sums = grad_ref[...]
    for r in refs[:-1]:
        sums = sums + r[...].astype(f32)
    row_gradient(text_ref[...], sums, scale_ref[0], refs[-1])


def body(image, text, logarithm_scale, bias):
    rows, width = image.shape
    dp_count, inner_count = lax.axis_size("dp"), lax.axis_size("inner")
    batch = rows * dp_count * inner_count
    scale = jnp.exp(logarithm_scale)
    block = shape((rows, width), bf16)
    wide_block = shape((rows, width), f32)

    text_dp, text_inner = (0, 2), (0, 1)
    image_dp, image_inner = range(0, dp_count, 4), range(0, inner_count, 2)

    image_near = {q: swapped(image, "inner", q) if q else image for q in image_inner}
    text_near = {q: swapped(text, "inner", q) if q else text for q in text_inner}
    texts = []
    for q in text_inner:
        for p in text_dp:
            fetched = swapped(text_near[q], "dp", p) if p else text_near[q]
            texts += [fetched, swapped(fetched, "dp", 1)]
    images = {
        (p, q): swapped(image_near[q], "dp", p) if p else image_near[q]
        for q in image_inner
        for p in image_dp
    }

    texts_held = rows * len(texts)
    block_flops = 2 * rows * texts_held * width
    text_embs = call(texts_kernel, shape((texts_held, width), bf16), *texts, flops=block_flops // 3)
    slopes, embs, heads, tails = {}, {}, {}, {}
    head_rows = direct_panels * rows + extra
    tail_width = width - direct_panels * lanes
    for place in sorted(images, key=lambda place: (place[0] and place[1], place[0], -place[1])):
        p, q = place
        if p or q:
            slopes[place], embs[place], heads[place], tails[place] = call(
                peer_kernel,
                (
                    shape((texts_held, rows), bf16),
                    block,
                    shape((head_rows, lanes), bf16),
                    shape((rows, tail_width), bf16 if p else f32),
                ),
                scale,
                bias,
                images[place],
                text_embs,
                flops=2 * block_flops,
                scalars=2,
            )
        else:
            slopes[place], embs[place], image_grad, loss = call(
                own_kernel,
                (shape((texts_held, rows), bf16), block, wide_block, shape((1, rows), f32)),
                scale,
                bias,
                image,
                text_embs,
                flops=2 * block_flops,
                scalars=2,
            )

    head_parts = [
        swapped_both(heads[p, q], p, q) if p and q else swapped(heads[p, q], *(("dp", p) if p else ("inner", q)))
        for p, q in heads
    ]
    tail_parts = []
    for q in image_inner:
        moved = [swapped(tails[p, q], "dp", p) for p in image_dp if p]
        if q:
            summed = call(add_kernel, shape((rows, tail_width), bf16), tails[0, q], *moved)
            moved = [swapped(summed, "inner", q)]
        tail_parts += moved

    ordered = sorted(slopes)
    pieces = [slopes[place] for place in ordered] + [embs[place] for place in ordered]
    crossing = call(
        functools.partial(other_core_kernel, len(ordered)),
        shape((texts_held // 2, width), bf16),
        *pieces,
        flops=len(ordered) * block_flops // 2,
    )
    crossed = swapped(crossing, "dp", 1)
    text_grad, *text_sent = call(
        functools.partial(own_core_kernel, len(ordered)),
        (wide_block,) + (block,) * (len(texts) // 2 - 1),
        crossed,
        *pieces,
        flops=len(ordered) * block_flops // 2,
    )
    text_places = [(p, q) for q in text_inner for p in text_dp][1:]
    text_parts = [
        swapped_both(part, p, q) if p and q else swapped(part, *(("dp", p) if p else ("inner", q)))
        for part, (p, q) in zip(text_sent, text_places)
    ]

    image_gradient, image_loss = call(
        functools.partial(image_end_kernel, batch, len(head_parts)),
        (wide_block, shape((1, rows), f32)),
        scale,
        image,
        image_grad,
        loss,
        *head_parts,
        *tail_parts,
        scalars=1,
        scratch=[pltpu.VMEM((rows, width), f32)],
    )
    text_gradient = call(text_end_kernel, wide_block, scale, text, text_grad, *text_parts, scalars=1)
    return (image_gradient, text_gradient, image_loss.reshape(rows))


def solution(mesh):
    return jax.shard_map(
        body,
        mesh=mesh,
        in_specs=(P(("dp", "inner"), None), P(("dp", "inner"), None), P(), P()),
        out_specs=(P(("dp", "inner"), None), P(("dp", "inner"), None), P(("dp", "inner"))),
        check_vma=False,
    )
```

time: 80.4 us -> 77.9 us (0.969)
  the two profiles are of different devices: /device:TPU:9 before, /device:TPU:0 now
where the time goes in v2:
time: 77.9 us; the launch traced here: 77.7 us
  waiting for transfers between devices  37.1 us (48%)
  starting transfers between devices  26.2 us (34%)
  Pallas kernels  11.2 us (14%)
  between operations  2.09 us (3%)
  local copies, waits for them, and re-layouts  1.19 us (2%)
    ppermute x18, waiting for transfers between devices, swapped(): lax.ppermute(value, axis, [(place, place ^ step) for place in range(lax.a...  36.6 us
    ppermute x18, starting transfers between devices, swapped(): lax.ppermute(value, axis, [(place, place ^ step) for place in range(lax.a...  22.2 us
    pallas_call x10, Pallas kernels, call(): pl.pallas_call(kernel, out_shape=out_shape, in_specs=[SMEM] * scalars + [...  11.2 us
    ppermute x2, starting transfers between devices, swapped_both(): return lax.ppermute(value, ('dp', 'inner'), pairs)  3.95 us
  transfers between devices with their start and end apart: 20, of which 10 were waited for; matrix products, arithmetic and copies ran while one was open for 0% of the time, Pallas kernels for 10%

profile of v2, /device:TPU:0, one launch (start us, length us, event | category | flops | bytes accessed | tf_op | source)
XLA Modules:
  0.0 77.7 jit_solution(11093792831210455140)
XLA Ops:
  0.6 3.1 %collective-permute-start.3 = (bf16[128,1152]{1,0:T(8,128)(2,1)}, bf16[128,1152]{1,0:T(8,128)(2,1)S(1)}, u32[]{:S(2)}, u32[]{:S(2)}) collective-permute-start(bf16[128,1152]{1,0:T(8,128)(2,1)} %text_ref.1), channel_id=1, source_target_pairs={{0,1},{1,0},{2,3},{3,2},{4,5},{5,4},{6,7},{7,6},{8,9},{9,8},{10,11... | collective-permute-start | bytes 884744 | tf_op jit(solution)/shard_map/ppermute | solution.py:20
  3.7 1.5 %collective-permute-start.1 = (bf16[128,1152]{1,0:T(8,128)(2,1)}, bf16[128,1152]{1,0:T(8,128)(2,1)S(1)}, u32[]{:S(2)}, u32[]{:S(2)}) collective-permute-start(bf16[128,1152]{1,0:T(8,128)(2,1)} %text_ref.1), channel_id=1, source_target_pairs={{0,8},{4,12},{8,0},{12,4},{16,24},{20,28},{24,16},{28,20},{1,9},{5... | collective-permute-start | bytes 884744 | tf_op jit(solution)/shard_map/ppermute | solution.py:20
  5.2 5.7 %collective-permute-done.3.refs_4_ = bf16[128,1152]{1,0:T(8,128)(2,1)S(1)} collective-permute-done((bf16[128,1152]{1,0:T(8,128)(2,1)}, bf16[128,1152]{1,0:T(8,128)(2,1)S(1)}, u32[]{:S(2)}, u32[]{:S(2)}) %collective-permute-start.3) | collective-permute-done | bytes 294944 | tf_op jit(solution)/shard_map/ppermute | solution.py:20
  10.9 1.7 %collective-permute-start.5 = (bf16[128,1152]{1,0:T(8,128)(2,1)S(1)}, bf16[128,1152]{1,0:T(8,128)(2,1)S(1)}, u32[]{:S(2)}, u32[]{:S(2)}) collective-permute-start(bf16[128,1152]{1,0:T(8,128)(2,1)S(1)} %collective-permute-done.3.refs_4_), channel_id=1, source_target_pairs={{0,8},{4,12},{8,0},{12,4},{16,24},{20,28},{24,16},{28,20},{1,9},{5... | collective-permute-start | bytes 884744 | tf_op jit(solution)/shard_map/ppermute | solution.py:20
  12.6 2.6 %collective-permute-start.7 = (bf16[128,1152]{1,0:T(8,128)(2,1)}, bf16[128,1152]{1,0:T(8,128)(2,1)S(1)}, u32[]{:S(2)}, u32[]{:S(2)}) collective-permute-start(bf16[128,1152]{1,0:T(8,128)(2,1)} %image_ref.3), channel_id=1, source_target_pairs={{0,2},{1,3},{2,0},{3,1},{4,6},{5,7},{6,4},{7,5},{8,10},{9,11},{10,... | collective-permute-start | bytes 884744 | tf_op jit(solution)/shard_map/ppermute | solution.py:20
  15.7 3.4 %collective-permute-done.5.refs_6_ = bf16[128,1152]{1,0:T(8,128)(2,1)S(1)} collective-permute-done((bf16[128,1152]{1,0:T(8,128)(2,1)S(1)}, bf16[128,1152]{1,0:T(8,128)(2,1)S(1)}, u32[]{:S(2)}, u32[]{:S(2)}) %collective-permute-start.5) | collective-permute-done | bytes 294944 | tf_op jit(solution)/shard_map/ppermute | solution.py:20
  19.1 8.5 %collective-permute-done.7.image_ref = bf16[128,1152]{1,0:T(8,128)(2,1)S(1)} collective-permute-done((bf16[128,1152]{1,0:T(8,128)(2,1)}, bf16[128,1152]{1,0:T(8,128)(2,1)S(1)}, u32[]{:S(2)}, u32[]{:S(2)}) %collective-permute-start.7) | collective-permute-done | bytes 294944 | tf_op jit(solution)/shard_map/ppermute | solution.py:20
  27.6 1.5 %collective-permute-start.11 = (bf16[128,1152]{1,0:T(8,128)(2,1)S(1)}, bf16[128,1152]{1,0:T(8,128)(2,1)S(1)}, u32[]{:S(2)}, u32[]{:S(2)}) collective-permute-start(bf16[128,1152]{1,0:T(8,128)(2,1)S(1)} %collective-permute-done.7.image_ref), channel_id=1, source_target_pairs={{0,16},{4,20},{8,24},{12,28},{16,0},{20,4},{24,8},{28,12},{1,17},{... | collective-permute-start | bytes 884744 | tf_op jit(solution)/shard_map/ppermute | solution.py:20
  32.9 1.6 %shard_map.68 = (bf16[1024,128]{1,0:T(8,128)(2,1)S(1)}, bf16[128,1152]{1,0:T(8,128)(2,1)S(1)}, f32[128,1152]{1,0:T(8,128)S(1)}, f32[1,128]{1,0:T(1,128)S(1)}) custom-call(f32[1]{0:T(128)S(6)} %exp.3.scale_ref, f32[1]{0:T(128)S(6)} %copy.8.bias_ref, bf16[128,1152]{1,0:T(8,128)(2,1)S(1)} %copy-done.2, bf16[1024,1152]{1,0:T(8,128)(2,1)S(1)} %shard_map.67.texts_ref), custom_call_target="tpu_custom_call" | custom-call | flops 603979776 | bytes 3801608 | tf_op jit(solution)/shard_map/pallas_call | solution.py:36
  34.6 1.6 %shard_map.69 = (bf16[1024,128]{1,0:T(8,128)(2,1)S(1)}, bf16[128,1152]{1,0:T(8,128)(2,1)S(1)}, bf16[656,128]{1,0:T(8,128)(2,1)S(1)}, f32[128,512]{1,0:T(8,128)S(1)}) custom-call(f32[1]{0:T(128)S(6)} %exp.3.scale_ref, f32[1]{0:T(128)S(6)} %copy.8.bias_ref, bf16[128,1152]{1,0:T(8,128)(2,1)S(1)} %collective-permute-done.7.image_ref, ...), custom_call_target="tpu_custom_call" | custom-call | flops 603979776 | bytes 3641352 | tf_op jit(solution)/shard_map/pallas_call | solution.py:36
  36.1 1.4 %collective-permute-done.11.image_ref = bf16[128,1152]{1,0:T(8,128)(2,1)S(1)} collective-permute-done((bf16[128,1152]{1,0:T(8,128)(2,1)S(1)}, bf16[128,1152]{1,0:T(8,128)(2,1)S(1)}, u32[]{:S(2)}, u32[]{:S(2)}) %collective-permute-start.11) | collective-permute-done | bytes 294944 | tf_op jit(solution)/shard_map/ppermute | solution.py:20
  37.6 1.6 %shard_map.71 = (bf16[1024,128]{1,0:T(8,128)(2,1)S(1)}, bf16[128,1152]{1,0:T(8,128)(2,1)S(1)}, bf16[656,128]{1,0:T(8,128)(2,1)S(1)}, bf16[128,512]{1,0:T(8,128)(2,1)S(1)}) custom-call(f32[1]{0:T(128)S(6)} %exp.3.scale_ref, f32[1]{0:T(128)S(6)} %copy.8.bias_ref, bf16[128,1152]{1,0:T(8,128)(2,1)S(1)} %collective-permute-done.11.image_ref, ...), custom_call_target="tpu_custom_call" | custom-call | flops 603979776 | bytes 3510280 | tf_op jit(solution)/shard_map/pallas_call | solution.py:36
  39.1 2.6 %collective-permute-done.9.image_ref = bf16[128,1152]{1,0:T(8,128)(2,1)S(1)} collective-permute-done((bf16[128,1152]{1,0:T(8,128)(2,1)}, bf16[128,1152]{1,0:T(8,128)(2,1)S(1)}, u32[]{:S(2)}, u32[]{:S(2)}) %collective-permute-start.9) | collective-permute-done | bytes 294944 | tf_op jit(solution)/shard_map/ppermute | solution.py:20
  41.8 1.6 %shard_map.70 = (bf16[1024,128]{1,0:T(8,128)(2,1)S(1)}, bf16[128,1152]{1,0:T(8,128)(2,1)S(1)}, bf16[656,128]{1,0:T(8,128)(2,1)S(1)}, bf16[128,512]{1,0:T(8,128)(2,1)S(1)}) custom-call(f32[1]{0:T(128)S(6)} %exp.3.scale_ref, f32[1]{0:T(128)S(6)} %copy.8.bias_ref, bf16[128,1152]{1,0:T(8,128)(2,1)S(1)} %collective-permute-done.9.image_ref, ...), custom_call_target="tpu_custom_call" | custom-call | flops 603979776 | bytes 3510280 | tf_op jit(solution)/shard_map/pallas_call | solution.py:36
  44.3 1.6 %collective-permute-start.14 = (bf16[128,512]{1,0:T(8,128)(2,1)S(1)}, bf16[128,512]{1,0:T(8,128)(2,1)S(1)}, u32[]{:S(2)}, u32[]{:S(2)}) collective-permute-start(bf16[128,512]{1,0:T(8,128)(2,1)S(1)} %get-tuple-element.32), channel_id=1, source_target_pairs={{0,16},{4,20},{8,24},{12,28},{16,0},{20,4},{24,8},{28,12},{1,17},{... | collective-permute-start | bytes 393224 | tf_op jit(solution)/shard_map/ppermute | solution.py:20
  49.4 1.3 %collective-permute-done.14.refs_1_ = bf16[128,512]{1,0:T(8,128)(2,1)S(1)} collective-permute-done((bf16[128,512]{1,0:T(8,128)(2,1)S(1)}, bf16[128,512]{1,0:T(8,128)(2,1)S(1)}, u32[]{:S(2)}, u32[]{:S(2)}) %collective-permute-start.14) | collective-permute-done | bytes 131104 | tf_op jit(solution)/shard_map/ppermute | solution.py:20
  50.7 3.8 %collective-permute-start.18 = (bf16[128,1152]{1,0:T(8,128)(2,1)S(1)}, bf16[128,1152]{1,0:T(8,128)(2,1)S(1)}, u32[]{:S(2)}, u32[]{:S(2)}) collective-permute-start(bf16[128,1152]{1,0:T(8,128)(2,1)S(1)} %get-tuple-element.44), channel_id=1, source_target_pairs={{0,1},{1,0},{2,3},{3,2},{4,5},{5,4},{6,7},{7,6},{8,9},{9,8},{10,11... | collective-permute-start | bytes 884744 | tf_op jit(solution)/shard_map/ppermute | solution.py:20
  54.5 1.1 %collective-permute-done.13.refs_3_ = bf16[128,512]{1,0:T(8,128)(2,1)S(1)} collective-permute-done((bf16[128,512]{1,0:T(8,128)(2,1)S(1)}, bf16[128,512]{1,0:T(8,128)(2,1)S(1)}, u32[]{:S(2)}, u32[]{:S(2)}) %collective-permute-start.13) | collective-permute-done | bytes 131104 | tf_op jit(solution)/shard_map/ppermute | solution.py:20
  55.6 3.3 %collective-permute-start.19 = (bf16[128,1152]{1,0:T(8,128)(2,1)S(1)}, bf16[128,1152]{1,0:T(8,128)(2,1)S(1)}, u32[]{:S(2)}, u32[]{:S(2)}) collective-permute-start(bf16[128,1152]{1,0:T(8,128)(2,1)S(1)} %get-tuple-element.45), channel_id=1, source_target_pairs={{0,9},{1,8},{2,11},{3,10},{4,13},{5,12},{6,15},{7,14},{8,1},{9,0},... | collective-permute-start | bytes 884744 | tf_op jit(solution)/shard_map/ppermute | solution.py:30
  58.9 3.3 %collective-permute-start.8 = (bf16[656,128]{1,0:T(8,128)(2,1)S(1)}, bf16[656,128]{1,0:T(8,128)(2,1)S(1)}, u32[]{:S(2)}, u32[]{:S(2)}) collective-permute-start(bf16[656,128]{1,0:T(8,128)(2,1)S(1)} %get-tuple-element.27), channel_id=1, source_target_pairs={{0,2},{1,3},{2,0},{3,1},{4,6},{5,7},{6,4},{7,5},{8,10},{9,11},{10,... | collective-permute-start | bytes 503816 | tf_op jit(solution)/shard_map/ppermute | solution.py:20
  62.3 9.0 %collective-permute-done.8.refs_0_ = bf16[656,128]{1,0:T(8,128)(2,1)S(1)} collective-permute-done((bf16[656,128]{1,0:T(8,128)(2,1)S(1)}, bf16[656,128]{1,0:T(8,128)(2,1)S(1)}, u32[]{:S(2)}, u32[]{:S(2)}) %collective-permute-start.8) | collective-permute-done | bytes 167968 | tf_op jit(solution)/shard_map/ppermute | solution.py:20
  71.4 3.5 %collective-permute-done.15.refs_4_ = bf16[128,512]{1,0:T(8,128)(2,1)S(1)} collective-permute-done((bf16[128,512]{1,0:T(8,128)(2,1)S(1)}, bf16[128,512]{1,0:T(8,128)(2,1)S(1)}, u32[]{:S(2)}, u32[]{:S(2)}) %collective-permute-start.15) | collective-permute-done | bytes 131104 | tf_op jit(solution)/shard_map/ppermute | solution.py:20
  74.8 1.2 %shard_map.73 = (f32[128,1152]{1,0:T(8,128)}, f32[1,128]{1,0:T(1,128)}) custom-call(f32[1]{0:T(128)S(6)} %exp.3.scale_ref, bf16[128,1152]{1,0:T(8,128)(2,1)S(1)} %copy-done.2, f32[128,1152]{1,0:T(8,128)S(1)} %get-tuple-element.25.grad_ref, f32[1,128]{1,0:T(1,128)S(1)} %get-tuple-element.26.loss_ref, bf16[656,128]{1,0:T(8,128)(2,1)S(1)} %collective-permute-done.8.refs_0_, ...), custom_call_target="tpu_custom_call" | custom-call | bytes 2241540 | tf_op jit(solution)/shard_map/pallas_call | solution.py:36
  76.6 1.2 %shard_map.76 = f32[128,1152]{1,0:T(8,128)} custom-call(f32[1]{0:T(128)S(6)} %exp.3.scale_ref, bf16[128,1152]{1,0:T(8,128)(2,1)S(1)} %copy-done.1, f32[128,1152]{1,0:T(8,128)S(1)} %get-tuple-element.42.grad_ref, bf16[128,1152]{1,0:T(8,128)(2,1)S(1)} %collective-permute-done.17.refs_0_, bf16[128,1152]{1,0:T(8,128)(2,1)S(1)} %collective-permute-done.18.refs_1_, ...), custom_call_target="tpu_custom_call" | custom-call | bytes 2359300 | tf_op jit(solution)/shard_map/pallas_call | solution.py:36
  (32 shorter events, 8.1 us)
Async XLA Ops:
  0.6 10.3 %collective-permute-start.3 = (bf16[128,1152]{1,0:T(8,128)(2,1)}, bf16[128,1152]{1,0:T(8,128)(2,1)S(1)}, u32[]{:S(2)}, u32[]{:S(2)}) collective-permute-start(bf16[128,1152]{1,0:T(8,128)(2,1)} %text_ref.1), channel_id=1, source_target_pairs={{0,1},{1,0},{2,3},{3,2},{4,5},{5,4},{6,7},{7,6},{8,9},{9,8},{10,11... | collective-permute-start | bytes 884744 | tf_op jit(solution)/shard_map/ppermute | solution.py:20
  3.7 12.0 %collective-permute-start.1 = (bf16[128,1152]{1,0:T(8,128)(2,1)}, bf16[128,1152]{1,0:T(8,128)(2,1)S(1)}, u32[]{:S(2)}, u32[]{:S(2)}) collective-permute-start(bf16[128,1152]{1,0:T(8,128)(2,1)} %text_ref.1), channel_id=1, source_target_pairs={{0,8},{4,12},{8,0},{12,4},{16,24},{20,28},{24,16},{28,20},{1,9},{5... | collective-permute-start | bytes 884744 | tf_op jit(solution)/shard_map/ppermute | solution.py:20
  10.9 8.2 %collective-permute-start.5 = (bf16[128,1152]{1,0:T(8,128)(2,1)S(1)}, bf16[128,1152]{1,0:T(8,128)(2,1)S(1)}, u32[]{:S(2)}, u32[]{:S(2)}) collective-permute-start(bf16[128,1152]{1,0:T(8,128)(2,1)S(1)} %collective-permute-done.3.refs_4_), channel_id=1, source_target_pairs={{0,8},{4,12},{8,0},{12,4},{16,24},{20,28},{24,16},{28,20},{1,9},{5... | collective-permute-start | bytes 884744 | tf_op jit(solution)/shard_map/ppermute | solution.py:20
  12.6 15.0 %collective-permute-start.7 = (bf16[128,1152]{1,0:T(8,128)(2,1)}, bf16[128,1152]{1,0:T(8,128)(2,1)S(1)}, u32[]{:S(2)}, u32[]{:S(2)}) collective-permute-start(bf16[128,1152]{1,0:T(8,128)(2,1)} %image_ref.3), channel_id=1, source_target_pairs={{0,2},{1,3},{2,0},{3,1},{4,6},{5,7},{6,4},{7,5},{8,10},{9,11},{10,... | collective-permute-start | bytes 884744 | tf_op jit(solution)/shard_map/ppermute | solution.py:20
  15.2 14.0 %collective-permute-start = (bf16[128,1152]{1,0:T(8,128)(2,1)}, bf16[128,1152]{1,0:T(8,128)(2,1)S(1)}, u32[]{:S(2)}, u32[]{:S(2)}) collective-permute-start(bf16[128,1152]{1,0:T(8,128)(2,1)} %text_ref.1), channel_id=1, source_target_pairs={{0,4},{4,0},{8,12},{12,8},{16,20},{20,16},{24,28},{28,24},{1,5},{5... | collective-permute-start | bytes 884744 | tf_op jit(solution)/shard_map/ppermute | solution.py:20
  15.2 15.8 %collective-permute-start.4 = (bf16[128,1152]{1,0:T(8,128)(2,1)S(1)}, bf16[128,1152]{1,0:T(8,128)(2,1)S(1)}, u32[]{:S(2)}, u32[]{:S(2)}) collective-permute-start(bf16[128,1152]{1,0:T(8,128)(2,1)S(1)} %collective-permute-done.3.refs_4_), channel_id=1, source_target_pairs={{0,4},{4,0},{8,12},{12,8},{16,20},{20,16},{24,28},{28,24},{1,5},{5... | collective-permute-start | bytes 884744 | tf_op jit(solution)/shard_map/ppermute | solution.py:20
  15.7 15.3 %collective-permute-start.2 = (bf16[128,1152]{1,0:T(8,128)(2,1)S(1)}, bf16[128,1152]{1,0:T(8,128)(2,1)S(1)}, u32[]{:S(2)}, u32[]{:S(2)}) collective-permute-start(bf16[128,1152]{1,0:T(8,128)(2,1)S(1)} %collective-permute-done.1.refs_2_), channel_id=1, source_target_pairs={{0,4},{4,0},{8,12},{12,8},{16,20},{20,16},{24,28},{28,24},{1,5},{5... | collective-permute-start | bytes 884744 | tf_op jit(solution)/shard_map/ppermute | solution.py:20
  19.1 11.9 %collective-permute-start.6 = (bf16[128,1152]{1,0:T(8,128)(2,1)S(1)}, bf16[128,1152]{1,0:T(8,128)(2,1)S(1)}, u32[]{:S(2)}, u32[]{:S(2)}) collective-permute-start(bf16[128,1152]{1,0:T(8,128)(2,1)S(1)} %collective-permute-done.5.refs_6_), channel_id=1, source_target_pairs={{0,4},{4,0},{8,12},{12,8},{16,20},{20,16},{24,28},{28,24},{1,5},{5... | collective-permute-start | bytes 884744 | tf_op jit(solution)/shard_map/ppermute | solution.py:20
  27.6 9.9 %collective-permute-start.11 = (bf16[128,1152]{1,0:T(8,128)(2,1)S(1)}, bf16[128,1152]{1,0:T(8,128)(2,1)S(1)}, u32[]{:S(2)}, u32[]{:S(2)}) collective-permute-start(bf16[128,1152]{1,0:T(8,128)(2,1)S(1)} %collective-permute-done.7.image_ref), channel_id=1, source_target_pairs={{0,16},{4,20},{8,24},{12,28},{16,0},{20,4},{24,8},{28,12},{1,17},{... | collective-permute-start | bytes 884744 | tf_op jit(solution)/shard_map/ppermute | solution.py:20
  29.1 12.6 %collective-permute-start.9 = (bf16[128,1152]{1,0:T(8,128)(2,1)}, bf16[128,1152]{1,0:T(8,128)(2,1)S(1)}, u32[]{:S(2)}, u32[]{:S(2)}) collective-permute-start(bf16[128,1152]{1,0:T(8,128)(2,1)} %image_ref.3), channel_id=1, source_target_pairs={{0,16},{4,20},{8,24},{12,28},{16,0},{20,4},{24,8},{28,12},{1,17},{... | collective-permute-start | bytes 884744 | tf_op jit(solution)/shard_map/ppermute | solution.py:20
  31.0 1.0 %copy-start = (bf16[128,1152]{1,0:T(8,128)(2,1)S(1)}, bf16[128,1152]{1,0:T(8,128)(2,1)}, u32[]{:S(2)}) copy-start(bf16[128,1152]{1,0:T(8,128)(2,1)} %text_ref.1) | copy-start | bytes 884740
  32.0 1.0 %copy-start.2 = (bf16[128,1152]{1,0:T(8,128)(2,1)S(1)}, bf16[128,1152]{1,0:T(8,128)(2,1)}, u32[]{:S(2)}) copy-start(bf16[128,1152]{1,0:T(8,128)(2,1)} %image_ref.3) | copy-start | bytes 884740
  44.2 3.7 %collective-permute-start.16 = (bf16[512,1152]{1,0:T(8,128)(2,1)S(1)}, bf16[512,1152]{1,0:T(8,128)(2,1)S(1)}, u32[]{:S(2)}, u32[]{:S(2)}) collective-permute-start(bf16[512,1152]{1,0:T(8,128)(2,1)S(1)} %shard_map.74), channel_id=1, source_target_pairs={{0,4},{4,0},{8,12},{12,8},{16,20},{20,16},{24,28},{28,24},{1,5},{5... | collective-permute-start | bytes 3538952 | tf_op jit(solution)/shard_map/ppermute | solution.py:20
  44.3 6.4 %collective-permute-start.14 = (bf16[128,512]{1,0:T(8,128)(2,1)S(1)}, bf16[128,512]{1,0:T(8,128)(2,1)S(1)}, u32[]{:S(2)}, u32[]{:S(2)}) collective-permute-start(bf16[128,512]{1,0:T(8,128)(2,1)S(1)} %get-tuple-element.32), channel_id=1, source_target_pairs={{0,16},{4,20},{8,24},{12,28},{16,0},{20,4},{24,8},{28,12},{1,17},{... | collective-permute-start | bytes 393224 | tf_op jit(solution)/shard_map/ppermute | solution.py:20
  45.9 9.7 %collective-permute-start.13 = (bf16[128,512]{1,0:T(8,128)(2,1)S(1)}, bf16[128,512]{1,0:T(8,128)(2,1)S(1)}, u32[]{:S(2)}, u32[]{:S(2)}) collective-permute-start(bf16[128,512]{1,0:T(8,128)(2,1)S(1)} %get-tuple-element.30), channel_id=1, source_target_pairs={{0,16},{4,20},{8,24},{12,28},{16,0},{20,4},{24,8},{28,12},{1,17},{... | collective-permute-start | bytes 393224 | tf_op jit(solution)/shard_map/ppermute | solution.py:20
  46.4 12.5 %collective-permute-start.12 = (bf16[656,128]{1,0:T(8,128)(2,1)S(1)}, bf16[656,128]{1,0:T(8,128)(2,1)S(1)}, u32[]{:S(2)}, u32[]{:S(2)}) collective-permute-start(bf16[656,128]{1,0:T(8,128)(2,1)S(1)} %get-tuple-element.29), channel_id=1, source_target_pairs={{0,18},{1,19},{2,16},{3,17},{4,22},{5,23},{6,20},{7,21},{8,26},{9,... | collective-permute-start | bytes 503816 | tf_op jit(solution)/shard_map/ppermute | solution.py:30
  47.0 15.2 %collective-permute-start.10 = (bf16[656,128]{1,0:T(8,128)(2,1)S(1)}, bf16[656,128]{1,0:T(8,128)(2,1)S(1)}, u32[]{:S(2)}, u32[]{:S(2)}) collective-permute-start(bf16[656,128]{1,0:T(8,128)(2,1)S(1)} %get-tuple-element.28), channel_id=1, source_target_pairs={{0,16},{4,20},{8,24},{12,28},{16,0},{20,4},{24,8},{28,12},{1,17},{... | collective-permute-start | bytes 503816 | tf_op jit(solution)/shard_map/ppermute | solution.py:20
  48.8 27.8 %copy-start.1 = (bf16[128,1152]{1,0:T(8,128)(2,1)S(1)}, bf16[128,1152]{1,0:T(8,128)(2,1)}, u32[]{:S(2)}) copy-start(bf16[128,1152]{1,0:T(8,128)(2,1)} %text_ref.1) | copy-start | bytes 884740
  48.8 27.2 %collective-permute-start.17 = (bf16[128,1152]{1,0:T(8,128)(2,1)S(1)}, bf16[128,1152]{1,0:T(8,128)(2,1)S(1)}, u32[]{:S(2)}, u32[]{:S(2)}) collective-permute-start(bf16[128,1152]{1,0:T(8,128)(2,1)S(1)} %get-tuple-element.43), channel_id=1, source_target_pairs={{0,8},{4,12},{8,0},{12,4},{16,24},{20,28},{24,16},{28,20},{1,9},{5... | collective-permute-start | bytes 884744 | tf_op jit(solution)/shard_map/ppermute | solution.py:20
  50.7 25.3 %collective-permute-start.18 = (bf16[128,1152]{1,0:T(8,128)(2,1)S(1)}, bf16[128,1152]{1,0:T(8,128)(2,1)S(1)}, u32[]{:S(2)}, u32[]{:S(2)}) collective-permute-start(bf16[128,1152]{1,0:T(8,128)(2,1)S(1)} %get-tuple-element.44), channel_id=1, source_target_pairs={{0,1},{1,0},{2,3},{3,2},{4,5},{5,4},{6,7},{7,6},{8,9},{9,8},{10,11... | collective-permute-start | bytes 884744 | tf_op jit(solution)/shard_map/ppermute | solution.py:20
  55.6 21.0 %collective-permute-start.19 = (bf16[128,1152]{1,0:T(8,128)(2,1)S(1)}, bf16[128,1152]{1,0:T(8,128)(2,1)S(1)}, u32[]{:S(2)}, u32[]{:S(2)}) collective-permute-start(bf16[128,1152]{1,0:T(8,128)(2,1)S(1)} %get-tuple-element.45), channel_id=1, source_target_pairs={{0,9},{1,8},{2,11},{3,10},{4,13},{5,12},{6,15},{7,14},{8,1},{9,0},... | collective-permute-start | bytes 884744 | tf_op jit(solution)/shard_map/ppermute | solution.py:30
  58.9 12.4 %collective-permute-start.8 = (bf16[656,128]{1,0:T(8,128)(2,1)S(1)}, bf16[656,128]{1,0:T(8,128)(2,1)S(1)}, u32[]{:S(2)}, u32[]{:S(2)}) collective-permute-start(bf16[656,128]{1,0:T(8,128)(2,1)S(1)} %get-tuple-element.27), channel_id=1, source_target_pairs={{0,2},{1,3},{2,0},{3,1},{4,6},{5,7},{6,4},{7,5},{8,10},{9,11},{10,... | collective-permute-start | bytes 503816 | tf_op jit(solution)/shard_map/ppermute | solution.py:20
  62.3 12.6 %collective-permute-start.15 = (bf16[128,512]{1,0:T(8,128)(2,1)S(1)}, bf16[128,512]{1,0:T(8,128)(2,1)S(1)}, u32[]{:S(2)}, u32[]{:S(2)}) collective-permute-start(bf16[128,512]{1,0:T(8,128)(2,1)S(1)} %shard_map.72), channel_id=1, source_target_pairs={{0,2},{1,3},{2,0},{3,1},{4,6},{5,7},{6,4},{7,5},{8,10},{9,11},{10,... | collective-permute-start | bytes 393224 | tf_op jit(solution)/shard_map/ppermute | solution.py:20

commit v3 on v2

v3 whole, which is shorter than its diff:
```python
import functools

import jax
import jax.numpy as jnp
from jax import lax
from jax.experimental import pallas as pl
from jax.experimental.pallas import tpu as pltpu
from jax.sharding import PartitionSpec as P

epsilon = 1e-06
f32, bf16 = jnp.float32, jnp.bfloat16
lanes = 128
extra = 16
direct_panels = 5
VMEM = pl.BlockSpec(memory_space=pltpu.VMEM)
SMEM = pl.BlockSpec(memory_space=pltpu.SMEM)
ANY = pl.BlockSpec(memory_space=pl.ANY)


def swapped(value, axis, step):
    return lax.ppermute(value, axis, [(place, place ^ step) for place in range(lax.axis_size(axis))])


def swapped_both(value, dp_step, inner_step):
    dp_count, inner_count = lax.axis_size("dp"), lax.axis_size("inner")
    pairs = [
        (d * inner_count + i, (d ^ dp_step) * inner_count + (i ^ inner_step))
        for d in range(dp_count)
        for i in range(inner_count)
    ]
    return lax.ppermute(value, ("dp", "inner"), pairs)


def call(kernel, out_shape, *operands, flops=0, scalars=0, scratch=(), after=()):
    moved = sum(o.size * o.dtype.itemsize for o in operands)
    moved += sum(o.size * o.dtype.itemsize for o in jax.tree.leaves(out_shape))
    body_of = kernel
    if after:
        body_of = lambda *refs: kernel(*refs[len(after) :])
    return pl.pallas_call(
        body_of,
        out_shape=out_shape,
        in_specs=[ANY] * len(after) + [SMEM] * scalars + [VMEM] * (len(operands) - scalars),
        out_specs=jax.tree.map(lambda _: VMEM, out_shape),
        scratch_shapes=scratch,
        compiler_params=pltpu.CompilerParams(vmem_limit_bytes=40 * 1024 * 1024),
        cost_estimate=pl.CostEstimate(flops=flops, bytes_accessed=moved, transcendentals=0),
    )(*after, *operands)


def shape(dims, kind):
    return jax.ShapeDtypeStruct(dims, kind)


def unit_of(rows):
    wide = rows.astype(f32)
    inverse = lax.rsqrt(jnp.sum(wide * wide, axis=-1, keepdims=True) + epsilon)
    return wide * inverse, inverse


def pair_terms(scale, offset, text_refs, image_emb, slopes_ref, own):
    rows = image_emb.shape[0]
    total = jnp.zeros((1, rows), f32)
    step = 256
    done = 0
    for texts in text_refs:
        for start in range(0, texts.shape[0], step):
            chunk = texts[start : min(start + step, texts.shape[0]), :]
            logits = (
                scale
                * lax.dot_general(
                    chunk, image_emb, (((1,), (1,)), ((), ())), preferred_element_type=f32
                )
                + offset
            )
            shrunk = jnp.exp(-jnp.abs(logits))
            softplus = jnp.maximum(logits, 0.0) + jnp.log1p(shrunk)
            sigmoid = jnp.where(logits >= 0.0, 1.0, shrunk) / (1.0 + shrunk)
            if own and done == 0:
                text_ids = lax.broadcasted_iota(jnp.int32, logits.shape, 0)
                image_ids = lax.broadcasted_iota(jnp.int32, logits.shape, 1)
                match = (text_ids == image_ids).astype(f32)
                softplus = softplus - match * logits
                sigmoid = sigmoid - match
            slopes_ref[done : done + chunk.shape[0], :] = sigmoid.astype(bf16)
            total = total + jnp.sum(softplus, axis=0, keepdims=True)
            done += chunk.shape[0]
    return total


def image_sums(slopes_ref, text_refs):
    total, done = None, 0
    for texts in text_refs:
        count = texts.shape[0]
        part = lax.dot_general(
            slopes_ref[done : done + count, :],
            texts[...],
            (((0,), (0,)), ((), ())),
            preferred_element_type=f32,
        )
        total, done = part if total is None else total + part, done + count
    return total


def stage_kernel(fetched, *refs):
    text_refs, image_ref = refs[: 2 + fetched], refs[2 + fetched]
    out_ref, half_ref, forward_refs = refs[3 + fetched], refs[4 + fetched], refs[5 + fetched :]
    rows = image_ref.shape[0]
    for place, raw in enumerate(text_refs):
        emb = unit_of(raw[...])[0].astype(bf16)
        out_ref[place * rows : (place + 1) * rows, :] = emb
        if place >= 2:
            forward_refs[place - 2][...] = emb
    half_ref[...] = unit_of(image_ref[rows // 2 :, :])[0].astype(bf16)


def own_kernel(scale_ref, bias_ref, image_ref, *refs):
    text_refs, (slopes_ref, emb_ref, grad_ref, loss_ref) = refs[:-4], refs[-4:]
    emb_ref[...] = unit_of(image_ref[...])[0].astype(bf16)
    loss_ref[...] = pair_terms(
        scale_ref[0], bias_ref[0], text_refs, emb_ref[...], slopes_ref, True
    )
    grad_ref[...] = image_sums(slopes_ref, text_refs)


def peer_kernel(texts, halves, scale_ref, bias_ref, *refs):
    text_refs, image_refs = refs[:texts], refs[texts : texts + (2 if halves else 1)]
    slopes_ref, emb_ref, head_ref, *tail_ref = refs[texts + len(image_refs) :]
    rows = emb_ref.shape[0]
    panels = (head_ref.shape[0] - extra) // rows
    if halves:
        emb_ref[: rows // 2, :] = unit_of(image_refs[0][...])[0].astype(bf16)
        emb_ref[rows // 2 :, :] = image_refs[1][...]
    else:
        emb_ref[...] = unit_of(image_refs[0][...])[0].astype(bf16)
    loss = pair_terms(scale_ref[0], bias_ref[0], text_refs, emb_ref[...], slopes_ref, False)
    sums = image_sums(slopes_ref, text_refs)
    for panel in range(panels):
        head_ref[panel * rows : (panel + 1) * rows, :] = sums[
            :, panel * lanes : (panel + 1) * lanes
        ].astype(bf16)
    if tail_ref:
        tail_ref[0][...] = sums[:, panels * lanes :].astype(tail_ref[0].dtype)
    high = loss.astype(bf16).astype(f32)
    which = lax.broadcasted_iota(jnp.int32, (extra, rows), 0)
    head_ref[panels * rows :, :] = jnp.where(which == 0, high, loss - high).astype(bf16)


def text_sums(slopes, embs, place, rows):
    left = jnp.concatenate([s[place * rows : (place + 1) * rows, :] for s in slopes], axis=1)
    return jnp.dot(left, embs, preferred_element_type=f32)


def other_core_kernel(count, *refs):
    slopes, emb_refs, sent_ref = refs[:count], refs[count : 2 * count], refs[2 * count]
    rows = emb_refs[0].shape[0]
    embs = jnp.concatenate([e[...] for e in emb_refs], axis=0)
    places = slopes[0].shape[0] // rows // 2
    for k in range(places):
        sent_ref[k * rows : (k + 1) * rows, :] = text_sums(slopes, embs, places + k, rows).astype(bf16)


def own_core_kernel(count, received_ref, *refs):
    slopes, emb_refs = refs[:count], refs[count : 2 * count]
    rows = emb_refs[0].shape[0]
    embs = jnp.concatenate([e[...] for e in emb_refs], axis=0)
    for k, out in enumerate(refs[2 * count :]):
        sums = text_sums(slopes, embs, k, rows) + received_ref[k * rows : (k + 1) * rows, :].astype(f32)
        out[...] = sums.astype(out.dtype)


def late_kernel(sums, parts, *refs):
    payloads = (len(refs) - 2 * sums - sums * parts) // 2
    own, received = refs[:sums], refs[sums : sums + sums * parts]
    passed, outs = refs[sums + sums * parts :][:payloads], refs[sums + sums * parts + payloads :]
    for k in range(sums):
        total = own[k][...]
        for part in received[k * parts : (k + 1) * parts]:
            total = total + part[...].astype(f32)
        outs[k][...] = total.astype(bf16)
    for source, target in zip(passed, outs[sums:]):
        target[...] = source[...]


def row_gradient(rows, sums, scale, out_ref):
    unit_rows, inverse = unit_of(rows)
    unit_grad = scale * sums
    out_ref[...] = (
        unit_grad - unit_rows * jnp.sum(unit_rows * unit_grad, axis=-1, keepdims=True)
    ) * inverse


def image_end_kernel(batch, heads, scale_ref, image_ref, grad_ref, loss_ref, *refs):
    out_ref, out_loss_ref, sums_ref = refs[-3:]
    head_refs, tail_refs = refs[:heads], refs[heads:-3]
    rows, width = image_ref.shape
    loss = loss_ref[...]
    for panel in range(width // lanes):
        cut = slice(panel * lanes, (panel + 1) * lanes)
        sums = grad_ref[:, cut]
        for r in head_refs:
            if (panel + 1) * rows <= r.shape[0] - extra:
                sums = sums + r[panel * rows : (panel + 1) * rows, :].astype(f32)
        for r in tail_refs:
            first = panel * lanes - (width - r.shape[1])
            if first >= 0:
                sums = sums + r[:, first : first + lanes].astype(f32)
        sums_ref[:, cut] = sums
    for r in head_refs:
        last = r[r.shape[0] - extra :, :].astype(f32)
        loss = loss + (last[0:1, :] + last[1:2, :])
    row_gradient(image_ref[...], sums_ref[...], scale_ref[0], out_ref)
    out_loss_ref[...] = loss / batch


def text_end_kernel(scale_ref, text_ref, grad_ref, *refs):
    sums = grad_ref[...]
    for r in refs[:-1]:
        sums = sums + r[...].astype(f32)
    row_gradient(text_ref[...], sums, scale_ref[0], refs[-1])


def body(image, text, logarithm_scale, bias):
    rows, width = image.shape
    dp_count, inner_count = lax.axis_size("dp"), lax.axis_size("inner")
    batch = rows * dp_count * inner_count
    scale = jnp.exp(logarithm_scale)
    block = shape((rows, width), bf16)
    wide_block = shape((rows, width), f32)

    text_places = [(0, 0), (2, 0), (0, 1), (2, 1)]
    image_dp, image_inner = range(4, dp_count, 4), range(2, inner_count, 2)

    first_half = image[: rows // 2]
    halves = {q: swapped(first_half, "inner", q) for q in image_inner}
    text_z = swapped(text, "inner", 1)
    text_x = swapped(text, "dp", 2)
    images = {(p, 0): (swapped(image, "dp", p),) for p in image_dp}
    near_texts, second_half, text_z_emb = call(
        functools.partial(stage_kernel, 1),
        (shape((3 * rows, width), bf16), shape((rows // 2, width), bf16), block),
        text,
        text_x,
        text_z,
        image,
        after=[*halves.values(), *(i for (i,) in images.values())],
    )

    far_text = swapped(text_z_emb, "dp", 2)
    near_swapped = swapped(near_texts, "dp", 1)
    second_halves = {q: swapped(second_half, "inner", q) for q in image_inner}
    for q in image_inner:
        images[0, q] = (halves[q], second_halves[q])
        for p in image_dp:
            images[p, q] = (swapped(halves[q], "dp", p), swapped(second_halves[q], "dp", p))
    far_swapped = swapped(far_text, "dp", 1)
    texts = [near_texts, far_text, near_swapped, far_swapped]

    texts_held = 2 * len(text_places) * rows
    block_flops = 2 * rows * texts_held * width
    slopes, embs, heads, tails, whole = {}, {}, {}, {}, {}
    head_rows = direct_panels * rows + extra
    tail_width = width - direct_panels * lanes
    first = [images[p, q][0] for p in image_dp for q in image_inner]
    for q in image_inner:
        slopes[0, q], embs[0, q], heads[0, q], tails[0, q] = call(
            functools.partial(peer_kernel, len(texts), True),
            (
                shape((texts_held, rows), bf16),
                block,
                shape((head_rows, lanes), bf16),
                shape((rows, tail_width), f32),
            ),
            scale,
            bias,
            *texts,
            *images[0, q],
            flops=2 * block_flops,
            scalars=2,
            after=first,
        )
    first = [heads[0, q] for q in image_inner]
    for p in image_dp:
        slopes[p, 0], embs[p, 0], whole[p] = call(
            functools.partial(peer_kernel, len(texts), False),
            (
                shape((texts_held, rows), bf16),
                block,
                shape((width // lanes * rows + extra, lanes), bf16),
            ),
            scale,
            bias,
            *texts,
            *images[p, 0],
            flops=2 * block_flops,
            scalars=2,
            after=first,
        )
    slopes[0, 0], embs[0, 0], image_grad, loss = call(
        own_kernel,
        (shape((texts_held, rows), bf16), block, wide_block, shape((1, rows), f32)),
        scale,
        bias,
        image,
        *texts,
        flops=2 * block_flops,
        scalars=2,
        after=first,
    )
    for p in image_dp:
        for q in image_inner:
            slopes[p, q], embs[p, q], heads[p, q], tails[p, q] = call(
                functools.partial(peer_kernel, len(texts), True),
                (
                    shape((texts_held, rows), bf16),
                    block,
                    shape((head_rows, lanes), bf16),
                    shape((rows, tail_width), bf16),
                ),
                scale,
                bias,
                *texts,
                *images[p, q],
                flops=2 * block_flops,
                scalars=2,
                after=[image_grad],
            )

    near_heads = [swapped(heads[0, q], "inner", q) for q in image_inner]
    far_heads = [swapped_both(heads[p, q], p, q) for p in image_dp for q in image_inner]
    moved_tails = [swapped(tails[p, q], "dp", p) for q in image_inner for p in image_dp]
    late = call(
        functools.partial(late_kernel, len(image_inner), len(image_dp)),
        [shape((rows, tail_width), bf16)] * len(image_inner)
        + [shape(whole[p].shape, bf16) for p in image_dp],
        *(tails[0, q] for q in image_inner),
        *moved_tails,
        *whole.values(),
        after=near_heads,
    )
    tail_parts = [swapped(part, "inner", q) for part, q in zip(late, image_inner)]
    whole_parts = [swapped(part, "dp", p) for part, p in zip(late[len(image_inner) :], image_dp)]

    ordered = sorted(slopes)
    pieces = [slopes[place] for place in ordered] + [embs[place] for place in ordered]
    crossing = call(
        functools.partial(other_core_kernel, len(ordered)),
        shape((texts_held // 2, width), bf16),
        *pieces,
        flops=len(ordered) * block_flops // 2,
    )
    crossed = swapped(crossing, "dp", 1)
    text_grad, *text_sent = call(
        functools.partial(own_core_kernel, len(ordered)),
        (wide_block,) + (block,) * (len(text_places) - 1),
        crossed,
        *pieces,
        flops=len(ordered) * block_flops // 2,
    )
    text_parts = [
        swapped_both(part, p, q) if p and q else swapped(part, *(("dp", p) if p else ("inner", q)))
        for part, (p, q) in zip(text_sent, text_places[1:])
    ]

    head_parts = near_heads + far_heads + whole_parts
    image_gradient, image_loss = call(
        functools.partial(image_end_kernel, batch, len(head_parts)),
        (wide_block, shape((1, rows), f32)),
        scale,
        image,
        image_grad,
        loss,
        *head_parts,
        *tail_parts,
        scalars=1,
        scratch=[pltpu.VMEM((rows, width), f32)],
    )
    text_gradient = call(text_end_kernel, wide_block, scale, text, text_grad, *text_parts, scalars=1)
    return (image_gradient, text_gradient, image_loss.reshape(rows))


def solution(mesh):
    return jax.shard_map(
        body,
        mesh=mesh,
        in_specs=(P(("dp", "inner"), None), P(("dp", "inner"), None), P(), P()),
        out_specs=(P(("dp", "inner"), None), P(("dp", "inner"), None), P(("dp", "inner"))),
        check_vma=False,
    )
```

time: 77.9 us -> 83.8 us (1.076)
  waiting for transfers between devices: 37.1 us -> 47 us
  starting transfers between devices: 26.2 us -> 20.1 us
  local copies, waits for them, and re-layouts: 1.19 us -> 2.89 us
    ppermute x18 -> x17, waiting for transfers between devices: 36.6 us -> 45.7 us  [swapped(): lax.ppermute(value, axis, [(place, place ^ step) for place in range(lax.a...]
    ppermute x18 -> x17, starting transfers between devices: 22.2 us -> 15 us  [swapped(): lax.ppermute(value, axis, [(place, place ^ step) for place in range(lax.a...]
    ppermute x2, starting transfers between devices: 3.95 us -> 5.12 us  [swapped_both(): return lax.ppermute(value, ('dp', 'inner'), pairs)]
    slice x0 -> x1, local copies, waits for them, and re-layouts: none -> 0.95 us  [body(): first_half = image[:rows // 2]]
    unnamed x6 -> x8, local copies, waits for them, and re-layouts: 1.19 us -> 1.93 us
  transfers between devices with their start and end apart: 20 -> 19, of which waited for: 10 -> 8; matrix products, arithmetic and copies ran while one was open for 0% -> 1% of each run, Pallas kernels for 10% -> 9%
where the time goes in v3:
time: 83.8 us; the launch traced here: 83.5 us
  waiting for transfers between devices  47 us (56%)
  starting transfers between devices  20.1 us (24%)
  Pallas kernels  11.4 us (14%)
  local copies, waits for them, and re-layouts  2.89 us (3%)
  between operations  2.11 us (3%)
    ppermute x17, waiting for transfers between devices, swapped(): lax.ppermute(value, axis, [(place, place ^ step) for place in range(lax.a...  45.7 us
    ppermute x17, starting transfers between devices, swapped(): lax.ppermute(value, axis, [(place, place ^ step) for place in range(lax.a...  15 us
    pallas_call x10, Pallas kernels, call(): pl.pallas_call(body_of, out_shape=out_shape, in_specs=[ANY] * len(after)...  11.4 us
    ppermute x2, starting transfers between devices, swapped_both(): return lax.ppermute(value, ('dp', 'inner'), pairs)  5.12 us
    unnamed x8, local copies, waits for them, and re-layouts  1.93 us
  transfers between devices with their start and end apart: 19, of which 8 were waited for; matrix products, arithmetic and copies ran while one was open for 1% of the time, Pallas kernels for 9%

profile of v3, /device:TPU:0, one launch (start us, length us, event | category | flops | bytes accessed | tf_op | source)
XLA Modules:
  0.0 83.5 jit_solution(8021524334888952458)
XLA Ops:
  0.6 3.1 %collective-permute-start.4 = (bf16[128,1152]{1,0:T(8,128)(2,1)}, bf16[128,1152]{1,0:T(8,128)(2,1)S(1)}, u32[]{:S(2)}, u32[]{:S(2)}) collective-permute-start(bf16[128,1152]{1,0:T(8,128)(2,1)} %text_ref.1), channel_id=1, source_target_pairs={{0,1},{1,0},{2,3},{3,2},{4,5},{5,4},{6,7},{7,6},{8,9},{9,8},{10,11... | collective-permute-start | bytes 884744 | tf_op jit(solution)/shard_map/ppermute | solution.py:21
  3.7 1.5 %collective-permute-start.3 = (bf16[128,1152]{1,0:T(8,128)(2,1)}, bf16[128,1152]{1,0:T(8,128)(2,1)S(1)}, u32[]{:S(2)}, u32[]{:S(2)}) collective-permute-start(bf16[128,1152]{1,0:T(8,128)(2,1)} %text_ref.1), channel_id=1, source_target_pairs={{0,8},{4,12},{8,0},{12,4},{16,24},{20,28},{24,16},{28,20},{1,9},{5... | collective-permute-start | bytes 884744 | tf_op jit(solution)/shard_map/ppermute | solution.py:21
  5.2 1.5 %collective-permute-start.2 = (bf16[128,1152]{1,0:T(8,128)(2,1)}, bf16[128,1152]{1,0:T(8,128)(2,1)S(1)}, u32[]{:S(2)}, u32[]{:S(2)}) collective-permute-start(bf16[128,1152]{1,0:T(8,128)(2,1)} %image_ref.1), channel_id=1, source_target_pairs={{0,16},{4,20},{8,24},{12,28},{16,0},{20,4},{24,8},{28,12},{1,17},{... | collective-permute-start | bytes 884744 | tf_op jit(solution)/shard_map/ppermute | solution.py:21
  6.7 1.0 %slice.3 = bf16[64,1152]{1,0:T(8,128)(2,1)S(1)} slice(bf16[128,1152]{1,0:T(8,128)(2,1)} %image_ref.1), slice={[0:64], [0:1152]} | slice | bytes 294912 | tf_op jit(solution)/shard_map/slice | solution.py:234
  7.7 2.7 %collective-permute-start = (bf16[64,1152]{1,0:T(8,128)(2,1)S(1)}, bf16[64,1152]{1,0:T(8,128)(2,1)S(1)}, u32[]{:S(2)}, u32[]{:S(2)}) collective-permute-start(bf16[64,1152]{1,0:T(8,128)(2,1)S(1)} %slice.3), channel_id=1, source_target_pairs={{0,2},{1,3},{2,0},{3,1},{4,6},{5,7},{6,4},{7,5},{8,10},{9,11},{10,... | collective-permute-start | bytes 442376 | tf_op jit(solution)/shard_map/ppermute | solution.py:21
  10.3 6.5 %collective-permute-done.refs_0_.refs_7_ = bf16[64,1152]{1,0:T(8,128)(2,1)S(1)} collective-permute-done((bf16[64,1152]{1,0:T(8,128)(2,1)S(1)}, bf16[64,1152]{1,0:T(8,128)(2,1)S(1)}, u32[]{:S(2)}, u32[]{:S(2)}) %collective-permute-start) | collective-permute-done | bytes 147488 | tf_op jit(solution)/shard_map/ppermute | solution.py:21
  17.8 1.0 %copy-done.2 = bf16[128,1152]{1,0:T(8,128)(2,1)S(1)} copy-done((bf16[128,1152]{1,0:T(8,128)(2,1)S(1)}, bf16[128,1152]{1,0:T(8,128)(2,1)}, u32[]{:S(2)}) %copy-start.2) | copy-done | bytes 294936
  19.3 9.3 %collective-permute-done.5.refs_4_.refs_5_ = bf16[128,1152]{1,0:T(8,128)(2,1)S(1)} collective-permute-done((bf16[128,1152]{1,0:T(8,128)(2,1)S(1)}, bf16[128,1152]{1,0:T(8,128)(2,1)S(1)}, u32[]{:S(2)}, u32[]{:S(2)}) %collective-permute-start.5) | collective-permute-done | bytes 294944 | tf_op jit(solution)/shard_map/ppermute | solution.py:21
  28.6 1.5 %collective-permute-start.1 = (bf16[64,1152]{1,0:T(8,128)(2,1)S(1)}, bf16[64,1152]{1,0:T(8,128)(2,1)S(1)}, u32[]{:S(2)}, u32[]{:S(2)}) collective-permute-start(bf16[64,1152]{1,0:T(8,128)(2,1)S(1)} %collective-permute-done.refs_0_.refs_7_), channel_id=1, source_target_pairs={{0,16},{4,20},{8,24},{12,28},{16,0},{20,4},{24,8},{28,12},{1,17},{... | collective-permute-start | bytes 442376 | tf_op jit(solution)/shard_map/ppermute | solution.py:21
  31.5 7.1 %collective-permute-done.8.refs_8_ = bf16[64,1152]{1,0:T(8,128)(2,1)S(1)} collective-permute-done((bf16[64,1152]{1,0:T(8,128)(2,1)S(1)}, bf16[64,1152]{1,0:T(8,128)(2,1)S(1)}, u32[]{:S(2)}, u32[]{:S(2)}) %collective-permute-start.8) | collective-permute-done | bytes 147488 | tf_op jit(solution)/shard_map/ppermute | solution.py:21
  38.6 1.7 %shard_map.68 = (bf16[1024,128]{1,0:T(8,128)(2,1)S(1)}, bf16[128,1152]{1,0:T(8,128)(2,1)S(1)}, bf16[656,128]{1,0:T(8,128)(2,1)S(1)}, f32[128,512]{1,0:T(8,128)S(1)}) custom-call(bf16[64,1152]{1,0:T(8,128)(2,1)S(1)} %collective-permute-done.1.refs_0_.refs_7_, f32[1]{0:T(128)S(6)} %exp.3.refs_1_.scale_ref, f32[1]{0:T(128)S(6)} %copy.8.refs_2_, ...), custom_call_target="tpu_custom_call" | custom-call | flops 603979776 | bytes 3641352 | tf_op jit(solution)/shard_map/pallas_call | solution.py:40
  40.3 1.7 %shard_map.71 = (bf16[1024,128]{1,0:T(8,128)(2,1)S(1)}, bf16[128,1152]{1,0:T(8,128)(2,1)S(1)}, bf16[1168,128]{1,0:T(8,128)(2,1)S(1)}) custom-call(bf16[656,128]{1,0:T(8,128)(2,1)S(1)} %get-tuple-element.32.refs_0_, f32[1]{0:T(128)S(6)} %exp.3.refs_1_.scale_ref, f32[1]{0:T(128)S(6)} %copy.8.refs_2_, bf16[384,1152]{1,0:T(8,128)(2,1)S(1)} %get-tuple-element.29.refs_3_.refs_4_, ...), custom_call_target="tpu_custom_call" | custom-call | flops 603979776 | bytes 3510280 | tf_op jit(solution)/shard_map/pallas_call | solution.py:40
  42.1 1.7 %shard_map.69 = (bf16[1024,128]{1,0:T(8,128)(2,1)S(1)}, bf16[128,1152]{1,0:T(8,128)(2,1)S(1)}, f32[128,1152]{1,0:T(8,128)S(1)}, f32[1,128]{1,0:T(1,128)S(1)}) custom-call(bf16[656,128]{1,0:T(8,128)(2,1)S(1)} %get-tuple-element.32.refs_0_, f32[1]{0:T(128)S(6)} %exp.3.refs_1_.scale_ref, f32[1]{0:T(128)S(6)} %copy.8.refs_2_, bf16[128,1152]{1,0:T(8,128)(2,1)S(1)} %copy-done.1, ...), custom_call_target="tpu_custom_call" | custom-call | flops 603979776 | bytes 3801608 | tf_op jit(solution)/shard_map/pallas_call | solution.py:40
  44.4 1.7 %shard_map.70 = (bf16[1024,128]{1,0:T(8,128)(2,1)S(1)}, bf16[128,1152]{1,0:T(8,128)(2,1)S(1)}, bf16[656,128]{1,0:T(8,128)(2,1)S(1)}, bf16[128,512]{1,0:T(8,128)(2,1)S(1)}) custom-call(f32[128,1152]{1,0:T(8,128)S(1)} %get-tuple-element.33.refs_0_.grad_ref, f32[1]{0:T(128)S(6)} %exp.3.refs_1_.scale_ref, f32[1]{0:T(128)S(6)} %copy.8.refs_2_, ...), custom_call_target="tpu_custom_call" | custom-call | flops 603979776 | bytes 3510280 | tf_op jit(solution)/shard_map/pallas_call | solution.py:40
  47.1 1.5 %collective-permute-start.12 = (bf16[128,512]{1,0:T(8,128)(2,1)S(1)}, bf16[128,512]{1,0:T(8,128)(2,1)S(1)}, u32[]{:S(2)}, u32[]{:S(2)}) collective-permute-start(bf16[128,512]{1,0:T(8,128)(2,1)S(1)} %get-tuple-element.37), channel_id=1, source_target_pairs={{0,16},{4,20},{8,24},{12,28},{16,0},{20,4},{24,8},{28,12},{1,17},{... | collective-permute-start | bytes 393224 | tf_op jit(solution)/shard_map/ppermute | solution.py:21
  48.7 2.8 %collective-permute-start.11 = (bf16[656,128]{1,0:T(8,128)(2,1)S(1)}, bf16[656,128]{1,0:T(8,128)(2,1)S(1)}, u32[]{:S(2)}, u32[]{:S(2)}) collective-permute-start(bf16[656,128]{1,0:T(8,128)(2,1)S(1)} %get-tuple-element.35), channel_id=1, source_target_pairs={{0,18},{1,19},{2,16},{3,17},{4,22},{5,23},{6,20},{7,21},{8,26},{9,... | collective-permute-start | bytes 503816 | tf_op jit(solution)/shard_map/ppermute | solution.py:31
  51.5 1.4 %collective-permute-done.12.refs_2_ = bf16[128,512]{1,0:T(8,128)(2,1)S(1)} collective-permute-done((bf16[128,512]{1,0:T(8,128)(2,1)S(1)}, bf16[128,512]{1,0:T(8,128)(2,1)S(1)}, u32[]{:S(2)}, u32[]{:S(2)}) %collective-permute-start.12) | collective-permute-done | bytes 131104 | tf_op jit(solution)/shard_map/ppermute | solution.py:21
  53.0 8.5 %collective-permute-done.9.refs_0_ = bf16[656,128]{1,0:T(8,128)(2,1)S(1)} collective-permute-done((bf16[656,128]{1,0:T(8,128)(2,1)S(1)}, bf16[656,128]{1,0:T(8,128)(2,1)S(1)}, u32[]{:S(2)}, u32[]{:S(2)}) %collective-permute-start.9) | collective-permute-done | bytes 167968 | tf_op jit(solution)/shard_map/ppermute | solution.py:21
  63.3 1.3 %collective-permute-start.16 = (bf16[128,1152]{1,0:T(8,128)(2,1)S(1)}, bf16[128,1152]{1,0:T(8,128)(2,1)S(1)}, u32[]{:S(2)}, u32[]{:S(2)}) collective-permute-start(bf16[128,1152]{1,0:T(8,128)(2,1)S(1)} %get-tuple-element.51), channel_id=1, source_target_pairs={{0,8},{4,12},{8,0},{12,4},{16,24},{20,28},{24,16},{28,20},{1,9},{5... | collective-permute-start | bytes 884744 | tf_op jit(solution)/shard_map/ppermute | solution.py:21
  64.6 2.3 %collective-permute-start.18 = (bf16[128,1152]{1,0:T(8,128)(2,1)S(1)}, bf16[128,1152]{1,0:T(8,128)(2,1)S(1)}, u32[]{:S(2)}, u32[]{:S(2)}) collective-permute-start(bf16[128,1152]{1,0:T(8,128)(2,1)S(1)} %get-tuple-element.53), channel_id=1, source_target_pairs={{0,9},{1,8},{2,11},{3,10},{4,13},{5,12},{6,15},{7,14},{8,1},{9,0},... | collective-permute-start | bytes 884744 | tf_op jit(solution)/shard_map/ppermute | solution.py:31
  67.7 12.2 %collective-permute-done.14.refs_3_ = bf16[128,512]{1,0:T(8,128)(2,1)S(1)} collective-permute-done((bf16[128,512]{1,0:T(8,128)(2,1)S(1)}, bf16[128,512]{1,0:T(8,128)(2,1)S(1)}, u32[]{:S(2)}, u32[]{:S(2)}) %collective-permute-start.14) | collective-permute-done | bytes 131104 | tf_op jit(solution)/shard_map/ppermute | solution.py:21
  79.9 1.2 %shard_map.73 = (f32[128,1152]{1,0:T(8,128)}, f32[1,128]{1,0:T(1,128)}) custom-call(f32[1]{0:T(128)S(6)} %exp.3.refs_1_.scale_ref, bf16[128,1152]{1,0:T(8,128)(2,1)S(1)} %copy-done.1, f32[128,1152]{1,0:T(8,128)S(1)} %get-tuple-element.33.refs_0_.grad_ref, f32[1,128]{1,0:T(1,128)S(1)} %get-tuple-element.34.loss_ref, ...), custom_call_target="tpu_custom_call" | custom-call | bytes 2241540 | tf_op jit(solution)/shard_map/pallas_call | solution.py:40
  81.1 1.3 %collective-permute-done.18.refs_2_ = bf16[128,1152]{1,0:T(8,128)(2,1)S(1)} collective-permute-done((bf16[128,1152]{1,0:T(8,128)(2,1)S(1)}, bf16[128,1152]{1,0:T(8,128)(2,1)S(1)}, u32[]{:S(2)}, u32[]{:S(2)}) %collective-permute-start.18) | collective-permute-done | bytes 294944 | tf_op jit(solution)/shard_map/ppermute | solution.py:31
  82.4 1.2 %shard_map.76 = f32[128,1152]{1,0:T(8,128)} custom-call(f32[1]{0:T(128)S(6)} %exp.3.refs_1_.scale_ref, bf16[128,1152]{1,0:T(8,128)(2,1)S(1)} %copy-done.3, f32[128,1152]{1,0:T(8,128)S(1)} %get-tuple-element.50.grad_ref, bf16[128,1152]{1,0:T(8,128)(2,1)S(1)} %collective-permute-done.16.refs_0_, bf16[128,1152]{1,0:T(8,128)(2,1)S(1)} %collective-permute-done.17.refs_1_, ...), custom_call_target="tpu_custom_call" | custom-call | bytes 2359300 | tf_op jit(solution)/shard_map/pallas_call | solution.py:40
  (33 shorter events, 5.7 us)
Async XLA Ops:
  0.6 16.2 %collective-permute-start.4 = (bf16[128,1152]{1,0:T(8,128)(2,1)}, bf16[128,1152]{1,0:T(8,128)(2,1)S(1)}, u32[]{:S(2)}, u32[]{:S(2)}) collective-permute-start(bf16[128,1152]{1,0:T(8,128)(2,1)} %text_ref.1), channel_id=1, source_target_pairs={{0,1},{1,0},{2,3},{3,2},{4,5},{5,4},{6,7},{7,6},{8,9},{9,8},{10,11... | collective-permute-start | bytes 884744 | tf_op jit(solution)/shard_map/ppermute | solution.py:21
  3.7 13.1 %collective-permute-start.3 = (bf16[128,1152]{1,0:T(8,128)(2,1)}, bf16[128,1152]{1,0:T(8,128)(2,1)S(1)}, u32[]{:S(2)}, u32[]{:S(2)}) collective-permute-start(bf16[128,1152]{1,0:T(8,128)(2,1)} %text_ref.1), channel_id=1, source_target_pairs={{0,8},{4,12},{8,0},{12,4},{16,24},{20,28},{24,16},{28,20},{1,9},{5... | collective-permute-start | bytes 884744 | tf_op jit(solution)/shard_map/ppermute | solution.py:21
  5.2 11.6 %collective-permute-start.2 = (bf16[128,1152]{1,0:T(8,128)(2,1)}, bf16[128,1152]{1,0:T(8,128)(2,1)S(1)}, u32[]{:S(2)}, u32[]{:S(2)}) collective-permute-start(bf16[128,1152]{1,0:T(8,128)(2,1)} %image_ref.1), channel_id=1, source_target_pairs={{0,16},{4,20},{8,24},{12,28},{16,0},{20,4},{24,8},{28,12},{1,17},{... | collective-permute-start | bytes 884744 | tf_op jit(solution)/shard_map/ppermute | solution.py:21
  7.7 9.1 %collective-permute-start = (bf16[64,1152]{1,0:T(8,128)(2,1)S(1)}, bf16[64,1152]{1,0:T(8,128)(2,1)S(1)}, u32[]{:S(2)}, u32[]{:S(2)}) collective-permute-start(bf16[64,1152]{1,0:T(8,128)(2,1)S(1)} %slice.3), channel_id=1, source_target_pairs={{0,2},{1,3},{2,0},{3,1},{4,6},{5,7},{6,4},{7,5},{8,10},{9,11},{10,... | collective-permute-start | bytes 442376 | tf_op jit(solution)/shard_map/ppermute | solution.py:21
  16.8 1.0 %copy-start = (bf16[128,1152]{1,0:T(8,128)(2,1)S(1)}, bf16[128,1152]{1,0:T(8,128)(2,1)}, u32[]{:S(2)}) copy-start(bf16[128,1152]{1,0:T(8,128)(2,1)} %image_ref.1) | copy-start | bytes 884740
  17.8 1.0 %copy-start.2 = (bf16[128,1152]{1,0:T(8,128)(2,1)S(1)}, bf16[128,1152]{1,0:T(8,128)(2,1)}, u32[]{:S(2)}) copy-start(bf16[128,1152]{1,0:T(8,128)(2,1)} %text_ref.1) | copy-start | bytes 884740
  19.1 19.4 %collective-permute-start.6 = (bf16[384,1152]{1,0:T(8,128)(2,1)S(1)}, bf16[384,1152]{1,0:T(8,128)(2,1)S(1)}, u32[]{:S(2)}, u32[]{:S(2)}) collective-permute-start(bf16[384,1152]{1,0:T(8,128)(2,1)S(1)} %get-tuple-element.29.refs_3_.refs_4_), channel_id=1, source_target_pairs={{0,4},{4,0},{8,12},{12,8},{16,20},{20,16},{24,28},{28,24},{1,5},{5... | collective-permute-start | bytes 2654216 | tf_op jit(solution)/shard_map/ppermute | solution.py:21
  19.2 9.4 %collective-permute-start.5 = (bf16[128,1152]{1,0:T(8,128)(2,1)S(1)}, bf16[128,1152]{1,0:T(8,128)(2,1)S(1)}, u32[]{:S(2)}, u32[]{:S(2)}) collective-permute-start(bf16[128,1152]{1,0:T(8,128)(2,1)S(1)} %get-tuple-element.30), channel_id=1, source_target_pairs={{0,8},{4,12},{8,0},{12,4},{16,24},{20,28},{24,16},{28,20},{1,9},{5... | collective-permute-start | bytes 884744 | tf_op jit(solution)/shard_map/ppermute | solution.py:21
  28.6 9.9 %collective-permute-start.7 = (bf16[128,1152]{1,0:T(8,128)(2,1)S(1)}, bf16[128,1152]{1,0:T(8,128)(2,1)S(1)}, u32[]{:S(2)}, u32[]{:S(2)}) collective-permute-start(bf16[128,1152]{1,0:T(8,128)(2,1)S(1)} %collective-permute-done.5.refs_4_.refs_5_), channel_id=1, source_target_pairs={{0,4},{4,0},{8,12},{12,8},{16,20},{20,16},{24,28},{28,24},{1,5},{5... | collective-permute-start | bytes 884744 | tf_op jit(solution)/shard_map/ppermute | solution.py:21
  28.6 9.9 %collective-permute-start.8 = (bf16[64,1152]{1,0:T(8,128)(2,1)S(1)}, bf16[64,1152]{1,0:T(8,128)(2,1)S(1)}, u32[]{:S(2)}, u32[]{:S(2)}) collective-permute-start(bf16[64,1152]{1,0:T(8,128)(2,1)S(1)} %get-tuple-element.31), channel_id=1, source_target_pairs={{0,2},{1,3},{2,0},{3,1},{4,6},{5,7},{6,4},{7,5},{8,10},{9,11},{10,... | collective-permute-start | bytes 442376 | tf_op jit(solution)/shard_map/ppermute | solution.py:21
  28.6 9.9 %collective-permute-start.1 = (bf16[64,1152]{1,0:T(8,128)(2,1)S(1)}, bf16[64,1152]{1,0:T(8,128)(2,1)S(1)}, u32[]{:S(2)}, u32[]{:S(2)}) collective-permute-start(bf16[64,1152]{1,0:T(8,128)(2,1)S(1)} %collective-permute-done.refs_0_.refs_7_), channel_id=1, source_target_pairs={{0,16},{4,20},{8,24},{12,28},{16,0},{20,4},{24,8},{28,12},{1,17},{... | collective-permute-start | bytes 442376 | tf_op jit(solution)/shard_map/ppermute | solution.py:21
  38.5 5.8 %collective-permute-start.10 = (bf16[64,1152]{1,0:T(8,128)(2,1)S(1)}, bf16[64,1152]{1,0:T(8,128)(2,1)S(1)}, u32[]{:S(2)}, u32[]{:S(2)}) collective-permute-start(bf16[64,1152]{1,0:T(8,128)(2,1)S(1)} %collective-permute-done.8.refs_8_), channel_id=1, source_target_pairs={{0,16},{4,20},{8,24},{12,28},{16,0},{20,4},{24,8},{28,12},{1,17},{... | collective-permute-start | bytes 442376 | tf_op jit(solution)/shard_map/ppermute | solution.py:21
  40.3 1.8 %copy-start.1 = (bf16[128,1152]{1,0:T(8,128)(2,1)S(1)}, bf16[128,1152]{1,0:T(8,128)(2,1)}, u32[]{:S(2)}) copy-start(bf16[128,1152]{1,0:T(8,128)(2,1)} %image_ref.1) | copy-start | bytes 884740
  47.0 15.4 %collective-permute-start.15 = (bf16[512,1152]{1,0:T(8,128)(2,1)S(1)}, bf16[512,1152]{1,0:T(8,128)(2,1)S(1)}, u32[]{:S(2)}, u32[]{:S(2)}) collective-permute-start(bf16[512,1152]{1,0:T(8,128)(2,1)S(1)} %shard_map.74), channel_id=1, source_target_pairs={{0,4},{4,0},{8,12},{12,8},{16,20},{20,16},{24,28},{28,24},{1,5},{5... | collective-permute-start | bytes 3538952 | tf_op jit(solution)/shard_map/ppermute | solution.py:21
  47.1 14.4 %collective-permute-start.9 = (bf16[656,128]{1,0:T(8,128)(2,1)S(1)}, bf16[656,128]{1,0:T(8,128)(2,1)S(1)}, u32[]{:S(2)}, u32[]{:S(2)}) collective-permute-start(bf16[656,128]{1,0:T(8,128)(2,1)S(1)} %get-tuple-element.32.refs_0_), channel_id=1, source_target_pairs={{0,2},{1,3},{2,0},{3,1},{4,6},{5,7},{6,4},{7,5},{8,10},{9,11},{10,... | collective-permute-start | bytes 503816 | tf_op jit(solution)/shard_map/ppermute | solution.py:21
  47.1 5.8 %collective-permute-start.12 = (bf16[128,512]{1,0:T(8,128)(2,1)S(1)}, bf16[128,512]{1,0:T(8,128)(2,1)S(1)}, u32[]{:S(2)}, u32[]{:S(2)}) collective-permute-start(bf16[128,512]{1,0:T(8,128)(2,1)S(1)} %get-tuple-element.37), channel_id=1, source_target_pairs={{0,16},{4,20},{8,24},{12,28},{16,0},{20,4},{24,8},{28,12},{1,17},{... | collective-permute-start | bytes 393224 | tf_op jit(solution)/shard_map/ppermute | solution.py:21
  48.7 18.2 %collective-permute-start.11 = (bf16[656,128]{1,0:T(8,128)(2,1)S(1)}, bf16[656,128]{1,0:T(8,128)(2,1)S(1)}, u32[]{:S(2)}, u32[]{:S(2)}) collective-permute-start(bf16[656,128]{1,0:T(8,128)(2,1)S(1)} %get-tuple-element.35), channel_id=1, source_target_pairs={{0,18},{1,19},{2,16},{3,17},{4,22},{5,23},{6,20},{7,21},{8,26},{9,... | collective-permute-start | bytes 503816 | tf_op jit(solution)/shard_map/ppermute | solution.py:31
  61.6 18.4 %collective-permute-start.13 = (bf16[1168,128]{1,0:T(8,128)(2,1)S(1)}, bf16[1168,128]{1,0:T(8,128)(2,1)S(1)}, u32[]{:S(2)}, u32[]{:S(2)}) collective-permute-start(bf16[1168,128]{1,0:T(8,128)(2,1)S(1)} %get-tuple-element.39), channel_id=1, source_target_pairs={{0,16},{4,20},{8,24},{12,28},{16,0},{20,4},{24,8},{28,12},{1,17},{... | collective-permute-start | bytes 897032 | tf_op jit(solution)/shard_map/ppermute | solution.py:21
  63.3 19.0 %copy-start.3 = (bf16[128,1152]{1,0:T(8,128)(2,1)S(1)}, bf16[128,1152]{1,0:T(8,128)(2,1)}, u32[]{:S(2)}) copy-start(bf16[128,1152]{1,0:T(8,128)(2,1)} %text_ref.1) | copy-start | bytes 884740
  63.3 17.8 %collective-permute-start.16 = (bf16[128,1152]{1,0:T(8,128)(2,1)S(1)}, bf16[128,1152]{1,0:T(8,128)(2,1)S(1)}, u32[]{:S(2)}, u32[]{:S(2)}) collective-permute-start(bf16[128,1152]{1,0:T(8,128)(2,1)S(1)} %get-tuple-element.51), channel_id=1, source_target_pairs={{0,8},{4,12},{8,0},{12,4},{16,24},{20,28},{24,16},{28,20},{1,9},{5... | collective-permute-start | bytes 884744 | tf_op jit(solution)/shard_map/ppermute | solution.py:21
  64.6 16.5 %collective-permute-start.17 = (bf16[128,1152]{1,0:T(8,128)(2,1)S(1)}, bf16[128,1152]{1,0:T(8,128)(2,1)S(1)}, u32[]{:S(2)}, u32[]{:S(2)}) collective-permute-start(bf16[128,1152]{1,0:T(8,128)(2,1)S(1)} %get-tuple-element.52), channel_id=1, source_target_pairs={{0,1},{1,0},{2,3},{3,2},{4,5},{5,4},{6,7},{7,6},{8,9},{9,8},{10,11... | collective-permute-start | bytes 884744 | tf_op jit(solution)/shard_map/ppermute | solution.py:21
  64.6 17.8 %collective-permute-start.18 = (bf16[128,1152]{1,0:T(8,128)(2,1)S(1)}, bf16[128,1152]{1,0:T(8,128)(2,1)S(1)}, u32[]{:S(2)}, u32[]{:S(2)}) collective-permute-start(bf16[128,1152]{1,0:T(8,128)(2,1)S(1)} %get-tuple-element.53), channel_id=1, source_target_pairs={{0,9},{1,8},{2,11},{3,10},{4,13},{5,12},{6,15},{7,14},{8,1},{9,0},... | collective-permute-start | bytes 884744 | tf_op jit(solution)/shard_map/ppermute | solution.py:31
  66.9 13.0 %collective-permute-start.14 = (bf16[128,512]{1,0:T(8,128)(2,1)S(1)}, bf16[128,512]{1,0:T(8,128)(2,1)S(1)}, u32[]{:S(2)}, u32[]{:S(2)}) collective-permute-start(bf16[128,512]{1,0:T(8,128)(2,1)S(1)} %get-tuple-element.40), channel_id=1, source_target_pairs={{0,2},{1,3},{2,0},{3,1},{4,6},{5,7},{6,4},{7,5},{8,10},{9,11},{10,... | collective-permute-start | bytes 393224 | tf_op jit(solution)/shard_map/ppermute | solution.py:21

commit v4 on v0

v4 whole, which is shorter than its diff:
```python
import functools

import jax
import jax.numpy as jnp
from jax import lax
from jax.experimental import pallas as pl
from jax.experimental.pallas import tpu as pltpu
from jax.sharding import PartitionSpec as P

epsilon = 1e-06
f32, bf16 = jnp.float32, jnp.bfloat16
lanes = 128
extra = 16
direct_panels = 2
VMEM = pl.BlockSpec(memory_space=pltpu.VMEM)
SMEM = pl.BlockSpec(memory_space=pltpu.SMEM)
ANY = pl.BlockSpec(memory_space=pl.ANY)


def swapped(value, axis, step):
    return lax.ppermute(value, axis, [(place, place ^ step) for place in range(lax.axis_size(axis))])


def swapped_both(value, dp_step, inner_step):
    dp_count, inner_count = lax.axis_size("dp"), lax.axis_size("inner")
    pairs = [
        (d * inner_count + i, (d ^ dp_step) * inner_count + (i ^ inner_step))
        for d in range(dp_count)
        for i in range(inner_count)
    ]
    return lax.ppermute(value, ("dp", "inner"), pairs)


def call(kernel, out_shape, *operands, flops=0, scalars=0, scratch=(), after=()):
    moved = sum(o.size * o.dtype.itemsize for o in operands)
    moved += sum(o.size * o.dtype.itemsize for o in jax.tree.leaves(out_shape))
    body_of = kernel
    if after:
        body_of = lambda *refs: kernel(*refs[len(after) :])
    return pl.pallas_call(
        body_of,
        out_shape=out_shape,
        in_specs=[ANY] * len(after) + [SMEM] * scalars + [VMEM] * (len(operands) - scalars),
        out_specs=jax.tree.map(lambda _: VMEM, out_shape),
        scratch_shapes=scratch,
        compiler_params=pltpu.CompilerParams(vmem_limit_bytes=40 * 1024 * 1024),
        cost_estimate=pl.CostEstimate(flops=flops, bytes_accessed=moved, transcendentals=0),
    )(*after, *operands)


def shape(dims, kind):
    return jax.ShapeDtypeStruct(dims, kind)


def unit_of(rows):
    wide = rows.astype(f32)
    inverse = lax.rsqrt(jnp.sum(wide * wide, axis=-1, keepdims=True) + epsilon)
    return wide * inverse, inverse


def pair_terms(scale, offset, text_refs, images_ref, slopes_ref, own):
    step = 256
    totals = []
    for left in range(0, images_ref.shape[0], step):
        images = images_ref[left : left + step, :]
        total, done = jnp.zeros((1, images.shape[0]), f32), 0
        for texts in text_refs:
            for start in range(0, texts.shape[0], step):
                chunk = texts[start : min(start + step, texts.shape[0]), :]
                logits = (
                    scale
                    * lax.dot_general(
                        chunk, images, (((1,), (1,)), ((), ())), preferred_element_type=f32
                    )
                    + offset
                )
                shrunk = jnp.exp(-jnp.abs(logits))
                softplus = jnp.maximum(logits, 0.0) + jnp.log1p(shrunk)
                sigmoid = jnp.where(logits >= 0.0, 1.0, shrunk) / (1.0 + shrunk)
                if own and done == 0 and left == 0:
                    text_ids = lax.broadcasted_iota(jnp.int32, logits.shape, 0)
                    image_ids = lax.broadcasted_iota(jnp.int32, logits.shape, 1)
                    match = ((text_ids == image_ids) & (text_ids < own)).astype(f32)
                    softplus = softplus - match * logits
                    sigmoid = sigmoid - match
                slopes_ref[done : done + chunk.shape[0], left : left + step] = sigmoid.astype(bf16)
                total = total + jnp.sum(softplus, axis=0, keepdims=True)
                done += chunk.shape[0]
        totals.append(total)
    return jnp.concatenate(totals, axis=1)


def own_rows_kernel(text_ref, image_ref, text_emb_ref, image_emb_ref):
    text_emb_ref[...] = unit_of(text_ref[...])[0].astype(bf16)
    image_emb_ref[...] = unit_of(image_ref[...])[0].astype(bf16)


def first_stage_kernel(own_ref, beside_ref, above_ref, *refs):
    count = (len(refs) - 2) // 2
    raw_refs, texts_ref, above_emb_ref, emb_refs = refs[:count], refs[count], refs[count + 1], refs[count + 2 :]
    rows = own_ref.shape[0]
    texts_ref[:rows, :] = own_ref[...]
    texts_ref[rows : 2 * rows, :] = unit_of(beside_ref[...])[0].astype(bf16)
    above = unit_of(above_ref[...])[0].astype(bf16)
    texts_ref[2 * rows :, :] = above
    above_emb_ref[...] = above
    for raw, emb in zip(raw_refs, emb_refs):
        emb[...] = unit_of(raw[...])[0].astype(bf16)


def copy_kernel(source_ref, target_ref):
    target_ref[...] = source_ref[...]


def own_core_pairs_kernel(scale_ref, bias_ref, near_ref, far_ref, *refs):
    image_refs, (images_ref, slopes_ref, loss_ref) = refs[:-3], refs[-3:]
    rows = far_ref.shape[0]
    for place, block in enumerate(image_refs):
        images_ref[place * rows : (place + 1) * rows, :] = block[...]
    loss_ref[...] = pair_terms(
        scale_ref[0], bias_ref[0], (near_ref, far_ref), images_ref, slopes_ref, rows
    )


def other_core_pairs_kernel(
    scale_ref, bias_ref, near_ref, far_ref, images_ref, first_loss_ref, slopes_ref, loss_ref, sent_ref
):
    loss_ref[...] = first_loss_ref[...] + pair_terms(
        scale_ref[0], bias_ref[0], (near_ref, far_ref), images_ref, slopes_ref, 0
    )
    sent_ref[...] = jnp.dot(slopes_ref[...], images_ref[...], preferred_element_type=f32).astype(bf16)


def loss_rows(loss):
    high = loss.astype(bf16).astype(f32)
    which = lax.broadcasted_iota(jnp.int32, (extra, loss.shape[1]), 0)
    return jnp.where(which == 0, high, loss - high).astype(bf16)


def image_sums_kernel(plain, loss_ref, *refs):
    slope_refs, text_refs, refs = refs[:2], refs[2:6], refs[6:]
    own_ref, own_loss_ref, plain_refs, head_refs, tail_refs = (
        refs[0],
        refs[1],
        refs[2 : 2 + plain],
        refs[2 + plain :: 2],
        refs[3 + plain :: 2],
    )
    rows, width = own_ref.shape
    step = 3 * lanes
    for left in range(0, width, step):
        total = None
        for slopes, texts in zip(slope_refs, (text_refs[:2], text_refs[2:])):
            done = 0
            for block in texts:
                part = lax.dot_general(
                    slopes[done : done + block.shape[0], :],
                    block[:, left : left + step],
                    (((0,), (0,)), ((), ())),
                    preferred_element_type=f32,
                )
                total, done = part if total is None else total + part, done + block.shape[0]
        own_ref[:, left : left + step] = total[:rows, :]
        for place, out in enumerate((*plain_refs, *head_refs), 1):
            panels = (out.shape[0] - extra) // rows
            sums = total[place * rows : (place + 1) * rows, :]
            for at in range(left, left + step, lanes):
                piece = sums[:, at - left : at - left + lanes]
                if at < panels * lanes:
                    out[at // lanes * rows : (at // lanes + 1) * rows, :] = piece.astype(bf16)
                else:
                    tail = tail_refs[place - 1 - plain]
                    tail[:, at - panels * lanes : at - panels * lanes + lanes] = piece.astype(tail.dtype)
    own_loss_ref[...] = loss_ref[:, :rows]
    for place, out in enumerate((*plain_refs, *head_refs), 1):
        out[out.shape[0] - extra :, :] = loss_rows(loss_ref[:, place * rows : (place + 1) * rows])


def text_sums_kernel(received_ref, slopes_ref, images_ref, *outs):
    rows = outs[0].shape[0]
    for k, out in enumerate(outs):
        cut = slice(k * rows, (k + 1) * rows)
        sums = jnp.dot(slopes_ref[cut, :], images_ref[...], preferred_element_type=f32)
        out[...] = (sums + received_ref[cut, :].astype(f32)).astype(out.dtype)


def late_kernel(sums, parts, *refs):
    payloads = (len(refs) - 2 * sums - sums * parts) // 2
    own, received = refs[:sums], refs[sums : sums + sums * parts]
    passed, outs = refs[sums + sums * parts :][:payloads], refs[sums + sums * parts + payloads :]
    for k in range(sums):
        total = own[k][...]
        for part in received[k * parts : (k + 1) * parts]:
            total = total + part[...].astype(f32)
        outs[k][...] = total.astype(bf16)
    for source, target in zip(passed, outs[sums:]):
        target[...] = source[...]


def row_gradient(rows, sums, scale, out_ref):
    unit_rows, inverse = unit_of(rows)
    unit_grad = scale * sums
    out_ref[...] = (
        unit_grad - unit_rows * jnp.sum(unit_rows * unit_grad, axis=-1, keepdims=True)
    ) * inverse


def image_end_kernel(batch, heads, scale_ref, image_ref, grad_ref, loss_ref, *refs):
    out_ref, out_loss_ref, sums_ref = refs[-3:]
    head_refs, tail_refs = refs[:heads], refs[heads:-3]
    rows, width = image_ref.shape
    loss = loss_ref[...]
    for panel in range(width // lanes):
        cut = slice(panel * lanes, (panel + 1) * lanes)
        sums = grad_ref[:, cut]
        for r in head_refs:
            if (panel + 1) * rows <= r.shape[0] - extra:
                sums = sums + r[panel * rows : (panel + 1) * rows, :].astype(f32)
        for r in tail_refs:
            first = panel * lanes - (width - r.shape[1])
            if first >= 0:
                sums = sums + r[:, first : first + lanes].astype(f32)
        sums_ref[:, cut] = sums
    for r in head_refs:
        last = r[r.shape[0] - extra :, :].astype(f32)
        loss = loss + (last[0:1, :] + last[1:2, :])
    row_gradient(image_ref[...], sums_ref[...], scale_ref[0], out_ref)
    out_loss_ref[...] = loss / batch


def text_end_kernel(scale_ref, text_ref, grad_ref, *refs):
    sums = grad_ref[...]
    for r in refs[:-1]:
        sums = sums + r[...].astype(f32)
    row_gradient(text_ref[...], sums, scale_ref[0], refs[-1])


def body(image, text, logarithm_scale, bias):
    rows, width = image.shape
    dp_count, inner_count = lax.axis_size("dp"), lax.axis_size("inner")
    batch = rows * dp_count * inner_count
    scale = jnp.exp(logarithm_scale)
    block = shape((rows, width), bf16)
    wide_block = shape((rows, width), f32)

    image_dp, image_inner = range(4, dp_count, 4), range(2, inner_count, 2)

    images_z = [swapped(image, "inner", q) for q in image_inner]
    text_z = swapped(text, "inner", 1)
    text_x = swapped(text, "dp", 2)
    images_y = [swapped(image, "dp", p) for p in image_dp]
    text_emb, image_emb = call(own_rows_kernel, (block, block), text, image)
    near_texts, text_z_emb, *embs = call(
        first_stage_kernel,
        (shape((3 * rows, width), bf16), block) + (block,) * (len(images_y) + len(images_z)),
        text_emb,
        text_x,
        text_z,
        *images_y,
        *images_z,
    )
    embs_y, embs_z = embs[: len(images_y)], embs[len(images_y) :]

    far_text = swapped(text_z_emb, "dp", 2)
    embs_yz = [swapped(emb, "dp", p) for emb in embs_z for p in image_dp]
    near_swapped = swapped(near_texts, "dp", 1)
    far_text = call(copy_kernel, block, far_text, after=embs_yz)
    far_swapped = swapped(far_text, "dp", 1)

    embs = [image_emb, *embs_y, *embs_z, *embs_yz]
    held, texts_half = len(embs) * rows, 4 * rows
    slopes_shape = shape((texts_half, held), bf16)
    pair_flops = 2 * held * texts_half * width
    images, own_core_slopes, loss = call(
        own_core_pairs_kernel,
        (shape((held, width), bf16), slopes_shape, shape((1, held), f32)),
        scale,
        bias,
        near_texts,
        far_text,
        *embs,
        flops=pair_flops,
        scalars=2,
    )
    other_core_slopes, loss, crossing = call(
        other_core_pairs_kernel,
        (slopes_shape, shape((1, held), f32), shape((texts_half, width), bf16)),
        scale,
        bias,
        near_swapped,
        far_swapped,
        images,
        loss,
        flops=2 * pair_flops,
        scalars=2,
    )
    crossed = swapped(crossing, "dp", 1)

    head_rows = direct_panels * rows + extra
    tail_width = width - direct_panels * lanes
    out_shapes = [wide_block, shape((1, rows), f32)]
    out_shapes += [shape((width // lanes * rows + extra, lanes), bf16)] * len(embs_y)
    for kind, count in ((f32, len(embs_z)), (bf16, len(embs_yz))):
        out_shapes += [shape((head_rows, lanes), bf16), shape((rows, tail_width), kind)] * count
    image_grad, own_loss, *sent = call(
        functools.partial(image_sums_kernel, len(embs_y)),
        out_shapes,
        loss,
        own_core_slopes,
        other_core_slopes,
        near_texts,
        far_text,
        near_swapped,
        far_swapped,
        flops=2 * pair_flops,
    )
    payloads_y, heads, tails = sent[: len(embs_y)], sent[len(embs_y) :: 2], sent[len(embs_y) + 1 :: 2]

    moved_tails = [
        swapped(tail, "dp", p)
        for tail, p in zip(tails[len(embs_z) :], [p for _ in image_inner for p in image_dp])
    ]
    z_heads = [swapped(head, "inner", q) for head, q in zip(heads, image_inner)]
    yz_heads = [
        swapped_both(head, p, q)
        for head, (p, q) in zip(heads[len(embs_z) :], [(p, q) for q in image_inner for p in image_dp])
    ]
    text_grad, text_x_sums, text_z_sums, text_xz_sums = call(
        text_sums_kernel,
        (wide_block, block, wide_block, block),
        crossed,
        own_core_slopes,
        images,
        flops=pair_flops,
        after=[image_grad],
    )
    moved_text = swapped(text_xz_sums, "dp", 2)

    late = call(
        functools.partial(late_kernel, len(image_inner), len(image_dp)),
        [shape((rows, tail_width), bf16)] * len(image_inner) + [shape(p.shape, bf16) for p in payloads_y],
        *tails[: len(embs_z)],
        *moved_tails,
        *payloads_y,
        after=z_heads + yz_heads,
    )
    tail_parts = [swapped(part, "inner", q) for part, q in zip(late, image_inner)]
    y_parts = [swapped(part, "dp", p) for part, p in zip(late[len(image_inner) :], image_dp)]
    late_text_z, late_text_x = call(
        functools.partial(late_kernel, 1, 1), [block, block], text_z_sums, moved_text, text_x_sums
    )
    text_parts = [swapped(late_text_z, "inner", 1), swapped(late_text_x, "dp", 2)]

    head_parts = z_heads + yz_heads + y_parts
    image_gradient, image_loss = call(
        functools.partial(image_end_kernel, batch, len(head_parts)),
        (wide_block, shape((1, rows), f32)),
        scale,
        image,
        image_grad,
        own_loss,
        *head_parts,
        *tail_parts,
        scalars=1,
        scratch=[pltpu.VMEM((rows, width), f32)],
    )
    text_gradient = call(text_end_kernel, wide_block, scale, text, text_grad, *text_parts, scalars=1)
    return (image_gradient, text_gradient, image_loss.reshape(rows))


def solution(mesh):
    return jax.shard_map(
        body,
        mesh=mesh,
        in_specs=(P(("dp", "inner"), None), P(("dp", "inner"), None), P(), P()),
        out_specs=(P(("dp", "inner"), None), P(("dp", "inner"), None), P(("dp", "inner"))),
        check_vma=False,
    )
```

time: 210 us -> 68 us (0.32)
  waiting for transfers between devices: 128 us -> 33.2 us
  matrix products: 36.6 us -> 0 us
  starting transfers between devices: 2.42 us -> 20.6 us
  between operations: 16.1 us -> 2.07 us
  blocking collectives: 10.1 us -> 0 us
  Pallas kernels: 0 us -> 10 us
  other arithmetic: 8.34 us -> 0 us
  local copies, waits for them, and re-layouts: 7.09 us -> 1.97 us
    dot_general x24 -> x0, matrix products: 36.6 us -> none  [the longest x8 20.2 us: block_terms(): lax.dot_general(images, block, (((1,), (1,)), ((), ())), preferred_elemen...]
    reduce_scatter x1 -> x0, waiting for transfers between devices: 33 us -> none  [body(): lax.psum_scatter(image_total, 'inner', scatter_dimension=0, tiled=True)]
    ppermute x15 -> x17, waiting for transfers between devices: 64.3 us -> 33.2 us  [the longest x16 29.5 us: swapped(): lax.ppermute(value, axis, [(place, place ^ step) for place in range(lax.a...]
    all_gather x1 -> x0, waiting for transfers between devices: 30.9 us -> none  [body(): images = lax.all_gather(image_emb, 'inner', axis=0, tiled=True)]
    ppermute x15 -> x17, starting transfers between devices: 2.34 us -> 20.6 us  [the longest x16 17.4 us: swapped(): lax.ppermute(value, axis, [(place, place ^ step) for place in range(lax.a...]
    unnamed x1 -> x0, blocking collectives: 10.1 us -> none
    pallas_call x0 -> x11, Pallas kernels: none -> 10 us  [call(): pl.pallas_call(body_of, out_shape=out_shape, in_specs=[ANY] * len(after)...]
    while x21 -> x0, local copies, waits for them, and re-layouts: 5.04 us -> none
  transfers between devices with their start and end apart: 17 -> 17, of which waited for: 16 -> 9; matrix products, arithmetic and copies ran while one was open for 15% -> 0% of each run, Pallas kernels for 0% -> 8%
where the time goes in v4:
time: 68 us; the launch traced here: 67.8 us
  waiting for transfers between devices  33.2 us (49%)
  starting transfers between devices  20.6 us (30%)
  Pallas kernels  10 us (15%)
  between operations  2.07 us (3%)
  local copies, waits for them, and re-layouts  1.97 us (3%)
    ppermute x16, waiting for transfers between devices, swapped(): lax.ppermute(value, axis, [(place, place ^ step) for place in range(lax.a...  29.5 us
    ppermute x16, starting transfers between devices, swapped(): lax.ppermute(value, axis, [(place, place ^ step) for place in range(lax.a...  17.4 us
    pallas_call x11, Pallas kernels, call(): pl.pallas_call(body_of, out_shape=out_shape, in_specs=[ANY] * len(after)...  10 us
    ppermute x1, waiting for transfers between devices, swapped_both(): return lax.ppermute(value, ('dp', 'inner'), pairs)  3.64 us
    ppermute x1, starting transfers between devices, swapped_both(): return lax.ppermute(value, ('dp', 'inner'), pairs)  3.23 us
    unnamed x8, local copies, waits for them, and re-layouts  1.97 us
  transfers between devices with their start and end apart: 17, of which 9 were waited for; matrix products, arithmetic and copies ran while one was open for 0% of the time, Pallas kernels for 8%

profile of v4, /device:TPU:0, one launch (start us, length us, event | category | flops | bytes accessed | tf_op | source)
XLA Modules:
  0.0 67.8 jit_solution(17470261902532820218)
XLA Ops:
  0.6 3.0 %collective-permute-start.2 = (bf16[128,1152]{1,0:T(8,128)(2,1)}, bf16[128,1152]{1,0:T(8,128)(2,1)S(1)}, u32[]{:S(2)}, u32[]{:S(2)}) collective-permute-start(bf16[128,1152]{1,0:T(8,128)(2,1)} %image_ref.3), channel_id=1, source_target_pairs={{0,16},{4,20},{8,24},{12,28},{16,0},{20,4},{24,8},{28,12},{1,17},{... | collective-permute-start | bytes 884744 | tf_op jit(solution)/shard_map/ppermute | solution.py:21
  3.7 2.6 %collective-permute-start.3 = (bf16[128,1152]{1,0:T(8,128)(2,1)}, bf16[128,1152]{1,0:T(8,128)(2,1)S(1)}, u32[]{:S(2)}, u32[]{:S(2)}) collective-permute-start(bf16[128,1152]{1,0:T(8,128)(2,1)} %image_ref.3), channel_id=1, source_target_pairs={{0,2},{1,3},{2,0},{3,1},{4,6},{5,7},{6,4},{7,5},{8,10},{9,11},{10,... | collective-permute-start | bytes 884744 | tf_op jit(solution)/shard_map/ppermute | solution.py:21
  6.3 1.5 %collective-permute-start = (bf16[128,1152]{1,0:T(8,128)(2,1)}, bf16[128,1152]{1,0:T(8,128)(2,1)S(1)}, u32[]{:S(2)}, u32[]{:S(2)}) collective-permute-start(bf16[128,1152]{1,0:T(8,128)(2,1)} %text_ref.3), channel_id=1, source_target_pairs={{0,8},{4,12},{8,0},{12,4},{16,24},{20,28},{24,16},{28,20},{1,9},{5... | collective-permute-start | bytes 884744 | tf_op jit(solution)/shard_map/ppermute | solution.py:21
  7.7 1.6 %collective-permute-start.1 = (bf16[128,1152]{1,0:T(8,128)(2,1)}, bf16[128,1152]{1,0:T(8,128)(2,1)S(1)}, u32[]{:S(2)}, u32[]{:S(2)}) collective-permute-start(bf16[128,1152]{1,0:T(8,128)(2,1)} %text_ref.3), channel_id=1, source_target_pairs={{0,1},{1,0},{2,3},{3,2},{4,5},{5,4},{6,7},{7,6},{8,9},{9,8},{10,11... | collective-permute-start | bytes 884744 | tf_op jit(solution)/shard_map/ppermute | solution.py:21
  9.3 1.0 %copy-done = bf16[128,1152]{1,0:T(8,128)(2,1)S(1)} copy-done((bf16[128,1152]{1,0:T(8,128)(2,1)S(1)}, bf16[128,1152]{1,0:T(8,128)(2,1)}, u32[]{:S(2)}) %copy-start) | copy-done | bytes 294936
  10.3 1.0 %copy-done.2 = bf16[128,1152]{1,0:T(8,128)(2,1)S(1)} copy-done((bf16[128,1152]{1,0:T(8,128)(2,1)S(1)}, bf16[128,1152]{1,0:T(8,128)(2,1)}, u32[]{:S(2)}) %copy-start.2) | copy-done | bytes 294936
  11.5 8.2 %collective-permute-done.3.refs_1_ = bf16[128,1152]{1,0:T(8,128)(2,1)S(1)} collective-permute-done((bf16[128,1152]{1,0:T(8,128)(2,1)}, bf16[128,1152]{1,0:T(8,128)(2,1)S(1)}, u32[]{:S(2)}, u32[]{:S(2)}) %collective-permute-start.3) | collective-permute-done | bytes 294944 | tf_op jit(solution)/shard_map/ppermute | solution.py:21
  19.7 1.4 %collective-permute-done.1.above_ref = bf16[128,1152]{1,0:T(8,128)(2,1)S(1)} collective-permute-done((bf16[128,1152]{1,0:T(8,128)(2,1)}, bf16[128,1152]{1,0:T(8,128)(2,1)S(1)}, u32[]{:S(2)}, u32[]{:S(2)}) %collective-permute-start.1) | collective-permute-done | bytes 294944 | tf_op jit(solution)/shard_map/ppermute | solution.py:21
  22.6 8.3 %collective-permute-done.6.refs_1_ = bf16[128,1152]{1,0:T(8,128)(2,1)S(1)} collective-permute-done((bf16[128,1152]{1,0:T(8,128)(2,1)S(1)}, bf16[128,1152]{1,0:T(8,128)(2,1)S(1)}, u32[]{:S(2)}, u32[]{:S(2)}) %collective-permute-start.6) | collective-permute-done | bytes 294944 | tf_op jit(solution)/shard_map/ppermute | solution.py:21
  32.7 1.7 %shard_map.70 = (bf16[512,1152]{1,0:T(8,128)(2,1)S(1)}, bf16[512,512]{1,0:T(8,128)(2,1)S(1)}, f32[1,512]{1,0:T(1,128)S(1)}) custom-call(f32[1]{0:T(128)S(6)} %exp.3.scale_ref, f32[1]{0:T(128)S(6)} %copy.8.bias_ref, bf16[384,1152]{1,0:T(8,128)(2,1)S(1)} %get-tuple-element.33.near_ref.refs_2_, bf16[128,1152]{1,0:T(8,128)(2,1)S(1)} %shard_map.69.far_ref.refs_3_, ...), custom_call_target="tpu_custom_call" | custom-call | flops 603979776 | bytes 4065288 | tf_op jit(solution)/shard_map/pallas_call | solution.py:40
  34.3 2.2 %shard_map.71 = (bf16[512,512]{1,0:T(8,128)(2,1)S(1)}, f32[1,512]{1,0:T(1,128)S(1)}, bf16[512,1152]{1,0:T(8,128)(2,1)S(1)}) custom-call(f32[1]{0:T(128)S(6)} %exp.3.scale_ref, f32[1]{0:T(128)S(6)} %copy.8.bias_ref, bf16[384,1152]{1,0:T(8,128)(2,1)S(1)} %collective-permute-done.4.near_ref.refs_4_, ...), custom_call_target="tpu_custom_call" | custom-call | flops 1207959552 | bytes 4067336 | tf_op jit(solution)/shard_map/pallas_call | solution.py:40
  37.1 2.3 %shard_map.72 = (f32[128,1152]{1,0:T(8,128)S(1)}, f32[1,128]{1,0:T(1,128)S(1)}, bf16[1168,128]{1,0:T(8,128)(2,1)S(1)}, bf16[272,128]{1,0:T(8,128)(2,1)S(1)}, f32...) custom-call(f32[1,512]{1,0:T(1,128)S(1)} %get-tuple-element.40.loss_ref, ...), custom_call_target="tpu_custom_call" | custom-call | flops 1207959552 | bytes 5126656 | tf_op jit(solution)/shard_map/pallas_call | solution.py:40
  39.6 0.9 %shard_map.75 = (f32[128,1152]{1,0:T(8,128)S(1)}, bf16[128,1152]{1,0:T(8,128)(2,1)S(1)}, f32[128,1152]{1,0:T(8,128)S(1)}, bf16[128,1152]{1,0:T(8,128)(2,1)S(1)}) custom-call(f32[128,1152]{1,0:T(8,128)S(1)} %get-tuple-element.43.grad_ref.refs_0_, bf16[512,1152]{1,0:T(8,128)(2,1)S(1)} %collective-permute-done.13.refs_1_, ...), custom_call_target="tpu_custom_call" | custom-call | flops 603979776 | bytes 4653056 | tf_op jit(solution)/shard_map/pallas_call | solution.py:40
  40.5 1.6 %collective-permute-start.14 = (bf16[128,1152]{1,0:T(8,128)(2,1)S(1)}, bf16[128,1152]{1,0:T(8,128)(2,1)S(1)}, u32[]{:S(2)}, u32[]{:S(2)}) collective-permute-start(bf16[128,1152]{1,0:T(8,128)(2,1)S(1)} %get-tuple-element.56), channel_id=1, source_target_pairs={{0,8},{4,12},{8,0},{12,4},{16,24},{20,28},{24,16},{28,20},{1,9},{5... | collective-permute-start | bytes 884744 | tf_op jit(solution)/shard_map/ppermute | solution.py:21
  42.5 0.7 %collective-permute-start.8 = (bf16[272,128]{1,0:T(8,128)(2,1)S(1)}, bf16[272,128]{1,0:T(8,128)(2,1)S(1)}, u32[]{:S(2)}, u32[]{:S(2)}) collective-permute-start(bf16[272,128]{1,0:T(8,128)(2,1)S(1)} %get-tuple-element.45), channel_id=1, source_target_pairs={{0,2},{1,3},{2,0},{3,1},{4,6},{5,7},{6,4},{7,5},{8,10},{9,11},{10,... | collective-permute-start | bytes 208904 | tf_op jit(solution)/shard_map/ppermute | solution.py:21
  43.2 3.2 %collective-permute-start.9 = (bf16[272,128]{1,0:T(8,128)(2,1)S(1)}, bf16[272,128]{1,0:T(8,128)(2,1)S(1)}, u32[]{:S(2)}, u32[]{:S(2)}) collective-permute-start(bf16[272,128]{1,0:T(8,128)(2,1)S(1)} %get-tuple-element.46), channel_id=1, source_target_pairs={{0,18},{1,19},{2,16},{3,17},{4,22},{5,23},{6,20},{7,21},{8,26},{9,... | collective-permute-start | bytes 208904 | tf_op jit(solution)/shard_map/ppermute | solution.py:31
  46.4 2.5 %collective-permute-done.8.refs_0_ = bf16[272,128]{1,0:T(8,128)(2,1)S(1)} collective-permute-done((bf16[272,128]{1,0:T(8,128)(2,1)S(1)}, bf16[272,128]{1,0:T(8,128)(2,1)S(1)}, u32[]{:S(2)}, u32[]{:S(2)}) %collective-permute-start.8) | collective-permute-done | bytes 69664 | tf_op jit(solution)/shard_map/ppermute | solution.py:21
  48.9 3.6 %collective-permute-done.9.refs_1_ = bf16[272,128]{1,0:T(8,128)(2,1)S(1)} collective-permute-done((bf16[272,128]{1,0:T(8,128)(2,1)S(1)}, bf16[272,128]{1,0:T(8,128)(2,1)S(1)}, u32[]{:S(2)}, u32[]{:S(2)}) %collective-permute-start.9) | collective-permute-done | bytes 69664 | tf_op jit(solution)/shard_map/ppermute | solution.py:31
  53.6 1.1 %collective-permute-start.16 = (bf16[128,1152]{1,0:T(8,128)(2,1)S(1)}, bf16[128,1152]{1,0:T(8,128)(2,1)S(1)}, u32[]{:S(2)}, u32[]{:S(2)}) collective-permute-start(bf16[128,1152]{1,0:T(8,128)(2,1)S(1)} %get-tuple-element.59), channel_id=1, source_target_pairs={{0,8},{4,12},{8,0},{12,4},{16,24},{20,28},{24,16},{28,20},{1,9},{5... | collective-permute-start | bytes 884744 | tf_op jit(solution)/shard_map/ppermute | solution.py:21
  54.6 2.3 %collective-permute-start.12 = (bf16[128,896]{1,0:T(8,128)(2,1)S(1)}, bf16[128,896]{1,0:T(8,128)(2,1)S(1)}, u32[]{:S(2)}, u32[]{:S(2)}) collective-permute-start(bf16[128,896]{1,0:T(8,128)(2,1)S(1)} %get-tuple-element.51), channel_id=1, source_target_pairs={{0,2},{1,3},{2,0},{3,1},{4,6},{5,7},{6,4},{7,5},{8,10},{9,11},{10,... | collective-permute-start | bytes 688136 | tf_op jit(solution)/shard_map/ppermute | solution.py:21
  56.9 7.7 %collective-permute-done.12.refs_3_ = bf16[128,896]{1,0:T(8,128)(2,1)S(1)} collective-permute-done((bf16[128,896]{1,0:T(8,128)(2,1)S(1)}, bf16[128,896]{1,0:T(8,128)(2,1)S(1)}, u32[]{:S(2)}, u32[]{:S(2)}) %collective-permute-start.12) | collective-permute-done | bytes 229408 | tf_op jit(solution)/shard_map/ppermute | solution.py:21
  64.5 1.2 %shard_map.74 = (f32[128,1152]{1,0:T(8,128)}, f32[1,128]{1,0:T(1,128)}) custom-call(f32[1]{0:T(128)S(6)} %exp.3.scale_ref, bf16[128,1152]{1,0:T(8,128)(2,1)S(1)} %copy-done.3, f32[128,1152]{1,0:T(8,128)S(1)} %get-tuple-element.43.grad_ref.refs_0_, f32[1,128]{1,0:T(1,128)S(1)} %get-tuple-element.44.loss_ref, ...), custom_call_target="tpu_custom_call" | custom-call | bytes 2143236 | tf_op jit(solution)/shard_map/pallas_call | solution.py:40
  65.7 1.0 %collective-permute-done.15.refs_0_ = bf16[128,1152]{1,0:T(8,128)(2,1)S(1)} collective-permute-done((bf16[128,1152]{1,0:T(8,128)(2,1)S(1)}, bf16[128,1152]{1,0:T(8,128)(2,1)S(1)}, u32[]{:S(2)}, u32[]{:S(2)}) %collective-permute-start.15) | collective-permute-done | bytes 294944 | tf_op jit(solution)/shard_map/ppermute | solution.py:21
  66.7 1.1 %shard_map.77 = f32[128,1152]{1,0:T(8,128)} custom-call(f32[1]{0:T(128)S(6)} %exp.3.scale_ref, bf16[128,1152]{1,0:T(8,128)(2,1)S(1)} %copy-done.1, f32[128,1152]{1,0:T(8,128)S(1)} %get-tuple-element.54.grad_ref, bf16[128,1152]{1,0:T(8,128)(2,1)S(1)} %collective-permute-done.15.refs_0_, bf16[128,1152]{1,0:T(8,128)(2,1)S(1)} %collective-permute-done.16.refs_1_), custom_call_target="tpu_custom_call" | custom-call | bytes 2064388 | tf_op jit(solution)/shard_map/pallas_call | solution.py:40
  (29 shorter events, 4.4 us)
Async XLA Ops:
  0.6 10.9 %collective-permute-start.2 = (bf16[128,1152]{1,0:T(8,128)(2,1)}, bf16[128,1152]{1,0:T(8,128)(2,1)S(1)}, u32[]{:S(2)}, u32[]{:S(2)}) collective-permute-start(bf16[128,1152]{1,0:T(8,128)(2,1)} %image_ref.3), channel_id=1, source_target_pairs={{0,16},{4,20},{8,24},{12,28},{16,0},{20,4},{24,8},{28,12},{1,17},{... | collective-permute-start | bytes 884744 | tf_op jit(solution)/shard_map/ppermute | solution.py:21
  3.7 16.0 %collective-permute-start.3 = (bf16[128,1152]{1,0:T(8,128)(2,1)}, bf16[128,1152]{1,0:T(8,128)(2,1)S(1)}, u32[]{:S(2)}, u32[]{:S(2)}) collective-permute-start(bf16[128,1152]{1,0:T(8,128)(2,1)} %image_ref.3), channel_id=1, source_target_pairs={{0,2},{1,3},{2,0},{3,1},{4,6},{5,7},{6,4},{7,5},{8,10},{9,11},{10,... | collective-permute-start | bytes 884744 | tf_op jit(solution)/shard_map/ppermute | solution.py:21
  6.3 13.4 %collective-permute-start = (bf16[128,1152]{1,0:T(8,128)(2,1)}, bf16[128,1152]{1,0:T(8,128)(2,1)S(1)}, u32[]{:S(2)}, u32[]{:S(2)}) collective-permute-start(bf16[128,1152]{1,0:T(8,128)(2,1)} %text_ref.3), channel_id=1, source_target_pairs={{0,8},{4,12},{8,0},{12,4},{16,24},{20,28},{24,16},{28,20},{1,9},{5... | collective-permute-start | bytes 884744 | tf_op jit(solution)/shard_map/ppermute | solution.py:21
  7.7 13.3 %collective-permute-start.1 = (bf16[128,1152]{1,0:T(8,128)(2,1)}, bf16[128,1152]{1,0:T(8,128)(2,1)S(1)}, u32[]{:S(2)}, u32[]{:S(2)}) collective-permute-start(bf16[128,1152]{1,0:T(8,128)(2,1)} %text_ref.3), channel_id=1, source_target_pairs={{0,1},{1,0},{2,3},{3,2},{4,5},{5,4},{6,7},{7,6},{8,9},{9,8},{10,11... | collective-permute-start | bytes 884744 | tf_op jit(solution)/shard_map/ppermute | solution.py:21
  9.3 1.0 %copy-start = (bf16[128,1152]{1,0:T(8,128)(2,1)S(1)}, bf16[128,1152]{1,0:T(8,128)(2,1)}, u32[]{:S(2)}) copy-start(bf16[128,1152]{1,0:T(8,128)(2,1)} %text_ref.3) | copy-start | bytes 884740
  10.3 1.0 %copy-start.2 = (bf16[128,1152]{1,0:T(8,128)(2,1)S(1)}, bf16[128,1152]{1,0:T(8,128)(2,1)}, u32[]{:S(2)}) copy-start(bf16[128,1152]{1,0:T(8,128)(2,1)} %image_ref.3) | copy-start | bytes 884740
  21.5 12.9 %collective-permute-start.4 = (bf16[384,1152]{1,0:T(8,128)(2,1)S(1)}, bf16[384,1152]{1,0:T(8,128)(2,1)S(1)}, u32[]{:S(2)}, u32[]{:S(2)}) collective-permute-start(bf16[384,1152]{1,0:T(8,128)(2,1)S(1)} %get-tuple-element.33.near_ref.refs_2_), channel_id=1, source_target_pairs={{0,4},{4,0},{8,12},{12,8},{16,20},{20,16},{24,28},{28,24},{1,5},{5... | collective-permute-start | bytes 2654216 | tf_op jit(solution)/shard_map/ppermute | solution.py:21
  21.5 9.4 %collective-permute-start.6 = (bf16[128,1152]{1,0:T(8,128)(2,1)S(1)}, bf16[128,1152]{1,0:T(8,128)(2,1)S(1)}, u32[]{:S(2)}, u32[]{:S(2)}) collective-permute-start(bf16[128,1152]{1,0:T(8,128)(2,1)S(1)} %get-tuple-element.35), channel_id=1, source_target_pairs={{0,8},{4,12},{8,0},{12,4},{16,24},{20,28},{24,16},{28,20},{1,9},{5... | collective-permute-start | bytes 884744 | tf_op jit(solution)/shard_map/ppermute | solution.py:21
  22.1 9.1 %collective-permute-start.5 = (bf16[128,1152]{1,0:T(8,128)(2,1)S(1)}, bf16[128,1152]{1,0:T(8,128)(2,1)S(1)}, u32[]{:S(2)}, u32[]{:S(2)}) collective-permute-start(bf16[128,1152]{1,0:T(8,128)(2,1)S(1)} %get-tuple-element.34.refs_2_), channel_id=1, source_target_pairs={{0,16},{4,20},{8,24},{12,28},{16,0},{20,4},{24,8},{28,12},{1,17},{... | collective-permute-start | bytes 884744 | tf_op jit(solution)/shard_map/ppermute | solution.py:21
  31.2 3.1 %collective-permute-start.7 = (bf16[128,1152]{1,0:T(8,128)(2,1)S(1)}, bf16[128,1152]{1,0:T(8,128)(2,1)S(1)}, u32[]{:S(2)}, u32[]{:S(2)}) collective-permute-start(bf16[128,1152]{1,0:T(8,128)(2,1)S(1)} %shard_map.69.far_ref.refs_3_), channel_id=1, source_target_pairs={{0,4},{4,0},{8,12},{12,8},{16,20},{20,16},{24,28},{28,24},{1,5},{5... | collective-permute-start | bytes 884744 | tf_op jit(solution)/shard_map/ppermute | solution.py:21
  36.6 3.0 %collective-permute-start.13 = (bf16[512,1152]{1,0:T(8,128)(2,1)S(1)}, bf16[512,1152]{1,0:T(8,128)(2,1)S(1)}, u32[]{:S(2)}, u32[]{:S(2)}) collective-permute-start(bf16[512,1152]{1,0:T(8,128)(2,1)S(1)} %get-tuple-element.53), channel_id=1, source_target_pairs={{0,4},{4,0},{8,12},{12,8},{16,20},{20,16},{24,28},{28,24},{1,5},{5... | collective-permute-start | bytes 3538952 | tf_op jit(solution)/shard_map/ppermute | solution.py:21
  40.5 24.1 %copy-start.3 = (bf16[128,1152]{1,0:T(8,128)(2,1)S(1)}, bf16[128,1152]{1,0:T(8,128)(2,1)}, u32[]{:S(2)}) copy-start(bf16[128,1152]{1,0:T(8,128)(2,1)} %image_ref.3) | copy-start | bytes 884740
  40.5 12.7 %collective-permute-start.14 = (bf16[128,1152]{1,0:T(8,128)(2,1)S(1)}, bf16[128,1152]{1,0:T(8,128)(2,1)S(1)}, u32[]{:S(2)}, u32[]{:S(2)}) collective-permute-start(bf16[128,1152]{1,0:T(8,128)(2,1)S(1)} %get-tuple-element.56), channel_id=1, source_target_pairs={{0,8},{4,12},{8,0},{12,4},{16,24},{20,28},{24,16},{28,20},{1,9},{5... | collective-permute-start | bytes 884744 | tf_op jit(solution)/shard_map/ppermute | solution.py:21
  42.0 10.5 %collective-permute-start.10 = (bf16[128,896]{1,0:T(8,128)(2,1)S(1)}, bf16[128,896]{1,0:T(8,128)(2,1)S(1)}, u32[]{:S(2)}, u32[]{:S(2)}) collective-permute-start(bf16[128,896]{1,0:T(8,128)(2,1)S(1)} %get-tuple-element.48), channel_id=1, source_target_pairs={{0,16},{4,20},{8,24},{12,28},{16,0},{20,4},{24,8},{28,12},{1,17},{... | collective-permute-start | bytes 688136 | tf_op jit(solution)/shard_map/ppermute | solution.py:21
  42.5 6.4 %collective-permute-start.8 = (bf16[272,128]{1,0:T(8,128)(2,1)S(1)}, bf16[272,128]{1,0:T(8,128)(2,1)S(1)}, u32[]{:S(2)}, u32[]{:S(2)}) collective-permute-start(bf16[272,128]{1,0:T(8,128)(2,1)S(1)} %get-tuple-element.45), channel_id=1, source_target_pairs={{0,2},{1,3},{2,0},{3,1},{4,6},{5,7},{6,4},{7,5},{8,10},{9,11},{10,... | collective-permute-start | bytes 208904 | tf_op jit(solution)/shard_map/ppermute | solution.py:21
  43.2 9.4 %collective-permute-start.9 = (bf16[272,128]{1,0:T(8,128)(2,1)S(1)}, bf16[272,128]{1,0:T(8,128)(2,1)S(1)}, u32[]{:S(2)}, u32[]{:S(2)}) collective-permute-start(bf16[272,128]{1,0:T(8,128)(2,1)S(1)} %get-tuple-element.46), channel_id=1, source_target_pairs={{0,18},{1,19},{2,16},{3,17},{4,22},{5,23},{6,20},{7,21},{8,26},{9,... | collective-permute-start | bytes 208904 | tf_op jit(solution)/shard_map/ppermute | solution.py:31
  52.6 11.9 %collective-permute-start.11 = (bf16[1168,128]{1,0:T(8,128)(2,1)S(1)}, bf16[1168,128]{1,0:T(8,128)(2,1)S(1)}, u32[]{:S(2)}, u32[]{:S(2)}) collective-permute-start(bf16[1168,128]{1,0:T(8,128)(2,1)S(1)} %get-tuple-element.50), channel_id=1, source_target_pairs={{0,16},{4,20},{8,24},{12,28},{16,0},{20,4},{24,8},{28,12},{1,17},{... | collective-permute-start | bytes 897032 | tf_op jit(solution)/shard_map/ppermute | solution.py:21
  53.2 13.5 %copy-start.1 = (bf16[128,1152]{1,0:T(8,128)(2,1)S(1)}, bf16[128,1152]{1,0:T(8,128)(2,1)}, u32[]{:S(2)}) copy-start(bf16[128,1152]{1,0:T(8,128)(2,1)} %text_ref.3) | copy-start | bytes 884740
  53.3 13.4 %collective-permute-start.15 = (bf16[128,1152]{1,0:T(8,128)(2,1)S(1)}, bf16[128,1152]{1,0:T(8,128)(2,1)S(1)}, u32[]{:S(2)}, u32[]{:S(2)}) collective-permute-start(bf16[128,1152]{1,0:T(8,128)(2,1)S(1)} %get-tuple-element.58), channel_id=1, source_target_pairs={{0,1},{1,0},{2,3},{3,2},{4,5},{5,4},{6,7},{7,6},{8,9},{9,8},{10,11... | collective-permute-start | bytes 884744 | tf_op jit(solution)/shard_map/ppermute | solution.py:21
  53.6 13.2 %collective-permute-start.16 = (bf16[128,1152]{1,0:T(8,128)(2,1)S(1)}, bf16[128,1152]{1,0:T(8,128)(2,1)S(1)}, u32[]{:S(2)}, u32[]{:S(2)}) collective-permute-start(bf16[128,1152]{1,0:T(8,128)(2,1)S(1)} %get-tuple-element.59), channel_id=1, source_target_pairs={{0,8},{4,12},{8,0},{12,4},{16,24},{20,28},{24,16},{28,20},{1,9},{5... | collective-permute-start | bytes 884744 | tf_op jit(solution)/shard_map/ppermute | solution.py:21
  54.6 9.9 %collective-permute-start.12 = (bf16[128,896]{1,0:T(8,128)(2,1)S(1)}, bf16[128,896]{1,0:T(8,128)(2,1)S(1)}, u32[]{:S(2)}, u32[]{:S(2)}) collective-permute-start(bf16[128,896]{1,0:T(8,128)(2,1)S(1)} %get-tuple-element.51), channel_id=1, source_target_pairs={{0,2},{1,3},{2,0},{3,1},{4,6},{5,7},{6,4},{7,5},{8,10},{9,11},{10,... | collective-permute-start | bytes 688136 | tf_op jit(solution)/shard_map/ppermute | solution.py:21

commit v5 on v4

--- a/solution.py
+++ b/solution.py
@@ -11,7 +11,8 @@
 f32, bf16 = jnp.float32, jnp.bfloat16
 lanes = 128
 extra = 16
-direct_panels = 2
+direct_panels = 4
+weights = {"z": 10, "p1": 10, "heads": 10, "late": 2, "far heads": 2, "end": 5, "text": 4}
 VMEM = pl.BlockSpec(memory_space=pltpu.VMEM)
 SMEM = pl.BlockSpec(memory_space=pltpu.SMEM)
 ANY = pl.BlockSpec(memory_space=pl.ANY)
@@ -31,7 +32,7 @@
     return lax.ppermute(value, ("dp", "inner"), pairs)
 
 
-def call(kernel, out_shape, *operands, flops=0, scalars=0, scratch=(), after=()):
+def call(kernel, out_shape, *operands, flops=0, weight=0, scalars=0, scratch=(), after=()):
     moved = sum(o.size * o.dtype.itemsize for o in operands)
     moved += sum(o.size * o.dtype.itemsize for o in jax.tree.leaves(out_shape))
     body_of = kernel
@@ -44,7 +45,7 @@
         out_specs=jax.tree.map(lambda _: VMEM, out_shape),
         scratch_shapes=scratch,
         compiler_params=pltpu.CompilerParams(vmem_limit_bytes=40 * 1024 * 1024),
-        cost_estimate=pl.CostEstimate(flops=flops, bytes_accessed=moved, transcendentals=0),
+        cost_estimate=pl.CostEstimate(flops=flops + weight * 1_000_000_000, bytes_accessed=moved, transcendentals=0),
     )(*after, *operands)
 
 
@@ -83,7 +84,7 @@
                     match = ((text_ids == image_ids) & (text_ids < own)).astype(f32)
                     softplus = softplus - match * logits
                     sigmoid = sigmoid - match
-                slopes_ref[done : done + chunk.shape[0], left : left + step] = sigmoid.astype(bf16)
+                slopes_ref[done : done + chunk.shape[0], left : left + images.shape[0]] = sigmoid.astype(bf16)
                 total = total + jnp.sum(softplus, axis=0, keepdims=True)
                 done += chunk.shape[0]
         totals.append(total)
@@ -95,21 +96,33 @@
     image_emb_ref[...] = unit_of(image_ref[...])[0].astype(bf16)
 
 
-def first_stage_kernel(own_ref, beside_ref, above_ref, *refs):
-    count = (len(refs) - 2) // 2
-    raw_refs, texts_ref, above_emb_ref, emb_refs = refs[:count], refs[count], refs[count + 1], refs[count + 2 :]
+def near_texts_kernel(own_ref, beside_ref, above_ref, texts_ref, above_emb_ref):
     rows = own_ref.shape[0]
     texts_ref[:rows, :] = own_ref[...]
     texts_ref[rows : 2 * rows, :] = unit_of(beside_ref[...])[0].astype(bf16)
     above = unit_of(above_ref[...])[0].astype(bf16)
     texts_ref[2 * rows :, :] = above
     above_emb_ref[...] = above
-    for raw, emb in zip(raw_refs, emb_refs):
+
+
+def unit_kernel(*refs):
+    for raw, emb in zip(refs[: len(refs) // 2], refs[len(refs) // 2 :]):
         emb[...] = unit_of(raw[...])[0].astype(bf16)
 
 
-def copy_kernel(source_ref, target_ref):
-    target_ref[...] = source_ref[...]
+def far_pairs_kernel(scale_ref, bias_ref, *refs):
+    text_refs, near_images_ref, near_slopes_ref, refs = refs[:4], refs[4], refs[5], refs[6:]
+    image_refs, (images_ref, own_slopes_ref, other_slopes_ref, loss_ref, sent_ref) = refs[:-5], refs[-5:]
+    rows = image_refs[0].shape[0]
+    for place, block in enumerate(image_refs):
+        images_ref[place * rows : (place + 1) * rows, :] = block[...]
+    loss = pair_terms(scale_ref[0], bias_ref[0], text_refs[2:], images_ref, other_slopes_ref, 0)
+    sums = jnp.dot(near_slopes_ref[...], near_images_ref[...], preferred_element_type=f32)
+    sums = sums + jnp.dot(other_slopes_ref[...], images_ref[...], preferred_element_type=f32)
+    sent_ref[...] = sums.astype(bf16)
+    loss_ref[...] = loss + pair_terms(
+        scale_ref[0], bias_ref[0], text_refs[:2], images_ref, own_slopes_ref, 0
+    )
 
 
 def own_core_pairs_kernel(scale_ref, bias_ref, near_ref, far_ref, *refs):
@@ -123,12 +136,11 @@
 
 
 def other_core_pairs_kernel(
-    scale_ref, bias_ref, near_ref, far_ref, images_ref, first_loss_ref, slopes_ref, loss_ref, sent_ref
+    scale_ref, bias_ref, near_ref, far_ref, images_ref, first_loss_ref, slopes_ref, loss_ref
 ):
     loss_ref[...] = first_loss_ref[...] + pair_terms(
         scale_ref[0], bias_ref[0], (near_ref, far_ref), images_ref, slopes_ref, 0
     )
-    sent_ref[...] = jnp.dot(slopes_ref[...], images_ref[...], preferred_element_type=f32).astype(bf16)
 
 
 def loss_rows(loss):
@@ -137,16 +149,12 @@
     return jnp.where(which == 0, high, loss - high).astype(bf16)
 
 
-def image_sums_kernel(plain, loss_ref, *refs):
+def image_sums_kernel(own, plain, loss_ref, *refs):
     slope_refs, text_refs, refs = refs[:2], refs[2:6], refs[6:]
-    own_ref, own_loss_ref, plain_refs, head_refs, tail_refs = (
-        refs[0],
-        refs[1],
-        refs[2 : 2 + plain],
-        refs[2 + plain :: 2],
-        refs[3 + plain :: 2],
-    )
-    rows, width = own_ref.shape
+    own_refs, refs = refs[: 2 * own], refs[2 * own :]
+    whole_refs = (*refs[:plain], *refs[plain::2])
+    tail_refs = (None,) * plain + tuple(refs[plain + 1 :: 2])
+    rows, width = text_refs[1].shape
     step = 3 * lanes
     for left in range(0, width, step):
         total = None
@@ -160,28 +168,36 @@
                     preferred_element_type=f32,
                 )
                 total, done = part if total is None else total + part, done + block.shape[0]
-        own_ref[:, left : left + step] = total[:rows, :]
-        for place, out in enumerate((*plain_refs, *head_refs), 1):
-            panels = (out.shape[0] - extra) // rows
-            sums = total[place * rows : (place + 1) * rows, :]
+        if own:
+            own_refs[0][:, left : left + step] = total[:rows, :]
+        for place, (out, tail) in enumerate(zip(whole_refs, tail_refs), own):
+            first = (out.shape[0] - extra) // rows * lanes
             for at in range(left, left + step, lanes):
-                piece = sums[:, at - left : at - left + lanes]
-                if at < panels * lanes:
+                piece = total[place * rows : (place + 1) * rows, at - left : at - left + lanes]
+                if at < first:
                     out[at // lanes * rows : (at // lanes + 1) * rows, :] = piece.astype(bf16)
                 else:
-                    tail = tail_refs[place - 1 - plain]
-                    tail[:, at - panels * lanes : at - panels * lanes + lanes] = piece.astype(tail.dtype)
-    own_loss_ref[...] = loss_ref[:, :rows]
-    for place, out in enumerate((*plain_refs, *head_refs), 1):
+                    tail[:, at - first : at - first + lanes] = piece.astype(tail.dtype)
+    if own:
+        own_refs[1][...] = loss_ref[:, :rows]
+    for place, out in enumerate(whole_refs, own):
         out[out.shape[0] - extra :, :] = loss_rows(loss_ref[:, place * rows : (place + 1) * rows])
 
 
-def text_sums_kernel(received_ref, slopes_ref, images_ref, *outs):
+def text_sums_kernel(groups, received_ref, *refs):
+    slope_refs, image_refs, outs = refs[:groups], refs[groups : 2 * groups], refs[2 * groups :]
     rows = outs[0].shape[0]
     for k, out in enumerate(outs):
         cut = slice(k * rows, (k + 1) * rows)
-        sums = jnp.dot(slopes_ref[cut, :], images_ref[...], preferred_element_type=f32)
-        out[...] = (sums + received_ref[cut, :].astype(f32)).astype(out.dtype)
+        sums = received_ref[cut, :].astype(f32)
+        for slopes, images in zip(slope_refs, image_refs):
+            sums = sums + jnp.dot(slopes[cut, :], images[...], preferred_element_type=f32)
+        out[...] = sums.astype(out.dtype)
+
+
+def late_heads_kernel(*refs):
+    for source, target in zip(refs[: len(refs) // 2], refs[len(refs) // 2 :]):
+        target[...] = source[...]
 
 
 def late_kernel(sums, parts, *refs):
@@ -245,113 +261,136 @@
 
     image_dp, image_inner = range(4, dp_count, 4), range(2, inner_count, 2)
 
+    text_z = swapped(text, "inner", 1)
     images_z = [swapped(image, "inner", q) for q in image_inner]
-    text_z = swapped(text, "inner", 1)
     text_x = swapped(text, "dp", 2)
     images_y = [swapped(image, "dp", p) for p in image_dp]
     text_emb, image_emb = call(own_rows_kernel, (block, block), text, image)
-    near_texts, text_z_emb, *embs = call(
-        first_stage_kernel,
-        (shape((3 * rows, width), bf16), block) + (block,) * (len(images_y) + len(images_z)),
-        text_emb,
-        text_x,
-        text_z,
-        *images_y,
-        *images_z,
-    )
-    embs_y, embs_z = embs[: len(images_y)], embs[len(images_y) :]
-
+
+    near_texts, text_z_emb = call(
+        near_texts_kernel, (shape((3 * rows, width), bf16), block), text_emb, text_x, text_z, after=images_y
+    )
     far_text = swapped(text_z_emb, "dp", 2)
+    near_swapped = swapped(near_texts, "dp", 1)
+    embs_z = call(unit_kernel, [block] * len(images_z), *images_z, weight=weights["z"])
     embs_yz = [swapped(emb, "dp", p) for emb in embs_z for p in image_dp]
-    near_swapped = swapped(near_texts, "dp", 1)
-    far_text = call(copy_kernel, block, far_text, after=embs_yz)
     far_swapped = swapped(far_text, "dp", 1)
-
-    embs = [image_emb, *embs_y, *embs_z, *embs_yz]
-    held, texts_half = len(embs) * rows, 4 * rows
-    slopes_shape = shape((texts_half, held), bf16)
-    pair_flops = 2 * held * texts_half * width
+    embs_y = call(unit_kernel, [block] * len(images_y), *images_y)
+
+    near, far = [image_emb, *embs_y, *embs_z], embs_yz
+    near_rows, far_rows, texts_half = len(near) * rows, len(far) * rows, 4 * rows
+    texts = [near_texts, far_text, near_swapped, far_swapped]
+    pair_flops = 2 * rows * texts_half * width
     images, own_core_slopes, loss = call(
         own_core_pairs_kernel,
-        (shape((held, width), bf16), slopes_shape, shape((1, held), f32)),
+        (shape((near_rows, width), bf16), shape((texts_half, near_rows), bf16), shape((1, near_rows), f32)),
         scale,
         bias,
-        near_texts,
-        far_text,
-        *embs,
-        flops=pair_flops,
+        *texts[:2],
+        *near,
+        flops=pair_flops * len(near),
+        weight=weights["p1"],
         scalars=2,
     )
-    other_core_slopes, loss, crossing = call(
+    other_core_slopes, loss = call(
         other_core_pairs_kernel,
-        (slopes_shape, shape((1, held), f32), shape((texts_half, width), bf16)),
+        (shape((texts_half, near_rows), bf16), shape((1, near_rows), f32)),
         scale,
         bias,
-        near_swapped,
-        far_swapped,
+        *texts[2:],
         images,
         loss,
-        flops=2 * pair_flops,
+        flops=pair_flops * len(near),
         scalars=2,
     )
-    crossed = swapped(crossing, "dp", 1)
-
     head_rows = direct_panels * rows + extra
     tail_width = width - direct_panels * lanes
-    out_shapes = [wide_block, shape((1, rows), f32)]
-    out_shapes += [shape((width // lanes * rows + extra, lanes), bf16)] * len(embs_y)
-    for kind, count in ((f32, len(embs_z)), (bf16, len(embs_yz))):
-        out_shapes += [shape((head_rows, lanes), bf16), shape((rows, tail_width), kind)] * count
     image_grad, own_loss, *sent = call(
-        functools.partial(image_sums_kernel, len(embs_y)),
-        out_shapes,
+        functools.partial(image_sums_kernel, 1, len(embs_y)),
+        [wide_block, shape((1, rows), f32)]
+        + [shape((width // lanes * rows + extra, lanes), bf16)] * len(embs_y)
+        + [shape((head_rows, lanes), bf16), shape((rows, tail_width), f32)] * len(embs_z),
         loss,
         own_core_slopes,
         other_core_slopes,
-        near_texts,
-        far_text,
-        near_swapped,
-        far_swapped,
-        flops=2 * pair_flops,
+        *texts,
+        flops=2 * pair_flops * len(near),
     )
     payloads_y, heads, tails = sent[: len(embs_y)], sent[len(embs_y) :: 2], sent[len(embs_y) + 1 :: 2]
-
-    moved_tails = [
-        swapped(tail, "dp", p)
-        for tail, p in zip(tails[len(embs_z) :], [p for _ in image_inner for p in image_dp])
-    ]
     z_heads = [swapped(head, "inner", q) for head, q in zip(heads, image_inner)]
-    yz_heads = [
-        swapped_both(head, p, q)
-        for head, (p, q) in zip(heads[len(embs_z) :], [(p, q) for q in image_inner for p in image_dp])
-    ]
+
+    far_images, far_own_slopes, far_other_slopes, loss, crossing = call(
+        far_pairs_kernel,
+        (
+            shape((far_rows, width), bf16),
+            shape((texts_half, far_rows), bf16),
+            shape((texts_half, far_rows), bf16),
+            shape((1, far_rows), f32),
+            shape((texts_half, width), bf16),
+        ),
+        scale,
+        bias,
+        *texts,
+        images,
+        other_core_slopes,
+        *far,
+        flops=pair_flops * (len(near) + 3 * len(far)),
+        scalars=2,
+        after=[image_grad],
+    )
+    crossed = swapped(crossing, "dp", 1)
+    sent = call(
+        functools.partial(image_sums_kernel, 0, 0),
+        [shape((head_rows, lanes), bf16), shape((rows, tail_width), bf16)] * len(far),
+        loss,
+        far_own_slopes,
+        far_other_slopes,
+        *texts,
+        flops=2 * pair_flops * len(far),
+    )
+    far_places = [(p, q) for q in image_inner for p in image_dp]
+    moved_tails = [swapped(tail, "dp", p) for tail, (p, q) in zip(sent[1::2], far_places)]
+    yz_heads = [swapped_both(head, p, q) for head, (p, q) in zip(sent[::2], far_places)]
     text_grad, text_x_sums, text_z_sums, text_xz_sums = call(
-        text_sums_kernel,
+        functools.partial(text_sums_kernel, 2),
         (wide_block, block, wide_block, block),
         crossed,
         own_core_slopes,
+        far_own_slopes,
         images,
-        flops=pair_flops,
-        after=[image_grad],
+        far_images,
+        flops=pair_flops * (len(near) + len(far)),
+        after=[sent[0]],
     )
     moved_text = swapped(text_xz_sums, "dp", 2)
-
+    (moved_text,) = call(late_heads_kernel, [block], moved_text, weight=weights["text"])
+
+    z_heads = call(late_heads_kernel, [shape(h.shape, bf16) for h in z_heads], *z_heads, weight=weights["heads"], after=[text_x_sums])
     late = call(
         functools.partial(late_kernel, len(image_inner), len(image_dp)),
         [shape((rows, tail_width), bf16)] * len(image_inner) + [shape(p.shape, bf16) for p in payloads_y],
-        *tails[: len(embs_z)],
+        *tails,
         *moved_tails,
         *payloads_y,
-        after=z_heads + yz_heads,
+        weight=weights["late"],
+        after=z_heads,
     )
     tail_parts = [swapped(part, "inner", q) for part, q in zip(late, image_inner)]
     y_parts = [swapped(part, "dp", p) for part, p in zip(late[len(image_inner) :], image_dp)]
+    yz_heads = call(
+        late_heads_kernel, [shape(h.shape, bf16) for h in yz_heads], *yz_heads, weight=weights["far heads"], after=late[:1]
+    )
     late_text_z, late_text_x = call(
-        functools.partial(late_kernel, 1, 1), [block, block], text_z_sums, moved_text, text_x_sums
+        functools.partial(late_kernel, 1, 1),
+        [block, block],
+        text_z_sums,
+        moved_text,
+        text_x_sums,
+        after=yz_heads,
     )
     text_parts = [swapped(late_text_z, "inner", 1), swapped(late_text_x, "dp", 2)]
 
-    head_parts = z_heads + yz_heads + y_parts
+    head_parts = [*z_heads, *yz_heads, *y_parts]
     image_gradient, image_loss = call(
         functools.partial(image_end_kernel, batch, len(head_parts)),
         (wide_block, shape((1, rows), f32)),
@@ -362,6 +401,7 @@
         *head_parts,
         *tail_parts,
         scalars=1,
+        weight=weights["end"],
         scratch=[pltpu.VMEM((rows, width), f32)],
     )
     text_gradient = call(text_end_kernel, wide_block, scale, text, text_grad, *text_parts, scalars=1)

time: 68 us -> 63.1 us (0.928)
  waiting for transfers between devices: 33.2 us -> 28.3 us
  starting transfers between devices: 20.6 us -> 19.2 us
  Pallas kernels: 10 us -> 11.4 us
    ppermute x1, waiting for transfers between devices: 3.64 us -> 0.06 us  [swapped_both(): return lax.ppermute(value, ('dp', 'inner'), pairs)]
    ppermute x1, starting transfers between devices: 3.23 us -> 1.74 us  [swapped_both(): return lax.ppermute(value, ('dp', 'inner'), pairs)]
    pallas_call x11 -> x17, Pallas kernels: 10 us -> 11.4 us  [call(): pl.pallas_call(body_of, out_shape=out_shape, in_specs=[ANY] * len(after)...]
    ppermute x16, waiting for transfers between devices: 29.5 us -> 28.2 us  [swapped(): lax.ppermute(value, axis, [(place, place ^ step) for place in range(lax.a...]
  transfers between devices with their start and end apart: 17 -> 17, of which waited for: 9 -> 8; matrix products, arithmetic and copies ran while one was open for 0% -> 0% of each run, Pallas kernels for 8% -> 13%
where the time goes in v5:
time: 63.1 us; the launch traced here: 62.9 us
  waiting for transfers between devices  28.3 us (45%)
  starting transfers between devices  19.2 us (30%)
  Pallas kernels  11.4 us (18%)
  between operations  2.11 us (3%)
  local copies, waits for them, and re-layouts  1.93 us (3%)
    ppermute x16, waiting for transfers between devices, swapped(): lax.ppermute(value, axis, [(place, place ^ step) for place in range(lax.a...  28.2 us
    ppermute x16, starting transfers between devices, swapped(): lax.ppermute(value, axis, [(place, place ^ step) for place in range(lax.a...  17.4 us
    pallas_call x17, Pallas kernels, call(): pl.pallas_call(body_of, out_shape=out_shape, in_specs=[ANY] * len(after)...  11.4 us
    unnamed x8, local copies, waits for them, and re-layouts  1.93 us
    ppermute x1, starting transfers between devices, swapped_both(): return lax.ppermute(value, ('dp', 'inner'), pairs)  1.74 us
  transfers between devices with their start and end apart: 17, of which 8 were waited for; matrix products, arithmetic and copies ran while one was open for 0% of the time, Pallas kernels for 13%

profile of v5, /device:TPU:0, one launch (start us, length us, event | category | flops | bytes accessed | tf_op | source)
XLA Modules:
  0.0 62.9 jit_solution(10923766772892805270)
XLA Ops:
  0.6 3.0 %collective-permute-start = (bf16[128,1152]{1,0:T(8,128)(2,1)}, bf16[128,1152]{1,0:T(8,128)(2,1)S(1)}, u32[]{:S(2)}, u32[]{:S(2)}) collective-permute-start(bf16[128,1152]{1,0:T(8,128)(2,1)} %image_ref.3), channel_id=1, source_target_pairs={{0,16},{4,20},{8,24},{12,28},{16,0},{20,4},{24,8},{28,12},{1,17},{... | collective-permute-start | bytes 884744 | tf_op jit(solution)/shard_map/ppermute | solution.py:22
  3.7 1.5 %collective-permute-start.1 = (bf16[128,1152]{1,0:T(8,128)(2,1)}, bf16[128,1152]{1,0:T(8,128)(2,1)S(1)}, u32[]{:S(2)}, u32[]{:S(2)}) collective-permute-start(bf16[128,1152]{1,0:T(8,128)(2,1)} %text_ref.3), channel_id=1, source_target_pairs={{0,8},{4,12},{8,0},{12,4},{16,24},{20,28},{24,16},{28,20},{1,9},{5... | collective-permute-start | bytes 884744 | tf_op jit(solution)/shard_map/ppermute | solution.py:22
  5.2 1.6 %collective-permute-start.2 = (bf16[128,1152]{1,0:T(8,128)(2,1)}, bf16[128,1152]{1,0:T(8,128)(2,1)S(1)}, u32[]{:S(2)}, u32[]{:S(2)}) collective-permute-start(bf16[128,1152]{1,0:T(8,128)(2,1)} %text_ref.3), channel_id=1, source_target_pairs={{0,1},{1,0},{2,3},{3,2},{4,5},{5,4},{6,7},{7,6},{8,9},{9,8},{10,11... | collective-permute-start | bytes 884744 | tf_op jit(solution)/shard_map/ppermute | solution.py:22
  6.7 2.6 %collective-permute-start.6 = (bf16[128,1152]{1,0:T(8,128)(2,1)}, bf16[128,1152]{1,0:T(8,128)(2,1)S(1)}, u32[]{:S(2)}, u32[]{:S(2)}) collective-permute-start(bf16[128,1152]{1,0:T(8,128)(2,1)} %image_ref.3), channel_id=1, source_target_pairs={{0,2},{1,3},{2,0},{3,1},{4,6},{5,7},{6,4},{7,5},{8,10},{9,11},{10,... | collective-permute-start | bytes 884744 | tf_op jit(solution)/shard_map/ppermute | solution.py:22
  9.3 1.0 %copy-done = bf16[128,1152]{1,0:T(8,128)(2,1)S(1)} copy-done((bf16[128,1152]{1,0:T(8,128)(2,1)S(1)}, bf16[128,1152]{1,0:T(8,128)(2,1)}, u32[]{:S(2)}) %copy-start) | copy-done | bytes 294936
  10.3 1.0 %copy-done.2 = bf16[128,1152]{1,0:T(8,128)(2,1)S(1)} copy-done((bf16[128,1152]{1,0:T(8,128)(2,1)S(1)}, bf16[128,1152]{1,0:T(8,128)(2,1)}, u32[]{:S(2)}) %copy-start.2) | copy-done | bytes 294936
  12.8 6.9 %collective-permute-done.2.refs_3_ = bf16[128,1152]{1,0:T(8,128)(2,1)S(1)} collective-permute-done((bf16[128,1152]{1,0:T(8,128)(2,1)}, bf16[128,1152]{1,0:T(8,128)(2,1)S(1)}, u32[]{:S(2)}, u32[]{:S(2)}) %collective-permute-start.2) | collective-permute-done | bytes 294944 | tf_op jit(solution)/shard_map/ppermute | solution.py:22
  20.6 1.5 %collective-permute-done.6.refs_0_ = bf16[128,1152]{1,0:T(8,128)(2,1)S(1)} collective-permute-done((bf16[128,1152]{1,0:T(8,128)(2,1)}, bf16[128,1152]{1,0:T(8,128)(2,1)S(1)}, u32[]{:S(2)}, u32[]{:S(2)}) %collective-permute-start.6) | collective-permute-done | bytes 294944 | tf_op jit(solution)/shard_map/ppermute | solution.py:22
  23.0 4.3 %collective-permute-done.4.far_ref.refs_3_.refs_4_ = bf16[128,1152]{1,0:T(8,128)(2,1)S(1)} collective-permute-done((bf16[128,1152]{1,0:T(8,128)(2,1)S(1)}, bf16[128,1152]{1,0:T(8,128)(2,1)S(1)}, u32[]{:S(2)}, u32[]{:S(2)}) %collective-permute-start.4) | collective-permute-done | bytes 294944 | tf_op jit(solution)/shard_map/ppermute | solution.py:22
  27.3 1.3 %shard_map.71 = (bf16[384,1152]{1,0:T(8,128)(2,1)S(1)}, bf16[512,384]{1,0:T(8,128)(2,1)S(1)}, f32[1,384]{1,0:T(1,128)S(1)}) custom-call(f32[1]{0:T(128)S(6)} %exp.3.scale_ref.refs_1_, f32[1]{0:T(128)S(6)} %copy.8.bias_ref.refs_2_, bf16[384,1152]{1,0:T(8,128)(2,1)S(1)} %get-tuple-element.35.near_ref.refs_2_.refs_3_, ...), custom_call_target="tpu_custom_call" | custom-call | flops 10452984832 | bytes 3343880 | tf_op jit(solution)/shard_map/pallas_call | solution.py:41
  28.9 1.2 %shard_map.72 = (bf16[512,384]{1,0:T(8,128)(2,1)S(1)}, f32[1,384]{1,0:T(1,128)S(1)}) custom-call(f32[1]{0:T(128)S(6)} %exp.3.scale_ref.refs_1_, f32[1]{0:T(128)S(6)} %copy.8.bias_ref.refs_2_, bf16[384,1152]{1,0:T(8,128)(2,1)S(1)} %collective-permute-done.3.near_ref.refs_4_.refs_5_, bf16[128,1152]{1,0:T(8,128)(2,1)S(1)} %collective-permute-done.5.far_ref.refs_5_.refs_6_, ...), custom_call_target="tpu_custom_call" | custom-call | flops 452984832 | bytes 2460680 | tf_op jit(solution)/shard_map/pallas_call | solution.py:41
  30.1 1.8 %shard_map.73 = (f32[128,1152]{1,0:T(8,128)S(1)}, f32[1,128]{1,0:T(1,128)S(1)}, bf16[1168,128]{1,0:T(8,128)(2,1)S(1)}, bf16[528,128]{1,0:T(8,128)(2,1)S(1)}, f32[128,640]{1,0:T(8,128)S(1)}) custom-call(f32[1,384]{1,0:T(1,128)S(1)} %get-tuple-element.40.loss_ref, bf16[512,384]{1,0:T(8,128)(2,1)S(1)} %get-tuple-element.41.refs_0_.refs_2_, ...), custom_call_target="tpu_custom_call" | custom-call | flops 905969664 | bytes 4499456 | tf_op jit(solution)/shard_map/pallas_call | solution.py:41
  31.9 2.0 %shard_map.74 = (bf16[128,1152]{1,0:T(8,128)(2,1)S(1)}, bf16[512,128]{1,0:T(8,128)(2,1)S(1)}, bf16[512,128]{1,0:T(8,128)(2,1)S(1)}, f32[1,128]{1,0:T(1,128)S(1)}, bf16[512,1152]{1,0:T(8,128)(2,1)S(1)}) custom-call(f32[128,1152]{1,0:T(8,128)S(1)} %get-tuple-element.43.refs_0_.grad_ref, f32[1]{0:T(128)S(6)} %exp.3.scale_ref.refs_1_, ...), custom_call_target="tpu_custom_call" | custom-call | flops 905969664 | bytes 5669384 | tf_op jit(solution)/shard_map/pallas_call | solution.py:41
  34.2 1.2 %collective-permute-start.9 = (bf16[528,128]{1,0:T(8,128)(2,1)S(1)}, bf16[528,128]{1,0:T(8,128)(2,1)S(1)}, u32[]{:S(2)}, u32[]{:S(2)}) collective-permute-start(bf16[528,128]{1,0:T(8,128)(2,1)S(1)} %get-tuple-element.52), channel_id=1, source_target_pairs={{0,2},{1,3},{2,0},{3,1},{4,6},{5,7},{6,4},{7,5},{8,10},{9,11},{10,... | collective-permute-start | bytes 405512 | tf_op jit(solution)/shard_map/ppermute | solution.py:22
  36.2 1.7 %collective-permute-start.11 = (bf16[528,128]{1,0:T(8,128)(2,1)S(1)}, bf16[528,128]{1,0:T(8,128)(2,1)S(1)}, u32[]{:S(2)}, u32[]{:S(2)}) collective-permute-start(bf16[528,128]{1,0:T(8,128)(2,1)S(1)} %get-tuple-element.48.refs_0_), channel_id=1, source_target_pairs={{0,18},{1,19},{2,16},{3,17},{4,22},{5,23},{6,20},{7,21},{8,26},{9,... | collective-permute-start | bytes 405512 | tf_op jit(solution)/shard_map/ppermute | solution.py:32
  37.9 1.5 %collective-permute-start.10 = (bf16[128,640]{1,0:T(8,128)(2,1)S(1)}, bf16[128,640]{1,0:T(8,128)(2,1)S(1)}, u32[]{:S(2)}, u32[]{:S(2)}) collective-permute-start(bf16[128,640]{1,0:T(8,128)(2,1)S(1)} %get-tuple-element.54), channel_id=1, source_target_pairs={{0,16},{4,20},{8,24},{12,28},{16,0},{20,4},{24,8},{28,12},{1,17},{... | collective-permute-start | bytes 491528 | tf_op jit(solution)/shard_map/ppermute | solution.py:22
  39.4 1.2 %shard_map.76 = (f32[128,1152]{1,0:T(8,128)S(1)}, bf16[128,1152]{1,0:T(8,128)(2,1)S(1)}, f32[128,1152]{1,0:T(8,128)S(1)}, bf16[128,1152]{1,0:T(8,128)(2,1)S(1)}) custom-call(bf16[528,128]{1,0:T(8,128)(2,1)S(1)} %get-tuple-element.48.refs_0_, bf16[512,1152]{1,0:T(8,128)(2,1)S(1)} %collective-permute-done.8.refs_1_, ...), custom_call_target="tpu_custom_call" | custom-call | flops 603979776 | bytes 4653056 | tf_op jit(solution)/shard_map/pallas_call | solution.py:41
  41.2 5.9 %collective-permute-done.9.refs_1_ = bf16[528,128]{1,0:T(8,128)(2,1)S(1)} collective-permute-done((bf16[528,128]{1,0:T(8,128)(2,1)S(1)}, bf16[528,128]{1,0:T(8,128)(2,1)S(1)}, u32[]{:S(2)}, u32[]{:S(2)}) %collective-permute-start.9) | collective-permute-done | bytes 135200 | tf_op jit(solution)/shard_map/ppermute | solution.py:22
  48.0 1.5 %collective-permute-start.12 = (bf16[1168,128]{1,0:T(8,128)(2,1)S(1)}, bf16[1168,128]{1,0:T(8,128)(2,1)S(1)}, u32[]{:S(2)}, u32[]{:S(2)}) collective-permute-start(bf16[1168,128]{1,0:T(8,128)(2,1)S(1)} %get-tuple-element.57), channel_id=1, source_target_pairs={{0,16},{4,20},{8,24},{12,28},{16,0},{20,4},{24,8},{28,12},{1,17},{... | collective-permute-start | bytes 897032 | tf_op jit(solution)/shard_map/ppermute | solution.py:22
  50.3 1.1 %collective-permute-start.16 = (bf16[128,1152]{1,0:T(8,128)(2,1)S(1)}, bf16[128,1152]{1,0:T(8,128)(2,1)S(1)}, u32[]{:S(2)}, u32[]{:S(2)}) collective-permute-start(bf16[128,1152]{1,0:T(8,128)(2,1)S(1)} %get-tuple-element.63), channel_id=1, source_target_pairs={{0,8},{4,12},{8,0},{12,4},{16,24},{20,28},{24,16},{28,20},{1,9},{5... | collective-permute-start | bytes 884744 | tf_op jit(solution)/shard_map/ppermute | solution.py:22
  51.4 5.7 %collective-permute-done.13.refs_3_ = bf16[128,640]{1,0:T(8,128)(2,1)S(1)} collective-permute-done((bf16[128,640]{1,0:T(8,128)(2,1)S(1)}, bf16[128,640]{1,0:T(8,128)(2,1)S(1)}, u32[]{:S(2)}, u32[]{:S(2)}) %collective-permute-start.13) | collective-permute-done | bytes 163872 | tf_op jit(solution)/shard_map/ppermute | solution.py:22
  57.1 1.2 %shard_map.80 = (f32[128,1152]{1,0:T(8,128)}, f32[1,128]{1,0:T(1,128)}) custom-call(f32[1]{0:T(128)S(6)} %exp.3.scale_ref.refs_1_, bf16[128,1152]{1,0:T(8,128)(2,1)S(1)} %copy-done.3, f32[128,1152]{1,0:T(8,128)S(1)} %get-tuple-element.43.refs_0_.grad_ref, f32[1,128]{1,0:T(1,128)S(1)} %get-tuple-element.44.loss_ref, bf16[528,128]{1,0:T(8,128)(2,1)S(1)} %shard_map.77.refs_0_, ...), custom_call_target="tpu_custom_call" | custom-call | flops 5000000000 | bytes 2208772 | tf_op jit(solution)/shard_map/pallas_call | solution.py:41
  58.2 3.5 %collective-permute-done.15.refs_0_ = bf16[128,1152]{1,0:T(8,128)(2,1)S(1)} collective-permute-done((bf16[128,1152]{1,0:T(8,128)(2,1)S(1)}, bf16[128,1152]{1,0:T(8,128)(2,1)S(1)}, u32[]{:S(2)}, u32[]{:S(2)}) %collective-permute-start.15) | collective-permute-done | bytes 294944 | tf_op jit(solution)/shard_map/ppermute | solution.py:22
  61.8 1.1 %shard_map.83 = f32[128,1152]{1,0:T(8,128)} custom-call(f32[1]{0:T(128)S(6)} %exp.3.scale_ref.refs_1_, bf16[128,1152]{1,0:T(8,128)(2,1)S(1)} %copy-done.1, f32[128,1152]{1,0:T(8,128)S(1)} %get-tuple-element.59.grad_ref, bf16[128,1152]{1,0:T(8,128)(2,1)S(1)} %collective-permute-done.15.refs_0_, bf16[128,1152]{1,0:T(8,128)(2,1)S(1)} %collective-permute-done.16.refs_1_), custom_call_target="tpu_custom_call" | custom-call | bytes 2064388 | tf_op jit(solution)/shard_map/pallas_call | solution.py:41
  (35 shorter events, 5.4 us)
Async XLA Ops:
  0.6 12.2 %collective-permute-start = (bf16[128,1152]{1,0:T(8,128)(2,1)}, bf16[128,1152]{1,0:T(8,128)(2,1)S(1)}, u32[]{:S(2)}, u32[]{:S(2)}) collective-permute-start(bf16[128,1152]{1,0:T(8,128)(2,1)} %image_ref.3), channel_id=1, source_target_pairs={{0,16},{4,20},{8,24},{12,28},{16,0},{20,4},{24,8},{28,12},{1,17},{... | collective-permute-start | bytes 884744 | tf_op jit(solution)/shard_map/ppermute | solution.py:22
  3.7 9.1 %collective-permute-start.1 = (bf16[128,1152]{1,0:T(8,128)(2,1)}, bf16[128,1152]{1,0:T(8,128)(2,1)S(1)}, u32[]{:S(2)}, u32[]{:S(2)}) collective-permute-start(bf16[128,1152]{1,0:T(8,128)(2,1)} %text_ref.3), channel_id=1, source_target_pairs={{0,8},{4,12},{8,0},{12,4},{16,24},{20,28},{24,16},{28,20},{1,9},{5... | collective-permute-start | bytes 884744 | tf_op jit(solution)/shard_map/ppermute | solution.py:22
  5.2 14.6 %collective-permute-start.2 = (bf16[128,1152]{1,0:T(8,128)(2,1)}, bf16[128,1152]{1,0:T(8,128)(2,1)S(1)}, u32[]{:S(2)}, u32[]{:S(2)}) collective-permute-start(bf16[128,1152]{1,0:T(8,128)(2,1)} %text_ref.3), channel_id=1, source_target_pairs={{0,1},{1,0},{2,3},{3,2},{4,5},{5,4},{6,7},{7,6},{8,9},{9,8},{10,11... | collective-permute-start | bytes 884744 | tf_op jit(solution)/shard_map/ppermute | solution.py:22
  6.7 15.4 %collective-permute-start.6 = (bf16[128,1152]{1,0:T(8,128)(2,1)}, bf16[128,1152]{1,0:T(8,128)(2,1)S(1)}, u32[]{:S(2)}, u32[]{:S(2)}) collective-permute-start(bf16[128,1152]{1,0:T(8,128)(2,1)} %image_ref.3), channel_id=1, source_target_pairs={{0,2},{1,3},{2,0},{3,1},{4,6},{5,7},{6,4},{7,5},{8,10},{9,11},{10,... | collective-permute-start | bytes 884744 | tf_op jit(solution)/shard_map/ppermute | solution.py:22
  9.3 1.0 %copy-start = (bf16[128,1152]{1,0:T(8,128)(2,1)S(1)}, bf16[128,1152]{1,0:T(8,128)(2,1)}, u32[]{:S(2)}) copy-start(bf16[128,1152]{1,0:T(8,128)(2,1)} %text_ref.3) | copy-start | bytes 884740
  10.3 1.0 %copy-start.2 = (bf16[128,1152]{1,0:T(8,128)(2,1)S(1)}, bf16[128,1152]{1,0:T(8,128)(2,1)}, u32[]{:S(2)}) copy-start(bf16[128,1152]{1,0:T(8,128)(2,1)} %image_ref.3) | copy-start | bytes 884740
  20.0 7.3 %collective-permute-start.4 = (bf16[128,1152]{1,0:T(8,128)(2,1)S(1)}, bf16[128,1152]{1,0:T(8,128)(2,1)S(1)}, u32[]{:S(2)}, u32[]{:S(2)}) collective-permute-start(bf16[128,1152]{1,0:T(8,128)(2,1)S(1)} %get-tuple-element.36), channel_id=1, source_target_pairs={{0,8},{4,12},{8,0},{12,4},{16,24},{20,28},{24,16},{28,20},{1,9},{5... | collective-permute-start | bytes 884744 | tf_op jit(solution)/shard_map/ppermute | solution.py:22
  22.3 9.6 %collective-permute-start.7 = (bf16[128,1152]{1,0:T(8,128)(2,1)S(1)}, bf16[128,1152]{1,0:T(8,128)(2,1)S(1)}, u32[]{:S(2)}, u32[]{:S(2)}) collective-permute-start(bf16[128,1152]{1,0:T(8,128)(2,1)S(1)} %shard_map.70.refs_2_), channel_id=1, source_target_pairs={{0,16},{4,20},{8,24},{12,28},{16,0},{20,4},{24,8},{28,12},{1,17},{... | collective-permute-start | bytes 884744 | tf_op jit(solution)/shard_map/ppermute | solution.py:22
  22.8 6.0 %collective-permute-start.3 = (bf16[384,1152]{1,0:T(8,128)(2,1)S(1)}, bf16[384,1152]{1,0:T(8,128)(2,1)S(1)}, u32[]{:S(2)}, u32[]{:S(2)}) collective-permute-start(bf16[384,1152]{1,0:T(8,128)(2,1)S(1)} %get-tuple-element.35.near_ref.refs_2_.refs_3_), channel_id=1, source_target_pairs={{0,4},{4,0},{8,12},{12,8},{16,20},{20,16},{24,28},{28,24},{1,5},{5... | collective-permute-start | bytes 2654216 | tf_op jit(solution)/shard_map/ppermute | solution.py:22
  27.3 1.6 %collective-permute-start.5 = (bf16[128,1152]{1,0:T(8,128)(2,1)S(1)}, bf16[128,1152]{1,0:T(8,128)(2,1)S(1)}, u32[]{:S(2)}, u32[]{:S(2)}) collective-permute-start(bf16[128,1152]{1,0:T(8,128)(2,1)S(1)} %collective-permute-done.4.far_ref.refs_3_.refs_4_), channel_id=1, source_target_pairs={{0,4},{4,0},{8,12},{12,8},{16,20},{20,16},{24,28},{28,24},{1,5},{5... | collective-permute-start | bytes 884744 | tf_op jit(solution)/shard_map/ppermute | solution.py:22
  33.9 5.5 %collective-permute-start.8 = (bf16[512,1152]{1,0:T(8,128)(2,1)S(1)}, bf16[512,1152]{1,0:T(8,128)(2,1)S(1)}, u32[]{:S(2)}, u32[]{:S(2)}) collective-permute-start(bf16[512,1152]{1,0:T(8,128)(2,1)S(1)} %get-tuple-element.49), channel_id=1, source_target_pairs={{0,4},{4,0},{8,12},{12,8},{16,20},{20,16},{24,28},{28,24},{1,5},{5... | collective-permute-start | bytes 3538952 | tf_op jit(solution)/shard_map/ppermute | solution.py:22
  34.2 12.9 %collective-permute-start.9 = (bf16[528,128]{1,0:T(8,128)(2,1)S(1)}, bf16[528,128]{1,0:T(8,128)(2,1)S(1)}, u32[]{:S(2)}, u32[]{:S(2)}) collective-permute-start(bf16[528,128]{1,0:T(8,128)(2,1)S(1)} %get-tuple-element.52), channel_id=1, source_target_pairs={{0,2},{1,3},{2,0},{3,1},{4,6},{5,7},{6,4},{7,5},{8,10},{9,11},{10,... | collective-permute-start | bytes 405512 | tf_op jit(solution)/shard_map/ppermute | solution.py:22
  36.2 13.4 %collective-permute-start.11 = (bf16[528,128]{1,0:T(8,128)(2,1)S(1)}, bf16[528,128]{1,0:T(8,128)(2,1)S(1)}, u32[]{:S(2)}, u32[]{:S(2)}) collective-permute-start(bf16[528,128]{1,0:T(8,128)(2,1)S(1)} %get-tuple-element.48.refs_0_), channel_id=1, source_target_pairs={{0,18},{1,19},{2,16},{3,17},{4,22},{5,23},{6,20},{7,21},{8,26},{9,... | collective-permute-start | bytes 405512 | tf_op jit(solution)/shard_map/ppermute | solution.py:32
  37.9 9.2 %collective-permute-start.10 = (bf16[128,640]{1,0:T(8,128)(2,1)S(1)}, bf16[128,640]{1,0:T(8,128)(2,1)S(1)}, u32[]{:S(2)}, u32[]{:S(2)}) collective-permute-start(bf16[128,640]{1,0:T(8,128)(2,1)S(1)} %get-tuple-element.54), channel_id=1, source_target_pairs={{0,16},{4,20},{8,24},{12,28},{16,0},{20,4},{24,8},{28,12},{1,17},{... | collective-permute-start | bytes 491528 | tf_op jit(solution)/shard_map/ppermute | solution.py:22
  40.6 8.9 %collective-permute-start.14 = (bf16[128,1152]{1,0:T(8,128)(2,1)S(1)}, bf16[128,1152]{1,0:T(8,128)(2,1)S(1)}, u32[]{:S(2)}, u32[]{:S(2)}) collective-permute-start(bf16[128,1152]{1,0:T(8,128)(2,1)S(1)} %get-tuple-element.61), channel_id=1, source_target_pairs={{0,8},{4,12},{8,0},{12,4},{16,24},{20,28},{24,16},{28,20},{1,9},{5... | collective-permute-start | bytes 884744 | tf_op jit(solution)/shard_map/ppermute | solution.py:22
  47.2 9.9 %collective-permute-start.13 = (bf16[128,640]{1,0:T(8,128)(2,1)S(1)}, bf16[128,640]{1,0:T(8,128)(2,1)S(1)}, u32[]{:S(2)}, u32[]{:S(2)}) collective-permute-start(bf16[128,640]{1,0:T(8,128)(2,1)S(1)} %get-tuple-element.56.refs_0_), channel_id=1, source_target_pairs={{0,2},{1,3},{2,0},{3,1},{4,6},{5,7},{6,4},{7,5},{8,10},{9,11},{10,... | collective-permute-start | bytes 491528 | tf_op jit(solution)/shard_map/ppermute | solution.py:22
  48.0 9.1 %collective-permute-start.12 = (bf16[1168,128]{1,0:T(8,128)(2,1)S(1)}, bf16[1168,128]{1,0:T(8,128)(2,1)S(1)}, u32[]{:S(2)}, u32[]{:S(2)}) collective-permute-start(bf16[1168,128]{1,0:T(8,128)(2,1)S(1)} %get-tuple-element.57), channel_id=1, source_target_pairs={{0,16},{4,20},{8,24},{12,28},{16,0},{20,4},{24,8},{28,12},{1,17},{... | collective-permute-start | bytes 897032 | tf_op jit(solution)/shard_map/ppermute | solution.py:22
  49.6 7.5 %copy-start.3 = (bf16[128,1152]{1,0:T(8,128)(2,1)S(1)}, bf16[128,1152]{1,0:T(8,128)(2,1)}, u32[]{:S(2)}) copy-start(bf16[128,1152]{1,0:T(8,128)(2,1)} %image_ref.3) | copy-start | bytes 884740
  49.7 12.1 %collective-permute-start.15 = (bf16[128,1152]{1,0:T(8,128)(2,1)S(1)}, bf16[128,1152]{1,0:T(8,128)(2,1)S(1)}, u32[]{:S(2)}, u32[]{:S(2)}) collective-permute-start(bf16[128,1152]{1,0:T(8,128)(2,1)S(1)} %get-tuple-element.62), channel_id=1, source_target_pairs={{0,1},{1,0},{2,3},{3,2},{4,5},{5,4},{6,7},{7,6},{8,9},{9,8},{10,11... | collective-permute-start | bytes 884744 | tf_op jit(solution)/shard_map/ppermute | solution.py:22
  50.3 11.5 %collective-permute-start.16 = (bf16[128,1152]{1,0:T(8,128)(2,1)S(1)}, bf16[128,1152]{1,0:T(8,128)(2,1)S(1)}, u32[]{:S(2)}, u32[]{:S(2)}) collective-permute-start(bf16[128,1152]{1,0:T(8,128)(2,1)S(1)} %get-tuple-element.63), channel_id=1, source_target_pairs={{0,8},{4,12},{8,0},{12,4},{16,24},{20,28},{24,16},{28,20},{1,9},{5... | collective-permute-start | bytes 884744 | tf_op jit(solution)/shard_map/ppermute | solution.py:22
  57.1 4.7 %copy-start.1 = (bf16[128,1152]{1,0:T(8,128)(2,1)S(1)}, bf16[128,1152]{1,0:T(8,128)(2,1)}, u32[]{:S(2)}) copy-start(bf16[128,1152]{1,0:T(8,128)(2,1)} %text_ref.3) | copy-start | bytes 884740

commit v6 on v5

--- a/solution.py
+++ b/solution.py
@@ -12,7 +12,7 @@
 lanes = 128
 extra = 16
 direct_panels = 4
-weights = {"z": 10, "p1": 10, "heads": 10, "late": 2, "far heads": 2, "end": 5, "text": 4}
+weights = {"z": 10, "p1": 10, "heads": 2, "late": 0, "far heads": 2, "end": 0, "text": 4, "text end": 10}
 VMEM = pl.BlockSpec(memory_space=pltpu.VMEM)
 SMEM = pl.BlockSpec(memory_space=pltpu.SMEM)
 ANY = pl.BlockSpec(memory_space=pl.ANY)
@@ -35,18 +35,18 @@
 def call(kernel, out_shape, *operands, flops=0, weight=0, scalars=0, scratch=(), after=()):
     moved = sum(o.size * o.dtype.itemsize for o in operands)
     moved += sum(o.size * o.dtype.itemsize for o in jax.tree.leaves(out_shape))
-    body_of = kernel
-    if after:
-        body_of = lambda *refs: kernel(*refs[len(after) :])
+    first, last = len(operands), len(operands) + len(after)
     return pl.pallas_call(
-        body_of,
+        lambda *refs: kernel(*refs[:first], *refs[last:]),
         out_shape=out_shape,
-        in_specs=[ANY] * len(after) + [SMEM] * scalars + [VMEM] * (len(operands) - scalars),
+        in_specs=[SMEM] * scalars + [VMEM] * (len(operands) - scalars) + [ANY] * len(after),
         out_specs=jax.tree.map(lambda _: VMEM, out_shape),
         scratch_shapes=scratch,
         compiler_params=pltpu.CompilerParams(vmem_limit_bytes=40 * 1024 * 1024),
-        cost_estimate=pl.CostEstimate(flops=flops + weight * 1_000_000_000, bytes_accessed=moved, transcendentals=0),
-    )(*after, *operands)
+        cost_estimate=pl.CostEstimate(
+            flops=flops + int(weight * 1e9), bytes_accessed=moved, transcendentals=0
+        ),
+    )(*operands, *after)
 
 
 def shape(dims, kind):
@@ -76,8 +76,12 @@
                     + offset
                 )
                 shrunk = jnp.exp(-jnp.abs(logits))
-                softplus = jnp.maximum(logits, 0.0) + jnp.log1p(shrunk)
-                sigmoid = jnp.where(logits >= 0.0, 1.0, shrunk) / (1.0 + shrunk)
+                raised = 1.0 + shrunk
+                inverse = pl.reciprocal(raised, approx=True)
+                inverse = inverse * (2.0 - raised * inverse)
+                log_raised = jnp.log(raised) + (shrunk - (raised - 1.0)) * inverse
+                softplus = jnp.maximum(logits, 0.0) + log_raised
+                sigmoid = jnp.where(logits >= 0.0, inverse, shrunk * inverse)
                 if own and done == 0 and left == 0:
                     text_ids = lax.broadcasted_iota(jnp.int32, logits.shape, 0)
                     image_ids = lax.broadcasted_iota(jnp.int32, logits.shape, 1)
@@ -96,13 +100,11 @@
     image_emb_ref[...] = unit_of(image_ref[...])[0].astype(bf16)
 
 
-def near_texts_kernel(own_ref, beside_ref, above_ref, texts_ref, above_emb_ref):
+def near_texts_kernel(above_ref, beside_ref, own_ref, texts_ref):
     rows = own_ref.shape[0]
     texts_ref[:rows, :] = own_ref[...]
     texts_ref[rows : 2 * rows, :] = unit_of(beside_ref[...])[0].astype(bf16)
-    above = unit_of(above_ref[...])[0].astype(bf16)
-    texts_ref[2 * rows :, :] = above
-    above_emb_ref[...] = above
+    texts_ref[2 * rows :, :] = above_ref[...]
 
 
 def unit_kernel(*refs):
@@ -261,18 +263,25 @@
 
     image_dp, image_inner = range(4, dp_count, 4), range(2, inner_count, 2)
 
+    images_y = [swapped(image, "dp", p) for p in image_dp]
+    text_x = swapped(text, "dp", 2)
+    images_z = [swapped(image, "inner", q) for q in image_inner]
     text_z = swapped(text, "inner", 1)
-    images_z = [swapped(image, "inner", q) for q in image_inner]
-    text_x = swapped(text, "dp", 2)
-    images_y = [swapped(image, "dp", p) for p in image_dp]
     text_emb, image_emb = call(own_rows_kernel, (block, block), text, image)
 
-    near_texts, text_z_emb = call(
-        near_texts_kernel, (shape((3 * rows, width), bf16), block), text_emb, text_x, text_z, after=images_y
+    text_z_emb, *embs_z = call(
+        unit_kernel, [block] * (1 + len(images_z)), text_z, *images_z, weight=weights["z"]
+    )
+    near_texts = call(
+        near_texts_kernel,
+        shape((3 * rows, width), bf16),
+        text_z_emb,
+        text_x,
+        text_emb,
+        after=images_y,
     )
     far_text = swapped(text_z_emb, "dp", 2)
     near_swapped = swapped(near_texts, "dp", 1)
-    embs_z = call(unit_kernel, [block] * len(images_z), *images_z, weight=weights["z"])
     embs_yz = [swapped(emb, "dp", p) for emb in embs_z for p in image_dp]
     far_swapped = swapped(far_text, "dp", 1)
     embs_y = call(unit_kernel, [block] * len(images_y), *images_y)
@@ -348,9 +357,6 @@
         *texts,
         flops=2 * pair_flops * len(far),
     )
-    far_places = [(p, q) for q in image_inner for p in image_dp]
-    moved_tails = [swapped(tail, "dp", p) for tail, (p, q) in zip(sent[1::2], far_places)]
-    yz_heads = [swapped_both(head, p, q) for head, (p, q) in zip(sent[::2], far_places)]
     text_grad, text_x_sums, text_z_sums, text_xz_sums = call(
         functools.partial(text_sums_kernel, 2),
         (wide_block, block, wide_block, block),
@@ -363,9 +369,30 @@
         after=[sent[0]],
     )
     moved_text = swapped(text_xz_sums, "dp", 2)
-    (moved_text,) = call(late_heads_kernel, [block], moved_text, weight=weights["text"])
-
-    z_heads = call(late_heads_kernel, [shape(h.shape, bf16) for h in z_heads], *z_heads, weight=weights["heads"], after=[text_x_sums])
+    sent = call(
+        late_heads_kernel, [shape(part.shape, bf16) for part in sent], *sent, after=[text_x_sums]
+    )
+    far_places = [(p, q) for q in image_inner for p in image_dp]
+    moved_tails = [swapped(tail, "dp", p) for tail, (p, q) in zip(sent[1::2], far_places)]
+    yz_heads = [swapped_both(head, p, q) for head, (p, q) in zip(sent[::2], far_places)]
+
+    z_heads = call(
+        late_heads_kernel,
+        [shape(h.shape, bf16) for h in z_heads],
+        *z_heads,
+        weight=weights["heads"],
+        after=[text_x_sums],
+    )
+    late_text_z, late_text_x = call(
+        functools.partial(late_kernel, 1, 1),
+        [block, block],
+        text_z_sums,
+        moved_text,
+        text_x_sums,
+        weight=weights["text"],
+        after=z_heads,
+    )
+    text_parts = [swapped(late_text_z, "inner", 1), swapped(late_text_x, "dp", 2)]
     late = call(
         functools.partial(late_kernel, len(image_inner), len(image_dp)),
         [shape((rows, tail_width), bf16)] * len(image_inner) + [shape(p.shape, bf16) for p in payloads_y],
@@ -373,22 +400,17 @@
         *moved_tails,
         *payloads_y,
         weight=weights["late"],
-        after=z_heads,
+        after=[late_text_z],
     )
     tail_parts = [swapped(part, "inner", q) for part, q in zip(late, image_inner)]
     y_parts = [swapped(part, "dp", p) for part, p in zip(late[len(image_inner) :], image_dp)]
     yz_heads = call(
-        late_heads_kernel, [shape(h.shape, bf16) for h in yz_heads], *yz_heads, weight=weights["far heads"], after=late[:1]
-    )
-    late_text_z, late_text_x = call(
-        functools.partial(late_kernel, 1, 1),
-        [block, block],
-        text_z_sums,
-        moved_text,
-        text_x_sums,
-        after=yz_heads,
-    )
-    text_parts = [swapped(late_text_z, "inner", 1), swapped(late_text_x, "dp", 2)]
+        late_heads_kernel,
+        [shape(h.shape, bf16) for h in yz_heads],
+        *yz_heads,
+        weight=weights["far heads"],
+        after=late[:1],
+    )
 
     head_parts = [*z_heads, *yz_heads, *y_parts]
     image_gradient, image_loss = call(
@@ -404,7 +426,7 @@
         weight=weights["end"],
         scratch=[pltpu.VMEM((rows, width), f32)],
     )
-    text_gradient = call(text_end_kernel, wide_block, scale, text, text_grad, *text_parts, scalars=1)
+    text_gradient = call(text_end_kernel, wide_block, scale, text, text_grad, *text_parts, scalars=1, weight=weights["text end"])
     return (image_gradient, text_gradient, image_loss.reshape(rows))
 
 

time: 63.1 us -> 63.1 us (level)
  starting transfers between devices: 19.2 us -> 26 us
  waiting for transfers between devices: 28.3 us -> 23.4 us
  local copies, waits for them, and re-layouts: 1.93 us -> 0.01 us
    ppermute x16, starting transfers between devices: 17.4 us -> 23.4 us  [swapped(): lax.ppermute(value, axis, [(place, place ^ step) for place in range(lax.a...]
    ppermute x16, waiting for transfers between devices: 28.2 us -> 23.4 us  [swapped(): lax.ppermute(value, axis, [(place, place ^ step) for place in range(lax.a...]
    unnamed x8 -> x4, local copies, waits for them, and re-layouts: 1.93 us -> 0.01 us
    ppermute x1, starting transfers between devices: 1.74 us -> 2.61 us  [swapped_both(): return lax.ppermute(value, ('dp', 'inner'), pairs)]
  transfers between devices with their start and end apart: 17 -> 17, of which waited for: 8 -> 9; matrix products, arithmetic and copies ran while one was open for 0% -> 0% of each run, Pallas kernels for 13% -> 13%
where the time goes in v6:
time: 63.1 us; the launch traced here: 63 us
  starting transfers between devices  26 us (41%)
  waiting for transfers between devices  23.4 us (37%)
  Pallas kernels  11.5 us (18%)
  between operations  2.08 us (3%)
    ppermute x16, waiting for transfers between devices, swapped(): lax.ppermute(value, axis, [(place, place ^ step) for place in range(lax.a...  23.4 us
    ppermute x16, starting transfers between devices, swapped(): lax.ppermute(value, axis, [(place, place ^ step) for place in range(lax.a...  23.4 us
    pallas_call x17, Pallas kernels, call(): pl.pallas_call(lambda *refs: kernel(*refs[:first], *refs[last:]), out_sha...  11.5 us
    ppermute x1, starting transfers between devices, swapped_both(): return lax.ppermute(value, ('dp', 'inner'), pairs)  2.61 us
  transfers between devices with their start and end apart: 17, of which 9 were waited for; matrix products, arithmetic and copies ran while one was open for 0% of the time, Pallas kernels for 13%

profile of v6, /device:TPU:0, one launch (start us, length us, event | category | flops | bytes accessed | tf_op | source)
XLA Modules:
  0.0 63.0 jit_solution(3978756045752823235)
XLA Ops:
  0.6 4.1 %collective-permute-start.1 = (bf16[128,1152]{1,0:T(8,128)(2,1)}, bf16[128,1152]{1,0:T(8,128)(2,1)S(1)}, u32[]{:S(2)}, u32[]{:S(2)}) collective-permute-start(bf16[128,1152]{1,0:T(8,128)(2,1)} %refs_1_.7), channel_id=1, source_target_pairs={{0,2},{1,3},{2,0},{3,1},{4,6},{5,7},{6,4},{7,5},{8,10},{9,11},{10,... | collective-permute-start | bytes 884744 | tf_op jit(solution)/shard_map/ppermute | solution.py:22
  4.8 1.6 %collective-permute-start = (bf16[128,1152]{1,0:T(8,128)(2,1)}, bf16[128,1152]{1,0:T(8,128)(2,1)S(1)}, u32[]{:S(2)}, u32[]{:S(2)}) collective-permute-start(bf16[128,1152]{1,0:T(8,128)(2,1)} %refs_1_.8), channel_id=1, source_target_pairs={{0,1},{1,0},{2,3},{3,2},{4,5},{5,4},{6,7},{7,6},{8,9},{9,8},{10,11... | collective-permute-start | bytes 884744 | tf_op jit(solution)/shard_map/ppermute | solution.py:22
  6.3 1.5 %collective-permute-start.3 = (bf16[128,1152]{1,0:T(8,128)(2,1)}, bf16[128,1152]{1,0:T(8,128)(2,1)S(1)}, u32[]{:S(2)}, u32[]{:S(2)}) collective-permute-start(bf16[128,1152]{1,0:T(8,128)(2,1)} %refs_1_.7), channel_id=1, source_target_pairs={{0,16},{4,20},{8,24},{12,28},{16,0},{20,4},{24,8},{28,12},{1,17},{... | collective-permute-start | bytes 884744 | tf_op jit(solution)/shard_map/ppermute | solution.py:22
  7.8 1.5 %collective-permute-start.2 = (bf16[128,1152]{1,0:T(8,128)(2,1)}, bf16[128,1152]{1,0:T(8,128)(2,1)S(1)}, u32[]{:S(2)}, u32[]{:S(2)}) collective-permute-start(bf16[128,1152]{1,0:T(8,128)(2,1)} %refs_1_.8), channel_id=1, source_target_pairs={{0,8},{4,12},{8,0},{12,4},{16,24},{20,28},{24,16},{28,20},{1,9},{5... | collective-permute-start | bytes 884744 | tf_op jit(solution)/shard_map/ppermute | solution.py:22
  9.3 9.1 %collective-permute-done.1.refs_1_ = bf16[128,1152]{1,0:T(8,128)(2,1)S(1)} collective-permute-done((bf16[128,1152]{1,0:T(8,128)(2,1)}, bf16[128,1152]{1,0:T(8,128)(2,1)S(1)}, u32[]{:S(2)}, u32[]{:S(2)}) %collective-permute-start.1) | collective-permute-done | bytes 294944 | tf_op jit(solution)/shard_map/ppermute | solution.py:22
  18.8 1.6 %collective-permute-start.5 = (bf16[128,1152]{1,0:T(8,128)(2,1)S(1)}, bf16[128,1152]{1,0:T(8,128)(2,1)S(1)}, u32[]{:S(2)}, u32[]{:S(2)}) collective-permute-start(bf16[128,1152]{1,0:T(8,128)(2,1)S(1)} %get-tuple-element.36.refs_0_), channel_id=1, source_target_pairs={{0,8},{4,12},{8,0},{12,4},{16,24},{20,28},{24,16},{28,20},{1,9},{5... | collective-permute-start | bytes 884744 | tf_op jit(solution)/shard_map/ppermute | solution.py:22
  21.9 1.6 %collective-permute-start.8 = (bf16[128,1152]{1,0:T(8,128)(2,1)S(1)}, bf16[128,1152]{1,0:T(8,128)(2,1)S(1)}, u32[]{:S(2)}, u32[]{:S(2)}) collective-permute-start(bf16[128,1152]{1,0:T(8,128)(2,1)S(1)} %get-tuple-element.39.refs_6_), channel_id=1, source_target_pairs={{0,16},{4,20},{8,24},{12,28},{16,0},{20,4},{24,8},{28,12},{1,17},{... | collective-permute-start | bytes 884744 | tf_op jit(solution)/shard_map/ppermute | solution.py:22
  23.9 2.9 %collective-permute-done.5.refs_3_.refs_4_ = bf16[128,1152]{1,0:T(8,128)(2,1)S(1)} collective-permute-done((bf16[128,1152]{1,0:T(8,128)(2,1)S(1)}, bf16[128,1152]{1,0:T(8,128)(2,1)S(1)}, u32[]{:S(2)}, u32[]{:S(2)}) %collective-permute-start.5) | collective-permute-done | bytes 294944 | tf_op jit(solution)/shard_map/ppermute | solution.py:22
  26.8 1.3 %shard_map.71 = (bf16[384,1152]{1,0:T(8,128)(2,1)S(1)}, bf16[512,384]{1,0:T(8,128)(2,1)S(1)}, f32[1,384]{1,0:T(1,128)S(1)}) custom-call(f32[1]{0:T(128)S(6)} %exp.3.refs_0_, f32[1]{0:T(128)S(6)} %copy.8.refs_1_, bf16[384,1152]{1,0:T(8,128)(2,1)S(1)} %shard_map.69.refs_2_.refs_3_, bf16[128,1152]{1,0:T(8,128)(2,1)S(1)} %collective-permute-done.5.refs_3_.refs_4_, ...), custom_call_target="tpu_custom_call" | custom-call | flops 10452984832 | bytes 3343880 | tf_op jit(solution)/shard_map/pallas_call | solution.py:39
  28.4 1.3 %shard_map.72 = (bf16[512,384]{1,0:T(8,128)(2,1)S(1)}, f32[1,384]{1,0:T(1,128)S(1)}) custom-call(f32[1]{0:T(128)S(6)} %exp.3.refs_0_, f32[1]{0:T(128)S(6)} %copy.8.refs_1_, bf16[384,1152]{1,0:T(8,128)(2,1)S(1)} %collective-permute-done.4.refs_2_.refs_5_.refs_4_, bf16[128,1152]{1,0:T(8,128)(2,1)S(1)} %collective-permute-done.6.refs_3_.refs_6_.refs_5_, ...), custom_call_target="tpu_custom_call" | custom-call | flops 452984832 | bytes 2460680 | tf_op jit(solution)/shard_map/pallas_call | solution.py:39
  29.7 1.8 %shard_map.73 = (f32[128,1152]{1,0:T(8,128)S(1)}, f32[1,128]{1,0:T(1,128)S(1)}, bf16[1168,128]{1,0:T(8,128)(2,1)S(1)}, bf16[528,128]{1,0:T(8,128)(2,1)S(1)}, f32[128,640]{1,0:T(8,128)S(1)}) custom-call(f32[1,384]{1,0:T(1,128)S(1)} %get-tuple-element.42.refs_0_, bf16[512,384]{1,0:T(8,128)(2,1)S(1)} %get-tuple-element.43.refs_1_, ...), custom_call_target="tpu_custom_call" | custom-call | flops 905969664 | bytes 4499456 | tf_op jit(solution)/shard_map/pallas_call | solution.py:39
  31.5 2.0 %shard_map.74 = (bf16[128,1152]{1,0:T(8,128)(2,1)S(1)}, bf16[512,128]{1,0:T(8,128)(2,1)S(1)}, bf16[512,128]{1,0:T(8,128)(2,1)S(1)}, f32[1,128]{1,0:T(1,128)S(1)}, bf16[512,1152]{1,0:T(8,128)(2,1)S(1)}) custom-call(f32[1]{0:T(128)S(6)} %exp.3.refs_0_, f32[1]{0:T(128)S(6)} %copy.8.refs_1_, bf16[384,1152]{1,0:T(8,128)(2,1)S(1)} %shard_map.69.refs_2_.refs_3_, ...), custom_call_target="tpu_custom_call" | custom-call | flops 905969664 | bytes 5669384 | tf_op jit(solution)/shard_map/pallas_call | solution.py:39
  33.8 1.4 %collective-permute-start.7 = (bf16[528,128]{1,0:T(8,128)(2,1)S(1)}, bf16[528,128]{1,0:T(8,128)(2,1)S(1)}, u32[]{:S(2)}, u32[]{:S(2)}) collective-permute-start(bf16[528,128]{1,0:T(8,128)(2,1)S(1)} %get-tuple-element.47), channel_id=1, source_target_pairs={{0,2},{1,3},{2,0},{3,1},{4,6},{5,7},{6,4},{7,5},{8,10},{9,11},{10,... | collective-permute-start | bytes 405512 | tf_op jit(solution)/shard_map/ppermute | solution.py:22
  36.4 1.2 %shard_map.76 = (f32[128,1152]{1,0:T(8,128)S(1)}, bf16[128,1152]{1,0:T(8,128)(2,1)S(1)}, f32[128,1152]{1,0:T(8,128)S(1)}, bf16[128,1152]{1,0:T(8,128)(2,1)S(1)}) custom-call(bf16[512,1152]{1,0:T(8,128)(2,1)S(1)} %collective-permute-done.9.refs_0_, bf16[512,384]{1,0:T(8,128)(2,1)S(1)} %get-tuple-element.43.refs_1_, ...), custom_call_target="tpu_custom_call" | custom-call | flops 603979776 | bytes 4653056 | tf_op jit(solution)/shard_map/pallas_call | solution.py:39
  37.6 1.3 %collective-permute-start.12 = (bf16[128,1152]{1,0:T(8,128)(2,1)S(1)}, bf16[128,1152]{1,0:T(8,128)(2,1)S(1)}, u32[]{:S(2)}, u32[]{:S(2)}) collective-permute-start(bf16[128,1152]{1,0:T(8,128)(2,1)S(1)} %get-tuple-element.61), channel_id=1, source_target_pairs={{0,8},{4,12},{8,0},{12,4},{16,24},{20,28},{24,16},{28,20},{1,9},{5... | collective-permute-start | bytes 884744 | tf_op jit(solution)/shard_map/ppermute | solution.py:22
  38.9 2.6 %collective-permute-start.10 = (bf16[528,128]{1,0:T(8,128)(2,1)S(1)}, bf16[528,128]{1,0:T(8,128)(2,1)S(1)}, u32[]{:S(2)}, u32[]{:S(2)}) collective-permute-start(bf16[528,128]{1,0:T(8,128)(2,1)S(1)} %get-tuple-element.56), channel_id=1, source_target_pairs={{0,18},{1,19},{2,16},{3,17},{4,22},{5,23},{6,20},{7,21},{8,26},{9,... | collective-permute-start | bytes 405512 | tf_op jit(solution)/shard_map/ppermute | solution.py:32
  42.0 1.3 %collective-permute-done.7.refs_0_ = bf16[528,128]{1,0:T(8,128)(2,1)S(1)} collective-permute-done((bf16[528,128]{1,0:T(8,128)(2,1)S(1)}, bf16[528,128]{1,0:T(8,128)(2,1)S(1)}, u32[]{:S(2)}, u32[]{:S(2)}) %collective-permute-start.7) | collective-permute-done | bytes 135200 | tf_op jit(solution)/shard_map/ppermute | solution.py:22
  43.3 3.5 %collective-permute-done.12.refs_1_ = bf16[128,1152]{1,0:T(8,128)(2,1)S(1)} collective-permute-done((bf16[128,1152]{1,0:T(8,128)(2,1)S(1)}, bf16[128,1152]{1,0:T(8,128)(2,1)S(1)}, u32[]{:S(2)}, u32[]{:S(2)}) %collective-permute-start.12) | collective-permute-done | bytes 294944 | tf_op jit(solution)/shard_map/ppermute | solution.py:22
  46.9 1.3 %collective-permute-start.16 = (bf16[128,1152]{1,0:T(8,128)(2,1)S(1)}, bf16[128,1152]{1,0:T(8,128)(2,1)S(1)}, u32[]{:S(2)}, u32[]{:S(2)}) collective-permute-start(bf16[128,1152]{1,0:T(8,128)(2,1)S(1)} %get-tuple-element.67), channel_id=1, source_target_pairs={{0,8},{4,12},{8,0},{12,4},{16,24},{20,28},{24,16},{28,20},{1,9},{5... | collective-permute-start | bytes 884744 | tf_op jit(solution)/shard_map/ppermute | solution.py:22
  48.2 3.0 %collective-permute-start.15 = (bf16[128,1152]{1,0:T(8,128)(2,1)S(1)}, bf16[128,1152]{1,0:T(8,128)(2,1)S(1)}, u32[]{:S(2)}, u32[]{:S(2)}) collective-permute-start(bf16[128,1152]{1,0:T(8,128)(2,1)S(1)} %get-tuple-element.62.refs_3_), channel_id=1, source_target_pairs={{0,1},{1,0},{2,3},{3,2},{4,5},{5,4},{6,7},{7,6},{8,9},{9,8},{10,11... | collective-permute-start | bytes 884744 | tf_op jit(solution)/shard_map/ppermute | solution.py:22
  51.2 2.2 %collective-permute-start.14 = (bf16[128,640]{1,0:T(8,128)(2,1)S(1)}, bf16[128,640]{1,0:T(8,128)(2,1)S(1)}, u32[]{:S(2)}, u32[]{:S(2)}) collective-permute-start(bf16[128,640]{1,0:T(8,128)(2,1)S(1)} %get-tuple-element.63.refs_1_), channel_id=1, source_target_pairs={{0,2},{1,3},{2,0},{3,1},{4,6},{5,7},{6,4},{7,5},{8,10},{9,11},{10,... | collective-permute-start | bytes 491528 | tf_op jit(solution)/shard_map/ppermute | solution.py:22
  53.4 1.5 %collective-permute-start.13 = (bf16[1168,128]{1,0:T(8,128)(2,1)S(1)}, bf16[1168,128]{1,0:T(8,128)(2,1)S(1)}, u32[]{:S(2)}, u32[]{:S(2)}) collective-permute-start(bf16[1168,128]{1,0:T(8,128)(2,1)S(1)} %get-tuple-element.64), channel_id=1, source_target_pairs={{0,16},{4,20},{8,24},{12,28},{16,0},{20,4},{24,8},{28,12},{1,17},{... | collective-permute-start | bytes 897032 | tf_op jit(solution)/shard_map/ppermute | solution.py:22
  55.3 5.4 %collective-permute-done.15.refs_3_ = bf16[128,1152]{1,0:T(8,128)(2,1)S(1)} collective-permute-done((bf16[128,1152]{1,0:T(8,128)(2,1)S(1)}, bf16[128,1152]{1,0:T(8,128)(2,1)S(1)}, u32[]{:S(2)}, u32[]{:S(2)}) %collective-permute-start.15) | collective-permute-done | bytes 294944 | tf_op jit(solution)/shard_map/ppermute | solution.py:22
  61.8 1.2 %shard_map.82 = (f32[128,1152]{1,0:T(8,128)}, f32[1,128]{1,0:T(1,128)}) custom-call(f32[1]{0:T(128)S(6)} %exp.3.refs_0_, bf16[128,1152]{1,0:T(8,128)(2,1)S(1)} %copy-done, f32[128,1152]{1,0:T(8,128)S(1)} %get-tuple-element.45.refs_9_.refs_2_, f32[1,128]{1,0:T(1,128)S(1)} %get-tuple-element.46.refs_3_, bf16[528,128]{1,0:T(8,128)(2,1)S(1)} %shard_map.77.refs_3_.refs_4_, ...), custom_call_target="tpu_custom_call" | custom-call | bytes 2208772 | tf_op jit(solution)/shard_map/pallas_call | solution.py:39
  (31 shorter events, 5.0 us)
Async XLA Ops:
  0.6 19.8 %copy-start = (bf16[128,1152]{1,0:T(8,128)(2,1)S(1)}, bf16[128,1152]{1,0:T(8,128)(2,1)}, u32[]{:S(2)}) copy-start(bf16[128,1152]{1,0:T(8,128)(2,1)} %refs_1_.7) | copy-start | bytes 884740
  0.6 19.8 %copy-start.1 = (bf16[128,1152]{1,0:T(8,128)(2,1)S(1)}, bf16[128,1152]{1,0:T(8,128)(2,1)}, u32[]{:S(2)}) copy-start(bf16[128,1152]{1,0:T(8,128)(2,1)} %refs_1_.8) | copy-start | bytes 884740
  0.6 17.7 %collective-permute-start.1 = (bf16[128,1152]{1,0:T(8,128)(2,1)}, bf16[128,1152]{1,0:T(8,128)(2,1)S(1)}, u32[]{:S(2)}, u32[]{:S(2)}) collective-permute-start(bf16[128,1152]{1,0:T(8,128)(2,1)} %refs_1_.7), channel_id=1, source_target_pairs={{0,2},{1,3},{2,0},{3,1},{4,6},{5,7},{6,4},{7,5},{8,10},{9,11},{10,... | collective-permute-start | bytes 884744 | tf_op jit(solution)/shard_map/ppermute | solution.py:22
  4.8 13.8 %collective-permute-start = (bf16[128,1152]{1,0:T(8,128)(2,1)}, bf16[128,1152]{1,0:T(8,128)(2,1)S(1)}, u32[]{:S(2)}, u32[]{:S(2)}) collective-permute-start(bf16[128,1152]{1,0:T(8,128)(2,1)} %refs_1_.8), channel_id=1, source_target_pairs={{0,1},{1,0},{2,3},{3,2},{4,5},{5,4},{6,7},{7,6},{8,9},{9,8},{10,11... | collective-permute-start | bytes 884744 | tf_op jit(solution)/shard_map/ppermute | solution.py:22
  6.3 17.2 %collective-permute-start.3 = (bf16[128,1152]{1,0:T(8,128)(2,1)}, bf16[128,1152]{1,0:T(8,128)(2,1)S(1)}, u32[]{:S(2)}, u32[]{:S(2)}) collective-permute-start(bf16[128,1152]{1,0:T(8,128)(2,1)} %refs_1_.7), channel_id=1, source_target_pairs={{0,16},{4,20},{8,24},{12,28},{16,0},{20,4},{24,8},{28,12},{1,17},{... | collective-permute-start | bytes 884744 | tf_op jit(solution)/shard_map/ppermute | solution.py:22
  7.8 15.7 %collective-permute-start.2 = (bf16[128,1152]{1,0:T(8,128)(2,1)}, bf16[128,1152]{1,0:T(8,128)(2,1)S(1)}, u32[]{:S(2)}, u32[]{:S(2)}) collective-permute-start(bf16[128,1152]{1,0:T(8,128)(2,1)} %refs_1_.8), channel_id=1, source_target_pairs={{0,8},{4,12},{8,0},{12,4},{16,24},{20,28},{24,16},{28,20},{1,9},{5... | collective-permute-start | bytes 884744 | tf_op jit(solution)/shard_map/ppermute | solution.py:22
  18.8 8.0 %collective-permute-start.5 = (bf16[128,1152]{1,0:T(8,128)(2,1)S(1)}, bf16[128,1152]{1,0:T(8,128)(2,1)S(1)}, u32[]{:S(2)}, u32[]{:S(2)}) collective-permute-start(bf16[128,1152]{1,0:T(8,128)(2,1)S(1)} %get-tuple-element.36.refs_0_), channel_id=1, source_target_pairs={{0,8},{4,12},{8,0},{12,4},{16,24},{20,28},{24,16},{28,20},{1,9},{5... | collective-permute-start | bytes 884744 | tf_op jit(solution)/shard_map/ppermute | solution.py:22
  21.9 9.5 %collective-permute-start.8 = (bf16[128,1152]{1,0:T(8,128)(2,1)S(1)}, bf16[128,1152]{1,0:T(8,128)(2,1)S(1)}, u32[]{:S(2)}, u32[]{:S(2)}) collective-permute-start(bf16[128,1152]{1,0:T(8,128)(2,1)S(1)} %get-tuple-element.39.refs_6_), channel_id=1, source_target_pairs={{0,16},{4,20},{8,24},{12,28},{16,0},{20,4},{24,8},{28,12},{1,17},{... | collective-permute-start | bytes 884744 | tf_op jit(solution)/shard_map/ppermute | solution.py:22
  23.7 4.7 %collective-permute-start.4 = (bf16[384,1152]{1,0:T(8,128)(2,1)S(1)}, bf16[384,1152]{1,0:T(8,128)(2,1)S(1)}, u32[]{:S(2)}, u32[]{:S(2)}) collective-permute-start(bf16[384,1152]{1,0:T(8,128)(2,1)S(1)} %shard_map.69.refs_2_.refs_3_), channel_id=1, source_target_pairs={{0,4},{4,0},{8,12},{12,8},{16,20},{20,16},{24,28},{28,24},{1,5},{5... | collective-permute-start | bytes 2654216 | tf_op jit(solution)/shard_map/ppermute | solution.py:22
  26.8 1.6 %collective-permute-start.6 = (bf16[128,1152]{1,0:T(8,128)(2,1)S(1)}, bf16[128,1152]{1,0:T(8,128)(2,1)S(1)}, u32[]{:S(2)}, u32[]{:S(2)}) collective-permute-start(bf16[128,1152]{1,0:T(8,128)(2,1)S(1)} %collective-permute-done.5.refs_3_.refs_4_), channel_id=1, source_target_pairs={{0,4},{4,0},{8,12},{12,8},{16,20},{20,16},{24,28},{28,24},{1,5},{5... | collective-permute-start | bytes 884744 | tf_op jit(solution)/shard_map/ppermute | solution.py:22
  33.5 2.9 %collective-permute-start.9 = (bf16[512,1152]{1,0:T(8,128)(2,1)S(1)}, bf16[512,1152]{1,0:T(8,128)(2,1)S(1)}, u32[]{:S(2)}, u32[]{:S(2)}) collective-permute-start(bf16[512,1152]{1,0:T(8,128)(2,1)S(1)} %get-tuple-element.48), channel_id=1, source_target_pairs={{0,4},{4,0},{8,12},{12,8},{16,20},{20,16},{24,28},{28,24},{1,5},{5... | collective-permute-start | bytes 3538952 | tf_op jit(solution)/shard_map/ppermute | solution.py:22
  33.8 9.5 %collective-permute-start.7 = (bf16[528,128]{1,0:T(8,128)(2,1)S(1)}, bf16[528,128]{1,0:T(8,128)(2,1)S(1)}, u32[]{:S(2)}, u32[]{:S(2)}) collective-permute-start(bf16[528,128]{1,0:T(8,128)(2,1)S(1)} %get-tuple-element.47), channel_id=1, source_target_pairs={{0,2},{1,3},{2,0},{3,1},{4,6},{5,7},{6,4},{7,5},{8,10},{9,11},{10,... | collective-permute-start | bytes 405512 | tf_op jit(solution)/shard_map/ppermute | solution.py:22
  37.6 9.2 %collective-permute-start.12 = (bf16[128,1152]{1,0:T(8,128)(2,1)S(1)}, bf16[128,1152]{1,0:T(8,128)(2,1)S(1)}, u32[]{:S(2)}, u32[]{:S(2)}) collective-permute-start(bf16[128,1152]{1,0:T(8,128)(2,1)S(1)} %get-tuple-element.61), channel_id=1, source_target_pairs={{0,8},{4,12},{8,0},{12,4},{16,24},{20,28},{24,16},{28,20},{1,9},{5... | collective-permute-start | bytes 884744 | tf_op jit(solution)/shard_map/ppermute | solution.py:22
  38.9 16.0 %collective-permute-start.10 = (bf16[528,128]{1,0:T(8,128)(2,1)S(1)}, bf16[528,128]{1,0:T(8,128)(2,1)S(1)}, u32[]{:S(2)}, u32[]{:S(2)}) collective-permute-start(bf16[528,128]{1,0:T(8,128)(2,1)S(1)} %get-tuple-element.56), channel_id=1, source_target_pairs={{0,18},{1,19},{2,16},{3,17},{4,22},{5,23},{6,20},{7,21},{8,26},{9,... | collective-permute-start | bytes 405512 | tf_op jit(solution)/shard_map/ppermute | solution.py:32
  41.5 9.6 %collective-permute-start.11 = (bf16[128,640]{1,0:T(8,128)(2,1)S(1)}, bf16[128,640]{1,0:T(8,128)(2,1)S(1)}, u32[]{:S(2)}, u32[]{:S(2)}) collective-permute-start(bf16[128,640]{1,0:T(8,128)(2,1)S(1)} %get-tuple-element.58), channel_id=1, source_target_pairs={{0,16},{4,20},{8,24},{12,28},{16,0},{20,4},{24,8},{28,12},{1,17},{... | collective-permute-start | bytes 491528 | tf_op jit(solution)/shard_map/ppermute | solution.py:22
  46.9 8.4 %collective-permute-start.16 = (bf16[128,1152]{1,0:T(8,128)(2,1)S(1)}, bf16[128,1152]{1,0:T(8,128)(2,1)S(1)}, u32[]{:S(2)}, u32[]{:S(2)}) collective-permute-start(bf16[128,1152]{1,0:T(8,128)(2,1)S(1)} %get-tuple-element.67), channel_id=1, source_target_pairs={{0,8},{4,12},{8,0},{12,4},{16,24},{20,28},{24,16},{28,20},{1,9},{5... | collective-permute-start | bytes 884744 | tf_op jit(solution)/shard_map/ppermute | solution.py:22
  48.2 12.5 %collective-permute-start.15 = (bf16[128,1152]{1,0:T(8,128)(2,1)S(1)}, bf16[128,1152]{1,0:T(8,128)(2,1)S(1)}, u32[]{:S(2)}, u32[]{:S(2)}) collective-permute-start(bf16[128,1152]{1,0:T(8,128)(2,1)S(1)} %get-tuple-element.62.refs_3_), channel_id=1, source_target_pairs={{0,1},{1,0},{2,3},{3,2},{4,5},{5,4},{6,7},{7,6},{8,9},{9,8},{10,11... | collective-permute-start | bytes 884744 | tf_op jit(solution)/shard_map/ppermute | solution.py:22
  51.2 10.6 %collective-permute-start.14 = (bf16[128,640]{1,0:T(8,128)(2,1)S(1)}, bf16[128,640]{1,0:T(8,128)(2,1)S(1)}, u32[]{:S(2)}, u32[]{:S(2)}) collective-permute-start(bf16[128,640]{1,0:T(8,128)(2,1)S(1)} %get-tuple-element.63.refs_1_), channel_id=1, source_target_pairs={{0,2},{1,3},{2,0},{3,1},{4,6},{5,7},{6,4},{7,5},{8,10},{9,11},{10,... | collective-permute-start | bytes 491528 | tf_op jit(solution)/shard_map/ppermute | solution.py:22
  53.4 8.4 %collective-permute-start.13 = (bf16[1168,128]{1,0:T(8,128)(2,1)S(1)}, bf16[1168,128]{1,0:T(8,128)(2,1)S(1)}, u32[]{:S(2)}, u32[]{:S(2)}) collective-permute-start(bf16[1168,128]{1,0:T(8,128)(2,1)S(1)} %get-tuple-element.64), channel_id=1, source_target_pairs={{0,16},{4,20},{8,24},{12,28},{16,0},{20,4},{24,8},{28,12},{1,17},{... | collective-permute-start | bytes 897032 | tf_op jit(solution)/shard_map/ppermute | solution.py:22

commit v7 on v0

v7 whole, which is shorter than its diff:
```python
import functools

import jax
import jax.numpy as jnp
from jax import lax
from jax.experimental import pallas as pl
from jax.experimental.pallas import tpu as pltpu
from jax.sharding import PartitionSpec as P

epsilon = 1e-06
f32, bf16 = jnp.float32, jnp.bfloat16
lanes = 128
extra = 16
weights = {"z": 10, "late": 2, "text": 2, "end": 0, "text end": 0}
VMEM = pl.BlockSpec(memory_space=pltpu.VMEM)
SMEM = pl.BlockSpec(memory_space=pltpu.SMEM)
ANY = pl.BlockSpec(memory_space=pl.ANY)


def swapped(value, axis, step):
    return lax.ppermute(value, axis, [(place, place ^ step) for place in range(lax.axis_size(axis))])


def call(kernel, out_shape, *operands, flops=0, weight=0, scalars=0, scratch=(), after=()):
    moved = sum(o.size * o.dtype.itemsize for o in operands)
    moved += sum(o.size * o.dtype.itemsize for o in jax.tree.leaves(out_shape))
    first, last = len(operands), len(operands) + len(after)
    return pl.pallas_call(
        lambda *refs: kernel(*refs[:first], *refs[last:]),
        out_shape=out_shape,
        in_specs=[SMEM] * scalars + [VMEM] * (len(operands) - scalars) + [ANY] * len(after),
        out_specs=jax.tree.map(lambda _: VMEM, out_shape),
        scratch_shapes=scratch,
        compiler_params=pltpu.CompilerParams(vmem_limit_bytes=40 * 1024 * 1024),
        cost_estimate=pl.CostEstimate(
            flops=flops + int(weight * 1e9), bytes_accessed=moved, transcendentals=0
        ),
    )(*operands, *after)


def shape(dims, kind):
    return jax.ShapeDtypeStruct(dims, kind)


def unit_of(rows):
    wide = rows.astype(f32)
    inverse = lax.rsqrt(jnp.sum(wide * wide, axis=-1, keepdims=True) + epsilon)
    return wide * inverse, inverse


def pair_terms(scale, offset, text_refs, image_refs, slopes_ref, own=0, losses=True):
    step = 256
    totals, left = [], 0
    for image_rows in image_refs:
        for at in range(0, image_rows.shape[0], step):
            images = image_rows[at : min(at + step, image_rows.shape[0]), :]
            count = images.shape[0]
            total, done = jnp.zeros((1, count), f32), 0
            for texts in text_refs:
                for start in range(0, texts.shape[0], step):
                    chunk = texts[start : min(start + step, texts.shape[0]), :]
                    logits = (
                        scale
                        * lax.dot_general(
                            chunk, images, (((1,), (1,)), ((), ())), preferred_element_type=f32
                        )
                        + offset
                    )
                    shrunk = jnp.exp(-jnp.abs(logits))
                    raised = 1.0 + shrunk
                    inverse = pl.reciprocal(raised, approx=True)
                    inverse = inverse * (2.0 - raised * inverse)
                    sigmoid = jnp.where(logits >= 0.0, inverse, shrunk * inverse)
                    match = None
                    if own and done == 0 and left == 0:
                        text_ids = lax.broadcasted_iota(jnp.int32, logits.shape, 0)
                        image_ids = lax.broadcasted_iota(jnp.int32, logits.shape, 1)
                        match = ((text_ids == image_ids) & (text_ids < own)).astype(f32)
                        sigmoid = sigmoid - match
                    slopes_ref[done : done + chunk.shape[0], left : left + count] = sigmoid.astype(bf16)
                    if losses:
                        log_raised = jnp.log(raised) + (shrunk - (raised - 1.0)) * inverse
                        softplus = jnp.maximum(logits, 0.0) + log_raised
                        if match is not None:
                            softplus = softplus - match * logits
                        total = total + jnp.sum(softplus, axis=0, keepdims=True)
                    done += chunk.shape[0]
            totals.append(total)
            left += count
    return jnp.concatenate(totals, axis=1)


def unit_kernel(*refs):
    for raw, emb in zip(refs[: len(refs) // 2], refs[len(refs) // 2 :]):
        emb[...] = unit_of(raw[...])[0].astype(bf16)


def copies_kernel(*refs):
    for source, target in zip(refs[: len(refs) // 2], refs[len(refs) // 2 :]):
        target[...] = source[...]


def near_kernel(held, *refs):
    out_ref, rows = refs[-1], refs[0].shape[0]
    for place, block in enumerate(refs[:-1]):
        emb = block[...] if place in held else unit_of(block[...])[0].astype(bf16)
        out_ref[place * rows : (place + 1) * rows, :] = emb


def near_pairs_kernel(own, scale_ref, bias_ref, near_ref, far_ref, images_ref, *refs):
    slopes_ref, loss_ref = refs[-2:]
    rows = far_ref.shape[0]
    texts = (near_ref.at[: 3 * rows, :], far_ref)
    loss = pair_terms(
        scale_ref[0], bias_ref[0], texts, (images_ref.at[3 * rows :, :],), slopes_ref, rows if own else 0
    )
    loss_ref[...] = loss if own else loss + refs[0][...]


def loss_rows(loss):
    high = loss.astype(bf16).astype(f32)
    which = lax.broadcasted_iota(jnp.int32, (extra, loss.shape[1]), 0)
    return jnp.where(which == 0, high, loss - high).astype(bf16)


def sums_in_parts(slope_refs, text_refs, width):
    step = 3 * lanes
    for left in range(0, width, step):
        total = None
        for slopes, texts in zip(slope_refs, text_refs):
            done = 0
            for block in texts:
                part = lax.dot_general(
                    slopes[done : done + block.shape[0], :],
                    block[:, left : left + step],
                    (((0,), (0,)), ((), ())),
                    preferred_element_type=f32,
                )
                total, done = part if total is None else total + part, done + block.shape[0]
        yield left, step, total


def put_panels(out, rows, left, sums):
    for at in range(0, sums.shape[1], lanes):
        panel = (left + at) // lanes
        out[panel * rows : (panel + 1) * rows, :] = sums[:, at : at + lanes].astype(out.dtype)


def far_kernel(count, scale_ref, bias_ref, near_ref, far_ref, near_swapped_ref, far_swapped_ref, *refs):
    image_refs, (own_slopes_ref, *sent_refs), other_slopes_ref = refs[:count], refs[count:-1], refs[-1]
    rows, width = far_ref.shape
    scale, offset = scale_ref[0], bias_ref[0]
    own_texts = (near_ref.at[: 3 * rows, :], far_ref)
    other_texts = (near_swapped_ref.at[: 3 * rows, :], far_swapped_ref)
    loss = pair_terms(scale, offset, own_texts, image_refs, own_slopes_ref)
    loss = loss + pair_terms(scale, offset, other_texts, image_refs, other_slopes_ref)
    slopes = (own_slopes_ref, other_slopes_ref)
    for left, step, total in sums_in_parts(slopes, (own_texts, other_texts), width):
        for place, out in enumerate(sent_refs):
            put_panels(out, rows, left, total[place * rows : (place + 1) * rows, :])
    for place, out in enumerate(sent_refs):
        out[width // lanes * rows :, :] = loss_rows(loss[:, place * rows : (place + 1) * rows])


def near_sums_kernel(
    plain, own_slopes_ref, other_slopes_ref, near_ref, far_ref, near_swapped_ref, far_swapped_ref, loss_ref, *refs
):
    own_ref, own_loss_ref, plain_refs, rest = refs[0], refs[1], refs[2 : 2 + plain], refs[2 + plain :]
    z_refs, z_loss_refs = rest[::2], rest[1::2]
    rows, width = far_ref.shape
    own_texts = (near_ref.at[: 3 * rows, :], far_ref)
    other_texts = (near_swapped_ref.at[: 3 * rows, :], far_swapped_ref)
    slopes = (own_slopes_ref, other_slopes_ref)
    for left, step, total in sums_in_parts(slopes, (own_texts, other_texts), width):
        own_ref[:, left : left + step] = total[:rows, :]
        for place, out in enumerate((*plain_refs, *z_refs), 1):
            put_panels(out, rows, left, total[place * rows : (place + 1) * rows, :])
    own_loss_ref[...] = loss_ref[:, :rows]
    for place, out in enumerate(plain_refs, 1):
        out[width // lanes * rows :, :] = loss_rows(loss_ref[:, place * rows : (place + 1) * rows])
    for place, out in enumerate(z_loss_refs, 1 + plain):
        out[...] = loss_ref[:, place * rows : (place + 1) * rows]


def text_kernel(
    count, scale_ref, bias_ref, near_ref, far_ref, near_swapped_ref, near_slopes_ref, far_slopes_ref, *refs
):
    far_refs, far_swapped_refs, outs, slopes_ref = refs[:count], refs[count : 2 * count], refs[2 * count : -1], refs[-1]
    rows, width = far_ref.shape
    own_texts = (near_ref.at[: 3 * rows, :], far_ref)
    swapped_images = (near_swapped_ref.at[3 * rows :, :], *far_swapped_refs)
    pair_terms(scale_ref[0], bias_ref[0], own_texts, swapped_images, slopes_ref, losses=False)
    terms, left = [], near_slopes_ref.shape[1]
    for slopes, blocks in (
        (near_slopes_ref, (near_ref.at[3 * rows :, :],)),
        (far_slopes_ref, far_refs),
        (slopes_ref, swapped_images),
    ):
        left = 0
        for images in blocks:
            terms.append((slopes.at[:, left : left + images.shape[0]], images))
            left += images.shape[0]
    step = 3 * lanes
    for left in range(0, width, step):
        total = None
        for slopes, images in terms:
            part = jnp.dot(slopes[...], images[:, left : left + step], preferred_element_type=f32)
            total = part if total is None else total + part
        for k, out in enumerate(outs):
            out[:, left : left + step] = total[k * rows : (k + 1) * rows, :].astype(out.dtype)


def late_image_kernel(zs, ys, *refs):
    sums, losses, refs = refs[:zs], refs[zs : 2 * zs], refs[2 * zs :]
    parts, payloads, outs = refs[: zs * ys], refs[zs * ys : zs * ys + ys], refs[zs * ys + ys :]
    for k in range(zs):
        height = sums[k].shape[0]
        total, loss = sums[k][...], losses[k][...]
        for part in parts[k * ys : (k + 1) * ys]:
            total = total + part[:height, :].astype(f32)
            last = part[height:, :].astype(f32)
            loss = loss + (last[0:1, :] + last[1:2, :])
        outs[k][:height, :] = total.astype(bf16)
        outs[k][height:, :] = loss_rows(loss)
    for source, target in zip(payloads, outs[zs:]):
        target[...] = source[...]


def late_text_kernel(sums_ref, part_ref, passed_ref, out_ref, passed_out_ref):
    out_ref[...] = (sums_ref[...] + part_ref[...].astype(f32)).astype(bf16)
    passed_out_ref[...] = passed_ref[...]


def row_gradient(rows, sums, scale, out_ref):
    unit_rows, inverse = unit_of(rows)
    unit_grad = scale * sums
    out_ref[...] = (
        unit_grad - unit_rows * jnp.sum(unit_rows * unit_grad, axis=-1, keepdims=True)
    ) * inverse


def image_end_kernel(batch, scale_ref, image_ref, grad_ref, loss_ref, *refs):
    parts, (out_ref, out_loss_ref, sums_ref) = refs[:-3], refs[-3:]
    rows, width = image_ref.shape
    loss = loss_ref[...]
    for panel in range(width // lanes):
        cut = slice(panel * lanes, (panel + 1) * lanes)
        sums = grad_ref[:, cut]
        for part in parts:
            sums = sums + part[panel * rows : (panel + 1) * rows, :].astype(f32)
        sums_ref[:, cut] = sums
    for part in parts:
        last = part[width // lanes * rows :, :].astype(f32)
        loss = loss + (last[0:1, :] + last[1:2, :])
    row_gradient(image_ref[...], sums_ref[...], scale_ref[0], out_ref)
    out_loss_ref[...] = loss / batch


def text_end_kernel(scale_ref, text_ref, grad_ref, *refs):
    sums = grad_ref[...]
    for r in refs[:-1]:
        sums = sums + r[...].astype(f32)
    row_gradient(text_ref[...], sums, scale_ref[0], refs[-1])


def body(image, text, logarithm_scale, bias):
    rows, width = image.shape
    dp_count, inner_count = lax.axis_size("dp"), lax.axis_size("inner")
    batch = rows * dp_count * inner_count
    scale = jnp.exp(logarithm_scale)
    block = shape((rows, width), bf16)
    wide_block = shape((rows, width), f32)

    image_dp, image_inner = range(4, dp_count, 4), range(2, inner_count, 2)

    images_y = [swapped(image, "dp", p) for p in image_dp]
    text_x = swapped(text, "dp", 2)
    images_z = [swapped(image, "inner", q) for q in image_inner]
    text_z = swapped(text, "inner", 1)
    text_emb, image_emb = call(unit_kernel, [block, block], text, image)
    text_z_emb, *embs_z = call(
        unit_kernel, [block] * (1 + len(images_z)), text_z, *images_z, weight=weights["z"], after=[text_emb]
    )
    far_text = swapped(text_z_emb, "dp", 2)
    far = [swapped(emb, "dp", p) for emb in embs_z for p in image_dp]
    far_places = [(p, q) for q in image_inner for p in image_dp]
    zs, ys = len(embs_z), len(images_y)

    held = {0, 2, 3, *range(4 + ys, 4 + ys + zs)}
    near = call(
        functools.partial(near_kernel, frozenset(held)),
        shape(((4 + ys + zs) * rows, width), bf16),
        text_emb,
        text_x,
        text_z_emb,
        image_emb,
        *images_y,
        *embs_z,
    )
    near_swapped = swapped(near, "dp", 1)
    far_text_swapped = swapped(far_text, "dp", 1)

    half, near_rows, far_rows = 4 * rows, (1 + ys + zs) * rows, len(far) * rows
    own_texts, other_texts = (near, far_text), (near_swapped, far_text_swapped)
    pair_flops = 2 * rows * half * width
    near_slopes, near_loss = shape((half, near_rows), bf16), shape((1, near_rows), f32)
    payload = shape((width // lanes * rows + extra, lanes), bf16)
    own_slopes, loss = call(
        functools.partial(near_pairs_kernel, True),
        (near_slopes, near_loss),
        scale,
        bias,
        *own_texts,
        near,
        flops=pair_flops * (1 + ys + zs),
        scalars=2,
    )
    passed = call(copies_kernel, [block] * len(far), *far, after=[loss])
    far_swapped = [swapped(emb, "dp", 1) for emb in passed]
    other_slopes, loss = call(
        functools.partial(near_pairs_kernel, False),
        (near_slopes, near_loss),
        scale,
        bias,
        *other_texts,
        near,
        loss,
        flops=pair_flops * (1 + ys + zs),
        scalars=2,
    )
    far_slopes, *far_sent = call(
        functools.partial(far_kernel, len(far)),
        [shape((half, far_rows), bf16)] + [payload] * len(far),
        scale,
        bias,
        *own_texts,
        *other_texts,
        *far,
        flops=4 * pair_flops * len(far),
        scalars=2,
        scratch=[pltpu.VMEM((half, far_rows), bf16)],
        after=[loss],
    )
    moved = [swapped(part, "dp", p) for part, (p, q) in zip(far_sent, far_places)]
    text_grad, text_x_sums, text_z_sums, text_xz_sums = call(
        functools.partial(text_kernel, len(far)),
        (wide_block, block, wide_block, block),
        scale,
        bias,
        *own_texts,
        near_swapped,
        own_slopes,
        far_slopes,
        *far,
        *far_swapped,
        flops=3 * pair_flops * (1 + ys + zs + len(far)),
        scalars=2,
        scratch=[pltpu.VMEM((half, near_rows + far_rows), bf16)],
        after=far_sent[:1],
    )
    moved_text = swapped(text_xz_sums, "dp", 2)
    image_grad, own_loss, *sums = call(
        functools.partial(near_sums_kernel, ys),
        [wide_block, shape((1, rows), f32)]
        + [payload] * ys
        + [shape((width // lanes * rows, lanes), f32), shape((1, rows), f32)] * zs,
        own_slopes,
        other_slopes,
        *own_texts,
        *other_texts,
        loss,
        flops=2 * pair_flops * (1 + ys + zs),
        after=[text_x_sums],
    )

    late = call(
        functools.partial(late_image_kernel, zs, ys),
        [payload] * (zs + ys),
        *sums[ys::2],
        *sums[ys + 1 :: 2],
        *moved,
        *sums[:ys],
        weight=weights["late"],
    )
    image_parts = [swapped(part, "inner", q) for part, q in zip(late, image_inner)]
    image_parts += [swapped(part, "dp", p) for part, p in zip(late[zs:], image_dp)]
    late_text_z, late_text_x = call(
        late_text_kernel,
        [block, block],
        text_z_sums,
        moved_text,
        text_x_sums,
        weight=weights["text"],
        after=late[:1],
    )
    text_parts = [swapped(late_text_z, "inner", 1), swapped(late_text_x, "dp", 2)]

    image_gradient, image_loss = call(
        functools.partial(image_end_kernel, batch),
        (wide_block, shape((1, rows), f32)),
        scale,
        image,
        image_grad,
        own_loss,
        *image_parts,
        scalars=1,
        weight=weights["end"],
        scratch=[pltpu.VMEM((rows, width), f32)],
    )
    text_gradient = call(
        text_end_kernel, wide_block, scale, text, text_grad, *text_parts, scalars=1, weight=weights["text end"]
    )
    return (image_gradient, text_gradient, image_loss.reshape(rows))


def solution(mesh):
    return jax.shard_map(
        body,
        mesh=mesh,
        in_specs=(P(("dp", "inner"), None), P(("dp", "inner"), None), P(), P()),
        out_specs=(P(("dp", "inner"), None), P(("dp", "inner"), None), P(("dp", "inner"))),
        check_vma=False,
    )
```

time: 210 us -> 64.4 us (0.31)
  waiting for transfers between devices: 128 us -> 26.1 us
  matrix products: 36.6 us -> 0 us
  starting transfers between devices: 2.42 us -> 21.6 us
  between operations: 16.1 us -> 2.09 us
  Pallas kernels: 0 us -> 12.5 us
  blocking collectives: 10.1 us -> 0 us
  other arithmetic: 8.34 us -> 0 us
  local copies, waits for them, and re-layouts: 7.09 us -> 1.97 us
    ppermute x15, waiting for transfers between devices: 64.3 us -> 26.1 us  [swapped(): lax.ppermute(value, axis, [(place, place ^ step) for place in range(lax.a...]
    dot_general x24 -> x0, matrix products: 36.6 us -> none  [the longest x8 20.2 us: block_terms(): lax.dot_general(images, block, (((1,), (1,)), ((), ())), preferred_elemen...]
    reduce_scatter x1 -> x0, waiting for transfers between devices: 33 us -> none  [body(): lax.psum_scatter(image_total, 'inner', scatter_dimension=0, tiled=True)]
    all_gather x1 -> x0, waiting for transfers between devices: 30.9 us -> none  [body(): images = lax.all_gather(image_emb, 'inner', axis=0, tiled=True)]
    ppermute x15, starting transfers between devices: 2.34 us -> 21.6 us  [swapped(): lax.ppermute(value, axis, [(place, place ^ step) for place in range(lax.a...]
    pallas_call x0 -> x13, Pallas kernels: none -> 12.5 us  [call(): pl.pallas_call(lambda *refs: kernel(*refs[:first], *refs[last:]), out_sha...]
    unnamed x1 -> x0, blocking collectives: 10.1 us -> none
    while x21 -> x0, local copies, waits for them, and re-layouts: 5.04 us -> none
  transfers between devices with their start and end apart: 17 -> 15, of which waited for: 16 -> 6; matrix products, arithmetic and copies ran while one was open for 15% -> 0% of each run, Pallas kernels for 0% -> 17%
where the time goes in v7:
time: 64.4 us; the launch traced here: 64.2 us
  waiting for transfers between devices  26.1 us (41%)
  starting transfers between devices  21.6 us (34%)
  Pallas kernels  12.5 us (19%)
  between operations  2.09 us (3%)
  local copies, waits for them, and re-layouts  1.97 us (3%)
    ppermute x15, waiting for transfers between devices, swapped(): lax.ppermute(value, axis, [(place, place ^ step) for place in range(lax.a...  26.1 us
    ppermute x15, starting transfers between devices, swapped(): lax.ppermute(value, axis, [(place, place ^ step) for place in range(lax.a...  21.6 us
    pallas_call x13, Pallas kernels, call(): pl.pallas_call(lambda *refs: kernel(*refs[:first], *refs[last:]), out_sha...  12.5 us
    unnamed x8, local copies, waits for them, and re-layouts  1.97 us
  transfers between devices with their start and end apart: 15, of which 6 were waited for; matrix products, arithmetic and copies ran while one was open for 0% of the time, Pallas kernels for 17%

profile of v7, /device:TPU:0, one launch (start us, length us, event | category | flops | bytes accessed | tf_op | source)
XLA Modules:
  0.0 64.2 jit_solution(17322435550458913448)
XLA Ops:
  0.6 4.1 %collective-permute-start.2 = (bf16[128,1152]{1,0:T(8,128)(2,1)}, bf16[128,1152]{1,0:T(8,128)(2,1)S(1)}, u32[]{:S(2)}, u32[]{:S(2)}) collective-permute-start(bf16[128,1152]{1,0:T(8,128)(2,1)} %refs_1_.8), channel_id=1, source_target_pairs={{0,2},{1,3},{2,0},{3,1},{4,6},{5,7},{6,4},{7,5},{8,10},{9,11},{10,... | collective-permute-start | bytes 884744 | tf_op jit(solution)/shard_map/ppermute | solution.py:21
  4.7 1.6 %collective-permute-start.1 = (bf16[128,1152]{1,0:T(8,128)(2,1)}, bf16[128,1152]{1,0:T(8,128)(2,1)S(1)}, u32[]{:S(2)}, u32[]{:S(2)}) collective-permute-start(bf16[128,1152]{1,0:T(8,128)(2,1)} %refs_1_.9), channel_id=1, source_target_pairs={{0,1},{1,0},{2,3},{3,2},{4,5},{5,4},{6,7},{7,6},{8,9},{9,8},{10,11... | collective-permute-start | bytes 884744 | tf_op jit(solution)/shard_map/ppermute | solution.py:21
  6.3 1.5 %collective-permute-start.3 = (bf16[128,1152]{1,0:T(8,128)(2,1)}, bf16[128,1152]{1,0:T(8,128)(2,1)S(1)}, u32[]{:S(2)}, u32[]{:S(2)}) collective-permute-start(bf16[128,1152]{1,0:T(8,128)(2,1)} %refs_1_.8), channel_id=1, source_target_pairs={{0,16},{4,20},{8,24},{12,28},{16,0},{20,4},{24,8},{28,12},{1,17},{... | collective-permute-start | bytes 884744 | tf_op jit(solution)/shard_map/ppermute | solution.py:21
  7.8 1.5 %collective-permute-start = (bf16[128,1152]{1,0:T(8,128)(2,1)}, bf16[128,1152]{1,0:T(8,128)(2,1)S(1)}, u32[]{:S(2)}, u32[]{:S(2)}) collective-permute-start(bf16[128,1152]{1,0:T(8,128)(2,1)} %refs_1_.9), channel_id=1, source_target_pairs={{0,8},{4,12},{8,0},{12,4},{16,24},{20,28},{24,16},{28,20},{1,9},{5... | collective-permute-start | bytes 884744 | tf_op jit(solution)/shard_map/ppermute | solution.py:21
  9.3 1.0 %copy-done = bf16[128,1152]{1,0:T(8,128)(2,1)S(1)} copy-done((bf16[128,1152]{1,0:T(8,128)(2,1)S(1)}, bf16[128,1152]{1,0:T(8,128)(2,1)}, u32[]{:S(2)}) %copy-start) | copy-done | bytes 294936
  11.5 6.9 %collective-permute-done.2.refs_1_ = bf16[128,1152]{1,0:T(8,128)(2,1)S(1)} collective-permute-done((bf16[128,1152]{1,0:T(8,128)(2,1)}, bf16[128,1152]{1,0:T(8,128)(2,1)S(1)}, u32[]{:S(2)}, u32[]{:S(2)}) %collective-permute-start.2) | collective-permute-done | bytes 294944 | tf_op jit(solution)/shard_map/ppermute | solution.py:21
  19.1 1.6 %collective-permute-start.4 = (bf16[128,1152]{1,0:T(8,128)(2,1)S(1)}, bf16[128,1152]{1,0:T(8,128)(2,1)S(1)}, u32[]{:S(2)}, u32[]{:S(2)}) collective-permute-start(bf16[128,1152]{1,0:T(8,128)(2,1)S(1)} %get-tuple-element.29.refs_2_), channel_id=1, source_target_pairs={{0,8},{4,12},{8,0},{12,4},{16,24},{20,28},{24,16},{28,20},{1,9},{5... | collective-permute-start | bytes 884744 | tf_op jit(solution)/shard_map/ppermute | solution.py:21
  20.8 1.5 %collective-permute-start.7 = (bf16[128,1152]{1,0:T(8,128)(2,1)S(1)}, bf16[128,1152]{1,0:T(8,128)(2,1)S(1)}, u32[]{:S(2)}, u32[]{:S(2)}) collective-permute-start(bf16[128,1152]{1,0:T(8,128)(2,1)S(1)} %get-tuple-element.31.refs_5_), channel_id=1, source_target_pairs={{0,16},{4,20},{8,24},{12,28},{16,0},{20,4},{24,8},{28,12},{1,17},{... | collective-permute-start | bytes 884744 | tf_op jit(solution)/shard_map/ppermute | solution.py:21
  22.3 6.3 %collective-permute-done.4.refs_3_ = bf16[128,1152]{1,0:T(8,128)(2,1)S(1)} collective-permute-done((bf16[128,1152]{1,0:T(8,128)(2,1)S(1)}, bf16[128,1152]{1,0:T(8,128)(2,1)S(1)}, u32[]{:S(2)}, u32[]{:S(2)}) %collective-permute-start.4) | collective-permute-done | bytes 294944 | tf_op jit(solution)/shard_map/ppermute | solution.py:21
  29.9 1.3 %shard_map.70 = (bf16[512,384]{1,0:T(8,128)(2,1)S(1)}, f32[1,384]{1,0:T(1,128)S(1)}) custom-call(f32[1]{0:T(128)S(6)} %exp.3.refs_0_, f32[1]{0:T(128)S(6)} %copy.8.refs_1_, bf16[768,1152]{1,0:T(8,128)(2,1)S(1)} %shard_map.69.refs_2_.refs_4_, bf16[128,1152]{1,0:T(8,128)(2,1)S(1)} %collective-permute-done.4.refs_3_, ...), custom_call_target="tpu_custom_call" | custom-call | flops 452984832 | bytes 4228616 | tf_op jit(solution)/shard_map/pallas_call | solution.py:28
  31.8 1.3 %shard_map.71 = (bf16[512,384]{1,0:T(8,128)(2,1)S(1)}, f32[1,384]{1,0:T(1,128)S(1)}) custom-call(f32[1]{0:T(128)S(6)} %exp.3.refs_0_, f32[1]{0:T(128)S(6)} %copy.8.refs_1_, bf16[768,1152]{1,0:T(8,128)(2,1)S(1)} %collective-permute-done.5.refs_2_.refs_4_, bf16[128,1152]{1,0:T(8,128)(2,1)S(1)} %collective-permute-done.6.refs_3_.refs_5_, ...), custom_call_target="tpu_custom_call" | custom-call | flops 452984832 | bytes 4230152 | tf_op jit(solution)/shard_map/pallas_call | solution.py:28
  33.1 1.6 %shard_map.72 = (bf16[512,128]{1,0:T(8,128)(2,1)S(1)}, bf16[1168,128]{1,0:T(8,128)(2,1)S(1)}) custom-call(f32[1]{0:T(128)S(6)} %exp.3.refs_0_, f32[1]{0:T(128)S(6)} %copy.8.refs_1_, bf16[768,1152]{1,0:T(8,128)(2,1)S(1)} %shard_map.69.refs_2_.refs_4_, bf16[128,1152]{1,0:T(8,128)(2,1)S(1)} %collective-permute-done.4.refs_3_, ...), custom_call_target="tpu_custom_call" | custom-call | flops 603979776 | bytes 4853768 | tf_op jit(solution)/shard_map/pallas_call | solution.py:28
  34.7 1.6 %collective-permute-start.9 = (bf16[1168,128]{1,0:T(8,128)(2,1)S(1)}, bf16[1168,128]{1,0:T(8,128)(2,1)S(1)}, u32[]{:S(2)}, u32[]{:S(2)}) collective-permute-start(bf16[1168,128]{1,0:T(8,128)(2,1)S(1)} %get-tuple-element.37.refs_9_), channel_id=1, source_target_pairs={{0,16},{4,20},{8,24},{12,28},{16,0},{20,4},{24,8},{28,12},{1,17},{... | collective-permute-start | bytes 897032 | tf_op jit(solution)/shard_map/ppermute | solution.py:21
  36.4 3.4 %shard_map.74 = (f32[128,1152]{1,0:T(8,128)S(1)}, bf16[128,1152]{1,0:T(8,128)(2,1)S(1)}, f32[128,1152]{1,0:T(8,128)S(1)}, bf16[128,1152]{1,0:T(8,128)(2,1)S(1)}) custom-call(f32[1]{0:T(128)S(6)} %exp.3.refs_0_, f32[1]{0:T(128)S(6)} %copy.8.refs_1_, bf16[768,1152]{1,0:T(8,128)(2,1)S(1)} %shard_map.69.refs_2_.refs_4_, ...), custom_call_target="tpu_custom_call" | custom-call | flops 1811939328 | bytes 6717448 | tf_op jit(solution)/shard_map/pallas_call | solution.py:28
  39.8 1.6 %collective-permute-start.12 = (bf16[128,1152]{1,0:T(8,128)(2,1)S(1)}, bf16[128,1152]{1,0:T(8,128)(2,1)S(1)}, u32[]{:S(2)}, u32[]{:S(2)}) collective-permute-start(bf16[128,1152]{1,0:T(8,128)(2,1)S(1)} %get-tuple-element.49), channel_id=1, source_target_pairs={{0,8},{4,12},{8,0},{12,4},{16,24},{20,28},{24,16},{28,20},{1,9},{5... | collective-permute-start | bytes 884744 | tf_op jit(solution)/shard_map/ppermute | solution.py:21
  41.4 1.8 %shard_map.75 = (f32[128,1152]{1,0:T(8,128)S(1)}, f32[1,128]{1,0:T(1,128)S(1)}, bf16[1168,128]{1,0:T(8,128)(2,1)S(1)}, f32[1152,128]{1,0:T(8,128)S(1)}, f32[1,128]{1,0:T(1,128)S(1)}) custom-call(bf16[512,384]{1,0:T(8,128)(2,1)S(1)} %get-tuple-element.32.refs_5_.refs_0_, bf16[512,384]{1,0:T(8,128)(2,1)S(1)} %get-tuple-element.34.refs_1_, ...), custom_call_target="tpu_custom_call" | custom-call | flops 905969664 | bytes 6396416 | tf_op jit(solution)/shard_map/pallas_call | solution.py:28
  43.9 1.6 %collective-permute-start.11 = (bf16[1168,128]{1,0:T(8,128)(2,1)S(1)}, bf16[1168,128]{1,0:T(8,128)(2,1)S(1)}, u32[]{:S(2)}, u32[]{:S(2)}) collective-permute-start(bf16[1168,128]{1,0:T(8,128)(2,1)S(1)} %get-tuple-element.45), channel_id=1, source_target_pairs={{0,16},{4,20},{8,24},{12,28},{16,0},{20,4},{24,8},{28,12},{1,17},{... | collective-permute-start | bytes 897032 | tf_op jit(solution)/shard_map/ppermute | solution.py:21
  45.6 1.3 %collective-permute-start.10 = (bf16[1168,128]{1,0:T(8,128)(2,1)S(1)}, bf16[1168,128]{1,0:T(8,128)(2,1)S(1)}, u32[]{:S(2)}, u32[]{:S(2)}) collective-permute-start(bf16[1168,128]{1,0:T(8,128)(2,1)S(1)} %get-tuple-element.44.refs_3_), channel_id=1, source_target_pairs={{0,2},{1,3},{2,0},{3,1},{4,6},{5,7},{6,4},{7,5},{8,10},{9,11},{10,... | collective-permute-start | bytes 897032 | tf_op jit(solution)/shard_map/ppermute | solution.py:21
  46.9 1.6 %collective-permute-done.12.refs_1_ = bf16[128,1152]{1,0:T(8,128)(2,1)S(1)} collective-permute-done((bf16[128,1152]{1,0:T(8,128)(2,1)S(1)}, bf16[128,1152]{1,0:T(8,128)(2,1)S(1)}, u32[]{:S(2)}, u32[]{:S(2)}) %collective-permute-start.12) | collective-permute-done | bytes 294944 | tf_op jit(solution)/shard_map/ppermute | solution.py:21
  48.6 1.5 %collective-permute-start.13 = (bf16[128,1152]{1,0:T(8,128)(2,1)S(1)}, bf16[128,1152]{1,0:T(8,128)(2,1)S(1)}, u32[]{:S(2)}, u32[]{:S(2)}) collective-permute-start(bf16[128,1152]{1,0:T(8,128)(2,1)S(1)} %get-tuple-element.50), channel_id=1, source_target_pairs={{0,1},{1,0},{2,3},{3,2},{4,5},{5,4},{6,7},{7,6},{8,9},{9,8},{10,11... | collective-permute-start | bytes 884744 | tf_op jit(solution)/shard_map/ppermute | solution.py:21
  50.1 1.5 %collective-permute-start.14 = (bf16[128,1152]{1,0:T(8,128)(2,1)S(1)}, bf16[128,1152]{1,0:T(8,128)(2,1)S(1)}, u32[]{:S(2)}, u32[]{:S(2)}) collective-permute-start(bf16[128,1152]{1,0:T(8,128)(2,1)S(1)} %get-tuple-element.51), channel_id=1, source_target_pairs={{0,8},{4,12},{8,0},{12,4},{16,24},{20,28},{24,16},{28,20},{1,9},{5... | collective-permute-start | bytes 884744 | tf_op jit(solution)/shard_map/ppermute | solution.py:21
  51.6 10.3 %collective-permute-done.13.refs_3_ = bf16[128,1152]{1,0:T(8,128)(2,1)S(1)} collective-permute-done((bf16[128,1152]{1,0:T(8,128)(2,1)S(1)}, bf16[128,1152]{1,0:T(8,128)(2,1)S(1)}, u32[]{:S(2)}, u32[]{:S(2)}) %collective-permute-start.13) | collective-permute-done | bytes 294944 | tf_op jit(solution)/shard_map/ppermute | solution.py:21
  61.9 1.1 %shard_map.79 = f32[128,1152]{1,0:T(8,128)} custom-call(f32[1]{0:T(128)S(6)} %exp.3.refs_0_, bf16[128,1152]{1,0:T(8,128)(2,1)S(1)} %copy-done.1, f32[128,1152]{1,0:T(8,128)S(1)} %get-tuple-element.47.refs_2_, bf16[128,1152]{1,0:T(8,128)(2,1)S(1)} %collective-permute-done.13.refs_3_, bf16[128,1152]{1,0:T(8,128)(2,1)S(1)} %collective-permute-done.14.refs_4_), custom_call_target="tpu_custom_call" | custom-call | bytes 2064388 | tf_op jit(solution)/shard_map/pallas_call | solution.py:28
  63.1 1.1 %shard_map.77 = (f32[128,1152]{1,0:T(8,128)}, f32[1,128]{1,0:T(1,128)}) custom-call(f32[1]{0:T(128)S(6)} %exp.3.refs_0_, bf16[128,1152]{1,0:T(8,128)(2,1)S(1)} %copy-done.3, f32[128,1152]{1,0:T(8,128)S(1)} %get-tuple-element.39.refs_2_, f32[1,128]{1,0:T(1,128)S(1)} %get-tuple-element.40.refs_3_, bf16[1168,128]{1,0:T(8,128)(2,1)S(1)} %collective-permute-done.10.refs_4_, ...), custom_call_target="tpu_custom_call" | custom-call | bytes 2073604 | tf_op jit(solution)/shard_map/pallas_call | solution.py:28
  (27 shorter events, 3.4 us)
Async XLA Ops:
  0.6 17.8 %collective-permute-start.2 = (bf16[128,1152]{1,0:T(8,128)(2,1)}, bf16[128,1152]{1,0:T(8,128)(2,1)S(1)}, u32[]{:S(2)}, u32[]{:S(2)}) collective-permute-start(bf16[128,1152]{1,0:T(8,128)(2,1)} %refs_1_.8), channel_id=1, source_target_pairs={{0,2},{1,3},{2,0},{3,1},{4,6},{5,7},{6,4},{7,5},{8,10},{9,11},{10,... | collective-permute-start | bytes 884744 | tf_op jit(solution)/shard_map/ppermute | solution.py:21
  4.7 13.8 %collective-permute-start.1 = (bf16[128,1152]{1,0:T(8,128)(2,1)}, bf16[128,1152]{1,0:T(8,128)(2,1)S(1)}, u32[]{:S(2)}, u32[]{:S(2)}) collective-permute-start(bf16[128,1152]{1,0:T(8,128)(2,1)} %refs_1_.9), channel_id=1, source_target_pairs={{0,1},{1,0},{2,3},{3,2},{4,5},{5,4},{6,7},{7,6},{8,9},{9,8},{10,11... | collective-permute-start | bytes 884744 | tf_op jit(solution)/shard_map/ppermute | solution.py:21
  6.3 12.5 %collective-permute-start.3 = (bf16[128,1152]{1,0:T(8,128)(2,1)}, bf16[128,1152]{1,0:T(8,128)(2,1)S(1)}, u32[]{:S(2)}, u32[]{:S(2)}) collective-permute-start(bf16[128,1152]{1,0:T(8,128)(2,1)} %refs_1_.8), channel_id=1, source_target_pairs={{0,16},{4,20},{8,24},{12,28},{16,0},{20,4},{24,8},{28,12},{1,17},{... | collective-permute-start | bytes 884744 | tf_op jit(solution)/shard_map/ppermute | solution.py:21
  7.8 11.0 %collective-permute-start = (bf16[128,1152]{1,0:T(8,128)(2,1)}, bf16[128,1152]{1,0:T(8,128)(2,1)S(1)}, u32[]{:S(2)}, u32[]{:S(2)}) collective-permute-start(bf16[128,1152]{1,0:T(8,128)(2,1)} %refs_1_.9), channel_id=1, source_target_pairs={{0,8},{4,12},{8,0},{12,4},{16,24},{20,28},{24,16},{28,20},{1,9},{5... | collective-permute-start | bytes 884744 | tf_op jit(solution)/shard_map/ppermute | solution.py:21
  9.3 1.0 %copy-start = (bf16[128,1152]{1,0:T(8,128)(2,1)S(1)}, bf16[128,1152]{1,0:T(8,128)(2,1)}, u32[]{:S(2)}) copy-start(bf16[128,1152]{1,0:T(8,128)(2,1)} %refs_1_.9) | copy-start | bytes 884740
  10.3 1.0 %copy-start.2 = (bf16[128,1152]{1,0:T(8,128)(2,1)S(1)}, bf16[128,1152]{1,0:T(8,128)(2,1)}, u32[]{:S(2)}) copy-start(bf16[128,1152]{1,0:T(8,128)(2,1)} %refs_1_.8) | copy-start | bytes 884740
  19.1 12.7 %collective-permute-start.5 = (bf16[768,1152]{1,0:T(8,128)(2,1)S(1)}, bf16[768,1152]{1,0:T(8,128)(2,1)S(1)}, u32[]{:S(2)}, u32[]{:S(2)}) collective-permute-start(bf16[768,1152]{1,0:T(8,128)(2,1)S(1)} %shard_map.69.refs_2_.refs_4_), channel_id=1, source_target_pairs={{0,4},{4,0},{8,12},{12,8},{16,20},{20,16},{24,28},{28,24},{1,5},{5... | collective-permute-start | bytes 5308424 | tf_op jit(solution)/shard_map/ppermute | solution.py:21
  19.1 9.4 %collective-permute-start.4 = (bf16[128,1152]{1,0:T(8,128)(2,1)S(1)}, bf16[128,1152]{1,0:T(8,128)(2,1)S(1)}, u32[]{:S(2)}, u32[]{:S(2)}) collective-permute-start(bf16[128,1152]{1,0:T(8,128)(2,1)S(1)} %get-tuple-element.29.refs_2_), channel_id=1, source_target_pairs={{0,8},{4,12},{8,0},{12,4},{16,24},{20,28},{24,16},{28,20},{1,9},{5... | collective-permute-start | bytes 884744 | tf_op jit(solution)/shard_map/ppermute | solution.py:21
  20.8 10.4 %collective-permute-start.7 = (bf16[128,1152]{1,0:T(8,128)(2,1)S(1)}, bf16[128,1152]{1,0:T(8,128)(2,1)S(1)}, u32[]{:S(2)}, u32[]{:S(2)}) collective-permute-start(bf16[128,1152]{1,0:T(8,128)(2,1)S(1)} %get-tuple-element.31.refs_5_), channel_id=1, source_target_pairs={{0,16},{4,20},{8,24},{12,28},{16,0},{20,4},{24,8},{28,12},{1,17},{... | collective-permute-start | bytes 884744 | tf_op jit(solution)/shard_map/ppermute | solution.py:21
  28.6 3.2 %collective-permute-start.6 = (bf16[128,1152]{1,0:T(8,128)(2,1)S(1)}, bf16[128,1152]{1,0:T(8,128)(2,1)S(1)}, u32[]{:S(2)}, u32[]{:S(2)}) collective-permute-start(bf16[128,1152]{1,0:T(8,128)(2,1)S(1)} %collective-permute-done.4.refs_3_), channel_id=1, source_target_pairs={{0,4},{4,0},{8,12},{12,8},{16,20},{20,16},{24,28},{28,24},{1,5},{5... | collective-permute-start | bytes 884744 | tf_op jit(solution)/shard_map/ppermute | solution.py:21
  31.2 5.1 %collective-permute-start.8 = (bf16[128,1152]{1,0:T(8,128)(2,1)S(1)}, bf16[128,1152]{1,0:T(8,128)(2,1)S(1)}, u32[]{:S(2)}, u32[]{:S(2)}) collective-permute-start(bf16[128,1152]{1,0:T(8,128)(2,1)S(1)} %shard_map.73), channel_id=1, source_target_pairs={{0,4},{4,0},{8,12},{12,8},{16,20},{20,16},{24,28},{28,24},{1,5},{5... | collective-permute-start | bytes 884744 | tf_op jit(solution)/shard_map/ppermute | solution.py:21
  34.7 9.1 %collective-permute-start.9 = (bf16[1168,128]{1,0:T(8,128)(2,1)S(1)}, bf16[1168,128]{1,0:T(8,128)(2,1)S(1)}, u32[]{:S(2)}, u32[]{:S(2)}) collective-permute-start(bf16[1168,128]{1,0:T(8,128)(2,1)S(1)} %get-tuple-element.37.refs_9_), channel_id=1, source_target_pairs={{0,16},{4,20},{8,24},{12,28},{16,0},{20,4},{24,8},{28,12},{1,17},{... | collective-permute-start | bytes 897032 | tf_op jit(solution)/shard_map/ppermute | solution.py:21
  39.8 8.7 %collective-permute-start.12 = (bf16[128,1152]{1,0:T(8,128)(2,1)S(1)}, bf16[128,1152]{1,0:T(8,128)(2,1)S(1)}, u32[]{:S(2)}, u32[]{:S(2)}) collective-permute-start(bf16[128,1152]{1,0:T(8,128)(2,1)S(1)} %get-tuple-element.49), channel_id=1, source_target_pairs={{0,8},{4,12},{8,0},{12,4},{16,24},{20,28},{24,16},{28,20},{1,9},{5... | collective-permute-start | bytes 884744 | tf_op jit(solution)/shard_map/ppermute | solution.py:21
  43.9 19.1 %collective-permute-start.11 = (bf16[1168,128]{1,0:T(8,128)(2,1)S(1)}, bf16[1168,128]{1,0:T(8,128)(2,1)S(1)}, u32[]{:S(2)}, u32[]{:S(2)}) collective-permute-start(bf16[1168,128]{1,0:T(8,128)(2,1)S(1)} %get-tuple-element.45), channel_id=1, source_target_pairs={{0,16},{4,20},{8,24},{12,28},{16,0},{20,4},{24,8},{28,12},{1,17},{... | collective-permute-start | bytes 897032 | tf_op jit(solution)/shard_map/ppermute | solution.py:21
  45.6 17.5 %collective-permute-start.10 = (bf16[1168,128]{1,0:T(8,128)(2,1)S(1)}, bf16[1168,128]{1,0:T(8,128)(2,1)S(1)}, u32[]{:S(2)}, u32[]{:S(2)}) collective-permute-start(bf16[1168,128]{1,0:T(8,128)(2,1)S(1)} %get-tuple-element.44.refs_3_), channel_id=1, source_target_pairs={{0,2},{1,3},{2,0},{3,1},{4,6},{5,7},{6,4},{7,5},{8,10},{9,11},{10,... | collective-permute-start | bytes 897032 | tf_op jit(solution)/shard_map/ppermute | solution.py:21
  48.5 13.4 %copy-start.1 = (bf16[128,1152]{1,0:T(8,128)(2,1)S(1)}, bf16[128,1152]{1,0:T(8,128)(2,1)}, u32[]{:S(2)}) copy-start(bf16[128,1152]{1,0:T(8,128)(2,1)} %refs_1_.9) | copy-start | bytes 884740
  48.6 14.4 %copy-start.3 = (bf16[128,1152]{1,0:T(8,128)(2,1)S(1)}, bf16[128,1152]{1,0:T(8,128)(2,1)}, u32[]{:S(2)}) copy-start(bf16[128,1152]{1,0:T(8,128)(2,1)} %refs_1_.8) | copy-start | bytes 884740
  48.6 13.3 %collective-permute-start.13 = (bf16[128,1152]{1,0:T(8,128)(2,1)S(1)}, bf16[128,1152]{1,0:T(8,128)(2,1)S(1)}, u32[]{:S(2)}, u32[]{:S(2)}) collective-permute-start(bf16[128,1152]{1,0:T(8,128)(2,1)S(1)} %get-tuple-element.50), channel_id=1, source_target_pairs={{0,1},{1,0},{2,3},{3,2},{4,5},{5,4},{6,7},{7,6},{8,9},{9,8},{10,11... | collective-permute-start | bytes 884744 | tf_op jit(solution)/shard_map/ppermute | solution.py:21
  50.1 11.8 %collective-permute-start.14 = (bf16[128,1152]{1,0:T(8,128)(2,1)S(1)}, bf16[128,1152]{1,0:T(8,128)(2,1)S(1)}, u32[]{:S(2)}, u32[]{:S(2)}) collective-permute-start(bf16[128,1152]{1,0:T(8,128)(2,1)S(1)} %get-tuple-element.51), channel_id=1, source_target_pairs={{0,8},{4,12},{8,0},{12,4},{16,24},{20,28},{24,16},{28,20},{1,9},{5... | collective-permute-start | bytes 884744 | tf_op jit(solution)/shard_map/ppermute | solution.py:21

commit v8 on v7

--- a/solution.py
+++ b/solution.py
@@ -11,7 +11,7 @@
 f32, bf16 = jnp.float32, jnp.bfloat16
 lanes = 128
 extra = 16
-weights = {"z": 10, "late": 2, "text": 2, "end": 0, "text end": 0}
+weights = {"x far": 10, "y far": 10, "x": 0, "a": 10, "b": 10, "late": 2, "text": 2, "end": 0, "text end": 0}
 VMEM = pl.BlockSpec(memory_space=pltpu.VMEM)
 SMEM = pl.BlockSpec(memory_space=pltpu.SMEM)
 ANY = pl.BlockSpec(memory_space=pl.ANY)
@@ -100,11 +100,27 @@
         target[...] = source[...]
 
 
-def near_kernel(held, *refs):
-    out_ref, rows = refs[-1], refs[0].shape[0]
+def own_rows_kernel(scale_ref, bias_ref, text_ref, image_ref, text_emb_ref, image_emb_ref, half_ref):
+    text_emb_ref[...] = unit_of(text_ref[...])[0].astype(bf16)
+    emb = unit_of(image_ref[...])[0].astype(bf16)
+    image_emb_ref[...] = emb
+    half_ref[...] = emb[emb.shape[0] // 2 :, :]
+
+
+def near_kernel(raw, *refs):
+    out_ref, start = refs[-1], 0
     for place, block in enumerate(refs[:-1]):
-        emb = block[...] if place in held else unit_of(block[...])[0].astype(bf16)
-        out_ref[place * rows : (place + 1) * rows, :] = emb
+        count = block.shape[0]
+        out_ref[start : start + count, :] = unit_of(block[...])[0].astype(bf16) if place in raw else block[...]
+        start += count
+
+
+def join_kernel(*refs):
+    count = len(refs) // 3
+    for first, second, out in zip(refs[:count], refs[count : 2 * count], refs[2 * count :]):
+        rows = first.shape[0]
+        out[:rows, :] = first[...]
+        out[rows:, :] = second[...]
 
 
 def near_pairs_kernel(own, scale_ref, bias_ref, near_ref, far_ref, images_ref, *refs):
@@ -273,34 +289,45 @@
 
     image_dp, image_inner = range(4, dp_count, 4), range(2, inner_count, 2)
 
+    half_block = shape((rows // 2, width), bf16)
+    text_z = swapped(text, "inner", 1)
+    text_x = swapped(text, "dp", 2)
+    first_half = image[: rows // 2]
+    first_z = [swapped(first_half, "inner", q) for q in image_inner]
     images_y = [swapped(image, "dp", p) for p in image_dp]
-    text_x = swapped(text, "dp", 2)
-    images_z = [swapped(image, "inner", q) for q in image_inner]
-    text_z = swapped(text, "inner", 1)
-    text_emb, image_emb = call(unit_kernel, [block, block], text, image)
-    text_z_emb, *embs_z = call(
-        unit_kernel, [block] * (1 + len(images_z)), text_z, *images_z, weight=weights["z"], after=[text_emb]
-    )
-    far_text = swapped(text_z_emb, "dp", 2)
-    far = [swapped(emb, "dp", p) for emb in embs_z for p in image_dp]
+    text_emb, image_emb, second_half = call(
+        own_rows_kernel, [block, block, half_block], scale, bias, text, image, scalars=2
+    )
+    second_z = [swapped(second_half, "inner", q) for q in image_inner]
+    zs, ys = len(first_z), len(images_y)
+
+    (text_z_emb,) = call(unit_kernel, [block], text_z, weight=weights["x"], after=[text_x, second_half])
+    (far_text,) = call(copies_kernel, [block], swapped(text_z_emb, "dp", 2), weight=weights["x far"])
     far_places = [(p, q) for q in image_inner for p in image_dp]
-    zs, ys = len(embs_z), len(images_y)
-
-    held = {0, 2, 3, *range(4 + ys, 4 + ys + zs)}
+    first_z = call(
+        unit_kernel, [half_block] * zs, *first_z, weight=weights["a"], after=[text_z_emb, *images_y]
+    )
+    first_far = [swapped(emb, "dp", p) for emb in first_z for p in image_dp]
+    first_far = call(
+        copies_kernel, [half_block] * (zs * ys), *first_far, weight=weights["y far"], after=[far_text]
+    )
+    second_z = call(copies_kernel, [half_block] * zs, *second_z, weight=weights["b"], after=first_z)
+    second_far = [swapped(emb, "dp", p) for emb in second_z for p in image_dp]
+
     near = call(
-        functools.partial(near_kernel, frozenset(held)),
+        functools.partial(near_kernel, frozenset({1, *range(4, 4 + ys)})),
         shape(((4 + ys + zs) * rows, width), bf16),
         text_emb,
         text_x,
         text_z_emb,
         image_emb,
         *images_y,
-        *embs_z,
+        *(part for both in zip(first_z, second_z) for part in both),
     )
     near_swapped = swapped(near, "dp", 1)
     far_text_swapped = swapped(far_text, "dp", 1)
 
-    half, near_rows, far_rows = 4 * rows, (1 + ys + zs) * rows, len(far) * rows
+    half, near_rows, far_rows = 4 * rows, (1 + ys + zs) * rows, zs * ys * rows
     own_texts, other_texts = (near, far_text), (near_swapped, far_text_swapped)
     pair_flops = 2 * rows * half * width
     near_slopes, near_loss = shape((half, near_rows), bf16), shape((1, near_rows), f32)
@@ -315,8 +342,8 @@
         flops=pair_flops * (1 + ys + zs),
         scalars=2,
     )
-    passed = call(copies_kernel, [block] * len(far), *far, after=[loss])
-    far_swapped = [swapped(emb, "dp", 1) for emb in passed]
+    far = call(join_kernel, [block] * (zs * ys), *first_far, *second_far, after=[loss])
+    far_swapped = [swapped(emb, "dp", 1) for emb in far]
     other_slopes, loss = call(
         functools.partial(near_pairs_kernel, False),
         (near_slopes, near_loss),

time: 64.4 us -> 63.4 us (0.984)
  starting transfers between devices: 21.6 us -> 16.5 us
  waiting for transfers between devices: 26.1 us -> 29.1 us
  local copies, waits for them, and re-layouts: 1.97 us -> 2.88 us
    ppermute x15 -> x17, starting transfers between devices: 21.6 us -> 16.5 us  [swapped(): lax.ppermute(value, axis, [(place, place ^ step) for place in range(lax.a...]
    ppermute x15 -> x17, waiting for transfers between devices: 26.1 us -> 29.1 us  [swapped(): lax.ppermute(value, axis, [(place, place ^ step) for place in range(lax.a...]
    slice x0 -> x1, local copies, waits for them, and re-layouts: none -> 0.95 us  [body(): first_half = image[:rows // 2]]
    pallas_call x13 -> x17, Pallas kernels: 12.5 us -> 12.6 us  [call(): pl.pallas_call(lambda *refs: kernel(*refs[:first], *refs[last:]), out_sha...]
  transfers between devices with their start and end apart: 15 -> 17, of which waited for: 6 -> 6; matrix products, arithmetic and copies ran while one was open for 0% -> 2% of each run, Pallas kernels for 17% -> 18%
where the time goes in v8:
time: 63.4 us; the launch traced here: 63.2 us
  waiting for transfers between devices  29.1 us (46%)
  starting transfers between devices  16.5 us (26%)
  Pallas kernels  12.6 us (20%)
  local copies, waits for them, and re-layouts  2.88 us (5%)
  between operations  2.13 us (3%)
    ppermute x17, waiting for transfers between devices, swapped(): lax.ppermute(value, axis, [(place, place ^ step) for place in range(lax.a...  29.1 us
    ppermute x17, starting transfers between devices, swapped(): lax.ppermute(value, axis, [(place, place ^ step) for place in range(lax.a...  16.5 us
    pallas_call x17, Pallas kernels, call(): pl.pallas_call(lambda *refs: kernel(*refs[:first], *refs[last:]), out_sha...  12.6 us
    unnamed x8, local copies, waits for them, and re-layouts  1.93 us
  transfers between devices with their start and end apart: 17, of which 6 were waited for; matrix products, arithmetic and copies ran while one was open for 2% of the time, Pallas kernels for 18%

profile of v8, /device:TPU:0, one launch (start us, length us, event | category | flops | bytes accessed | tf_op | source)
XLA Modules:
  0.0 63.2 jit_solution(15449972201954685022)
XLA Ops:
  0.6 3.0 %collective-permute-start = (bf16[128,1152]{1,0:T(8,128)(2,1)}, bf16[128,1152]{1,0:T(8,128)(2,1)S(1)}, u32[]{:S(2)}, u32[]{:S(2)}) collective-permute-start(bf16[128,1152]{1,0:T(8,128)(2,1)} %refs_1_.8), channel_id=1, source_target_pairs={{0,8},{4,12},{8,0},{12,4},{16,24},{20,28},{24,16},{28,20},{1,9},{5... | collective-permute-start | bytes 884744 | tf_op jit(solution)/shard_map/ppermute | solution.py:21
  3.6 1.6 %collective-permute-start.1 = (bf16[128,1152]{1,0:T(8,128)(2,1)}, bf16[128,1152]{1,0:T(8,128)(2,1)S(1)}, u32[]{:S(2)}, u32[]{:S(2)}) collective-permute-start(bf16[128,1152]{1,0:T(8,128)(2,1)} %refs_1_.8), channel_id=1, source_target_pairs={{0,1},{1,0},{2,3},{3,2},{4,5},{5,4},{6,7},{7,6},{8,9},{9,8},{10,11... | collective-permute-start | bytes 884744 | tf_op jit(solution)/shard_map/ppermute | solution.py:21
  5.2 1.5 %collective-permute-start.2 = (bf16[128,1152]{1,0:T(8,128)(2,1)}, bf16[128,1152]{1,0:T(8,128)(2,1)S(1)}, u32[]{:S(2)}, u32[]{:S(2)}) collective-permute-start(bf16[128,1152]{1,0:T(8,128)(2,1)} %refs_1_.7), channel_id=1, source_target_pairs={{0,16},{4,20},{8,24},{12,28},{16,0},{20,4},{24,8},{28,12},{1,17},{... | collective-permute-start | bytes 884744 | tf_op jit(solution)/shard_map/ppermute | solution.py:21
  6.7 1.0 %slice.3 = bf16[64,1152]{1,0:T(8,128)(2,1)S(1)} slice(bf16[128,1152]{1,0:T(8,128)(2,1)} %refs_1_.7), slice={[0:64], [0:1152]} | slice | bytes 294912 | tf_op jit(solution)/shard_map/slice | solution.py:295
  7.7 2.7 %collective-permute-start.3 = (bf16[64,1152]{1,0:T(8,128)(2,1)S(1)}, bf16[64,1152]{1,0:T(8,128)(2,1)S(1)}, u32[]{:S(2)}, u32[]{:S(2)}) collective-permute-start(bf16[64,1152]{1,0:T(8,128)(2,1)S(1)} %slice.3), channel_id=1, source_target_pairs={{0,2},{1,3},{2,0},{3,1},{4,6},{5,7},{6,4},{7,5},{8,10},{9,11},{10,... | collective-permute-start | bytes 442376 | tf_op jit(solution)/shard_map/ppermute | solution.py:21
  11.7 1.0 %copy-done = bf16[128,1152]{1,0:T(8,128)(2,1)S(1)} copy-done((bf16[128,1152]{1,0:T(8,128)(2,1)S(1)}, bf16[128,1152]{1,0:T(8,128)(2,1)}, u32[]{:S(2)}) %copy-start) | copy-done | bytes 294936
  12.6 1.0 %copy-done.2 = bf16[128,1152]{1,0:T(8,128)(2,1)S(1)} copy-done((bf16[128,1152]{1,0:T(8,128)(2,1)S(1)}, bf16[128,1152]{1,0:T(8,128)(2,1)}, u32[]{:S(2)}) %copy-start.2) | copy-done | bytes 294936
  14.2 1.3 %collective-permute-done.1.refs_0_ = bf16[128,1152]{1,0:T(8,128)(2,1)S(1)} collective-permute-done((bf16[128,1152]{1,0:T(8,128)(2,1)}, bf16[128,1152]{1,0:T(8,128)(2,1)S(1)}, u32[]{:S(2)}, u32[]{:S(2)}) %collective-permute-start.1) | collective-permute-done | bytes 294944 | tf_op jit(solution)/shard_map/ppermute | solution.py:21
  16.2 2.1 %collective-permute-start.8 = (bf16[64,1152]{1,0:T(8,128)(2,1)S(1)}, bf16[64,1152]{1,0:T(8,128)(2,1)S(1)}, u32[]{:S(2)}, u32[]{:S(2)}) collective-permute-start(bf16[64,1152]{1,0:T(8,128)(2,1)S(1)} %shard_map.69.refs_1_.refs_5_), channel_id=1, source_target_pairs={{0,16},{4,20},{8,24},{12,28},{16,0},{20,4},{24,8},{28,12},{1,17},{... | collective-permute-start | bytes 442376 | tf_op jit(solution)/shard_map/ppermute | solution.py:21
  18.3 5.5 %collective-permute-done.4.refs_0_ = bf16[64,1152]{1,0:T(8,128)(2,1)S(1)} collective-permute-done((bf16[64,1152]{1,0:T(8,128)(2,1)S(1)}, bf16[64,1152]{1,0:T(8,128)(2,1)S(1)}, u32[]{:S(2)}, u32[]{:S(2)}) %collective-permute-start.4) | collective-permute-done | bytes 147488 | tf_op jit(solution)/shard_map/ppermute | solution.py:21
  23.8 1.2 %collective-permute-start.9 = (bf16[64,1152]{1,0:T(8,128)(2,1)S(1)}, bf16[64,1152]{1,0:T(8,128)(2,1)S(1)}, u32[]{:S(2)}, u32[]{:S(2)}) collective-permute-start(bf16[64,1152]{1,0:T(8,128)(2,1)S(1)} %shard_map.70.refs_6_), channel_id=1, source_target_pairs={{0,16},{4,20},{8,24},{12,28},{16,0},{20,4},{24,8},{28,12},{1,17},{... | collective-permute-start | bytes 442376 | tf_op jit(solution)/shard_map/ppermute | solution.py:21
  26.0 1.3 %shard_map.73 = (bf16[512,384]{1,0:T(8,128)(2,1)S(1)}, f32[1,384]{1,0:T(1,128)S(1)}) custom-call(f32[1]{0:T(128)S(6)} %exp.3.refs_0_, f32[1]{0:T(128)S(6)} %copy.8.refs_1_, bf16[768,1152]{1,0:T(8,128)(2,1)S(1)} %shard_map.71.refs_2_.refs_4_, bf16[128,1152]{1,0:T(8,128)(2,1)S(1)} %shard_map.72.refs_3_.refs_1_, bf16[768,1152]{1,0:T(8,128)(2,1)S(1)} %shard_map.71.refs_2_.refs_4_), custom_call_target="tpu_custom_call" | custom-call | flops 452984832 | bytes 4228616 | tf_op jit(solution)/shard_map/pallas_call | solution.py:28
  27.3 2.4 %collective-permute-done.9.refs_1_ = bf16[64,1152]{1,0:T(8,128)(2,1)S(1)} collective-permute-done((bf16[64,1152]{1,0:T(8,128)(2,1)S(1)}, bf16[64,1152]{1,0:T(8,128)(2,1)S(1)}, u32[]{:S(2)}, u32[]{:S(2)}) %collective-permute-start.9) | collective-permute-done | bytes 147488 | tf_op jit(solution)/shard_map/ppermute | solution.py:21
  29.8 1.3 %shard_map.74 = (bf16[512,384]{1,0:T(8,128)(2,1)S(1)}, f32[1,384]{1,0:T(1,128)S(1)}) custom-call(f32[1]{0:T(128)S(6)} %exp.3.refs_0_, f32[1]{0:T(128)S(6)} %copy.8.refs_1_, bf16[768,1152]{1,0:T(8,128)(2,1)S(1)} %collective-permute-done.6.refs_2_.refs_4_, bf16[128,1152]{1,0:T(8,128)(2,1)S(1)} %collective-permute-done.7.refs_3_.refs_5_, ...), custom_call_target="tpu_custom_call" | custom-call | flops 452984832 | bytes 4230152 | tf_op jit(solution)/shard_map/pallas_call | solution.py:28
  31.1 1.7 %shard_map.77 = (bf16[512,128]{1,0:T(8,128)(2,1)S(1)}, bf16[1168,128]{1,0:T(8,128)(2,1)S(1)}) custom-call(f32[1]{0:T(128)S(6)} %exp.3.refs_0_, f32[1]{0:T(128)S(6)} %copy.8.refs_1_, bf16[768,1152]{1,0:T(8,128)(2,1)S(1)} %shard_map.71.refs_2_.refs_4_, bf16[128,1152]{1,0:T(8,128)(2,1)S(1)} %shard_map.72.refs_3_.refs_1_, ...), custom_call_target="tpu_custom_call" | custom-call | flops 603979776 | bytes 4853768 | tf_op jit(solution)/shard_map/pallas_call | solution.py:28
  32.7 0.8 %collective-permute-start.11 = (bf16[1168,128]{1,0:T(8,128)(2,1)S(1)}, bf16[1168,128]{1,0:T(8,128)(2,1)S(1)}, u32[]{:S(2)}, u32[]{:S(2)}) collective-permute-start(bf16[1168,128]{1,0:T(8,128)(2,1)S(1)} %get-tuple-element.35.refs_9_), channel_id=1, source_target_pairs={{0,16},{4,20},{8,24},{12,28},{16,0},{20,4},{24,8},{28,12},{1,17},{... | collective-permute-start | bytes 897032 | tf_op jit(solution)/shard_map/ppermute | solution.py:21
  33.5 3.4 %shard_map.78 = (f32[128,1152]{1,0:T(8,128)S(1)}, bf16[128,1152]{1,0:T(8,128)(2,1)S(1)}, f32[128,1152]{1,0:T(8,128)S(1)}, bf16[128,1152]{1,0:T(8,128)(2,1)S(1)}) custom-call(f32[1]{0:T(128)S(6)} %exp.3.refs_0_, f32[1]{0:T(128)S(6)} %copy.8.refs_1_, bf16[768,1152]{1,0:T(8,128)(2,1)S(1)} %shard_map.71.refs_2_.refs_4_, ...), custom_call_target="tpu_custom_call" | custom-call | flops 1811939328 | bytes 6717448 | tf_op jit(solution)/shard_map/pallas_call | solution.py:28
  37.5 1.8 %shard_map.79 = (f32[128,1152]{1,0:T(8,128)S(1)}, f32[1,128]{1,0:T(1,128)S(1)}, bf16[1168,128]{1,0:T(8,128)(2,1)S(1)}, f32[1152,128]{1,0:T(8,128)S(1)}, f32[1,128]{1,0:T(1,128)S(1)}) custom-call(bf16[512,384]{1,0:T(8,128)(2,1)S(1)} %get-tuple-element.30.refs_5_.refs_0_, bf16[512,384]{1,0:T(8,128)(2,1)S(1)} %get-tuple-element.32.refs_1_, ...), custom_call_target="tpu_custom_call" | custom-call | flops 905969664 | bytes 6396416 | tf_op jit(solution)/shard_map/pallas_call | solution.py:28
  39.3 2.9 %collective-permute-done.11.refs_2_ = bf16[1168,128]{1,0:T(8,128)(2,1)S(1)} collective-permute-done((bf16[1168,128]{1,0:T(8,128)(2,1)S(1)}, bf16[1168,128]{1,0:T(8,128)(2,1)S(1)}, u32[]{:S(2)}, u32[]{:S(2)}) %collective-permute-start.11) | collective-permute-done | bytes 299040 | tf_op jit(solution)/shard_map/ppermute | solution.py:21
  42.3 0.8 %collective-permute-start.13 = (bf16[1168,128]{1,0:T(8,128)(2,1)S(1)}, bf16[1168,128]{1,0:T(8,128)(2,1)S(1)}, u32[]{:S(2)}, u32[]{:S(2)}) collective-permute-start(bf16[1168,128]{1,0:T(8,128)(2,1)S(1)} %get-tuple-element.43), channel_id=1, source_target_pairs={{0,16},{4,20},{8,24},{12,28},{16,0},{20,4},{24,8},{28,12},{1,17},{... | collective-permute-start | bytes 897032 | tf_op jit(solution)/shard_map/ppermute | solution.py:21
  43.1 3.0 %collective-permute-done.14.refs_1_ = bf16[128,1152]{1,0:T(8,128)(2,1)S(1)} collective-permute-done((bf16[128,1152]{1,0:T(8,128)(2,1)S(1)}, bf16[128,1152]{1,0:T(8,128)(2,1)S(1)}, u32[]{:S(2)}, u32[]{:S(2)}) %collective-permute-start.14) | collective-permute-done | bytes 294944 | tf_op jit(solution)/shard_map/ppermute | solution.py:21
  46.9 14.0 %collective-permute-done.15.refs_3_ = bf16[128,1152]{1,0:T(8,128)(2,1)S(1)} collective-permute-done((bf16[128,1152]{1,0:T(8,128)(2,1)S(1)}, bf16[128,1152]{1,0:T(8,128)(2,1)S(1)}, u32[]{:S(2)}, u32[]{:S(2)}) %collective-permute-start.15) | collective-permute-done | bytes 294944 | tf_op jit(solution)/shard_map/ppermute | solution.py:21
  60.9 1.1 %shard_map.83 = f32[128,1152]{1,0:T(8,128)} custom-call(f32[1]{0:T(128)S(6)} %exp.3.refs_0_, bf16[128,1152]{1,0:T(8,128)(2,1)S(1)} %copy-done.3, f32[128,1152]{1,0:T(8,128)S(1)} %get-tuple-element.45.refs_2_, bf16[128,1152]{1,0:T(8,128)(2,1)S(1)} %collective-permute-done.15.refs_3_, bf16[128,1152]{1,0:T(8,128)(2,1)S(1)} %collective-permute-done.16.refs_4_), custom_call_target="tpu_custom_call" | custom-call | bytes 2064388 | tf_op jit(solution)/shard_map/pallas_call | solution.py:28
  62.0 1.1 %shard_map.81 = (f32[128,1152]{1,0:T(8,128)}, f32[1,128]{1,0:T(1,128)}) custom-call(f32[1]{0:T(128)S(6)} %exp.3.refs_0_, bf16[128,1152]{1,0:T(8,128)(2,1)S(1)} %copy-done.1, f32[128,1152]{1,0:T(8,128)S(1)} %get-tuple-element.37.refs_2_, f32[1,128]{1,0:T(1,128)S(1)} %get-tuple-element.38.refs_3_, bf16[1168,128]{1,0:T(8,128)(2,1)S(1)} %collective-permute-done.12.refs_4_, ...), custom_call_target="tpu_custom_call" | custom-call | bytes 2073604 | tf_op jit(solution)/shard_map/pallas_call | solution.py:28
  (36 shorter events, 3.8 us)
Async XLA Ops:
  0.6 13.6 %collective-permute-start = (bf16[128,1152]{1,0:T(8,128)(2,1)}, bf16[128,1152]{1,0:T(8,128)(2,1)S(1)}, u32[]{:S(2)}, u32[]{:S(2)}) collective-permute-start(bf16[128,1152]{1,0:T(8,128)(2,1)} %refs_1_.8), channel_id=1, source_target_pairs={{0,8},{4,12},{8,0},{12,4},{16,24},{20,28},{24,16},{28,20},{1,9},{5... | collective-permute-start | bytes 884744 | tf_op jit(solution)/shard_map/ppermute | solution.py:21
  3.6 11.8 %collective-permute-start.1 = (bf16[128,1152]{1,0:T(8,128)(2,1)}, bf16[128,1152]{1,0:T(8,128)(2,1)S(1)}, u32[]{:S(2)}, u32[]{:S(2)}) collective-permute-start(bf16[128,1152]{1,0:T(8,128)(2,1)} %refs_1_.8), channel_id=1, source_target_pairs={{0,1},{1,0},{2,3},{3,2},{4,5},{5,4},{6,7},{7,6},{8,9},{9,8},{10,11... | collective-permute-start | bytes 884744 | tf_op jit(solution)/shard_map/ppermute | solution.py:21
  5.2 10.9 %collective-permute-start.2 = (bf16[128,1152]{1,0:T(8,128)(2,1)}, bf16[128,1152]{1,0:T(8,128)(2,1)S(1)}, u32[]{:S(2)}, u32[]{:S(2)}) collective-permute-start(bf16[128,1152]{1,0:T(8,128)(2,1)} %refs_1_.7), channel_id=1, source_target_pairs={{0,16},{4,20},{8,24},{12,28},{16,0},{20,4},{24,8},{28,12},{1,17},{... | collective-permute-start | bytes 884744 | tf_op jit(solution)/shard_map/ppermute | solution.py:21
  7.7 8.4 %collective-permute-start.3 = (bf16[64,1152]{1,0:T(8,128)(2,1)S(1)}, bf16[64,1152]{1,0:T(8,128)(2,1)S(1)}, u32[]{:S(2)}, u32[]{:S(2)}) collective-permute-start(bf16[64,1152]{1,0:T(8,128)(2,1)S(1)} %slice.3), channel_id=1, source_target_pairs={{0,2},{1,3},{2,0},{3,1},{4,6},{5,7},{6,4},{7,5},{8,10},{9,11},{10,... | collective-permute-start | bytes 442376 | tf_op jit(solution)/shard_map/ppermute | solution.py:21
  11.7 1.0 %copy-start = (bf16[128,1152]{1,0:T(8,128)(2,1)S(1)}, bf16[128,1152]{1,0:T(8,128)(2,1)}, u32[]{:S(2)}) copy-start(bf16[128,1152]{1,0:T(8,128)(2,1)} %refs_1_.7) | copy-start | bytes 884740
  12.6 1.0 %copy-start.2 = (bf16[128,1152]{1,0:T(8,128)(2,1)S(1)}, bf16[128,1152]{1,0:T(8,128)(2,1)}, u32[]{:S(2)}) copy-start(bf16[128,1152]{1,0:T(8,128)(2,1)} %refs_1_.8) | copy-start | bytes 884740
  13.8 10.0 %collective-permute-start.4 = (bf16[64,1152]{1,0:T(8,128)(2,1)S(1)}, bf16[64,1152]{1,0:T(8,128)(2,1)S(1)}, u32[]{:S(2)}, u32[]{:S(2)}) collective-permute-start(bf16[64,1152]{1,0:T(8,128)(2,1)S(1)} %get-tuple-element.28.refs_2_), channel_id=1, source_target_pairs={{0,2},{1,3},{2,0},{3,1},{4,6},{5,7},{6,4},{7,5},{8,10},{9,11},{10,... | collective-permute-start | bytes 442376 | tf_op jit(solution)/shard_map/ppermute | solution.py:21
  15.6 9.8 %collective-permute-start.5 = (bf16[128,1152]{1,0:T(8,128)(2,1)S(1)}, bf16[128,1152]{1,0:T(8,128)(2,1)S(1)}, u32[]{:S(2)}, u32[]{:S(2)}) collective-permute-start(bf16[128,1152]{1,0:T(8,128)(2,1)S(1)} %shard_map.68.refs_1_.refs_2_), channel_id=1, source_target_pairs={{0,8},{4,12},{8,0},{12,4},{16,24},{20,28},{24,16},{28,20},{1,9},{5... | collective-permute-start | bytes 884744 | tf_op jit(solution)/shard_map/ppermute | solution.py:21
  16.2 9.8 %collective-permute-start.8 = (bf16[64,1152]{1,0:T(8,128)(2,1)S(1)}, bf16[64,1152]{1,0:T(8,128)(2,1)S(1)}, u32[]{:S(2)}, u32[]{:S(2)}) collective-permute-start(bf16[64,1152]{1,0:T(8,128)(2,1)S(1)} %shard_map.69.refs_1_.refs_5_), channel_id=1, source_target_pairs={{0,16},{4,20},{8,24},{12,28},{16,0},{20,4},{24,8},{28,12},{1,17},{... | collective-permute-start | bytes 442376 | tf_op jit(solution)/shard_map/ppermute | solution.py:21
  23.8 5.8 %collective-permute-start.9 = (bf16[64,1152]{1,0:T(8,128)(2,1)S(1)}, bf16[64,1152]{1,0:T(8,128)(2,1)S(1)}, u32[]{:S(2)}, u32[]{:S(2)}) collective-permute-start(bf16[64,1152]{1,0:T(8,128)(2,1)S(1)} %shard_map.70.refs_6_), channel_id=1, source_target_pairs={{0,16},{4,20},{8,24},{12,28},{16,0},{20,4},{24,8},{28,12},{1,17},{... | collective-permute-start | bytes 442376 | tf_op jit(solution)/shard_map/ppermute | solution.py:21
  25.3 4.5 %collective-permute-start.6 = (bf16[768,1152]{1,0:T(8,128)(2,1)S(1)}, bf16[768,1152]{1,0:T(8,128)(2,1)S(1)}, u32[]{:S(2)}, u32[]{:S(2)}) collective-permute-start(bf16[768,1152]{1,0:T(8,128)(2,1)S(1)} %shard_map.71.refs_2_.refs_4_), channel_id=1, source_target_pairs={{0,4},{4,0},{8,12},{12,8},{16,20},{20,16},{24,28},{28,24},{1,5},{5... | collective-permute-start | bytes 5308424 | tf_op jit(solution)/shard_map/ppermute | solution.py:21
  25.4 4.3 %collective-permute-start.7 = (bf16[128,1152]{1,0:T(8,128)(2,1)S(1)}, bf16[128,1152]{1,0:T(8,128)(2,1)S(1)}, u32[]{:S(2)}, u32[]{:S(2)}) collective-permute-start(bf16[128,1152]{1,0:T(8,128)(2,1)S(1)} %shard_map.72.refs_3_.refs_1_), channel_id=1, source_target_pairs={{0,4},{4,0},{8,12},{12,8},{16,20},{20,16},{24,28},{28,24},{1,5},{5... | collective-permute-start | bytes 884744 | tf_op jit(solution)/shard_map/ppermute | solution.py:21
  29.7 3.8 %collective-permute-start.10 = (bf16[128,1152]{1,0:T(8,128)(2,1)S(1)}, bf16[128,1152]{1,0:T(8,128)(2,1)S(1)}, u32[]{:S(2)}, u32[]{:S(2)}) collective-permute-start(bf16[128,1152]{1,0:T(8,128)(2,1)S(1)} %shard_map.76.refs_6_.refs_7_), channel_id=1, source_target_pairs={{0,4},{4,0},{8,12},{12,8},{16,20},{20,16},{24,28},{28,24},{1,5},{5... | collective-permute-start | bytes 884744 | tf_op jit(solution)/shard_map/ppermute | solution.py:21
  32.7 9.5 %collective-permute-start.11 = (bf16[1168,128]{1,0:T(8,128)(2,1)S(1)}, bf16[1168,128]{1,0:T(8,128)(2,1)S(1)}, u32[]{:S(2)}, u32[]{:S(2)}) collective-permute-start(bf16[1168,128]{1,0:T(8,128)(2,1)S(1)} %get-tuple-element.35.refs_9_), channel_id=1, source_target_pairs={{0,16},{4,20},{8,24},{12,28},{16,0},{20,4},{24,8},{28,12},{1,17},{... | collective-permute-start | bytes 897032 | tf_op jit(solution)/shard_map/ppermute | solution.py:21
  36.9 9.2 %collective-permute-start.14 = (bf16[128,1152]{1,0:T(8,128)(2,1)S(1)}, bf16[128,1152]{1,0:T(8,128)(2,1)S(1)}, u32[]{:S(2)}, u32[]{:S(2)}) collective-permute-start(bf16[128,1152]{1,0:T(8,128)(2,1)S(1)} %get-tuple-element.47), channel_id=1, source_target_pairs={{0,8},{4,12},{8,0},{12,4},{16,24},{20,28},{24,16},{28,20},{1,9},{5... | collective-permute-start | bytes 884744 | tf_op jit(solution)/shard_map/ppermute | solution.py:21
  42.3 19.7 %collective-permute-start.13 = (bf16[1168,128]{1,0:T(8,128)(2,1)S(1)}, bf16[1168,128]{1,0:T(8,128)(2,1)S(1)}, u32[]{:S(2)}, u32[]{:S(2)}) collective-permute-start(bf16[1168,128]{1,0:T(8,128)(2,1)S(1)} %get-tuple-element.43), channel_id=1, source_target_pairs={{0,16},{4,20},{8,24},{12,28},{16,0},{20,4},{24,8},{28,12},{1,17},{... | collective-permute-start | bytes 897032 | tf_op jit(solution)/shard_map/ppermute | solution.py:21
  43.1 18.9 %collective-permute-start.12 = (bf16[1168,128]{1,0:T(8,128)(2,1)S(1)}, bf16[1168,128]{1,0:T(8,128)(2,1)S(1)}, u32[]{:S(2)}, u32[]{:S(2)}) collective-permute-start(bf16[1168,128]{1,0:T(8,128)(2,1)S(1)} %get-tuple-element.42.refs_3_), channel_id=1, source_target_pairs={{0,2},{1,3},{2,0},{3,1},{4,6},{5,7},{6,4},{7,5},{8,10},{9,11},{10,... | collective-permute-start | bytes 897032 | tf_op jit(solution)/shard_map/ppermute | solution.py:21
  46.1 14.8 %copy-start.3 = (bf16[128,1152]{1,0:T(8,128)(2,1)S(1)}, bf16[128,1152]{1,0:T(8,128)(2,1)}, u32[]{:S(2)}) copy-start(bf16[128,1152]{1,0:T(8,128)(2,1)} %refs_1_.8) | copy-start | bytes 884740
  46.2 15.8 %copy-start.1 = (bf16[128,1152]{1,0:T(8,128)(2,1)S(1)}, bf16[128,1152]{1,0:T(8,128)(2,1)}, u32[]{:S(2)}) copy-start(bf16[128,1152]{1,0:T(8,128)(2,1)} %refs_1_.7) | copy-start | bytes 884740
  46.2 14.7 %collective-permute-start.15 = (bf16[128,1152]{1,0:T(8,128)(2,1)S(1)}, bf16[128,1152]{1,0:T(8,128)(2,1)S(1)}, u32[]{:S(2)}, u32[]{:S(2)}) collective-permute-start(bf16[128,1152]{1,0:T(8,128)(2,1)S(1)} %get-tuple-element.48), channel_id=1, source_target_pairs={{0,1},{1,0},{2,3},{3,2},{4,5},{5,4},{6,7},{7,6},{8,9},{9,8},{10,11... | collective-permute-start | bytes 884744 | tf_op jit(solution)/shard_map/ppermute | solution.py:21
  46.3 14.6 %collective-permute-start.16 = (bf16[128,1152]{1,0:T(8,128)(2,1)S(1)}, bf16[128,1152]{1,0:T(8,128)(2,1)S(1)}, u32[]{:S(2)}, u32[]{:S(2)}) collective-permute-start(bf16[128,1152]{1,0:T(8,128)(2,1)S(1)} %get-tuple-element.49), channel_id=1, source_target_pairs={{0,8},{4,12},{8,0},{12,4},{16,24},{20,28},{24,16},{28,20},{1,9},{5... | collective-permute-start | bytes 884744 | tf_op jit(solution)/shard_map/ppermute | solution.py:21

commit v9 on v8

--- a/solution.py
+++ b/solution.py
@@ -11,7 +11,7 @@
 f32, bf16 = jnp.float32, jnp.bfloat16
 lanes = 128
 extra = 16
-weights = {"x far": 10, "y far": 10, "x": 0, "a": 10, "b": 10, "late": 2, "text": 2, "end": 0, "text end": 0}
+weights = {"x far": 10, "y far": 10, "x": 0, "a": 10, "b": 10, "late": 2, "text": 2, "end": 5}
 VMEM = pl.BlockSpec(memory_space=pltpu.VMEM)
 SMEM = pl.BlockSpec(memory_space=pltpu.SMEM)
 ANY = pl.BlockSpec(memory_space=pl.ANY)
@@ -198,19 +198,26 @@
         out[...] = loss_ref[:, place * rows : (place + 1) * rows]
 
 
+def swapped_pairs_kernel(scale_ref, bias_ref, near_ref, far_ref, near_swapped_ref, slopes_ref):
+    rows = far_ref.shape[0]
+    own_texts = (near_ref.at[: 3 * rows, :], far_ref)
+    images = (near_swapped_ref.at[3 * rows :, :],)
+    pair_terms(scale_ref[0], bias_ref[0], own_texts, images, slopes_ref, losses=False)
+
+
 def text_kernel(
-    count, scale_ref, bias_ref, near_ref, far_ref, near_swapped_ref, near_slopes_ref, far_slopes_ref, *refs
+    count, scale_ref, bias_ref, near_ref, far_ref, near_swapped_ref, near_slopes_ref, far_slopes_ref, other_slopes_ref, *refs
 ):
     far_refs, far_swapped_refs, outs, slopes_ref = refs[:count], refs[count : 2 * count], refs[2 * count : -1], refs[-1]
     rows, width = far_ref.shape
     own_texts = (near_ref.at[: 3 * rows, :], far_ref)
-    swapped_images = (near_swapped_ref.at[3 * rows :, :], *far_swapped_refs)
-    pair_terms(scale_ref[0], bias_ref[0], own_texts, swapped_images, slopes_ref, losses=False)
-    terms, left = [], near_slopes_ref.shape[1]
+    pair_terms(scale_ref[0], bias_ref[0], own_texts, far_swapped_refs, slopes_ref, losses=False)
+    terms = []
     for slopes, blocks in (
         (near_slopes_ref, (near_ref.at[3 * rows :, :],)),
+        (other_slopes_ref, (near_swapped_ref.at[3 * rows :, :],)),
         (far_slopes_ref, far_refs),
-        (slopes_ref, swapped_images),
+        (slopes_ref, far_swapped_refs),
     ):
         left = 0
         for images in blocks:
@@ -227,8 +234,7 @@
 
 
 def late_image_kernel(zs, ys, *refs):
-    sums, losses, refs = refs[:zs], refs[zs : 2 * zs], refs[2 * zs :]
-    parts, payloads, outs = refs[: zs * ys], refs[zs * ys : zs * ys + ys], refs[zs * ys + ys :]
+    sums, losses, parts, outs = refs[:zs], refs[zs : 2 * zs], refs[2 * zs : -zs], refs[-zs:]
     for k in range(zs):
         height = sums[k].shape[0]
         total, loss = sums[k][...], losses[k][...]
@@ -238,13 +244,13 @@
             loss = loss + (last[0:1, :] + last[1:2, :])
         outs[k][:height, :] = total.astype(bf16)
         outs[k][height:, :] = loss_rows(loss)
-    for source, target in zip(payloads, outs[zs:]):
+
+
+def late_text_kernel(sums_ref, part_ref, *refs):
+    count = len(refs) // 2
+    refs[count][...] = (sums_ref[...] + part_ref[...].astype(f32)).astype(bf16)
+    for source, target in zip(refs[:count], refs[count + 1 :]):
         target[...] = source[...]
-
-
-def late_text_kernel(sums_ref, part_ref, passed_ref, out_ref, passed_out_ref):
-    out_ref[...] = (sums_ref[...] + part_ref[...].astype(f32)).astype(bf16)
-    passed_out_ref[...] = passed_ref[...]
 
 
 def row_gradient(rows, sums, scale, out_ref):
@@ -255,9 +261,9 @@
     ) * inverse
 
 
-def image_end_kernel(batch, scale_ref, image_ref, grad_ref, loss_ref, *refs):
-    parts, (out_ref, out_loss_ref, sums_ref) = refs[:-3], refs[-3:]
-    rows, width = image_ref.shape
+def part_sums_kernel(grad_ref, loss_ref, *refs):
+    parts, (sums_ref, out_loss_ref) = refs[:-2], refs[-2:]
+    rows, width = grad_ref.shape
     loss = loss_ref[...]
     for panel in range(width // lanes):
         cut = slice(panel * lanes, (panel + 1) * lanes)
@@ -268,8 +274,14 @@
     for part in parts:
         last = part[width // lanes * rows :, :].astype(f32)
         loss = loss + (last[0:1, :] + last[1:2, :])
+    out_loss_ref[...] = loss
+
+
+def image_end_kernel(batch, scale_ref, image_ref, grad_ref, loss_ref, *refs):
+    parts, (out_ref, out_loss_ref, sums_ref) = refs[:-3], refs[-3:]
+    part_sums_kernel(grad_ref, loss_ref, *parts, sums_ref, out_loss_ref)
     row_gradient(image_ref[...], sums_ref[...], scale_ref[0], out_ref)
-    out_loss_ref[...] = loss / batch
+    out_loss_ref[...] = out_loss_ref[...] / batch
 
 
 def text_end_kernel(scale_ref, text_ref, grad_ref, *refs):
@@ -342,7 +354,18 @@
         flops=pair_flops * (1 + ys + zs),
         scalars=2,
     )
-    far = call(join_kernel, [block] * (zs * ys), *first_far, *second_far, after=[loss])
+    swapped_slopes = call(
+        swapped_pairs_kernel,
+        near_slopes,
+        scale,
+        bias,
+        *own_texts,
+        near_swapped,
+        flops=pair_flops * (1 + ys + zs),
+        scalars=2,
+        after=[own_slopes],
+    )
+    far = call(join_kernel, [block] * (zs * ys), *first_far, *second_far, after=[swapped_slopes])
     far_swapped = [swapped(emb, "dp", 1) for emb in far]
     other_slopes, loss = call(
         functools.partial(near_pairs_kernel, False),
@@ -354,6 +377,7 @@
         loss,
         flops=pair_flops * (1 + ys + zs),
         scalars=2,
+        after=[swapped_slopes],
     )
     far_slopes, *far_sent = call(
         functools.partial(far_kernel, len(far)),
@@ -378,11 +402,12 @@
         near_swapped,
         own_slopes,
         far_slopes,
+        swapped_slopes,
         *far,
         *far_swapped,
         flops=3 * pair_flops * (1 + ys + zs + len(far)),
         scalars=2,
-        scratch=[pltpu.VMEM((half, near_rows + far_rows), bf16)],
+        scratch=[pltpu.VMEM((half, far_rows), bf16)],
         after=far_sent[:1],
     )
     moved_text = swapped(text_xz_sums, "dp", 2)
@@ -402,24 +427,27 @@
 
     late = call(
         functools.partial(late_image_kernel, zs, ys),
-        [payload] * (zs + ys),
+        [payload] * zs,
         *sums[ys::2],
         *sums[ys + 1 :: 2],
         *moved,
-        *sums[:ys],
         weight=weights["late"],
     )
-    image_parts = [swapped(part, "inner", q) for part, q in zip(late, image_inner)]
-    image_parts += [swapped(part, "dp", p) for part, p in zip(late[zs:], image_dp)]
-    late_text_z, late_text_x = call(
+    z_parts = [swapped(part, "inner", q) for part, q in zip(late, image_inner)]
+    image_grad, own_loss = call(
+        part_sums_kernel, (wide_block, shape((1, rows), f32)), image_grad, own_loss, *z_parts, weight=weights["end"]
+    )
+    late_text_z, late_text_x, *late_y = call(
         late_text_kernel,
-        [block, block],
+        [block, block] + [payload] * ys,
         text_z_sums,
         moved_text,
         text_x_sums,
+        *sums[:ys],
         weight=weights["text"],
         after=late[:1],
     )
+    image_parts = [swapped(part, "dp", p) for part, p in zip(late_y, image_dp)]
     text_parts = [swapped(late_text_z, "inner", 1), swapped(late_text_x, "dp", 2)]
 
     image_gradient, image_loss = call(
@@ -431,11 +459,10 @@
         own_loss,
         *image_parts,
         scalars=1,
-        weight=weights["end"],
         scratch=[pltpu.VMEM((rows, width), f32)],
     )
     text_gradient = call(
-        text_end_kernel, wide_block, scale, text, text_grad, *text_parts, scalars=1, weight=weights["text end"]
+        text_end_kernel, wide_block, scale, text, text_grad, *text_parts, scalars=1, after=[image_gradient]
     )
     return (image_gradient, text_gradient, image_loss.reshape(rows))
 

time: 63.4 us -> 63 us (level)
  waiting for transfers between devices: 29.1 us -> 25.7 us
  local copies, waits for them, and re-layouts: 2.88 us -> 4.81 us
  starting transfers between devices: 16.5 us -> 17.2 us
    ppermute x17, waiting for transfers between devices: 29.1 us -> 25.7 us  [swapped(): lax.ppermute(value, axis, [(place, place ^ step) for place in range(lax.a...]
    unnamed x8 -> x10, local copies, waits for them, and re-layouts: 1.93 us -> 3.86 us
    ppermute x17, starting transfers between devices: 16.5 us -> 17.2 us  [swapped(): lax.ppermute(value, axis, [(place, place ^ step) for place in range(lax.a...]
    pallas_call x17 -> x19, Pallas kernels: 12.6 us -> 12.9 us  [call(): pl.pallas_call(lambda *refs: kernel(*refs[:first], *refs[last:]), out_sha...]
  transfers between devices with their start and end apart: 17 -> 17, of which waited for: 6 -> 7; matrix products, arithmetic and copies ran while one was open for 2% -> 2% of each run, Pallas kernels for 18% -> 19%
where the time goes in v9:
time: 63 us; the launch traced here: 62.7 us
  waiting for transfers between devices  25.7 us (41%)
  starting transfers between devices  17.2 us (27%)
  Pallas kernels  12.9 us (20%)
  local copies, waits for them, and re-layouts  4.81 us (8%)
  between operations  2.13 us (3%)
    ppermute x17, waiting for transfers between devices, swapped(): lax.ppermute(value, axis, [(place, place ^ step) for place in range(lax.a...  25.7 us
    ppermute x17, starting transfers between devices, swapped(): lax.ppermute(value, axis, [(place, place ^ step) for place in range(lax.a...  17.2 us
    pallas_call x19, Pallas kernels, call(): pl.pallas_call(lambda *refs: kernel(*refs[:first], *refs[last:]), out_sha...  12.9 us
    unnamed x10, local copies, waits for them, and re-layouts  3.86 us
  transfers between devices with their start and end apart: 17, of which 7 were waited for; matrix products, arithmetic and copies ran while one was open for 2% of the time, Pallas kernels for 19%

profile of v9, /device:TPU:0, one launch (start us, length us, event | category | flops | bytes accessed | tf_op | source)
XLA Modules:
  0.0 62.7 jit_solution(2024190138607408848)
XLA Ops:
  0.6 3.0 %collective-permute-start = (bf16[128,1152]{1,0:T(8,128)(2,1)}, bf16[128,1152]{1,0:T(8,128)(2,1)S(1)}, u32[]{:S(2)}, u32[]{:S(2)}) collective-permute-start(bf16[128,1152]{1,0:T(8,128)(2,1)} %refs_1_.9), channel_id=1, source_target_pairs={{0,8},{4,12},{8,0},{12,4},{16,24},{20,28},{24,16},{28,20},{1,9},{5... | collective-permute-start | bytes 884744 | tf_op jit(solution)/shard_map/ppermute | solution.py:21
  3.6 1.6 %collective-permute-start.1 = (bf16[128,1152]{1,0:T(8,128)(2,1)}, bf16[128,1152]{1,0:T(8,128)(2,1)S(1)}, u32[]{:S(2)}, u32[]{:S(2)}) collective-permute-start(bf16[128,1152]{1,0:T(8,128)(2,1)} %refs_1_.9), channel_id=1, source_target_pairs={{0,1},{1,0},{2,3},{3,2},{4,5},{5,4},{6,7},{7,6},{8,9},{9,8},{10,11... | collective-permute-start | bytes 884744 | tf_op jit(solution)/shard_map/ppermute | solution.py:21
  5.2 1.5 %collective-permute-start.2 = (bf16[128,1152]{1,0:T(8,128)(2,1)}, bf16[128,1152]{1,0:T(8,128)(2,1)S(1)}, u32[]{:S(2)}, u32[]{:S(2)}) collective-permute-start(bf16[128,1152]{1,0:T(8,128)(2,1)} %refs_1_.8), channel_id=1, source_target_pairs={{0,16},{4,20},{8,24},{12,28},{16,0},{20,4},{24,8},{28,12},{1,17},{... | collective-permute-start | bytes 884744 | tf_op jit(solution)/shard_map/ppermute | solution.py:21
  7.7 2.7 %collective-permute-start.3 = (bf16[64,1152]{1,0:T(8,128)(2,1)S(1)}, bf16[64,1152]{1,0:T(8,128)(2,1)S(1)}, u32[]{:S(2)}, u32[]{:S(2)}) collective-permute-start(bf16[64,1152]{1,0:T(8,128)(2,1)S(1)} %slice.3), channel_id=1, source_target_pairs={{0,2},{1,3},{2,0},{3,1},{4,6},{5,7},{6,4},{7,5},{8,10},{9,11},{10,... | collective-permute-start | bytes 442376 | tf_op jit(solution)/shard_map/ppermute | solution.py:21
  12.6 1.0 %copy-done.2 = bf16[128,1152]{1,0:T(8,128)(2,1)S(1)} copy-done((bf16[128,1152]{1,0:T(8,128)(2,1)S(1)}, bf16[128,1152]{1,0:T(8,128)(2,1)}, u32[]{:S(2)}) %copy-start.2) | copy-done | bytes 294936
  14.2 1.3 %collective-permute-done.1.refs_0_ = bf16[128,1152]{1,0:T(8,128)(2,1)S(1)} collective-permute-done((bf16[128,1152]{1,0:T(8,128)(2,1)}, bf16[128,1152]{1,0:T(8,128)(2,1)S(1)}, u32[]{:S(2)}, u32[]{:S(2)}) %collective-permute-start.1) | collective-permute-done | bytes 294944 | tf_op jit(solution)/shard_map/ppermute | solution.py:21
  16.2 2.1 %collective-permute-start.8 = (bf16[64,1152]{1,0:T(8,128)(2,1)S(1)}, bf16[64,1152]{1,0:T(8,128)(2,1)S(1)}, u32[]{:S(2)}, u32[]{:S(2)}) collective-permute-start(bf16[64,1152]{1,0:T(8,128)(2,1)S(1)} %shard_map.69.refs_1_.refs_5_), channel_id=1, source_target_pairs={{0,16},{4,20},{8,24},{12,28},{16,0},{20,4},{24,8},{28,12},{1,17},{... | collective-permute-start | bytes 442376 | tf_op jit(solution)/shard_map/ppermute | solution.py:21
  18.3 5.5 %collective-permute-done.4.refs_0_ = bf16[64,1152]{1,0:T(8,128)(2,1)S(1)} collective-permute-done((bf16[64,1152]{1,0:T(8,128)(2,1)S(1)}, bf16[64,1152]{1,0:T(8,128)(2,1)S(1)}, u32[]{:S(2)}, u32[]{:S(2)}) %collective-permute-start.4) | collective-permute-done | bytes 147488 | tf_op jit(solution)/shard_map/ppermute | solution.py:21
  23.8 1.2 %collective-permute-start.9 = (bf16[64,1152]{1,0:T(8,128)(2,1)S(1)}, bf16[64,1152]{1,0:T(8,128)(2,1)S(1)}, u32[]{:S(2)}, u32[]{:S(2)}) collective-permute-start(bf16[64,1152]{1,0:T(8,128)(2,1)S(1)} %shard_map.70.refs_6_), channel_id=1, source_target_pairs={{0,16},{4,20},{8,24},{12,28},{16,0},{20,4},{24,8},{28,12},{1,17},{... | collective-permute-start | bytes 442376 | tf_op jit(solution)/shard_map/ppermute | solution.py:21
  26.0 1.3 %shard_map.73 = (bf16[512,384]{1,0:T(8,128)(2,1)S(1)}, f32[1,384]{1,0:T(1,128)S(1)}) custom-call(f32[1]{0:T(128)S(6)} %exp.3.refs_0_, f32[1]{0:T(128)S(6)} %copy.8.refs_1_, bf16[768,1152]{1,0:T(8,128)(2,1)S(1)} %shard_map.71.refs_2_.refs_4_, bf16[128,1152]{1,0:T(8,128)(2,1)S(1)} %shard_map.72.refs_3_.refs_1_, bf16[768,1152]{1,0:T(8,128)(2,1)S(1)} %shard_map.71.refs_2_.refs_4_), custom_call_target="tpu_custom_call" | custom-call | flops 452984832 | bytes 4228616 | tf_op jit(solution)/shard_map/pallas_call | solution.py:28
  27.3 1.8 %collective-permute-done.6.refs_4_.refs_2_ = bf16[768,1152]{1,0:T(8,128)(2,1)S(1)} collective-permute-done((bf16[768,1152]{1,0:T(8,128)(2,1)S(1)}, bf16[768,1152]{1,0:T(8,128)(2,1)S(1)}, u32[]{:S(2)}, u32[]{:S(2)}) %collective-permute-start.6) | collective-permute-done | bytes 1769504 | tf_op jit(solution)/shard_map/ppermute | solution.py:21
  29.1 1.0 %shard_map.74.refs_6_.refs_2_.refs_7_ = bf16[512,384]{1,0:T(8,128)(2,1)S(1)} custom-call(f32[1]{0:T(128)S(6)} %exp.3.refs_0_, f32[1]{0:T(128)S(6)} %copy.8.refs_1_, bf16[768,1152]{1,0:T(8,128)(2,1)S(1)} %shard_map.71.refs_2_.refs_4_, bf16[128,1152]{1,0:T(8,128)(2,1)S(1)} %shard_map.72.refs_3_.refs_1_, ...), custom_call_target="tpu_custom_call" | custom-call | flops 452984832 | bytes 4227080 | tf_op jit(solution)/shard_map/pallas_call | solution.py:28
  30.4 1.3 %shard_map.75 = (bf16[512,384]{1,0:T(8,128)(2,1)S(1)}, f32[1,384]{1,0:T(1,128)S(1)}) custom-call(f32[1]{0:T(128)S(6)} %exp.3.refs_0_, f32[1]{0:T(128)S(6)} %copy.8.refs_1_, bf16[768,1152]{1,0:T(8,128)(2,1)S(1)} %collective-permute-done.6.refs_4_.refs_2_, bf16[128,1152]{1,0:T(8,128)(2,1)S(1)} %collective-permute-done.7.refs_3_.refs_5_, ...), custom_call_target="tpu_custom_call" | custom-call | flops 452984832 | bytes 4230152 | tf_op jit(solution)/shard_map/pallas_call | solution.py:28
  31.6 1.7 %shard_map.78 = (bf16[512,128]{1,0:T(8,128)(2,1)S(1)}, bf16[1168,128]{1,0:T(8,128)(2,1)S(1)}) custom-call(f32[1]{0:T(128)S(6)} %exp.3.refs_0_, f32[1]{0:T(128)S(6)} %copy.8.refs_1_, bf16[768,1152]{1,0:T(8,128)(2,1)S(1)} %shard_map.71.refs_2_.refs_4_, bf16[128,1152]{1,0:T(8,128)(2,1)S(1)} %shard_map.72.refs_3_.refs_1_, ...), custom_call_target="tpu_custom_call" | custom-call | flops 603979776 | bytes 4853768 | tf_op jit(solution)/shard_map/pallas_call | solution.py:28
  33.3 1.0 %collective-permute-start.11 = (bf16[1168,128]{1,0:T(8,128)(2,1)S(1)}, bf16[1168,128]{1,0:T(8,128)(2,1)S(1)}, u32[]{:S(2)}, u32[]{:S(2)}) collective-permute-start(bf16[1168,128]{1,0:T(8,128)(2,1)S(1)} %get-tuple-element.36.refs_10_), channel_id=1, source_target_pairs={{0,16},{4,20},{8,24},{12,28},{16,0},{20,4},{24,8},{28,12},{1,17},{... | collective-permute-start | bytes 897032 | tf_op jit(solution)/shard_map/ppermute | solution.py:21
  34.3 2.6 %shard_map.79 = (f32[128,1152]{1,0:T(8,128)S(1)}, bf16[128,1152]{1,0:T(8,128)(2,1)S(1)}, f32[128,1152]{1,0:T(8,128)S(1)}, bf16[128,1152]{1,0:T(8,128)(2,1)S(1)}) custom-call(f32[1]{0:T(128)S(6)} %exp.3.refs_0_, f32[1]{0:T(128)S(6)} %copy.8.refs_1_, bf16[768,1152]{1,0:T(8,128)(2,1)S(1)} %shard_map.71.refs_2_.refs_4_, ...), custom_call_target="tpu_custom_call" | custom-call | flops 1811939328 | bytes 7110664 | tf_op jit(solution)/shard_map/pallas_call | solution.py:28
  37.4 1.8 %shard_map.80 = (f32[128,1152]{1,0:T(8,128)S(1)}, f32[1,128]{1,0:T(1,128)S(1)}, bf16[1168,128]{1,0:T(8,128)(2,1)S(1)}, f32[1152,128]{1,0:T(8,128)S(1)}, f32[1,128]{1,0:T(1,128)S(1)}) custom-call(bf16[512,384]{1,0:T(8,128)(2,1)S(1)} %get-tuple-element.31.refs_5_.refs_0_, bf16[512,384]{1,0:T(8,128)(2,1)S(1)} %get-tuple-element.33.refs_1_, ...), custom_call_target="tpu_custom_call" | custom-call | flops 905969664 | bytes 6396416 | tf_op jit(solution)/shard_map/pallas_call | solution.py:28
  39.2 3.5 %collective-permute-done.11.refs_2_ = bf16[1168,128]{1,0:T(8,128)(2,1)S(1)} collective-permute-done((bf16[1168,128]{1,0:T(8,128)(2,1)S(1)}, bf16[1168,128]{1,0:T(8,128)(2,1)S(1)}, u32[]{:S(2)}, u32[]{:S(2)}) %collective-permute-start.11) | collective-permute-done | bytes 299040 | tf_op jit(solution)/shard_map/ppermute | solution.py:21
  42.9 3.0 %collective-permute-done.13.refs_1_ = bf16[128,1152]{1,0:T(8,128)(2,1)S(1)} collective-permute-done((bf16[128,1152]{1,0:T(8,128)(2,1)S(1)}, bf16[128,1152]{1,0:T(8,128)(2,1)S(1)}, u32[]{:S(2)}, u32[]{:S(2)}) %collective-permute-start.13) | collective-permute-done | bytes 294944 | tf_op jit(solution)/shard_map/ppermute | solution.py:21
  46.7 1.2 %collective-permute-start.14 = (bf16[1168,128]{1,0:T(8,128)(2,1)S(1)}, bf16[1168,128]{1,0:T(8,128)(2,1)S(1)}, u32[]{:S(2)}, u32[]{:S(2)}) collective-permute-start(bf16[1168,128]{1,0:T(8,128)(2,1)S(1)} %get-tuple-element.47), channel_id=1, source_target_pairs={{0,16},{4,20},{8,24},{12,28},{16,0},{20,4},{24,8},{28,12},{1,17},{... | collective-permute-start | bytes 897032 | tf_op jit(solution)/shard_map/ppermute | solution.py:21
  47.9 10.0 %collective-permute-done.12.refs_2_ = bf16[1168,128]{1,0:T(8,128)(2,1)S(1)} collective-permute-done((bf16[1168,128]{1,0:T(8,128)(2,1)S(1)}, bf16[1168,128]{1,0:T(8,128)(2,1)S(1)}, u32[]{:S(2)}, u32[]{:S(2)}) %collective-permute-start.12) | collective-permute-done | bytes 299040 | tf_op jit(solution)/shard_map/ppermute | solution.py:21
  58.8 1.1 %shard_map.84 = (f32[128,1152]{1,0:T(8,128)}, f32[1,128]{1,0:T(1,128)}) custom-call(f32[1]{0:T(128)S(6)} %exp.3.refs_0_, bf16[128,1152]{1,0:T(8,128)(2,1)S(1)} %copy-done.1, f32[128,1152]{1,0:T(8,128)S(1)} %get-tuple-element.42.refs_2_, f32[1,128]{1,0:T(1,128)S(1)} %get-tuple-element.43.refs_3_, bf16[1168,128]{1,0:T(8,128)(2,1)S(1)} %collective-permute-done.14.refs_4_), custom_call_target="tpu_custom_call" | custom-call | bytes 1774596 | tf_op jit(solution)/shard_map/pallas_call | solution.py:28
  60.6 1.1 %copy-done.4 = f32[128,1152]{1,0:T(8,128)S(1)} copy-done((f32[128,1152]{1,0:T(8,128)S(1)}, f32[128,1152]{1,0:T(8,128)}, u32[]{:S(2)}) %copy-start.4) | copy-done | bytes 589848
  61.6 1.1 %shard_map.85 = f32[128,1152]{1,0:T(8,128)} custom-call(f32[1]{0:T(128)S(6)} %exp.3.refs_0_, bf16[128,1152]{1,0:T(8,128)(2,1)S(1)} %copy-done.3, f32[128,1152]{1,0:T(8,128)S(1)} %get-tuple-element.49.refs_2_, bf16[128,1152]{1,0:T(8,128)(2,1)S(1)} %collective-permute-done.15.refs_3_, bf16[128,1152]{1,0:T(8,128)(2,1)S(1)} %collective-permute-done.16.refs_4_, ...), custom_call_target="tpu_custom_call" | custom-call | bytes 2064388 | tf_op jit(solution)/shard_map/pallas_call | solution.py:28
  (40 shorter events, 7.5 us)
Async XLA Ops:
  0.6 13.6 %collective-permute-start = (bf16[128,1152]{1,0:T(8,128)(2,1)}, bf16[128,1152]{1,0:T(8,128)(2,1)S(1)}, u32[]{:S(2)}, u32[]{:S(2)}) collective-permute-start(bf16[128,1152]{1,0:T(8,128)(2,1)} %refs_1_.9), channel_id=1, source_target_pairs={{0,8},{4,12},{8,0},{12,4},{16,24},{20,28},{24,16},{28,20},{1,9},{5... | collective-permute-start | bytes 884744 | tf_op jit(solution)/shard_map/ppermute | solution.py:21
  3.6 11.8 %collective-permute-start.1 = (bf16[128,1152]{1,0:T(8,128)(2,1)}, bf16[128,1152]{1,0:T(8,128)(2,1)S(1)}, u32[]{:S(2)}, u32[]{:S(2)}) collective-permute-start(bf16[128,1152]{1,0:T(8,128)(2,1)} %refs_1_.9), channel_id=1, source_target_pairs={{0,1},{1,0},{2,3},{3,2},{4,5},{5,4},{6,7},{7,6},{8,9},{9,8},{10,11... | collective-permute-start | bytes 884744 | tf_op jit(solution)/shard_map/ppermute | solution.py:21
  5.2 10.9 %collective-permute-start.2 = (bf16[128,1152]{1,0:T(8,128)(2,1)}, bf16[128,1152]{1,0:T(8,128)(2,1)S(1)}, u32[]{:S(2)}, u32[]{:S(2)}) collective-permute-start(bf16[128,1152]{1,0:T(8,128)(2,1)} %refs_1_.8), channel_id=1, source_target_pairs={{0,16},{4,20},{8,24},{12,28},{16,0},{20,4},{24,8},{28,12},{1,17},{... | collective-permute-start | bytes 884744 | tf_op jit(solution)/shard_map/ppermute | solution.py:21
  7.7 8.4 %collective-permute-start.3 = (bf16[64,1152]{1,0:T(8,128)(2,1)S(1)}, bf16[64,1152]{1,0:T(8,128)(2,1)S(1)}, u32[]{:S(2)}, u32[]{:S(2)}) collective-permute-start(bf16[64,1152]{1,0:T(8,128)(2,1)S(1)} %slice.3), channel_id=1, source_target_pairs={{0,2},{1,3},{2,0},{3,1},{4,6},{5,7},{6,4},{7,5},{8,10},{9,11},{10,... | collective-permute-start | bytes 442376 | tf_op jit(solution)/shard_map/ppermute | solution.py:21
  11.7 1.0 %copy-start = (bf16[128,1152]{1,0:T(8,128)(2,1)S(1)}, bf16[128,1152]{1,0:T(8,128)(2,1)}, u32[]{:S(2)}) copy-start(bf16[128,1152]{1,0:T(8,128)(2,1)} %refs_1_.8) | copy-start | bytes 884740
  12.6 1.0 %copy-start.2 = (bf16[128,1152]{1,0:T(8,128)(2,1)S(1)}, bf16[128,1152]{1,0:T(8,128)(2,1)}, u32[]{:S(2)}) copy-start(bf16[128,1152]{1,0:T(8,128)(2,1)} %refs_1_.9) | copy-start | bytes 884740
  13.8 10.0 %collective-permute-start.4 = (bf16[64,1152]{1,0:T(8,128)(2,1)S(1)}, bf16[64,1152]{1,0:T(8,128)(2,1)S(1)}, u32[]{:S(2)}, u32[]{:S(2)}) collective-permute-start(bf16[64,1152]{1,0:T(8,128)(2,1)S(1)} %get-tuple-element.29.refs_2_), channel_id=1, source_target_pairs={{0,2},{1,3},{2,0},{3,1},{4,6},{5,7},{6,4},{7,5},{8,10},{9,11},{10,... | collective-permute-start | bytes 442376 | tf_op jit(solution)/shard_map/ppermute | solution.py:21
  15.6 9.8 %collective-permute-start.5 = (bf16[128,1152]{1,0:T(8,128)(2,1)S(1)}, bf16[128,1152]{1,0:T(8,128)(2,1)S(1)}, u32[]{:S(2)}, u32[]{:S(2)}) collective-permute-start(bf16[128,1152]{1,0:T(8,128)(2,1)S(1)} %shard_map.68.refs_1_.refs_2_), channel_id=1, source_target_pairs={{0,8},{4,12},{8,0},{12,4},{16,24},{20,28},{24,16},{28,20},{1,9},{5... | collective-permute-start | bytes 884744 | tf_op jit(solution)/shard_map/ppermute | solution.py:21
  16.2 9.8 %collective-permute-start.8 = (bf16[64,1152]{1,0:T(8,128)(2,1)S(1)}, bf16[64,1152]{1,0:T(8,128)(2,1)S(1)}, u32[]{:S(2)}, u32[]{:S(2)}) collective-permute-start(bf16[64,1152]{1,0:T(8,128)(2,1)S(1)} %shard_map.69.refs_1_.refs_5_), channel_id=1, source_target_pairs={{0,16},{4,20},{8,24},{12,28},{16,0},{20,4},{24,8},{28,12},{1,17},{... | collective-permute-start | bytes 442376 | tf_op jit(solution)/shard_map/ppermute | solution.py:21
  23.8 6.3 %collective-permute-start.9 = (bf16[64,1152]{1,0:T(8,128)(2,1)S(1)}, bf16[64,1152]{1,0:T(8,128)(2,1)S(1)}, u32[]{:S(2)}, u32[]{:S(2)}) collective-permute-start(bf16[64,1152]{1,0:T(8,128)(2,1)S(1)} %shard_map.70.refs_6_), channel_id=1, source_target_pairs={{0,16},{4,20},{8,24},{12,28},{16,0},{20,4},{24,8},{28,12},{1,17},{... | collective-permute-start | bytes 442376 | tf_op jit(solution)/shard_map/ppermute | solution.py:21
  25.3 3.8 %collective-permute-start.6 = (bf16[768,1152]{1,0:T(8,128)(2,1)S(1)}, bf16[768,1152]{1,0:T(8,128)(2,1)S(1)}, u32[]{:S(2)}, u32[]{:S(2)}) collective-permute-start(bf16[768,1152]{1,0:T(8,128)(2,1)S(1)} %shard_map.71.refs_2_.refs_4_), channel_id=1, source_target_pairs={{0,4},{4,0},{8,12},{12,8},{16,20},{20,16},{24,28},{28,24},{1,5},{5... | collective-permute-start | bytes 5308424 | tf_op jit(solution)/shard_map/ppermute | solution.py:21
  25.4 4.9 %collective-permute-start.7 = (bf16[128,1152]{1,0:T(8,128)(2,1)S(1)}, bf16[128,1152]{1,0:T(8,128)(2,1)S(1)}, u32[]{:S(2)}, u32[]{:S(2)}) collective-permute-start(bf16[128,1152]{1,0:T(8,128)(2,1)S(1)} %shard_map.72.refs_3_.refs_1_), channel_id=1, source_target_pairs={{0,4},{4,0},{8,12},{12,8},{16,20},{20,16},{24,28},{28,24},{1,5},{5... | collective-permute-start | bytes 884744 | tf_op jit(solution)/shard_map/ppermute | solution.py:21
  30.2 4.1 %collective-permute-start.10 = (bf16[128,1152]{1,0:T(8,128)(2,1)S(1)}, bf16[128,1152]{1,0:T(8,128)(2,1)S(1)}, u32[]{:S(2)}, u32[]{:S(2)}) collective-permute-start(bf16[128,1152]{1,0:T(8,128)(2,1)S(1)} %shard_map.77.refs_6_.refs_8_), channel_id=1, source_target_pairs={{0,4},{4,0},{8,12},{12,8},{16,20},{20,16},{24,28},{28,24},{1,5},{5... | collective-permute-start | bytes 884744 | tf_op jit(solution)/shard_map/ppermute | solution.py:21
  33.3 9.4 %collective-permute-start.11 = (bf16[1168,128]{1,0:T(8,128)(2,1)S(1)}, bf16[1168,128]{1,0:T(8,128)(2,1)S(1)}, u32[]{:S(2)}, u32[]{:S(2)}) collective-permute-start(bf16[1168,128]{1,0:T(8,128)(2,1)S(1)} %get-tuple-element.36.refs_10_), channel_id=1, source_target_pairs={{0,16},{4,20},{8,24},{12,28},{16,0},{20,4},{24,8},{28,12},{1,17},{... | collective-permute-start | bytes 897032 | tf_op jit(solution)/shard_map/ppermute | solution.py:21
  36.9 9.1 %collective-permute-start.13 = (bf16[128,1152]{1,0:T(8,128)(2,1)S(1)}, bf16[128,1152]{1,0:T(8,128)(2,1)S(1)}, u32[]{:S(2)}, u32[]{:S(2)}) collective-permute-start(bf16[128,1152]{1,0:T(8,128)(2,1)S(1)} %get-tuple-element.45), channel_id=1, source_target_pairs={{0,8},{4,12},{8,0},{12,4},{16,24},{20,28},{24,16},{28,20},{1,9},{5... | collective-permute-start | bytes 884744 | tf_op jit(solution)/shard_map/ppermute | solution.py:21
  42.8 15.0 %collective-permute-start.12 = (bf16[1168,128]{1,0:T(8,128)(2,1)S(1)}, bf16[1168,128]{1,0:T(8,128)(2,1)S(1)}, u32[]{:S(2)}, u32[]{:S(2)}) collective-permute-start(bf16[1168,128]{1,0:T(8,128)(2,1)S(1)} %shard_map.81.refs_4_), channel_id=1, source_target_pairs={{0,2},{1,3},{2,0},{3,1},{4,6},{5,7},{6,4},{7,5},{8,10},{9,11},{10,... | collective-permute-start | bytes 897032 | tf_op jit(solution)/shard_map/ppermute | solution.py:21
  46.0 14.5 %collective-permute-start.15 = (bf16[128,1152]{1,0:T(8,128)(2,1)S(1)}, bf16[128,1152]{1,0:T(8,128)(2,1)S(1)}, u32[]{:S(2)}, u32[]{:S(2)}) collective-permute-start(bf16[128,1152]{1,0:T(8,128)(2,1)S(1)} %get-tuple-element.50), channel_id=1, source_target_pairs={{0,1},{1,0},{2,3},{3,2},{4,5},{5,4},{6,7},{7,6},{8,9},{9,8},{10,11... | collective-permute-start | bytes 884744 | tf_op jit(solution)/shard_map/ppermute | solution.py:21
  46.1 14.4 %collective-permute-start.16 = (bf16[128,1152]{1,0:T(8,128)(2,1)S(1)}, bf16[128,1152]{1,0:T(8,128)(2,1)S(1)}, u32[]{:S(2)}, u32[]{:S(2)}) collective-permute-start(bf16[128,1152]{1,0:T(8,128)(2,1)S(1)} %get-tuple-element.51), channel_id=1, source_target_pairs={{0,8},{4,12},{8,0},{12,4},{16,24},{20,28},{24,16},{28,20},{1,9},{5... | collective-permute-start | bytes 884744 | tf_op jit(solution)/shard_map/ppermute | solution.py:21
  46.7 11.2 %collective-permute-start.14 = (bf16[1168,128]{1,0:T(8,128)(2,1)S(1)}, bf16[1168,128]{1,0:T(8,128)(2,1)S(1)}, u32[]{:S(2)}, u32[]{:S(2)}) collective-permute-start(bf16[1168,128]{1,0:T(8,128)(2,1)S(1)} %get-tuple-element.47), channel_id=1, source_target_pairs={{0,16},{4,20},{8,24},{12,28},{16,0},{20,4},{24,8},{28,12},{1,17},{... | collective-permute-start | bytes 897032 | tf_op jit(solution)/shard_map/ppermute | solution.py:21
  57.8 1.0 %copy-start.1 = (bf16[128,1152]{1,0:T(8,128)(2,1)S(1)}, bf16[128,1152]{1,0:T(8,128)(2,1)}, u32[]{:S(2)}) copy-start(bf16[128,1152]{1,0:T(8,128)(2,1)} %refs_1_.8) | copy-start | bytes 884740
  57.8 2.7 %copy-start.3 = (bf16[128,1152]{1,0:T(8,128)(2,1)S(1)}, bf16[128,1152]{1,0:T(8,128)(2,1)}, u32[]{:S(2)}) copy-start(bf16[128,1152]{1,0:T(8,128)(2,1)} %refs_1_.9) | copy-start | bytes 884740
  60.5 1.1 %copy-start.4 = (f32[128,1152]{1,0:T(8,128)S(1)}, f32[128,1152]{1,0:T(8,128)}, u32[]{:S(2)}) copy-start(f32[128,1152]{1,0:T(8,128)} %get-tuple-element.25.refs_5_) | copy-start | bytes 1769476

commit v10 on v9

--- a/solution.py
+++ b/solution.py
@@ -100,7 +100,11 @@
         target[...] = source[...]
 
 
-def own_rows_kernel(scale_ref, bias_ref, text_ref, image_ref, text_emb_ref, image_emb_ref, half_ref):
+def own_rows_kernel(
+    scale_ref, bias_ref, text_ref, image_ref, text_emb_ref, image_emb_ref, half_ref, text_out_ref, image_out_ref
+):
+    text_out_ref[...] = text_ref[...]
+    image_out_ref[...] = image_ref[...]
     text_emb_ref[...] = unit_of(text_ref[...])[0].astype(bf16)
     emb = unit_of(image_ref[...])[0].astype(bf16)
     image_emb_ref[...] = emb
@@ -126,9 +130,9 @@
 def near_pairs_kernel(own, scale_ref, bias_ref, near_ref, far_ref, images_ref, *refs):
     slopes_ref, loss_ref = refs[-2:]
     rows = far_ref.shape[0]
-    texts = (near_ref.at[: 3 * rows, :], far_ref)
+    texts = (near_ref, far_ref)
     loss = pair_terms(
-        scale_ref[0], bias_ref[0], texts, (images_ref.at[3 * rows :, :],), slopes_ref, rows if own else 0
+        scale_ref[0], bias_ref[0], texts, (images_ref,), slopes_ref, rows if own else 0
     )
     loss_ref[...] = loss if own else loss + refs[0][...]
 
@@ -166,8 +170,8 @@
     image_refs, (own_slopes_ref, *sent_refs), other_slopes_ref = refs[:count], refs[count:-1], refs[-1]
     rows, width = far_ref.shape
     scale, offset = scale_ref[0], bias_ref[0]
-    own_texts = (near_ref.at[: 3 * rows, :], far_ref)
-    other_texts = (near_swapped_ref.at[: 3 * rows, :], far_swapped_ref)
+    own_texts = (near_ref, far_ref)
+    other_texts = (near_swapped_ref, far_swapped_ref)
     loss = pair_terms(scale, offset, own_texts, image_refs, own_slopes_ref)
     loss = loss + pair_terms(scale, offset, other_texts, image_refs, other_slopes_ref)
     slopes = (own_slopes_ref, other_slopes_ref)
@@ -184,8 +188,8 @@
     own_ref, own_loss_ref, plain_refs, rest = refs[0], refs[1], refs[2 : 2 + plain], refs[2 + plain :]
     z_refs, z_loss_refs = rest[::2], rest[1::2]
     rows, width = far_ref.shape
-    own_texts = (near_ref.at[: 3 * rows, :], far_ref)
-    other_texts = (near_swapped_ref.at[: 3 * rows, :], far_swapped_ref)
+    own_texts = (near_ref, far_ref)
+    other_texts = (near_swapped_ref, far_swapped_ref)
     slopes = (own_slopes_ref, other_slopes_ref)
     for left, step, total in sums_in_parts(slopes, (own_texts, other_texts), width):
         own_ref[:, left : left + step] = total[:rows, :]
@@ -198,24 +202,31 @@
         out[...] = loss_ref[:, place * rows : (place + 1) * rows]
 
 
-def swapped_pairs_kernel(scale_ref, bias_ref, near_ref, far_ref, near_swapped_ref, slopes_ref):
-    rows = far_ref.shape[0]
-    own_texts = (near_ref.at[: 3 * rows, :], far_ref)
-    images = (near_swapped_ref.at[3 * rows :, :],)
-    pair_terms(scale_ref[0], bias_ref[0], own_texts, images, slopes_ref, losses=False)
+def swapped_pairs_kernel(scale_ref, bias_ref, near_ref, far_ref, images_ref, slopes_ref):
+    pair_terms(scale_ref[0], bias_ref[0], (near_ref, far_ref), (images_ref,), slopes_ref, losses=False)
 
 
 def text_kernel(
-    count, scale_ref, bias_ref, near_ref, far_ref, near_swapped_ref, near_slopes_ref, far_slopes_ref, other_slopes_ref, *refs
+    count,
+    scale_ref,
+    bias_ref,
+    near_ref,
+    far_ref,
+    images_ref,
+    images_swapped_ref,
+    near_slopes_ref,
+    far_slopes_ref,
+    other_slopes_ref,
+    *refs,
 ):
     far_refs, far_swapped_refs, outs, slopes_ref = refs[:count], refs[count : 2 * count], refs[2 * count : -1], refs[-1]
     rows, width = far_ref.shape
-    own_texts = (near_ref.at[: 3 * rows, :], far_ref)
+    own_texts = (near_ref, far_ref)
     pair_terms(scale_ref[0], bias_ref[0], own_texts, far_swapped_refs, slopes_ref, losses=False)
     terms = []
     for slopes, blocks in (
-        (near_slopes_ref, (near_ref.at[3 * rows :, :],)),
-        (other_slopes_ref, (near_swapped_ref.at[3 * rows :, :],)),
+        (near_slopes_ref, (images_ref,)),
+        (other_slopes_ref, (images_swapped_ref,)),
         (far_slopes_ref, far_refs),
         (slopes_ref, far_swapped_refs),
     ):
@@ -307,40 +318,45 @@
     first_half = image[: rows // 2]
     first_z = [swapped(first_half, "inner", q) for q in image_inner]
     images_y = [swapped(image, "dp", p) for p in image_dp]
-    text_emb, image_emb, second_half = call(
-        own_rows_kernel, [block, block, half_block], scale, bias, text, image, scalars=2
+    text_emb, image_emb, second_half, text_rows, image_rows = call(
+        own_rows_kernel, [block, block, half_block, block, block], scale, bias, text, image, scalars=2
     )
     second_z = [swapped(second_half, "inner", q) for q in image_inner]
     zs, ys = len(first_z), len(images_y)
 
     (text_z_emb,) = call(unit_kernel, [block], text_z, weight=weights["x"], after=[text_x, second_half])
-    (far_text,) = call(copies_kernel, [block], swapped(text_z_emb, "dp", 2), weight=weights["x far"])
+    near_texts = call(
+        functools.partial(near_kernel, frozenset({1})),
+        shape((3 * rows, width), bf16),
+        text_emb,
+        text_x,
+        text_z_emb,
+    )
+    texts_swapped = swapped(near_texts, "dp", 1)
     far_places = [(p, q) for q in image_inner for p in image_dp]
     first_z = call(
         unit_kernel, [half_block] * zs, *first_z, weight=weights["a"], after=[text_z_emb, *images_y]
     )
     first_far = [swapped(emb, "dp", p) for emb in first_z for p in image_dp]
+    second_z = call(copies_kernel, [half_block] * zs, *second_z, weight=weights["b"], after=[*first_z, texts_swapped])
+    (far_text,) = call(copies_kernel, [block], swapped(text_z_emb, "dp", 2), weight=weights["x far"], after=second_z)
     first_far = call(
         copies_kernel, [half_block] * (zs * ys), *first_far, weight=weights["y far"], after=[far_text]
     )
-    second_z = call(copies_kernel, [half_block] * zs, *second_z, weight=weights["b"], after=first_z)
     second_far = [swapped(emb, "dp", p) for emb in second_z for p in image_dp]
 
-    near = call(
-        functools.partial(near_kernel, frozenset({1, *range(4, 4 + ys)})),
-        shape(((4 + ys + zs) * rows, width), bf16),
-        text_emb,
-        text_x,
-        text_z_emb,
+    near_images = call(
+        functools.partial(near_kernel, frozenset(range(1, 1 + ys))),
+        shape(((1 + ys + zs) * rows, width), bf16),
         image_emb,
         *images_y,
         *(part for both in zip(first_z, second_z) for part in both),
     )
-    near_swapped = swapped(near, "dp", 1)
+    images_swapped = swapped(near_images, "dp", 1)
     far_text_swapped = swapped(far_text, "dp", 1)
 
     half, near_rows, far_rows = 4 * rows, (1 + ys + zs) * rows, zs * ys * rows
-    own_texts, other_texts = (near, far_text), (near_swapped, far_text_swapped)
+    own_texts, other_texts = (near_texts, far_text), (texts_swapped, far_text_swapped)
     pair_flops = 2 * rows * half * width
     near_slopes, near_loss = shape((half, near_rows), bf16), shape((1, near_rows), f32)
     payload = shape((width // lanes * rows + extra, lanes), bf16)
@@ -350,7 +366,7 @@
         scale,
         bias,
         *own_texts,
-        near,
+        near_images,
         flops=pair_flops * (1 + ys + zs),
         scalars=2,
     )
@@ -360,25 +376,13 @@
         scale,
         bias,
         *own_texts,
-        near_swapped,
+        images_swapped,
         flops=pair_flops * (1 + ys + zs),
         scalars=2,
         after=[own_slopes],
     )
     far = call(join_kernel, [block] * (zs * ys), *first_far, *second_far, after=[swapped_slopes])
     far_swapped = [swapped(emb, "dp", 1) for emb in far]
-    other_slopes, loss = call(
-        functools.partial(near_pairs_kernel, False),
-        (near_slopes, near_loss),
-        scale,
-        bias,
-        *other_texts,
-        near,
-        loss,
-        flops=pair_flops * (1 + ys + zs),
-        scalars=2,
-        after=[swapped_slopes],
-    )
     far_slopes, *far_sent = call(
         functools.partial(far_kernel, len(far)),
         [shape((half, far_rows), bf16)] + [payload] * len(far),
@@ -390,7 +394,7 @@
         flops=4 * pair_flops * len(far),
         scalars=2,
         scratch=[pltpu.VMEM((half, far_rows), bf16)],
-        after=[loss],
+        after=[swapped_slopes],
     )
     moved = [swapped(part, "dp", p) for part, (p, q) in zip(far_sent, far_places)]
     text_grad, text_x_sums, text_z_sums, text_xz_sums = call(
@@ -399,7 +403,8 @@
         scale,
         bias,
         *own_texts,
-        near_swapped,
+        near_images,
+        images_swapped,
         own_slopes,
         far_slopes,
         swapped_slopes,
@@ -411,6 +416,18 @@
         after=far_sent[:1],
     )
     moved_text = swapped(text_xz_sums, "dp", 2)
+    other_slopes, loss = call(
+        functools.partial(near_pairs_kernel, False),
+        (near_slopes, near_loss),
+        scale,
+        bias,
+        *other_texts,
+        near_images,
+        loss,
+        flops=pair_flops * (1 + ys + zs),
+        scalars=2,
+        after=[text_x_sums],
+    )
     image_grad, own_loss, *sums = call(
         functools.partial(near_sums_kernel, ys),
         [wide_block, shape((1, rows), f32)]
@@ -454,7 +471,7 @@
         functools.partial(image_end_kernel, batch),
         (wide_block, shape((1, rows), f32)),
         scale,
-        image,
+        image_rows,
         image_grad,
         own_loss,
         *image_parts,
@@ -462,7 +479,7 @@
         scratch=[pltpu.VMEM((rows, width), f32)],
     )
     text_gradient = call(
-        text_end_kernel, wide_block, scale, text, text_grad, *text_parts, scalars=1, after=[image_gradient]
+        text_end_kernel, wide_block, scale, text_rows, text_grad, *text_parts, scalars=1, after=[image_gradient]
     )
     return (image_gradient, text_gradient, image_loss.reshape(rows))
 

time: 63 us -> 60.1 us (0.954)
  local copies, waits for them, and re-layouts: 4.81 us -> 2.98 us
  waiting for transfers between devices: 25.7 us -> 24 us
    unnamed x10 -> x6, local copies, waits for them, and re-layouts: 3.86 us -> 2.02 us
    ppermute x17 -> x18, waiting for transfers between devices: 25.7 us -> 24 us  [swapped(): lax.ppermute(value, axis, [(place, place ^ step) for place in range(lax.a...]
    ppermute x17 -> x18, starting transfers between devices: 17.2 us -> 17.8 us  [swapped(): lax.ppermute(value, axis, [(place, place ^ step) for place in range(lax.a...]
    pallas_call x19 -> x20, Pallas kernels: 12.9 us -> 12.9 us  [call(): pl.pallas_call(lambda *refs: kernel(*refs[:first], *refs[last:]), out_sha...]
  transfers between devices with their start and end apart: 17 -> 18, of which waited for: 7 -> 7; matrix products, arithmetic and copies ran while one was open for 2% -> 2% of each run, Pallas kernels for 19% -> 20%
where the time goes in v10:
time: 60.1 us; the launch traced here: 59.8 us
  waiting for transfers between devices  24 us (40%)
  starting transfers between devices  17.8 us (30%)
  Pallas kernels  12.9 us (21%)
  local copies, waits for them, and re-layouts  2.98 us (5%)
  between operations  2.16 us (4%)
    ppermute x18, waiting for transfers between devices, swapped(): lax.ppermute(value, axis, [(place, place ^ step) for place in range(lax.a...  24 us
    ppermute x18, starting transfers between devices, swapped(): lax.ppermute(value, axis, [(place, place ^ step) for place in range(lax.a...  17.8 us
    pallas_call x20, Pallas kernels, call(): pl.pallas_call(lambda *refs: kernel(*refs[:first], *refs[last:]), out_sha...  12.9 us
    unnamed x6, local copies, waits for them, and re-layouts  2.02 us
  transfers between devices with their start and end apart: 18, of which 7 were waited for; matrix products, arithmetic and copies ran while one was open for 2% of the time, Pallas kernels for 20%

profile of v10, /device:TPU:0, one launch (start us, length us, event | category | flops | bytes accessed | tf_op | source)
XLA Modules:
  0.0 59.8 jit_solution(955436408073801849)
XLA Ops:
  0.6 3.1 %collective-permute-start.1 = (bf16[128,1152]{1,0:T(8,128)(2,1)}, bf16[128,1152]{1,0:T(8,128)(2,1)S(1)}, u32[]{:S(2)}, u32[]{:S(2)}) collective-permute-start(bf16[128,1152]{1,0:T(8,128)(2,1)} %refs_2_.1), channel_id=1, source_target_pairs={{0,1},{1,0},{2,3},{3,2},{4,5},{5,4},{6,7},{7,6},{8,9},{9,8},{10,11... | collective-permute-start | bytes 884744 | tf_op jit(solution)/shard_map/ppermute | solution.py:21
  3.7 1.5 %collective-permute-start = (bf16[128,1152]{1,0:T(8,128)(2,1)}, bf16[128,1152]{1,0:T(8,128)(2,1)S(1)}, u32[]{:S(2)}, u32[]{:S(2)}) collective-permute-start(bf16[128,1152]{1,0:T(8,128)(2,1)} %refs_2_.1), channel_id=1, source_target_pairs={{0,8},{4,12},{8,0},{12,4},{16,24},{20,28},{24,16},{28,20},{1,9},{5... | collective-permute-start | bytes 884744 | tf_op jit(solution)/shard_map/ppermute | solution.py:21
  5.2 1.5 %collective-permute-start.5 = (bf16[128,1152]{1,0:T(8,128)(2,1)}, bf16[128,1152]{1,0:T(8,128)(2,1)S(1)}, u32[]{:S(2)}, u32[]{:S(2)}) collective-permute-start(bf16[128,1152]{1,0:T(8,128)(2,1)} %refs_3_.1), channel_id=1, source_target_pairs={{0,16},{4,20},{8,24},{12,28},{16,0},{20,4},{24,8},{28,12},{1,17},{... | collective-permute-start | bytes 884744 | tf_op jit(solution)/shard_map/ppermute | solution.py:21
  6.7 1.0 %slice.3 = bf16[64,1152]{1,0:T(8,128)(2,1)S(1)} slice(bf16[128,1152]{1,0:T(8,128)(2,1)} %refs_3_.1), slice={[0:64], [0:1152]} | slice | bytes 294912 | tf_op jit(solution)/shard_map/slice | solution.py:318
  7.7 2.7 %collective-permute-start.4 = (bf16[64,1152]{1,0:T(8,128)(2,1)S(1)}, bf16[64,1152]{1,0:T(8,128)(2,1)S(1)}, u32[]{:S(2)}, u32[]{:S(2)}) collective-permute-start(bf16[64,1152]{1,0:T(8,128)(2,1)S(1)} %slice.3), channel_id=1, source_target_pairs={{0,2},{1,3},{2,0},{3,1},{4,6},{5,7},{6,4},{7,5},{8,10},{9,11},{10,... | collective-permute-start | bytes 442376 | tf_op jit(solution)/shard_map/ppermute | solution.py:21
  11.7 1.0 %copy-done.2 = bf16[128,1152]{1,0:T(8,128)(2,1)S(1)} copy-done((bf16[128,1152]{1,0:T(8,128)(2,1)S(1)}, bf16[128,1152]{1,0:T(8,128)(2,1)}, u32[]{:S(2)}) %copy-start.2) | copy-done | bytes 294936
  13.5 2.6 %collective-permute-start.2 = (bf16[128,1152]{1,0:T(8,128)(2,1)S(1)}, bf16[128,1152]{1,0:T(8,128)(2,1)S(1)}, u32[]{:S(2)}, u32[]{:S(2)}) collective-permute-start(bf16[128,1152]{1,0:T(8,128)(2,1)S(1)} %shard_map.68.refs_2_.refs_1_), channel_id=1, source_target_pairs={{0,8},{4,12},{8,0},{12,4},{16,24},{20,28},{24,16},{28,20},{1,9},{5... | collective-permute-start | bytes 884744 | tf_op jit(solution)/shard_map/ppermute | solution.py:21
  16.3 4.1 %collective-permute-done.4.refs_0_ = bf16[64,1152]{1,0:T(8,128)(2,1)S(1)} collective-permute-done((bf16[64,1152]{1,0:T(8,128)(2,1)S(1)}, bf16[64,1152]{1,0:T(8,128)(2,1)S(1)}, u32[]{:S(2)}, u32[]{:S(2)}) %collective-permute-start.4) | collective-permute-done | bytes 147488 | tf_op jit(solution)/shard_map/ppermute | solution.py:21
  20.6 2.6 %collective-permute-done.3.refs_0_ = bf16[64,1152]{1,0:T(8,128)(2,1)S(1)} collective-permute-done((bf16[64,1152]{1,0:T(8,128)(2,1)S(1)}, bf16[64,1152]{1,0:T(8,128)(2,1)S(1)}, u32[]{:S(2)}, u32[]{:S(2)}) %collective-permute-start.3) | collective-permute-done | bytes 147488 | tf_op jit(solution)/shard_map/ppermute | solution.py:21
  23.2 1.0 %collective-permute-start.10 = (bf16[64,1152]{1,0:T(8,128)(2,1)S(1)}, bf16[64,1152]{1,0:T(8,128)(2,1)S(1)}, u32[]{:S(2)}, u32[]{:S(2)}) collective-permute-start(bf16[64,1152]{1,0:T(8,128)(2,1)S(1)} %shard_map.71.refs_1_.refs_3_), channel_id=1, source_target_pairs={{0,16},{4,20},{8,24},{12,28},{16,0},{20,4},{24,8},{28,12},{1,17},{... | collective-permute-start | bytes 442376 | tf_op jit(solution)/shard_map/ppermute | solution.py:21
  25.8 1.3 %shard_map.74 = (bf16[512,384]{1,0:T(8,128)(2,1)S(1)}, f32[1,384]{1,0:T(1,128)S(1)}) custom-call(f32[1]{0:T(128)S(6)} %exp.3.refs_0_, f32[1]{0:T(128)S(6)} %copy.8.refs_1_, bf16[384,1152]{1,0:T(8,128)(2,1)S(1)} %shard_map.69.refs_2_, bf16[128,1152]{1,0:T(8,128)(2,1)S(1)} %shard_map.72.refs_3_.refs_1_, bf16[384,1152]{1,0:T(8,128)(2,1)S(1)} %shard_map.73.refs_4_), custom_call_target="tpu_custom_call" | custom-call | flops 452984832 | bytes 2459144 | tf_op jit(solution)/shard_map/pallas_call | solution.py:28
  27.1 1.0 %shard_map.76.refs_2_.refs_7_.refs_8_ = bf16[512,384]{1,0:T(8,128)(2,1)S(1)} custom-call(f32[1]{0:T(128)S(6)} %exp.3.refs_0_, f32[1]{0:T(128)S(6)} %copy.8.refs_1_, bf16[384,1152]{1,0:T(8,128)(2,1)S(1)} %shard_map.69.refs_2_, bf16[128,1152]{1,0:T(8,128)(2,1)S(1)} %shard_map.72.refs_3_.refs_1_, bf16[384,1152]{1,0:T(8,128)(2,1)S(1)} %collective-permute-done.8.refs_4_.refs_5_, ...), custom_call_target="tpu_custom_call" | custom-call | flops 452984832 | bytes 2457608 | tf_op jit(solution)/shard_map/pallas_call | solution.py:28
  29.0 1.7 %shard_map.78 = (bf16[512,128]{1,0:T(8,128)(2,1)S(1)}, bf16[1168,128]{1,0:T(8,128)(2,1)S(1)}) custom-call(f32[1]{0:T(128)S(6)} %exp.3.refs_0_, f32[1]{0:T(128)S(6)} %copy.8.refs_1_, bf16[384,1152]{1,0:T(8,128)(2,1)S(1)} %shard_map.69.refs_2_, bf16[128,1152]{1,0:T(8,128)(2,1)S(1)} %shard_map.72.refs_3_.refs_1_, ...), custom_call_target="tpu_custom_call" | custom-call | flops 603979776 | bytes 3084296 | tf_op jit(solution)/shard_map/pallas_call | solution.py:28
  30.7 1.0 %collective-permute-start.12 = (bf16[1168,128]{1,0:T(8,128)(2,1)S(1)}, bf16[1168,128]{1,0:T(8,128)(2,1)S(1)}, u32[]{:S(2)}, u32[]{:S(2)}) collective-permute-start(bf16[1168,128]{1,0:T(8,128)(2,1)S(1)} %get-tuple-element.37.refs_11_), channel_id=1, source_target_pairs={{0,16},{4,20},{8,24},{12,28},{16,0},{20,4},{24,8},{28,12},{1,17},{... | collective-permute-start | bytes 897032 | tf_op jit(solution)/shard_map/ppermute | solution.py:21
  31.7 2.6 %shard_map.79 = (f32[128,1152]{1,0:T(8,128)S(1)}, bf16[128,1152]{1,0:T(8,128)(2,1)S(1)}, f32[128,1152]{1,0:T(8,128)S(1)}, bf16[128,1152]{1,0:T(8,128)(2,1)S(1)}) custom-call(f32[1]{0:T(128)S(6)} %exp.3.refs_0_, f32[1]{0:T(128)S(6)} %copy.8.refs_1_, bf16[384,1152]{1,0:T(8,128)(2,1)S(1)} %shard_map.69.refs_2_, ...), custom_call_target="tpu_custom_call" | custom-call | flops 1811939328 | bytes 6225928 | tf_op jit(solution)/shard_map/pallas_call | solution.py:28
  35.0 1.3 %shard_map.80 = (bf16[512,384]{1,0:T(8,128)(2,1)S(1)}, f32[1,384]{1,0:T(1,128)S(1)}) custom-call(f32[1]{0:T(128)S(6)} %exp.3.refs_0_, f32[1]{0:T(128)S(6)} %copy.8.refs_1_, bf16[384,1152]{1,0:T(8,128)(2,1)S(1)} %collective-permute-done.6.refs_2_.refs_4_, bf16[128,1152]{1,0:T(8,128)(2,1)S(1)} %collective-permute-done.7.refs_5_.refs_3_, ...), custom_call_target="tpu_custom_call" | custom-call | flops 452984832 | bytes 2460680 | tf_op jit(solution)/shard_map/pallas_call | solution.py:28
  36.3 1.8 %shard_map.81 = (f32[128,1152]{1,0:T(8,128)S(1)}, f32[1,128]{1,0:T(1,128)S(1)}, bf16[1168,128]{1,0:T(8,128)(2,1)S(1)}, f32[1152,128]{1,0:T(8,128)S(1)}, f32[1,128]{1,0:T(1,128)S(1)}) custom-call(bf16[512,384]{1,0:T(8,128)(2,1)S(1)} %get-tuple-element.34.refs_5_.refs_6_.refs_0_, bf16[512,384]{1,0:T(8,128)(2,1)S(1)} %get-tuple-element.39.refs_1_, ...), custom_call_target="tpu_custom_call" | custom-call | flops 905969664 | bytes 4626944 | tf_op jit(solution)/shard_map/pallas_call | solution.py:28
  38.0 2.2 %collective-permute-done.12.refs_2_ = bf16[1168,128]{1,0:T(8,128)(2,1)S(1)} collective-permute-done((bf16[1168,128]{1,0:T(8,128)(2,1)S(1)}, bf16[1168,128]{1,0:T(8,128)(2,1)S(1)}, u32[]{:S(2)}, u32[]{:S(2)}) %collective-permute-start.12) | collective-permute-done | bytes 299040 | tf_op jit(solution)/shard_map/ppermute | solution.py:21
  40.4 3.1 %collective-permute-done.14.refs_1_ = bf16[128,1152]{1,0:T(8,128)(2,1)S(1)} collective-permute-done((bf16[128,1152]{1,0:T(8,128)(2,1)S(1)}, bf16[128,1152]{1,0:T(8,128)(2,1)S(1)}, u32[]{:S(2)}, u32[]{:S(2)}) %collective-permute-start.14) | collective-permute-done | bytes 294944 | tf_op jit(solution)/shard_map/ppermute | solution.py:21
  43.6 1.0 %collective-permute-start.16 = (bf16[128,1152]{1,0:T(8,128)(2,1)S(1)}, bf16[128,1152]{1,0:T(8,128)(2,1)S(1)}, u32[]{:S(2)}, u32[]{:S(2)}) collective-permute-start(bf16[128,1152]{1,0:T(8,128)(2,1)S(1)} %get-tuple-element.54), channel_id=1, source_target_pairs={{0,1},{1,0},{2,3},{3,2},{4,5},{5,4},{6,7},{7,6},{8,9},{9,8},{10,11... | collective-permute-start | bytes 884744 | tf_op jit(solution)/shard_map/ppermute | solution.py:21
  46.1 10.3 %collective-permute-done.13.refs_2_ = bf16[1168,128]{1,0:T(8,128)(2,1)S(1)} collective-permute-done((bf16[1168,128]{1,0:T(8,128)(2,1)S(1)}, bf16[1168,128]{1,0:T(8,128)(2,1)S(1)}, u32[]{:S(2)}, u32[]{:S(2)}) %collective-permute-start.13) | collective-permute-done | bytes 299040 | tf_op jit(solution)/shard_map/ppermute | solution.py:21
  56.5 1.1 %shard_map.85 = (f32[128,1152]{1,0:T(8,128)}, f32[1,128]{1,0:T(1,128)}) custom-call(f32[1]{0:T(128)S(6)} %exp.3.refs_0_, bf16[128,1152]{1,0:T(8,128)(2,1)S(1)} %get-tuple-element.30.refs_1_, f32[128,1152]{1,0:T(8,128)S(1)} %get-tuple-element.45.refs_2_, f32[1,128]{1,0:T(1,128)S(1)} %get-tuple-element.46.refs_3_, ...), custom_call_target="tpu_custom_call" | custom-call | bytes 1774596 | tf_op jit(solution)/shard_map/pallas_call | solution.py:28
  57.6 1.1 %copy-done.1 = f32[128,1152]{1,0:T(8,128)S(1)} copy-done((f32[128,1152]{1,0:T(8,128)S(1)}, f32[128,1152]{1,0:T(8,128)}, u32[]{:S(2)}) %copy-start.1) | copy-done | bytes 589848
  58.7 1.1 %shard_map.86 = f32[128,1152]{1,0:T(8,128)} custom-call(f32[1]{0:T(128)S(6)} %exp.3.refs_0_, bf16[128,1152]{1,0:T(8,128)(2,1)S(1)} %get-tuple-element.52.refs_1_, f32[128,1152]{1,0:T(8,128)S(1)} %get-tuple-element.53.refs_2_, bf16[128,1152]{1,0:T(8,128)(2,1)S(1)} %collective-permute-done.16.refs_3_, bf16[128,1152]{1,0:T(8,128)(2,1)S(1)} %collective-permute-done.17.refs_4_, ...), custom_call_target="tpu_custom_call" | custom-call | bytes 2064388 | tf_op jit(solution)/shard_map/pallas_call | solution.py:28
  (39 shorter events, 6.3 us)
Async XLA Ops:
  0.6 11.1 %copy-start = (bf16[128,1152]{1,0:T(8,128)(2,1)S(1)}, bf16[128,1152]{1,0:T(8,128)(2,1)}, u32[]{:S(2)}) copy-start(bf16[128,1152]{1,0:T(8,128)(2,1)} %refs_3_.1) | copy-start | bytes 884740
  0.6 12.7 %collective-permute-start.1 = (bf16[128,1152]{1,0:T(8,128)(2,1)}, bf16[128,1152]{1,0:T(8,128)(2,1)S(1)}, u32[]{:S(2)}, u32[]{:S(2)}) collective-permute-start(bf16[128,1152]{1,0:T(8,128)(2,1)} %refs_2_.1), channel_id=1, source_target_pairs={{0,1},{1,0},{2,3},{3,2},{4,5},{5,4},{6,7},{7,6},{8,9},{9,8},{10,11... | collective-permute-start | bytes 884744 | tf_op jit(solution)/shard_map/ppermute | solution.py:21
  3.7 9.6 %collective-permute-start = (bf16[128,1152]{1,0:T(8,128)(2,1)}, bf16[128,1152]{1,0:T(8,128)(2,1)S(1)}, u32[]{:S(2)}, u32[]{:S(2)}) collective-permute-start(bf16[128,1152]{1,0:T(8,128)(2,1)} %refs_2_.1), channel_id=1, source_target_pairs={{0,8},{4,12},{8,0},{12,4},{16,24},{20,28},{24,16},{28,20},{1,9},{5... | collective-permute-start | bytes 884744 | tf_op jit(solution)/shard_map/ppermute | solution.py:21
  5.2 15.2 %collective-permute-start.5 = (bf16[128,1152]{1,0:T(8,128)(2,1)}, bf16[128,1152]{1,0:T(8,128)(2,1)S(1)}, u32[]{:S(2)}, u32[]{:S(2)}) collective-permute-start(bf16[128,1152]{1,0:T(8,128)(2,1)} %refs_3_.1), channel_id=1, source_target_pairs={{0,16},{4,20},{8,24},{12,28},{16,0},{20,4},{24,8},{28,12},{1,17},{... | collective-permute-start | bytes 884744 | tf_op jit(solution)/shard_map/ppermute | solution.py:21
  7.7 12.7 %collective-permute-start.4 = (bf16[64,1152]{1,0:T(8,128)(2,1)S(1)}, bf16[64,1152]{1,0:T(8,128)(2,1)S(1)}, u32[]{:S(2)}, u32[]{:S(2)}) collective-permute-start(bf16[64,1152]{1,0:T(8,128)(2,1)S(1)} %slice.3), channel_id=1, source_target_pairs={{0,2},{1,3},{2,0},{3,1},{4,6},{5,7},{6,4},{7,5},{8,10},{9,11},{10,... | collective-permute-start | bytes 442376 | tf_op jit(solution)/shard_map/ppermute | solution.py:21
  11.7 1.0 %copy-start.2 = (bf16[128,1152]{1,0:T(8,128)(2,1)S(1)}, bf16[128,1152]{1,0:T(8,128)(2,1)}, u32[]{:S(2)}) copy-start(bf16[128,1152]{1,0:T(8,128)(2,1)} %refs_2_.1) | copy-start | bytes 884740
  12.9 10.3 %collective-permute-start.3 = (bf16[64,1152]{1,0:T(8,128)(2,1)S(1)}, bf16[64,1152]{1,0:T(8,128)(2,1)S(1)}, u32[]{:S(2)}, u32[]{:S(2)}) collective-permute-start(bf16[64,1152]{1,0:T(8,128)(2,1)S(1)} %get-tuple-element.32.refs_2_), channel_id=1, source_target_pairs={{0,2},{1,3},{2,0},{3,1},{4,6},{5,7},{6,4},{7,5},{8,10},{9,11},{10,... | collective-permute-start | bytes 442376 | tf_op jit(solution)/shard_map/ppermute | solution.py:21
  13.5 10.7 %collective-permute-start.2 = (bf16[128,1152]{1,0:T(8,128)(2,1)S(1)}, bf16[128,1152]{1,0:T(8,128)(2,1)S(1)}, u32[]{:S(2)}, u32[]{:S(2)}) collective-permute-start(bf16[128,1152]{1,0:T(8,128)(2,1)S(1)} %shard_map.68.refs_2_.refs_1_), channel_id=1, source_target_pairs={{0,8},{4,12},{8,0},{12,4},{16,24},{20,28},{24,16},{28,20},{1,9},{5... | collective-permute-start | bytes 884744 | tf_op jit(solution)/shard_map/ppermute | solution.py:21
  16.2 7.0 %collective-permute-start.6 = (bf16[384,1152]{1,0:T(8,128)(2,1)S(1)}, bf16[384,1152]{1,0:T(8,128)(2,1)S(1)}, u32[]{:S(2)}, u32[]{:S(2)}) collective-permute-start(bf16[384,1152]{1,0:T(8,128)(2,1)S(1)} %shard_map.69.refs_2_), channel_id=1, source_target_pairs={{0,4},{4,0},{8,12},{12,8},{16,20},{20,16},{24,28},{28,24},{1,5},{5... | collective-permute-start | bytes 2654216 | tf_op jit(solution)/shard_map/ppermute | solution.py:21
  20.5 5.3 %collective-permute-start.9 = (bf16[64,1152]{1,0:T(8,128)(2,1)S(1)}, bf16[64,1152]{1,0:T(8,128)(2,1)S(1)}, u32[]{:S(2)}, u32[]{:S(2)}) collective-permute-start(bf16[64,1152]{1,0:T(8,128)(2,1)S(1)} %shard_map.70.refs_1_.refs_2_), channel_id=1, source_target_pairs={{0,16},{4,20},{8,24},{12,28},{16,0},{20,4},{24,8},{28,12},{1,17},{... | collective-permute-start | bytes 442376 | tf_op jit(solution)/shard_map/ppermute | solution.py:21
  23.2 5.7 %collective-permute-start.10 = (bf16[64,1152]{1,0:T(8,128)(2,1)S(1)}, bf16[64,1152]{1,0:T(8,128)(2,1)S(1)}, u32[]{:S(2)}, u32[]{:S(2)}) collective-permute-start(bf16[64,1152]{1,0:T(8,128)(2,1)S(1)} %shard_map.71.refs_1_.refs_3_), channel_id=1, source_target_pairs={{0,16},{4,20},{8,24},{12,28},{16,0},{20,4},{24,8},{28,12},{1,17},{... | collective-permute-start | bytes 442376 | tf_op jit(solution)/shard_map/ppermute | solution.py:21
  24.2 4.8 %collective-permute-start.7 = (bf16[128,1152]{1,0:T(8,128)(2,1)S(1)}, bf16[128,1152]{1,0:T(8,128)(2,1)S(1)}, u32[]{:S(2)}, u32[]{:S(2)}) collective-permute-start(bf16[128,1152]{1,0:T(8,128)(2,1)S(1)} %shard_map.72.refs_3_.refs_1_), channel_id=1, source_target_pairs={{0,4},{4,0},{8,12},{12,8},{16,20},{20,16},{24,28},{28,24},{1,5},{5... | collective-permute-start | bytes 884744 | tf_op jit(solution)/shard_map/ppermute | solution.py:21
  24.4 2.7 %collective-permute-start.8 = (bf16[384,1152]{1,0:T(8,128)(2,1)S(1)}, bf16[384,1152]{1,0:T(8,128)(2,1)S(1)}, u32[]{:S(2)}, u32[]{:S(2)}) collective-permute-start(bf16[384,1152]{1,0:T(8,128)(2,1)S(1)} %shard_map.73.refs_4_), channel_id=1, source_target_pairs={{0,4},{4,0},{8,12},{12,8},{16,20},{20,16},{24,28},{28,24},{1,5},{5... | collective-permute-start | bytes 2654216 | tf_op jit(solution)/shard_map/ppermute | solution.py:21
  28.9 2.8 %collective-permute-start.11 = (bf16[128,1152]{1,0:T(8,128)(2,1)S(1)}, bf16[128,1152]{1,0:T(8,128)(2,1)S(1)}, u32[]{:S(2)}, u32[]{:S(2)}) collective-permute-start(bf16[128,1152]{1,0:T(8,128)(2,1)S(1)} %shard_map.77.refs_6_.refs_9_), channel_id=1, source_target_pairs={{0,4},{4,0},{8,12},{12,8},{16,20},{20,16},{24,28},{28,24},{1,5},{5... | collective-permute-start | bytes 884744 | tf_op jit(solution)/shard_map/ppermute | solution.py:21
  30.7 9.6 %collective-permute-start.12 = (bf16[1168,128]{1,0:T(8,128)(2,1)S(1)}, bf16[1168,128]{1,0:T(8,128)(2,1)S(1)}, u32[]{:S(2)}, u32[]{:S(2)}) collective-permute-start(bf16[1168,128]{1,0:T(8,128)(2,1)S(1)} %get-tuple-element.37.refs_11_), channel_id=1, source_target_pairs={{0,16},{4,20},{8,24},{12,28},{16,0},{20,4},{24,8},{28,12},{1,17},{... | collective-permute-start | bytes 897032 | tf_op jit(solution)/shard_map/ppermute | solution.py:21
  34.3 9.2 %collective-permute-start.14 = (bf16[128,1152]{1,0:T(8,128)(2,1)S(1)}, bf16[128,1152]{1,0:T(8,128)(2,1)S(1)}, u32[]{:S(2)}, u32[]{:S(2)}) collective-permute-start(bf16[128,1152]{1,0:T(8,128)(2,1)S(1)} %get-tuple-element.48), channel_id=1, source_target_pairs={{0,8},{4,12},{8,0},{12,4},{16,24},{20,28},{24,16},{28,20},{1,9},{5... | collective-permute-start | bytes 884744 | tf_op jit(solution)/shard_map/ppermute | solution.py:21
  40.3 16.2 %collective-permute-start.13 = (bf16[1168,128]{1,0:T(8,128)(2,1)S(1)}, bf16[1168,128]{1,0:T(8,128)(2,1)S(1)}, u32[]{:S(2)}, u32[]{:S(2)}) collective-permute-start(bf16[1168,128]{1,0:T(8,128)(2,1)S(1)} %shard_map.82.refs_4_), channel_id=1, source_target_pairs={{0,2},{1,3},{2,0},{3,1},{4,6},{5,7},{6,4},{7,5},{8,10},{9,11},{10,... | collective-permute-start | bytes 897032 | tf_op jit(solution)/shard_map/ppermute | solution.py:21
  43.6 14.0 %collective-permute-start.16 = (bf16[128,1152]{1,0:T(8,128)(2,1)S(1)}, bf16[128,1152]{1,0:T(8,128)(2,1)S(1)}, u32[]{:S(2)}, u32[]{:S(2)}) collective-permute-start(bf16[128,1152]{1,0:T(8,128)(2,1)S(1)} %get-tuple-element.54), channel_id=1, source_target_pairs={{0,1},{1,0},{2,3},{3,2},{4,5},{5,4},{6,7},{7,6},{8,9},{9,8},{10,11... | collective-permute-start | bytes 884744 | tf_op jit(solution)/shard_map/ppermute | solution.py:21
  44.6 13.1 %collective-permute-start.17 = (bf16[128,1152]{1,0:T(8,128)(2,1)S(1)}, bf16[128,1152]{1,0:T(8,128)(2,1)S(1)}, u32[]{:S(2)}, u32[]{:S(2)}) collective-permute-start(bf16[128,1152]{1,0:T(8,128)(2,1)S(1)} %get-tuple-element.55), channel_id=1, source_target_pairs={{0,8},{4,12},{8,0},{12,4},{16,24},{20,28},{24,16},{28,20},{1,9},{5... | collective-permute-start | bytes 884744 | tf_op jit(solution)/shard_map/ppermute | solution.py:21
  45.3 11.2 %collective-permute-start.15 = (bf16[1168,128]{1,0:T(8,128)(2,1)S(1)}, bf16[1168,128]{1,0:T(8,128)(2,1)S(1)}, u32[]{:S(2)}, u32[]{:S(2)}) collective-permute-start(bf16[1168,128]{1,0:T(8,128)(2,1)S(1)} %get-tuple-element.50), channel_id=1, source_target_pairs={{0,16},{4,20},{8,24},{12,28},{16,0},{20,4},{24,8},{28,12},{1,17},{... | collective-permute-start | bytes 897032 | tf_op jit(solution)/shard_map/ppermute | solution.py:21
  57.6 1.1 %copy-start.1 = (f32[128,1152]{1,0:T(8,128)S(1)}, f32[128,1152]{1,0:T(8,128)}, u32[]{:S(2)}) copy-start(f32[128,1152]{1,0:T(8,128)} %get-tuple-element.27.refs_5_) | copy-start | bytes 1769476

commit v11 on v10

--- a/solution.py
+++ b/solution.py
@@ -11,7 +11,7 @@
 f32, bf16 = jnp.float32, jnp.bfloat16
 lanes = 128
 extra = 16
-weights = {"x far": 10, "y far": 10, "x": 0, "a": 10, "b": 10, "late": 2, "text": 2, "end": 5}
+weights = {"x far": 10, "y far": 10, "x": 0, "a": 10, "b": 10, "late": 2, "gate": 2, "end": 2}
 VMEM = pl.BlockSpec(memory_space=pltpu.VMEM)
 SMEM = pl.BlockSpec(memory_space=pltpu.SMEM)
 ANY = pl.BlockSpec(memory_space=pl.ANY)
@@ -19,6 +19,16 @@
 
 def swapped(value, axis, step):
     return lax.ppermute(value, axis, [(place, place ^ step) for place in range(lax.axis_size(axis))])
+
+
+def swapped_both(value, dp_step, inner_step):
+    dp_count, inner_count = lax.axis_size("dp"), lax.axis_size("inner")
+    pairs = [
+        (d * inner_count + i, (d ^ dp_step) * inner_count + (i ^ inner_step))
+        for d in range(dp_count)
+        for i in range(inner_count)
+    ]
+    return lax.ppermute(value, ("dp", "inner"), pairs)
 
 
 def call(kernel, out_shape, *operands, flops=0, weight=0, scalars=0, scratch=(), after=()):
@@ -257,11 +267,8 @@
         outs[k][height:, :] = loss_rows(loss)
 
 
-def late_text_kernel(sums_ref, part_ref, *refs):
-    count = len(refs) // 2
-    refs[count][...] = (sums_ref[...] + part_ref[...].astype(f32)).astype(bf16)
-    for source, target in zip(refs[:count], refs[count + 1 :]):
-        target[...] = source[...]
+def gate_kernel(out_ref):
+    out_ref[...] = jnp.zeros_like(out_ref)
 
 
 def row_gradient(rows, sums, scale, out_ref):
@@ -399,7 +406,7 @@
     moved = [swapped(part, "dp", p) for part, (p, q) in zip(far_sent, far_places)]
     text_grad, text_x_sums, text_z_sums, text_xz_sums = call(
         functools.partial(text_kernel, len(far)),
-        (wide_block, block, wide_block, block),
+        (wide_block, block, block, block),
         scale,
         bias,
         *own_texts,
@@ -415,7 +422,11 @@
         scratch=[pltpu.VMEM((half, far_rows), bf16)],
         after=far_sent[:1],
     )
-    moved_text = swapped(text_xz_sums, "dp", 2)
+    text_parts = [
+        swapped_both(text_xz_sums, 2, 1),
+        swapped(text_z_sums, "inner", 1),
+        swapped(text_x_sums, "dp", 2),
+    ]
     other_slopes, loss = call(
         functools.partial(near_pairs_kernel, False),
         (near_slopes, near_loss),
@@ -451,21 +462,11 @@
         weight=weights["late"],
     )
     z_parts = [swapped(part, "inner", q) for part, q in zip(late, image_inner)]
+    gate = call(gate_kernel, shape((8, lanes), f32), weight=weights["gate"], after=text_parts[:2])
     image_grad, own_loss = call(
-        part_sums_kernel, (wide_block, shape((1, rows), f32)), image_grad, own_loss, *z_parts, weight=weights["end"]
-    )
-    late_text_z, late_text_x, *late_y = call(
-        late_text_kernel,
-        [block, block] + [payload] * ys,
-        text_z_sums,
-        moved_text,
-        text_x_sums,
-        *sums[:ys],
-        weight=weights["text"],
-        after=late[:1],
-    )
-    image_parts = [swapped(part, "dp", p) for part, p in zip(late_y, image_dp)]
-    text_parts = [swapped(late_text_z, "inner", 1), swapped(late_text_x, "dp", 2)]
+        part_sums_kernel, (wide_block, shape((1, rows), f32)), image_grad, own_loss, *z_parts, weight=weights["end"], after=[gate]
+    )
+    image_parts = [swapped(part, "dp", p) for part, p in zip(sums[:ys], image_dp)]
 
     image_gradient, image_loss = call(
         functools.partial(image_end_kernel, batch),

time: 60.1 us -> 59.8 us (level)
  waiting for transfers between devices: 24 us -> 21 us
  starting transfers between devices: 17.8 us -> 20.5 us
    ppermute x18 -> x17, waiting for transfers between devices: 24 us -> 13.6 us  [swapped(): lax.ppermute(value, axis, [(place, place ^ step) for place in range(lax.a...]
    ppermute x0 -> x1, waiting for transfers between devices: none -> 7.4 us  [swapped_both(): return lax.ppermute(value, ('dp', 'inner'), pairs)]
    ppermute x18 -> x17, starting transfers between devices: 17.8 us -> 20.3 us  [swapped(): lax.ppermute(value, axis, [(place, place ^ step) for place in range(lax.a...]
where the time goes in v11:
time: 59.8 us; the launch traced here: 59.5 us
  waiting for transfers between devices  21 us (35%)
  starting transfers between devices  20.5 us (34%)
  Pallas kernels  12.8 us (21%)
  local copies, waits for them, and re-layouts  2.98 us (5%)
  between operations  2.14 us (4%)
    ppermute x17, starting transfers between devices, swapped(): lax.ppermute(value, axis, [(place, place ^ step) for place in range(lax.a...  20.3 us
    ppermute x17, waiting for transfers between devices, swapped(): lax.ppermute(value, axis, [(place, place ^ step) for place in range(lax.a...  13.6 us
    pallas_call x20, Pallas kernels, call(): pl.pallas_call(lambda *refs: kernel(*refs[:first], *refs[last:]), out_sha...  12.8 us
    ppermute x1, waiting for transfers between devices, swapped_both(): return lax.ppermute(value, ('dp', 'inner'), pairs)  7.4 us
    unnamed x6, local copies, waits for them, and re-layouts  2.03 us
  transfers between devices with their start and end apart: 18, of which 7 were waited for; matrix products, arithmetic and copies ran while one was open for 2% of the time, Pallas kernels for 20%

profile of v11, /device:TPU:0, one launch (start us, length us, event | category | flops | bytes accessed | tf_op | source)
XLA Modules:
  0.0 59.5 jit_solution(5288451978310778849)
XLA Ops:
  0.6 3.1 %collective-permute-start.1 = (bf16[128,1152]{1,0:T(8,128)(2,1)}, bf16[128,1152]{1,0:T(8,128)(2,1)S(1)}, u32[]{:S(2)}, u32[]{:S(2)}) collective-permute-start(bf16[128,1152]{1,0:T(8,128)(2,1)} %refs_2_.1), channel_id=1, source_target_pairs={{0,1},{1,0},{2,3},{3,2},{4,5},{5,4},{6,7},{7,6},{8,9},{9,8},{10,11... | collective-permute-start | bytes 884744 | tf_op jit(solution)/shard_map/ppermute | solution.py:21
  3.7 1.5 %collective-permute-start = (bf16[128,1152]{1,0:T(8,128)(2,1)}, bf16[128,1152]{1,0:T(8,128)(2,1)S(1)}, u32[]{:S(2)}, u32[]{:S(2)}) collective-permute-start(bf16[128,1152]{1,0:T(8,128)(2,1)} %refs_2_.1), channel_id=1, source_target_pairs={{0,8},{4,12},{8,0},{12,4},{16,24},{20,28},{24,16},{28,20},{1,9},{5... | collective-permute-start | bytes 884744 | tf_op jit(solution)/shard_map/ppermute | solution.py:21
  5.2 1.5 %collective-permute-start.5 = (bf16[128,1152]{1,0:T(8,128)(2,1)}, bf16[128,1152]{1,0:T(8,128)(2,1)S(1)}, u32[]{:S(2)}, u32[]{:S(2)}) collective-permute-start(bf16[128,1152]{1,0:T(8,128)(2,1)} %refs_3_.1), channel_id=1, source_target_pairs={{0,16},{4,20},{8,24},{12,28},{16,0},{20,4},{24,8},{28,12},{1,17},{... | collective-permute-start | bytes 884744 | tf_op jit(solution)/shard_map/ppermute | solution.py:21
  7.7 2.7 %collective-permute-start.4 = (bf16[64,1152]{1,0:T(8,128)(2,1)S(1)}, bf16[64,1152]{1,0:T(8,128)(2,1)S(1)}, u32[]{:S(2)}, u32[]{:S(2)}) collective-permute-start(bf16[64,1152]{1,0:T(8,128)(2,1)S(1)} %slice.3), channel_id=1, source_target_pairs={{0,2},{1,3},{2,0},{3,1},{4,6},{5,7},{6,4},{7,5},{8,10},{9,11},{10,... | collective-permute-start | bytes 442376 | tf_op jit(solution)/shard_map/ppermute | solution.py:21
  13.5 2.6 %collective-permute-start.2 = (bf16[128,1152]{1,0:T(8,128)(2,1)S(1)}, bf16[128,1152]{1,0:T(8,128)(2,1)S(1)}, u32[]{:S(2)}, u32[]{:S(2)}) collective-permute-start(bf16[128,1152]{1,0:T(8,128)(2,1)S(1)} %shard_map.68.refs_2_.refs_1_), channel_id=1, source_target_pairs={{0,8},{4,12},{8,0},{12,4},{16,24},{20,28},{24,16},{28,20},{1,9},{5... | collective-permute-start | bytes 884744 | tf_op jit(solution)/shard_map/ppermute | solution.py:21
  16.3 4.1 %collective-permute-done.4.refs_0_ = bf16[64,1152]{1,0:T(8,128)(2,1)S(1)} collective-permute-done((bf16[64,1152]{1,0:T(8,128)(2,1)S(1)}, bf16[64,1152]{1,0:T(8,128)(2,1)S(1)}, u32[]{:S(2)}, u32[]{:S(2)}) %collective-permute-start.4) | collective-permute-done | bytes 147488 | tf_op jit(solution)/shard_map/ppermute | solution.py:21
  20.6 2.6 %collective-permute-done.3.refs_0_ = bf16[64,1152]{1,0:T(8,128)(2,1)S(1)} collective-permute-done((bf16[64,1152]{1,0:T(8,128)(2,1)S(1)}, bf16[64,1152]{1,0:T(8,128)(2,1)S(1)}, u32[]{:S(2)}, u32[]{:S(2)}) %collective-permute-start.3) | collective-permute-done | bytes 147488 | tf_op jit(solution)/shard_map/ppermute | solution.py:21
  23.2 1.0 %collective-permute-start.10 = (bf16[64,1152]{1,0:T(8,128)(2,1)S(1)}, bf16[64,1152]{1,0:T(8,128)(2,1)S(1)}, u32[]{:S(2)}, u32[]{:S(2)}) collective-permute-start(bf16[64,1152]{1,0:T(8,128)(2,1)S(1)} %shard_map.71.refs_1_.refs_3_), channel_id=1, source_target_pairs={{0,16},{4,20},{8,24},{12,28},{16,0},{20,4},{24,8},{28,12},{1,17},{... | collective-permute-start | bytes 442376 | tf_op jit(solution)/shard_map/ppermute | solution.py:21
  25.8 1.3 %shard_map.74 = (bf16[512,384]{1,0:T(8,128)(2,1)S(1)}, f32[1,384]{1,0:T(1,128)S(1)}) custom-call(f32[1]{0:T(128)S(6)} %exp.3.refs_0_, f32[1]{0:T(128)S(6)} %copy.8.refs_1_, bf16[384,1152]{1,0:T(8,128)(2,1)S(1)} %shard_map.69.refs_2_, bf16[128,1152]{1,0:T(8,128)(2,1)S(1)} %shard_map.72.refs_3_.refs_1_, bf16[384,1152]{1,0:T(8,128)(2,1)S(1)} %shard_map.73.refs_4_), custom_call_target="tpu_custom_call" | custom-call | flops 452984832 | bytes 2459144 | tf_op jit(solution)/shard_map/pallas_call | solution.py:38
  27.1 1.0 %shard_map.76.refs_2_.refs_7_.refs_8_ = bf16[512,384]{1,0:T(8,128)(2,1)S(1)} custom-call(f32[1]{0:T(128)S(6)} %exp.3.refs_0_, f32[1]{0:T(128)S(6)} %copy.8.refs_1_, bf16[384,1152]{1,0:T(8,128)(2,1)S(1)} %shard_map.69.refs_2_, bf16[128,1152]{1,0:T(8,128)(2,1)S(1)} %shard_map.72.refs_3_.refs_1_, bf16[384,1152]{1,0:T(8,128)(2,1)S(1)} %collective-permute-done.8.refs_4_.refs_5_, ...), custom_call_target="tpu_custom_call" | custom-call | flops 452984832 | bytes 2457608 | tf_op jit(solution)/shard_map/pallas_call | solution.py:38
  29.0 1.7 %shard_map.78 = (bf16[512,128]{1,0:T(8,128)(2,1)S(1)}, bf16[1168,128]{1,0:T(8,128)(2,1)S(1)}) custom-call(f32[1]{0:T(128)S(6)} %exp.3.refs_0_, f32[1]{0:T(128)S(6)} %copy.8.refs_1_, bf16[384,1152]{1,0:T(8,128)(2,1)S(1)} %shard_map.69.refs_2_, bf16[128,1152]{1,0:T(8,128)(2,1)S(1)} %shard_map.72.refs_3_.refs_1_, ...), custom_call_target="tpu_custom_call" | custom-call | flops 603979776 | bytes 3084296 | tf_op jit(solution)/shard_map/pallas_call | solution.py:38
  30.7 1.0 %collective-permute-start.12 = (bf16[1168,128]{1,0:T(8,128)(2,1)S(1)}, bf16[1168,128]{1,0:T(8,128)(2,1)S(1)}, u32[]{:S(2)}, u32[]{:S(2)}) collective-permute-start(bf16[1168,128]{1,0:T(8,128)(2,1)S(1)} %get-tuple-element.34.refs_11_), channel_id=1, source_target_pairs={{0,16},{4,20},{8,24},{12,28},{16,0},{20,4},{24,8},{28,12},{1,17},{... | collective-permute-start | bytes 897032 | tf_op jit(solution)/shard_map/ppermute | solution.py:21
  31.7 2.6 %shard_map.79 = (f32[128,1152]{1,0:T(8,128)S(1)}, bf16[128,1152]{1,0:T(8,128)(2,1)S(1)}, bf16[128,1152]{1,0:T(8,128)(2,1)S(1)}, bf16[128,1152]{1,0:T(8,128)(2,1)S(1)}) custom-call(f32[1]{0:T(128)S(6)} %exp.3.refs_0_, f32[1]{0:T(128)S(6)} %copy.8.refs_1_, bf16[384,1152]{1,0:T(8,128)(2,1)S(1)} %shard_map.69.refs_2_, ...), custom_call_target="tpu_custom_call" | custom-call | flops 1811939328 | bytes 5931016 | tf_op jit(solution)/shard_map/pallas_call | solution.py:38
  34.5 1.9 %collective-permute-start.15 = (bf16[128,1152]{1,0:T(8,128)(2,1)S(1)}, bf16[128,1152]{1,0:T(8,128)(2,1)S(1)}, u32[]{:S(2)}, u32[]{:S(2)}) collective-permute-start(bf16[128,1152]{1,0:T(8,128)(2,1)S(1)} %get-tuple-element.43), channel_id=1, source_target_pairs={{0,1},{1,0},{2,3},{3,2},{4,5},{5,4},{6,7},{7,6},{8,9},{9,8},{10,11... | collective-permute-start | bytes 884744 | tf_op jit(solution)/shard_map/ppermute | solution.py:21
  36.4 1.3 %shard_map.80 = (bf16[512,384]{1,0:T(8,128)(2,1)S(1)}, f32[1,384]{1,0:T(1,128)S(1)}) custom-call(f32[1]{0:T(128)S(6)} %exp.3.refs_0_, f32[1]{0:T(128)S(6)} %copy.8.refs_1_, bf16[384,1152]{1,0:T(8,128)(2,1)S(1)} %collective-permute-done.6.refs_2_.refs_4_, bf16[128,1152]{1,0:T(8,128)(2,1)S(1)} %collective-permute-done.7.refs_5_.refs_3_, ...), custom_call_target="tpu_custom_call" | custom-call | flops 452984832 | bytes 2460680 | tf_op jit(solution)/shard_map/pallas_call | solution.py:38
  37.7 1.8 %shard_map.81 = (f32[128,1152]{1,0:T(8,128)S(1)}, f32[1,128]{1,0:T(1,128)S(1)}, bf16[1168,128]{1,0:T(8,128)(2,1)S(1)}, f32[1152,128]{1,0:T(8,128)S(1)}, f32[1,128]{1,0:T(1,128)S(1)}) custom-call(bf16[512,384]{1,0:T(8,128)(2,1)S(1)} %get-tuple-element.31.refs_5_.refs_6_.refs_0_, bf16[512,384]{1,0:T(8,128)(2,1)S(1)} %get-tuple-element.36.refs_1_, ...), custom_call_target="tpu_custom_call" | custom-call | flops 905969664 | bytes 4626944 | tf_op jit(solution)/shard_map/pallas_call | solution.py:38
  40.3 1.2 %collective-permute-start.13 = (bf16[1168,128]{1,0:T(8,128)(2,1)S(1)}, bf16[1168,128]{1,0:T(8,128)(2,1)S(1)}, u32[]{:S(2)}, u32[]{:S(2)}) collective-permute-start(bf16[1168,128]{1,0:T(8,128)(2,1)S(1)} %shard_map.82), channel_id=1, source_target_pairs={{0,2},{1,3},{2,0},{3,1},{4,6},{5,7},{6,4},{7,5},{8,10},{9,11},{10,... | collective-permute-start | bytes 897032 | tf_op jit(solution)/shard_map/ppermute | solution.py:21
  41.4 1.4 %collective-permute-start.17 = (bf16[128,1152]{1,0:T(8,128)(2,1)S(1)}, bf16[128,1152]{1,0:T(8,128)(2,1)S(1)}, u32[]{:S(2)}, u32[]{:S(2)}) collective-permute-start(bf16[128,1152]{1,0:T(8,128)(2,1)S(1)} %get-tuple-element.35.refs_6_.refs_7_), channel_id=1, source_target_pairs={{0,8},{4,12},{8,0},{12,4},{16,24},{20,28},{24,16},{28,20},{1,9},{5... | collective-permute-start | bytes 884744 | tf_op jit(solution)/shard_map/ppermute | solution.py:21
  42.8 1.3 %collective-permute-start.16 = (bf16[1168,128]{1,0:T(8,128)(2,1)S(1)}, bf16[1168,128]{1,0:T(8,128)(2,1)S(1)}, u32[]{:S(2)}, u32[]{:S(2)}) collective-permute-start(bf16[1168,128]{1,0:T(8,128)(2,1)S(1)} %get-tuple-element.46), channel_id=1, source_target_pairs={{0,16},{4,20},{8,24},{12,28},{16,0},{20,4},{24,8},{28,12},{1,17},{... | collective-permute-start | bytes 897032 | tf_op jit(solution)/shard_map/ppermute | solution.py:21
  44.1 7.4 %collective-permute-done.14.refs_0_.refs_3_ = bf16[128,1152]{1,0:T(8,128)(2,1)S(1)} collective-permute-done((bf16[128,1152]{1,0:T(8,128)(2,1)S(1)}, bf16[128,1152]{1,0:T(8,128)(2,1)S(1)}, u32[]{:S(2)}, u32[]{:S(2)}) %collective-permute-start.14) | collective-permute-done | bytes 294944 | tf_op jit(solution)/shard_map/ppermute | solution.py:31
  51.5 4.6 %collective-permute-done.15.refs_1_.refs_4_ = bf16[128,1152]{1,0:T(8,128)(2,1)S(1)} collective-permute-done((bf16[128,1152]{1,0:T(8,128)(2,1)S(1)}, bf16[128,1152]{1,0:T(8,128)(2,1)S(1)}, u32[]{:S(2)}, u32[]{:S(2)}) %collective-permute-start.15) | collective-permute-done | bytes 294944 | tf_op jit(solution)/shard_map/ppermute | solution.py:21
  56.2 1.1 %shard_map.85 = (f32[128,1152]{1,0:T(8,128)}, f32[1,128]{1,0:T(1,128)}) custom-call(f32[1]{0:T(128)S(6)} %exp.3.refs_0_, bf16[128,1152]{1,0:T(8,128)(2,1)S(1)} %get-tuple-element.27.refs_1_, f32[128,1152]{1,0:T(8,128)S(1)} %get-tuple-element.44.refs_2_, f32[1,128]{1,0:T(1,128)S(1)} %get-tuple-element.45.refs_3_, ...), custom_call_target="tpu_custom_call" | custom-call | bytes 1774596 | tf_op jit(solution)/shard_map/pallas_call | solution.py:38
  57.3 1.1 %copy-done.1 = f32[128,1152]{1,0:T(8,128)S(1)} copy-done((f32[128,1152]{1,0:T(8,128)S(1)}, f32[128,1152]{1,0:T(8,128)}, u32[]{:S(2)}) %copy-start.1) | copy-done | bytes 589848
  58.4 1.2 %shard_map.86 = f32[128,1152]{1,0:T(8,128)} custom-call(f32[1]{0:T(128)S(6)} %exp.3.refs_0_, bf16[128,1152]{1,0:T(8,128)(2,1)S(1)} %get-tuple-element.48.refs_1_, f32[128,1152]{1,0:T(8,128)S(1)} %get-tuple-element.49.refs_2_, bf16[128,1152]{1,0:T(8,128)(2,1)S(1)} %collective-permute-done.14.refs_0_.refs_3_, ...), custom_call_target="tpu_custom_call" | custom-call | bytes 2359300 | tf_op jit(solution)/shard_map/pallas_call | solution.py:38
  (39 shorter events, 6.7 us)
Async XLA Ops:
  0.6 11.1 %copy-start = (bf16[128,1152]{1,0:T(8,128)(2,1)S(1)}, bf16[128,1152]{1,0:T(8,128)(2,1)}, u32[]{:S(2)}) copy-start(bf16[128,1152]{1,0:T(8,128)(2,1)} %refs_3_.1) | copy-start | bytes 884740
  0.6 12.7 %collective-permute-start.1 = (bf16[128,1152]{1,0:T(8,128)(2,1)}, bf16[128,1152]{1,0:T(8,128)(2,1)S(1)}, u32[]{:S(2)}, u32[]{:S(2)}) collective-permute-start(bf16[128,1152]{1,0:T(8,128)(2,1)} %refs_2_.1), channel_id=1, source_target_pairs={{0,1},{1,0},{2,3},{3,2},{4,5},{5,4},{6,7},{7,6},{8,9},{9,8},{10,11... | collective-permute-start | bytes 884744 | tf_op jit(solution)/shard_map/ppermute | solution.py:21
  3.7 9.6 %collective-permute-start = (bf16[128,1152]{1,0:T(8,128)(2,1)}, bf16[128,1152]{1,0:T(8,128)(2,1)S(1)}, u32[]{:S(2)}, u32[]{:S(2)}) collective-permute-start(bf16[128,1152]{1,0:T(8,128)(2,1)} %refs_2_.1), channel_id=1, source_target_pairs={{0,8},{4,12},{8,0},{12,4},{16,24},{20,28},{24,16},{28,20},{1,9},{5... | collective-permute-start | bytes 884744 | tf_op jit(solution)/shard_map/ppermute | solution.py:21
  5.2 15.2 %collective-permute-start.5 = (bf16[128,1152]{1,0:T(8,128)(2,1)}, bf16[128,1152]{1,0:T(8,128)(2,1)S(1)}, u32[]{:S(2)}, u32[]{:S(2)}) collective-permute-start(bf16[128,1152]{1,0:T(8,128)(2,1)} %refs_3_.1), channel_id=1, source_target_pairs={{0,16},{4,20},{8,24},{12,28},{16,0},{20,4},{24,8},{28,12},{1,17},{... | collective-permute-start | bytes 884744 | tf_op jit(solution)/shard_map/ppermute | solution.py:21
  7.7 12.7 %collective-permute-start.4 = (bf16[64,1152]{1,0:T(8,128)(2,1)S(1)}, bf16[64,1152]{1,0:T(8,128)(2,1)S(1)}, u32[]{:S(2)}, u32[]{:S(2)}) collective-permute-start(bf16[64,1152]{1,0:T(8,128)(2,1)S(1)} %slice.3), channel_id=1, source_target_pairs={{0,2},{1,3},{2,0},{3,1},{4,6},{5,7},{6,4},{7,5},{8,10},{9,11},{10,... | collective-permute-start | bytes 442376 | tf_op jit(solution)/shard_map/ppermute | solution.py:21
  11.7 1.0 %copy-start.2 = (bf16[128,1152]{1,0:T(8,128)(2,1)S(1)}, bf16[128,1152]{1,0:T(8,128)(2,1)}, u32[]{:S(2)}) copy-start(bf16[128,1152]{1,0:T(8,128)(2,1)} %refs_2_.1) | copy-start | bytes 884740
  12.9 10.3 %collective-permute-start.3 = (bf16[64,1152]{1,0:T(8,128)(2,1)S(1)}, bf16[64,1152]{1,0:T(8,128)(2,1)S(1)}, u32[]{:S(2)}, u32[]{:S(2)}) collective-permute-start(bf16[64,1152]{1,0:T(8,128)(2,1)S(1)} %get-tuple-element.29.refs_2_), channel_id=1, source_target_pairs={{0,2},{1,3},{2,0},{3,1},{4,6},{5,7},{6,4},{7,5},{8,10},{9,11},{10,... | collective-permute-start | bytes 442376 | tf_op jit(solution)/shard_map/ppermute | solution.py:21
  13.5 10.7 %collective-permute-start.2 = (bf16[128,1152]{1,0:T(8,128)(2,1)S(1)}, bf16[128,1152]{1,0:T(8,128)(2,1)S(1)}, u32[]{:S(2)}, u32[]{:S(2)}) collective-permute-start(bf16[128,1152]{1,0:T(8,128)(2,1)S(1)} %shard_map.68.refs_2_.refs_1_), channel_id=1, source_target_pairs={{0,8},{4,12},{8,0},{12,4},{16,24},{20,28},{24,16},{28,20},{1,9},{5... | collective-permute-start | bytes 884744 | tf_op jit(solution)/shard_map/ppermute | solution.py:21
  16.2 7.0 %collective-permute-start.6 = (bf16[384,1152]{1,0:T(8,128)(2,1)S(1)}, bf16[384,1152]{1,0:T(8,128)(2,1)S(1)}, u32[]{:S(2)}, u32[]{:S(2)}) collective-permute-start(bf16[384,1152]{1,0:T(8,128)(2,1)S(1)} %shard_map.69.refs_2_), channel_id=1, source_target_pairs={{0,4},{4,0},{8,12},{12,8},{16,20},{20,16},{24,28},{28,24},{1,5},{5... | collective-permute-start | bytes 2654216 | tf_op jit(solution)/shard_map/ppermute | solution.py:21
  20.5 5.3 %collective-permute-start.9 = (bf16[64,1152]{1,0:T(8,128)(2,1)S(1)}, bf16[64,1152]{1,0:T(8,128)(2,1)S(1)}, u32[]{:S(2)}, u32[]{:S(2)}) collective-permute-start(bf16[64,1152]{1,0:T(8,128)(2,1)S(1)} %shard_map.70.refs_1_.refs_2_), channel_id=1, source_target_pairs={{0,16},{4,20},{8,24},{12,28},{16,0},{20,4},{24,8},{28,12},{1,17},{... | collective-permute-start | bytes 442376 | tf_op jit(solution)/shard_map/ppermute | solution.py:21
  23.2 5.7 %collective-permute-start.10 = (bf16[64,1152]{1,0:T(8,128)(2,1)S(1)}, bf16[64,1152]{1,0:T(8,128)(2,1)S(1)}, u32[]{:S(2)}, u32[]{:S(2)}) collective-permute-start(bf16[64,1152]{1,0:T(8,128)(2,1)S(1)} %shard_map.71.refs_1_.refs_3_), channel_id=1, source_target_pairs={{0,16},{4,20},{8,24},{12,28},{16,0},{20,4},{24,8},{28,12},{1,17},{... | collective-permute-start | bytes 442376 | tf_op jit(solution)/shard_map/ppermute | solution.py:21
  24.2 4.8 %collective-permute-start.7 = (bf16[128,1152]{1,0:T(8,128)(2,1)S(1)}, bf16[128,1152]{1,0:T(8,128)(2,1)S(1)}, u32[]{:S(2)}, u32[]{:S(2)}) collective-permute-start(bf16[128,1152]{1,0:T(8,128)(2,1)S(1)} %shard_map.72.refs_3_.refs_1_), channel_id=1, source_target_pairs={{0,4},{4,0},{8,12},{12,8},{16,20},{20,16},{24,28},{28,24},{1,5},{5... | collective-permute-start | bytes 884744 | tf_op jit(solution)/shard_map/ppermute | solution.py:21
  24.4 2.7 %collective-permute-start.8 = (bf16[384,1152]{1,0:T(8,128)(2,1)S(1)}, bf16[384,1152]{1,0:T(8,128)(2,1)S(1)}, u32[]{:S(2)}, u32[]{:S(2)}) collective-permute-start(bf16[384,1152]{1,0:T(8,128)(2,1)S(1)} %shard_map.73.refs_4_), channel_id=1, source_target_pairs={{0,4},{4,0},{8,12},{12,8},{16,20},{20,16},{24,28},{28,24},{1,5},{5... | collective-permute-start | bytes 2654216 | tf_op jit(solution)/shard_map/ppermute | solution.py:21
  28.9 2.8 %collective-permute-start.11 = (bf16[128,1152]{1,0:T(8,128)(2,1)S(1)}, bf16[128,1152]{1,0:T(8,128)(2,1)S(1)}, u32[]{:S(2)}, u32[]{:S(2)}) collective-permute-start(bf16[128,1152]{1,0:T(8,128)(2,1)S(1)} %shard_map.77.refs_6_.refs_9_), channel_id=1, source_target_pairs={{0,4},{4,0},{8,12},{12,8},{16,20},{20,16},{24,28},{28,24},{1,5},{5... | collective-permute-start | bytes 884744 | tf_op jit(solution)/shard_map/ppermute | solution.py:21
  30.7 9.6 %collective-permute-start.12 = (bf16[1168,128]{1,0:T(8,128)(2,1)S(1)}, bf16[1168,128]{1,0:T(8,128)(2,1)S(1)}, u32[]{:S(2)}, u32[]{:S(2)}) collective-permute-start(bf16[1168,128]{1,0:T(8,128)(2,1)S(1)} %get-tuple-element.34.refs_11_), channel_id=1, source_target_pairs={{0,16},{4,20},{8,24},{12,28},{16,0},{20,4},{24,8},{28,12},{1,17},{... | collective-permute-start | bytes 897032 | tf_op jit(solution)/shard_map/ppermute | solution.py:21
  34.3 17.2 %collective-permute-start.14 = (bf16[128,1152]{1,0:T(8,128)(2,1)S(1)}, bf16[128,1152]{1,0:T(8,128)(2,1)S(1)}, u32[]{:S(2)}, u32[]{:S(2)}) collective-permute-start(bf16[128,1152]{1,0:T(8,128)(2,1)S(1)} %get-tuple-element.42), channel_id=1, source_target_pairs={{0,9},{1,8},{2,11},{3,10},{4,13},{5,12},{6,15},{7,14},{8,1},{9,0},... | collective-permute-start | bytes 884744 | tf_op jit(solution)/shard_map/ppermute | solution.py:31
  34.5 21.6 %collective-permute-start.15 = (bf16[128,1152]{1,0:T(8,128)(2,1)S(1)}, bf16[128,1152]{1,0:T(8,128)(2,1)S(1)}, u32[]{:S(2)}, u32[]{:S(2)}) collective-permute-start(bf16[128,1152]{1,0:T(8,128)(2,1)S(1)} %get-tuple-element.43), channel_id=1, source_target_pairs={{0,1},{1,0},{2,3},{3,2},{4,5},{5,4},{6,7},{7,6},{8,9},{9,8},{10,11... | collective-permute-start | bytes 884744 | tf_op jit(solution)/shard_map/ppermute | solution.py:21
  40.3 15.8 %collective-permute-start.13 = (bf16[1168,128]{1,0:T(8,128)(2,1)S(1)}, bf16[1168,128]{1,0:T(8,128)(2,1)S(1)}, u32[]{:S(2)}, u32[]{:S(2)}) collective-permute-start(bf16[1168,128]{1,0:T(8,128)(2,1)S(1)} %shard_map.82), channel_id=1, source_target_pairs={{0,2},{1,3},{2,0},{3,1},{4,6},{5,7},{6,4},{7,5},{8,10},{9,11},{10,... | collective-permute-start | bytes 897032 | tf_op jit(solution)/shard_map/ppermute | solution.py:21
  41.4 15.8 %collective-permute-start.17 = (bf16[128,1152]{1,0:T(8,128)(2,1)S(1)}, bf16[128,1152]{1,0:T(8,128)(2,1)S(1)}, u32[]{:S(2)}, u32[]{:S(2)}) collective-permute-start(bf16[128,1152]{1,0:T(8,128)(2,1)S(1)} %get-tuple-element.35.refs_6_.refs_7_), channel_id=1, source_target_pairs={{0,8},{4,12},{8,0},{12,4},{16,24},{20,28},{24,16},{28,20},{1,9},{5... | collective-permute-start | bytes 884744 | tf_op jit(solution)/shard_map/ppermute | solution.py:21
  42.8 13.4 %collective-permute-start.16 = (bf16[1168,128]{1,0:T(8,128)(2,1)S(1)}, bf16[1168,128]{1,0:T(8,128)(2,1)S(1)}, u32[]{:S(2)}, u32[]{:S(2)}) collective-permute-start(bf16[1168,128]{1,0:T(8,128)(2,1)S(1)} %get-tuple-element.46), channel_id=1, source_target_pairs={{0,16},{4,20},{8,24},{12,28},{16,0},{20,4},{24,8},{28,12},{1,17},{... | collective-permute-start | bytes 897032 | tf_op jit(solution)/shard_map/ppermute | solution.py:21
  57.3 1.1 %copy-start.1 = (f32[128,1152]{1,0:T(8,128)S(1)}, f32[128,1152]{1,0:T(8,128)}, u32[]{:S(2)}) copy-start(f32[128,1152]{1,0:T(8,128)} %get-tuple-element.24.refs_6_) | copy-start | bytes 1769476

commit v12 on v11

--- a/solution.py
+++ b/solution.py
@@ -11,7 +11,7 @@
 f32, bf16 = jnp.float32, jnp.bfloat16
 lanes = 128
 extra = 16
-weights = {"x far": 10, "y far": 10, "x": 0, "a": 10, "b": 10, "late": 2, "gate": 2, "end": 2}
+weights = {"x far": 10, "y far": 10, "x": 0, "a": 10, "b": 10, "late": 2, "gate": 2}
 VMEM = pl.BlockSpec(memory_space=pltpu.VMEM)
 SMEM = pl.BlockSpec(memory_space=pltpu.SMEM)
 ANY = pl.BlockSpec(memory_space=pl.ANY)
@@ -255,7 +255,8 @@
 
 
 def late_image_kernel(zs, ys, *refs):
-    sums, losses, parts, outs = refs[:zs], refs[zs : 2 * zs], refs[2 * zs : -zs], refs[-zs:]
+    sums, losses, refs = refs[:zs], refs[zs : 2 * zs], refs[2 * zs :]
+    parts, payloads, outs = refs[: zs * ys], refs[zs * ys : zs * ys + ys], refs[zs * ys + ys :]
     for k in range(zs):
         height = sums[k].shape[0]
         total, loss = sums[k][...], losses[k][...]
@@ -265,6 +266,8 @@
             loss = loss + (last[0:1, :] + last[1:2, :])
         outs[k][:height, :] = total.astype(bf16)
         outs[k][height:, :] = loss_rows(loss)
+    for source, target in zip(payloads, outs[zs:]):
+        target[...] = source[...]
 
 
 def gate_kernel(out_ref):
@@ -279,34 +282,25 @@
     ) * inverse
 
 
-def part_sums_kernel(grad_ref, loss_ref, *refs):
-    parts, (sums_ref, out_loss_ref) = refs[:-2], refs[-2:]
-    rows, width = grad_ref.shape
+def end_kernel(batch, images, scale_ref, image_ref, text_ref, grad_ref, loss_ref, text_grad_ref, *refs):
+    parts, text_parts, (out_ref, text_out_ref, out_loss_ref, sums_ref) = refs[:images], refs[images:-4], refs[-4:]
+    rows, width = image_ref.shape
     loss = loss_ref[...]
+    for part in parts:
+        last = part[width // lanes * rows :, :].astype(f32)
+        loss = loss + (last[0:1, :] + last[1:2, :])
+    out_loss_ref[...] = loss / batch
     for panel in range(width // lanes):
         cut = slice(panel * lanes, (panel + 1) * lanes)
         sums = grad_ref[:, cut]
         for part in parts:
             sums = sums + part[panel * rows : (panel + 1) * rows, :].astype(f32)
         sums_ref[:, cut] = sums
-    for part in parts:
-        last = part[width // lanes * rows :, :].astype(f32)
-        loss = loss + (last[0:1, :] + last[1:2, :])
-    out_loss_ref[...] = loss
-
-
-def image_end_kernel(batch, scale_ref, image_ref, grad_ref, loss_ref, *refs):
-    parts, (out_ref, out_loss_ref, sums_ref) = refs[:-3], refs[-3:]
-    part_sums_kernel(grad_ref, loss_ref, *parts, sums_ref, out_loss_ref)
     row_gradient(image_ref[...], sums_ref[...], scale_ref[0], out_ref)
-    out_loss_ref[...] = out_loss_ref[...] / batch
-
-
-def text_end_kernel(scale_ref, text_ref, grad_ref, *refs):
-    sums = grad_ref[...]
-    for r in refs[:-1]:
-        sums = sums + r[...].astype(f32)
-    row_gradient(text_ref[...], sums, scale_ref[0], refs[-1])
+    sums = text_grad_ref[...]
+    for part in text_parts:
+        sums = sums + part[...].astype(f32)
+    row_gradient(text_ref[...], sums, scale_ref[0], text_out_ref)
 
 
 def body(image, text, logarithm_scale, bias):
@@ -455,32 +449,30 @@
 
     late = call(
         functools.partial(late_image_kernel, zs, ys),
-        [payload] * zs,
+        [payload] * (zs + ys),
         *sums[ys::2],
         *sums[ys + 1 :: 2],
         *moved,
+        *sums[:ys],
         weight=weights["late"],
     )
     z_parts = [swapped(part, "inner", q) for part, q in zip(late, image_inner)]
     gate = call(gate_kernel, shape((8, lanes), f32), weight=weights["gate"], after=text_parts[:2])
-    image_grad, own_loss = call(
-        part_sums_kernel, (wide_block, shape((1, rows), f32)), image_grad, own_loss, *z_parts, weight=weights["end"], after=[gate]
-    )
-    image_parts = [swapped(part, "dp", p) for part, p in zip(sums[:ys], image_dp)]
-
-    image_gradient, image_loss = call(
-        functools.partial(image_end_kernel, batch),
-        (wide_block, shape((1, rows), f32)),
+    image_parts = [*z_parts, *(swapped(part, "dp", p) for part, p in zip(late[zs:], image_dp))]
+    image_gradient, text_gradient, image_loss = call(
+        functools.partial(end_kernel, batch, len(image_parts)),
+        (wide_block, wide_block, shape((1, rows), f32)),
         scale,
         image_rows,
+        text_rows,
         image_grad,
         own_loss,
+        text_grad,
         *image_parts,
+        *text_parts,
         scalars=1,
         scratch=[pltpu.VMEM((rows, width), f32)],
-    )
-    text_gradient = call(
-        text_end_kernel, wide_block, scale, text_rows, text_grad, *text_parts, scalars=1, after=[image_gradient]
+        after=[gate],
     )
     return (image_gradient, text_gradient, image_loss.reshape(rows))
 

time: 59.8 us -> 57.9 us (0.968)
  local copies, waits for them, and re-layouts: 2.98 us -> 1.92 us
  Pallas kernels: 12.8 us -> 12.1 us
    unnamed x6 -> x4, local copies, waits for them, and re-layouts: 2.03 us -> 0.96 us
    pallas_call x20 -> x18, Pallas kernels: 12.8 us -> 12.1 us  [call(): pl.pallas_call(lambda *refs: kernel(*refs[:first], *refs[last:]), out_sha...]
  transfers between devices with their start and end apart: 18 -> 18, of which waited for: 7 -> 7; matrix products, arithmetic and copies ran while one was open for 2% -> 2% of each run, Pallas kernels for 20% -> 18%
where the time goes in v12:
time: 57.9 us; the launch traced here: 57.7 us
  waiting for transfers between devices  21 us (36%)
  starting transfers between devices  20.6 us (36%)
  Pallas kernels  12.1 us (21%)
  between operations  2.14 us (4%)
  local copies, waits for them, and re-layouts  1.92 us (3%)
    ppermute x17, starting transfers between devices, swapped(): lax.ppermute(value, axis, [(place, place ^ step) for place in range(lax.a...  20.3 us
    ppermute x17, waiting for transfers between devices, swapped(): lax.ppermute(value, axis, [(place, place ^ step) for place in range(lax.a...  13.6 us
    pallas_call x18, Pallas kernels, call(): pl.pallas_call(lambda *refs: kernel(*refs[:first], *refs[last:]), out_sha...  12.1 us
    ppermute x1, waiting for transfers between devices, swapped_both(): return lax.ppermute(value, ('dp', 'inner'), pairs)  7.39 us
  transfers between devices with their start and end apart: 18, of which 7 were waited for; matrix products, arithmetic and copies ran while one was open for 2% of the time, Pallas kernels for 18%

profile of v12, /device:TPU:0, one launch (start us, length us, event | category | flops | bytes accessed | tf_op | source)
XLA Modules:
  0.0 57.7 jit_solution(15812601881939277615)
XLA Ops:
  0.6 3.1 %collective-permute-start.1 = (bf16[128,1152]{1,0:T(8,128)(2,1)}, bf16[128,1152]{1,0:T(8,128)(2,1)S(1)}, u32[]{:S(2)}, u32[]{:S(2)}) collective-permute-start(bf16[128,1152]{1,0:T(8,128)(2,1)} %refs_2_.1), channel_id=1, source_target_pairs={{0,1},{1,0},{2,3},{3,2},{4,5},{5,4},{6,7},{7,6},{8,9},{9,8},{10,11... | collective-permute-start | bytes 884744 | tf_op jit(solution)/shard_map/ppermute | solution.py:21
  3.7 1.5 %collective-permute-start = (bf16[128,1152]{1,0:T(8,128)(2,1)}, bf16[128,1152]{1,0:T(8,128)(2,1)S(1)}, u32[]{:S(2)}, u32[]{:S(2)}) collective-permute-start(bf16[128,1152]{1,0:T(8,128)(2,1)} %refs_2_.1), channel_id=1, source_target_pairs={{0,8},{4,12},{8,0},{12,4},{16,24},{20,28},{24,16},{28,20},{1,9},{5... | collective-permute-start | bytes 884744 | tf_op jit(solution)/shard_map/ppermute | solution.py:21
  5.2 1.5 %collective-permute-start.5 = (bf16[128,1152]{1,0:T(8,128)(2,1)}, bf16[128,1152]{1,0:T(8,128)(2,1)S(1)}, u32[]{:S(2)}, u32[]{:S(2)}) collective-permute-start(bf16[128,1152]{1,0:T(8,128)(2,1)} %refs_3_.1), channel_id=1, source_target_pairs={{0,16},{4,20},{8,24},{12,28},{16,0},{20,4},{24,8},{28,12},{1,17},{... | collective-permute-start | bytes 884744 | tf_op jit(solution)/shard_map/ppermute | solution.py:21
  6.7 1.0 %slice.3 = bf16[64,1152]{1,0:T(8,128)(2,1)S(1)} slice(bf16[128,1152]{1,0:T(8,128)(2,1)} %refs_3_.1), slice={[0:64], [0:1152]} | slice | bytes 294912 | tf_op jit(solution)/shard_map/slice | solution.py:319
  7.7 2.7 %collective-permute-start.4 = (bf16[64,1152]{1,0:T(8,128)(2,1)S(1)}, bf16[64,1152]{1,0:T(8,128)(2,1)S(1)}, u32[]{:S(2)}, u32[]{:S(2)}) collective-permute-start(bf16[64,1152]{1,0:T(8,128)(2,1)S(1)} %slice.3), channel_id=1, source_target_pairs={{0,2},{1,3},{2,0},{3,1},{4,6},{5,7},{6,4},{7,5},{8,10},{9,11},{10,... | collective-permute-start | bytes 442376 | tf_op jit(solution)/shard_map/ppermute | solution.py:21
  11.7 1.0 %copy-done.1 = bf16[128,1152]{1,0:T(8,128)(2,1)S(1)} copy-done((bf16[128,1152]{1,0:T(8,128)(2,1)S(1)}, bf16[128,1152]{1,0:T(8,128)(2,1)}, u32[]{:S(2)}) %copy-start.1) | copy-done | bytes 294936
  13.5 2.6 %collective-permute-start.2 = (bf16[128,1152]{1,0:T(8,128)(2,1)S(1)}, bf16[128,1152]{1,0:T(8,128)(2,1)S(1)}, u32[]{:S(2)}, u32[]{:S(2)}) collective-permute-start(bf16[128,1152]{1,0:T(8,128)(2,1)S(1)} %shard_map.68.refs_2_.refs_1_), channel_id=1, source_target_pairs={{0,8},{4,12},{8,0},{12,4},{16,24},{20,28},{24,16},{28,20},{1,9},{5... | collective-permute-start | bytes 884744 | tf_op jit(solution)/shard_map/ppermute | solution.py:21
  16.3 4.1 %collective-permute-done.4.refs_0_ = bf16[64,1152]{1,0:T(8,128)(2,1)S(1)} collective-permute-done((bf16[64,1152]{1,0:T(8,128)(2,1)S(1)}, bf16[64,1152]{1,0:T(8,128)(2,1)S(1)}, u32[]{:S(2)}, u32[]{:S(2)}) %collective-permute-start.4) | collective-permute-done | bytes 147488 | tf_op jit(solution)/shard_map/ppermute | solution.py:21
  20.6 2.6 %collective-permute-done.3.refs_0_ = bf16[64,1152]{1,0:T(8,128)(2,1)S(1)} collective-permute-done((bf16[64,1152]{1,0:T(8,128)(2,1)S(1)}, bf16[64,1152]{1,0:T(8,128)(2,1)S(1)}, u32[]{:S(2)}, u32[]{:S(2)}) %collective-permute-start.3) | collective-permute-done | bytes 147488 | tf_op jit(solution)/shard_map/ppermute | solution.py:21
  23.2 1.0 %collective-permute-start.10 = (bf16[64,1152]{1,0:T(8,128)(2,1)S(1)}, bf16[64,1152]{1,0:T(8,128)(2,1)S(1)}, u32[]{:S(2)}, u32[]{:S(2)}) collective-permute-start(bf16[64,1152]{1,0:T(8,128)(2,1)S(1)} %shard_map.71.refs_1_.refs_3_), channel_id=1, source_target_pairs={{0,16},{4,20},{8,24},{12,28},{16,0},{20,4},{24,8},{28,12},{1,17},{... | collective-permute-start | bytes 442376 | tf_op jit(solution)/shard_map/ppermute | solution.py:21
  25.8 1.3 %shard_map.74 = (bf16[512,384]{1,0:T(8,128)(2,1)S(1)}, f32[1,384]{1,0:T(1,128)S(1)}) custom-call(f32[1]{0:T(128)S(6)} %exp.3.refs_0_, f32[1]{0:T(128)S(6)} %copy.8.refs_1_, bf16[384,1152]{1,0:T(8,128)(2,1)S(1)} %shard_map.69.refs_2_, bf16[128,1152]{1,0:T(8,128)(2,1)S(1)} %shard_map.72.refs_3_.refs_1_, bf16[384,1152]{1,0:T(8,128)(2,1)S(1)} %shard_map.73.refs_4_), custom_call_target="tpu_custom_call" | custom-call | flops 452984832 | bytes 2459144 | tf_op jit(solution)/shard_map/pallas_call | solution.py:38
  27.1 1.0 %shard_map.76.refs_2_.refs_7_.refs_8_ = bf16[512,384]{1,0:T(8,128)(2,1)S(1)} custom-call(f32[1]{0:T(128)S(6)} %exp.3.refs_0_, f32[1]{0:T(128)S(6)} %copy.8.refs_1_, bf16[384,1152]{1,0:T(8,128)(2,1)S(1)} %shard_map.69.refs_2_, bf16[128,1152]{1,0:T(8,128)(2,1)S(1)} %shard_map.72.refs_3_.refs_1_, bf16[384,1152]{1,0:T(8,128)(2,1)S(1)} %collective-permute-done.8.refs_4_.refs_5_, ...), custom_call_target="tpu_custom_call" | custom-call | flops 452984832 | bytes 2457608 | tf_op jit(solution)/shard_map/pallas_call | solution.py:38
  29.0 1.7 %shard_map.78 = (bf16[512,128]{1,0:T(8,128)(2,1)S(1)}, bf16[1168,128]{1,0:T(8,128)(2,1)S(1)}) custom-call(f32[1]{0:T(128)S(6)} %exp.3.refs_0_, f32[1]{0:T(128)S(6)} %copy.8.refs_1_, bf16[384,1152]{1,0:T(8,128)(2,1)S(1)} %shard_map.69.refs_2_, bf16[128,1152]{1,0:T(8,128)(2,1)S(1)} %shard_map.72.refs_3_.refs_1_, ...), custom_call_target="tpu_custom_call" | custom-call | flops 603979776 | bytes 3084296 | tf_op jit(solution)/shard_map/pallas_call | solution.py:38
  30.7 1.0 %collective-permute-start.12 = (bf16[1168,128]{1,0:T(8,128)(2,1)S(1)}, bf16[1168,128]{1,0:T(8,128)(2,1)S(1)}, u32[]{:S(2)}, u32[]{:S(2)}) collective-permute-start(bf16[1168,128]{1,0:T(8,128)(2,1)S(1)} %get-tuple-element.36.refs_11_), channel_id=1, source_target_pairs={{0,16},{4,20},{8,24},{12,28},{16,0},{20,4},{24,8},{28,12},{1,17},{... | collective-permute-start | bytes 897032 | tf_op jit(solution)/shard_map/ppermute | solution.py:21
  31.7 2.6 %shard_map.79 = (f32[128,1152]{1,0:T(8,128)S(1)}, bf16[128,1152]{1,0:T(8,128)(2,1)S(1)}, bf16[128,1152]{1,0:T(8,128)(2,1)S(1)}, bf16[128,1152]{1,0:T(8,128)(2,1)S(1)}) custom-call(f32[1]{0:T(128)S(6)} %exp.3.refs_0_, f32[1]{0:T(128)S(6)} %copy.8.refs_1_, bf16[384,1152]{1,0:T(8,128)(2,1)S(1)} %shard_map.69.refs_2_, ...), custom_call_target="tpu_custom_call" | custom-call | flops 1811939328 | bytes 5931016 | tf_op jit(solution)/shard_map/pallas_call | solution.py:38
  34.6 1.9 %collective-permute-start.16 = (bf16[128,1152]{1,0:T(8,128)(2,1)S(1)}, bf16[128,1152]{1,0:T(8,128)(2,1)S(1)}, u32[]{:S(2)}, u32[]{:S(2)}) collective-permute-start(bf16[128,1152]{1,0:T(8,128)(2,1)S(1)} %get-tuple-element.49), channel_id=1, source_target_pairs={{0,1},{1,0},{2,3},{3,2},{4,5},{5,4},{6,7},{7,6},{8,9},{9,8},{10,11... | collective-permute-start | bytes 884744 | tf_op jit(solution)/shard_map/ppermute | solution.py:21
  36.4 1.3 %shard_map.80 = (bf16[512,384]{1,0:T(8,128)(2,1)S(1)}, f32[1,384]{1,0:T(1,128)S(1)}) custom-call(f32[1]{0:T(128)S(6)} %exp.3.refs_0_, f32[1]{0:T(128)S(6)} %copy.8.refs_1_, bf16[384,1152]{1,0:T(8,128)(2,1)S(1)} %collective-permute-done.6.refs_2_.refs_4_, bf16[128,1152]{1,0:T(8,128)(2,1)S(1)} %collective-permute-done.7.refs_5_.refs_3_, ...), custom_call_target="tpu_custom_call" | custom-call | flops 452984832 | bytes 2460680 | tf_op jit(solution)/shard_map/pallas_call | solution.py:38
  37.7 1.8 %shard_map.81 = (f32[128,1152]{1,0:T(8,128)S(1)}, f32[1,128]{1,0:T(1,128)S(1)}, bf16[1168,128]{1,0:T(8,128)(2,1)S(1)}, f32[1152,128]{1,0:T(8,128)S(1)}, f32[1,128]{1,0:T(1,128)S(1)}) custom-call(bf16[512,384]{1,0:T(8,128)(2,1)S(1)} %get-tuple-element.33.refs_5_.refs_6_.refs_0_, bf16[512,384]{1,0:T(8,128)(2,1)S(1)} %get-tuple-element.38.refs_1_, ...), custom_call_target="tpu_custom_call" | custom-call | flops 905969664 | bytes 4626944 | tf_op jit(solution)/shard_map/pallas_call | solution.py:38
  40.3 1.2 %collective-permute-start.13 = (bf16[1168,128]{1,0:T(8,128)(2,1)S(1)}, bf16[1168,128]{1,0:T(8,128)(2,1)S(1)}, u32[]{:S(2)}, u32[]{:S(2)}) collective-permute-start(bf16[1168,128]{1,0:T(8,128)(2,1)S(1)} %get-tuple-element.46), channel_id=1, source_target_pairs={{0,2},{1,3},{2,0},{3,1},{4,6},{5,7},{6,4},{7,5},{8,10},{9,11},{10,... | collective-permute-start | bytes 897032 | tf_op jit(solution)/shard_map/ppermute | solution.py:21
  41.5 1.4 %collective-permute-start.14 = (bf16[1168,128]{1,0:T(8,128)(2,1)S(1)}, bf16[1168,128]{1,0:T(8,128)(2,1)S(1)}, u32[]{:S(2)}, u32[]{:S(2)}) collective-permute-start(bf16[1168,128]{1,0:T(8,128)(2,1)S(1)} %get-tuple-element.47), channel_id=1, source_target_pairs={{0,16},{4,20},{8,24},{12,28},{16,0},{20,4},{24,8},{28,12},{1,17},{... | collective-permute-start | bytes 897032 | tf_op jit(solution)/shard_map/ppermute | solution.py:21
  42.9 1.3 %collective-permute-start.17 = (bf16[128,1152]{1,0:T(8,128)(2,1)S(1)}, bf16[128,1152]{1,0:T(8,128)(2,1)S(1)}, u32[]{:S(2)}, u32[]{:S(2)}) collective-permute-start(bf16[128,1152]{1,0:T(8,128)(2,1)S(1)} %get-tuple-element.37.refs_6_.refs_7_), channel_id=1, source_target_pairs={{0,8},{4,12},{8,0},{12,4},{16,24},{20,28},{24,16},{28,20},{1,9},{5... | collective-permute-start | bytes 884744 | tf_op jit(solution)/shard_map/ppermute | solution.py:21
  44.1 7.4 %collective-permute-done.15.refs_0_.refs_8_ = bf16[128,1152]{1,0:T(8,128)(2,1)S(1)} collective-permute-done((bf16[128,1152]{1,0:T(8,128)(2,1)S(1)}, bf16[128,1152]{1,0:T(8,128)(2,1)S(1)}, u32[]{:S(2)}, u32[]{:S(2)}) %collective-permute-start.15) | collective-permute-done | bytes 294944 | tf_op jit(solution)/shard_map/ppermute | solution.py:31
  51.5 4.6 %collective-permute-done.16.refs_1_.refs_9_ = bf16[128,1152]{1,0:T(8,128)(2,1)S(1)} collective-permute-done((bf16[128,1152]{1,0:T(8,128)(2,1)S(1)}, bf16[128,1152]{1,0:T(8,128)(2,1)S(1)}, u32[]{:S(2)}, u32[]{:S(2)}) %collective-permute-start.16) | collective-permute-done | bytes 294944 | tf_op jit(solution)/shard_map/ppermute | solution.py:21
  56.2 1.6 %shard_map.84 = (f32[128,1152]{1,0:T(8,128)}, f32[128,1152]{1,0:T(8,128)}, f32[1,128]{1,0:T(1,128)}) custom-call(f32[1]{0:T(128)S(6)} %exp.3.refs_0_, bf16[128,1152]{1,0:T(8,128)(2,1)S(1)} %get-tuple-element.28.refs_1_, bf16[128,1152]{1,0:T(8,128)(2,1)S(1)} %get-tuple-element.29.refs_2_, f32[128,1152]{1,0:T(8,128)S(1)} %get-tuple-element.40.refs_3_, ...), custom_call_target="tpu_custom_call" | custom-call | bytes 4432900 | tf_op jit(solution)/shard_map/pallas_call | solution.py:38
  (35 shorter events, 4.8 us)
Async XLA Ops:
  0.6 11.1 %copy-start = (bf16[128,1152]{1,0:T(8,128)(2,1)S(1)}, bf16[128,1152]{1,0:T(8,128)(2,1)}, u32[]{:S(2)}) copy-start(bf16[128,1152]{1,0:T(8,128)(2,1)} %refs_3_.1) | copy-start | bytes 884740
  0.6 12.7 %collective-permute-start.1 = (bf16[128,1152]{1,0:T(8,128)(2,1)}, bf16[128,1152]{1,0:T(8,128)(2,1)S(1)}, u32[]{:S(2)}, u32[]{:S(2)}) collective-permute-start(bf16[128,1152]{1,0:T(8,128)(2,1)} %refs_2_.1), channel_id=1, source_target_pairs={{0,1},{1,0},{2,3},{3,2},{4,5},{5,4},{6,7},{7,6},{8,9},{9,8},{10,11... | collective-permute-start | bytes 884744 | tf_op jit(solution)/shard_map/ppermute | solution.py:21
  3.7 9.6 %collective-permute-start = (bf16[128,1152]{1,0:T(8,128)(2,1)}, bf16[128,1152]{1,0:T(8,128)(2,1)S(1)}, u32[]{:S(2)}, u32[]{:S(2)}) collective-permute-start(bf16[128,1152]{1,0:T(8,128)(2,1)} %refs_2_.1), channel_id=1, source_target_pairs={{0,8},{4,12},{8,0},{12,4},{16,24},{20,28},{24,16},{28,20},{1,9},{5... | collective-permute-start | bytes 884744 | tf_op jit(solution)/shard_map/ppermute | solution.py:21
  5.2 15.2 %collective-permute-start.5 = (bf16[128,1152]{1,0:T(8,128)(2,1)}, bf16[128,1152]{1,0:T(8,128)(2,1)S(1)}, u32[]{:S(2)}, u32[]{:S(2)}) collective-permute-start(bf16[128,1152]{1,0:T(8,128)(2,1)} %refs_3_.1), channel_id=1, source_target_pairs={{0,16},{4,20},{8,24},{12,28},{16,0},{20,4},{24,8},{28,12},{1,17},{... | collective-permute-start | bytes 884744 | tf_op jit(solution)/shard_map/ppermute | solution.py:21
  7.7 12.7 %collective-permute-start.4 = (bf16[64,1152]{1,0:T(8,128)(2,1)S(1)}, bf16[64,1152]{1,0:T(8,128)(2,1)S(1)}, u32[]{:S(2)}, u32[]{:S(2)}) collective-permute-start(bf16[64,1152]{1,0:T(8,128)(2,1)S(1)} %slice.3), channel_id=1, source_target_pairs={{0,2},{1,3},{2,0},{3,1},{4,6},{5,7},{6,4},{7,5},{8,10},{9,11},{10,... | collective-permute-start | bytes 442376 | tf_op jit(solution)/shard_map/ppermute | solution.py:21
  11.7 1.0 %copy-start.1 = (bf16[128,1152]{1,0:T(8,128)(2,1)S(1)}, bf16[128,1152]{1,0:T(8,128)(2,1)}, u32[]{:S(2)}) copy-start(bf16[128,1152]{1,0:T(8,128)(2,1)} %refs_2_.1) | copy-start | bytes 884740
  12.9 10.3 %collective-permute-start.3 = (bf16[64,1152]{1,0:T(8,128)(2,1)S(1)}, bf16[64,1152]{1,0:T(8,128)(2,1)S(1)}, u32[]{:S(2)}, u32[]{:S(2)}) collective-permute-start(bf16[64,1152]{1,0:T(8,128)(2,1)S(1)} %get-tuple-element.31.refs_2_), channel_id=1, source_target_pairs={{0,2},{1,3},{2,0},{3,1},{4,6},{5,7},{6,4},{7,5},{8,10},{9,11},{10,... | collective-permute-start | bytes 442376 | tf_op jit(solution)/shard_map/ppermute | solution.py:21
  13.5 10.7 %collective-permute-start.2 = (bf16[128,1152]{1,0:T(8,128)(2,1)S(1)}, bf16[128,1152]{1,0:T(8,128)(2,1)S(1)}, u32[]{:S(2)}, u32[]{:S(2)}) collective-permute-start(bf16[128,1152]{1,0:T(8,128)(2,1)S(1)} %shard_map.68.refs_2_.refs_1_), channel_id=1, source_target_pairs={{0,8},{4,12},{8,0},{12,4},{16,24},{20,28},{24,16},{28,20},{1,9},{5... | collective-permute-start | bytes 884744 | tf_op jit(solution)/shard_map/ppermute | solution.py:21
  16.2 7.0 %collective-permute-start.6 = (bf16[384,1152]{1,0:T(8,128)(2,1)S(1)}, bf16[384,1152]{1,0:T(8,128)(2,1)S(1)}, u32[]{:S(2)}, u32[]{:S(2)}) collective-permute-start(bf16[384,1152]{1,0:T(8,128)(2,1)S(1)} %shard_map.69.refs_2_), channel_id=1, source_target_pairs={{0,4},{4,0},{8,12},{12,8},{16,20},{20,16},{24,28},{28,24},{1,5},{5... | collective-permute-start | bytes 2654216 | tf_op jit(solution)/shard_map/ppermute | solution.py:21
  20.5 5.3 %collective-permute-start.9 = (bf16[64,1152]{1,0:T(8,128)(2,1)S(1)}, bf16[64,1152]{1,0:T(8,128)(2,1)S(1)}, u32[]{:S(2)}, u32[]{:S(2)}) collective-permute-start(bf16[64,1152]{1,0:T(8,128)(2,1)S(1)} %shard_map.70.refs_1_.refs_2_), channel_id=1, source_target_pairs={{0,16},{4,20},{8,24},{12,28},{16,0},{20,4},{24,8},{28,12},{1,17},{... | collective-permute-start | bytes 442376 | tf_op jit(solution)/shard_map/ppermute | solution.py:21
  23.2 5.7 %collective-permute-start.10 = (bf16[64,1152]{1,0:T(8,128)(2,1)S(1)}, bf16[64,1152]{1,0:T(8,128)(2,1)S(1)}, u32[]{:S(2)}, u32[]{:S(2)}) collective-permute-start(bf16[64,1152]{1,0:T(8,128)(2,1)S(1)} %shard_map.71.refs_1_.refs_3_), channel_id=1, source_target_pairs={{0,16},{4,20},{8,24},{12,28},{16,0},{20,4},{24,8},{28,12},{1,17},{... | collective-permute-start | bytes 442376 | tf_op jit(solution)/shard_map/ppermute | solution.py:21
  24.2 4.8 %collective-permute-start.7 = (bf16[128,1152]{1,0:T(8,128)(2,1)S(1)}, bf16[128,1152]{1,0:T(8,128)(2,1)S(1)}, u32[]{:S(2)}, u32[]{:S(2)}) collective-permute-start(bf16[128,1152]{1,0:T(8,128)(2,1)S(1)} %shard_map.72.refs_3_.refs_1_), channel_id=1, source_target_pairs={{0,4},{4,0},{8,12},{12,8},{16,20},{20,16},{24,28},{28,24},{1,5},{5... | collective-permute-start | bytes 884744 | tf_op jit(solution)/shard_map/ppermute | solution.py:21
  24.4 2.7 %collective-permute-start.8 = (bf16[384,1152]{1,0:T(8,128)(2,1)S(1)}, bf16[384,1152]{1,0:T(8,128)(2,1)S(1)}, u32[]{:S(2)}, u32[]{:S(2)}) collective-permute-start(bf16[384,1152]{1,0:T(8,128)(2,1)S(1)} %shard_map.73.refs_4_), channel_id=1, source_target_pairs={{0,4},{4,0},{8,12},{12,8},{16,20},{20,16},{24,28},{28,24},{1,5},{5... | collective-permute-start | bytes 2654216 | tf_op jit(solution)/shard_map/ppermute | solution.py:21
  28.9 2.8 %collective-permute-start.11 = (bf16[128,1152]{1,0:T(8,128)(2,1)S(1)}, bf16[128,1152]{1,0:T(8,128)(2,1)S(1)}, u32[]{:S(2)}, u32[]{:S(2)}) collective-permute-start(bf16[128,1152]{1,0:T(8,128)(2,1)S(1)} %shard_map.77.refs_6_.refs_9_), channel_id=1, source_target_pairs={{0,4},{4,0},{8,12},{12,8},{16,20},{20,16},{24,28},{28,24},{1,5},{5... | collective-permute-start | bytes 884744 | tf_op jit(solution)/shard_map/ppermute | solution.py:21
  30.7 9.6 %collective-permute-start.12 = (bf16[1168,128]{1,0:T(8,128)(2,1)S(1)}, bf16[1168,128]{1,0:T(8,128)(2,1)S(1)}, u32[]{:S(2)}, u32[]{:S(2)}) collective-permute-start(bf16[1168,128]{1,0:T(8,128)(2,1)S(1)} %get-tuple-element.36.refs_11_), channel_id=1, source_target_pairs={{0,16},{4,20},{8,24},{12,28},{16,0},{20,4},{24,8},{28,12},{1,17},{... | collective-permute-start | bytes 897032 | tf_op jit(solution)/shard_map/ppermute | solution.py:21
  34.3 17.2 %collective-permute-start.15 = (bf16[128,1152]{1,0:T(8,128)(2,1)S(1)}, bf16[128,1152]{1,0:T(8,128)(2,1)S(1)}, u32[]{:S(2)}, u32[]{:S(2)}) collective-permute-start(bf16[128,1152]{1,0:T(8,128)(2,1)S(1)} %get-tuple-element.48), channel_id=1, source_target_pairs={{0,9},{1,8},{2,11},{3,10},{4,13},{5,12},{6,15},{7,14},{8,1},{9,0},... | collective-permute-start | bytes 884744 | tf_op jit(solution)/shard_map/ppermute | solution.py:31
  34.6 21.6 %collective-permute-start.16 = (bf16[128,1152]{1,0:T(8,128)(2,1)S(1)}, bf16[128,1152]{1,0:T(8,128)(2,1)S(1)}, u32[]{:S(2)}, u32[]{:S(2)}) collective-permute-start(bf16[128,1152]{1,0:T(8,128)(2,1)S(1)} %get-tuple-element.49), channel_id=1, source_target_pairs={{0,1},{1,0},{2,3},{3,2},{4,5},{5,4},{6,7},{7,6},{8,9},{9,8},{10,11... | collective-permute-start | bytes 884744 | tf_op jit(solution)/shard_map/ppermute | solution.py:21
  40.3 15.9 %collective-permute-start.13 = (bf16[1168,128]{1,0:T(8,128)(2,1)S(1)}, bf16[1168,128]{1,0:T(8,128)(2,1)S(1)}, u32[]{:S(2)}, u32[]{:S(2)}) collective-permute-start(bf16[1168,128]{1,0:T(8,128)(2,1)S(1)} %get-tuple-element.46), channel_id=1, source_target_pairs={{0,2},{1,3},{2,0},{3,1},{4,6},{5,7},{6,4},{7,5},{8,10},{9,11},{10,... | collective-permute-start | bytes 897032 | tf_op jit(solution)/shard_map/ppermute | solution.py:21
  41.5 14.7 %collective-permute-start.14 = (bf16[1168,128]{1,0:T(8,128)(2,1)S(1)}, bf16[1168,128]{1,0:T(8,128)(2,1)S(1)}, u32[]{:S(2)}, u32[]{:S(2)}) collective-permute-start(bf16[1168,128]{1,0:T(8,128)(2,1)S(1)} %get-tuple-element.47), channel_id=1, source_target_pairs={{0,16},{4,20},{8,24},{12,28},{16,0},{20,4},{24,8},{28,12},{1,17},{... | collective-permute-start | bytes 897032 | tf_op jit(solution)/shard_map/ppermute | solution.py:21
  42.9 13.3 %collective-permute-start.17 = (bf16[128,1152]{1,0:T(8,128)(2,1)S(1)}, bf16[128,1152]{1,0:T(8,128)(2,1)S(1)}, u32[]{:S(2)}, u32[]{:S(2)}) collective-permute-start(bf16[128,1152]{1,0:T(8,128)(2,1)S(1)} %get-tuple-element.37.refs_6_.refs_7_), channel_id=1, source_target_pairs={{0,8},{4,12},{8,0},{12,4},{16,24},{20,28},{24,16},{28,20},{1,9},{5... | collective-permute-start | bytes 884744 | tf_op jit(solution)/shard_map/ppermute | solution.py:21

commit v13 on v12

--- a/solution.py
+++ b/solution.py
@@ -58,46 +58,47 @@
     return wide * inverse, inverse
 
 
+def joined(refs):
+    return refs[0][...] if len(refs) == 1 else jnp.concatenate([ref[...] for ref in refs], axis=0)
+
+
 def pair_terms(scale, offset, text_refs, image_refs, slopes_ref, own=0, losses=True):
-    step = 256
-    totals, left = [], 0
-    for image_rows in image_refs:
-        for at in range(0, image_rows.shape[0], step):
-            images = image_rows[at : min(at + step, image_rows.shape[0]), :]
-            count = images.shape[0]
-            total, done = jnp.zeros((1, count), f32), 0
-            for texts in text_refs:
-                for start in range(0, texts.shape[0], step):
-                    chunk = texts[start : min(start + step, texts.shape[0]), :]
-                    logits = (
-                        scale
-                        * lax.dot_general(
-                            chunk, images, (((1,), (1,)), ((), ())), preferred_element_type=f32
-                        )
-                        + offset
-                    )
-                    shrunk = jnp.exp(-jnp.abs(logits))
-                    raised = 1.0 + shrunk
-                    inverse = pl.reciprocal(raised, approx=True)
-                    inverse = inverse * (2.0 - raised * inverse)
-                    sigmoid = jnp.where(logits >= 0.0, inverse, shrunk * inverse)
-                    match = None
-                    if own and done == 0 and left == 0:
-                        text_ids = lax.broadcasted_iota(jnp.int32, logits.shape, 0)
-                        image_ids = lax.broadcasted_iota(jnp.int32, logits.shape, 1)
-                        match = ((text_ids == image_ids) & (text_ids < own)).astype(f32)
-                        sigmoid = sigmoid - match
-                    slopes_ref[done : done + chunk.shape[0], left : left + count] = sigmoid.astype(bf16)
-                    if losses:
-                        log_raised = jnp.log(raised) + (shrunk - (raised - 1.0)) * inverse
-                        softplus = jnp.maximum(logits, 0.0) + log_raised
-                        if match is not None:
-                            softplus = softplus - match * logits
-                        total = total + jnp.sum(softplus, axis=0, keepdims=True)
-                    done += chunk.shape[0]
-            totals.append(total)
-            left += count
-    return jnp.concatenate(totals, axis=1)
+    texts, all_images = joined(text_refs), joined(image_refs)
+    totals = []
+    for left in range(0, all_images.shape[0], 256):
+        images = all_images[left : min(left + 256, all_images.shape[0]), :]
+        total = jnp.zeros((1, images.shape[0]), f32)
+        for start in range(0, texts.shape[0], 256):
+            logits = (
+                scale
+                * lax.dot_general(
+                    texts[start : start + 256, :],
+                    images,
+                    (((1,), (1,)), ((), ())),
+                    preferred_element_type=f32,
+                )
+                + offset
+            )
+            shrunk = jnp.exp(-jnp.abs(logits))
+            raised = 1.0 + shrunk
+            inverse = pl.reciprocal(raised, approx=True)
+            inverse = inverse * (2.0 - raised * inverse)
+            sigmoid = jnp.where(logits >= 0.0, inverse, shrunk * inverse)
+            match = None
+            if own and left == 0 and start < own:
+                text_ids = start + lax.broadcasted_iota(jnp.int32, logits.shape, 0)
+                image_ids = lax.broadcasted_iota(jnp.int32, logits.shape, 1)
+                match = ((text_ids == image_ids) & (text_ids < own)).astype(f32)
+                sigmoid = sigmoid - match
+            slopes_ref[start : start + 256, left : left + images.shape[0]] = sigmoid.astype(bf16)
+            if losses:
+                log_raised = jnp.log(raised) + (shrunk - (raised - 1.0)) * inverse
+                softplus = jnp.maximum(logits, 0.0) + log_raised
+                if match is not None:
+                    softplus = softplus - match * logits
+                total = total + jnp.sum(softplus, axis=0, keepdims=True)
+        totals.append(total)
+    return jnp.concatenate(totals, axis=1) if losses else None
 
 
 def unit_kernel(*refs):
@@ -153,20 +154,22 @@
     return jnp.where(which == 0, high, loss - high).astype(bf16)
 
 
+def column_cuts(width):
+    step = 4 * lanes
+    return [(left, min(step, width - left)) for left in range(0, width, step)]
+
+
 def sums_in_parts(slope_refs, text_refs, width):
-    step = 3 * lanes
-    for left in range(0, width, step):
+    for left, step in column_cuts(width):
         total = None
         for slopes, texts in zip(slope_refs, text_refs):
-            done = 0
-            for block in texts:
-                part = lax.dot_general(
-                    slopes[done : done + block.shape[0], :],
-                    block[:, left : left + step],
-                    (((0,), (0,)), ((), ())),
-                    preferred_element_type=f32,
-                )
-                total, done = part if total is None else total + part, done + block.shape[0]
+            part = lax.dot_general(
+                slopes[...],
+                joined([block.at[:, left : left + step] for block in texts]),
+                (((0,), (0,)), ((), ())),
+                preferred_element_type=f32,
+            )
+            total = part if total is None else total + part
         yield left, step, total
 
 
@@ -233,25 +236,21 @@
     rows, width = far_ref.shape
     own_texts = (near_ref, far_ref)
     pair_terms(scale_ref[0], bias_ref[0], own_texts, far_swapped_refs, slopes_ref, losses=False)
-    terms = []
-    for slopes, blocks in (
-        (near_slopes_ref, (images_ref,)),
-        (other_slopes_ref, (images_swapped_ref,)),
-        (far_slopes_ref, far_refs),
-        (slopes_ref, far_swapped_refs),
-    ):
-        left = 0
-        for images in blocks:
-            terms.append((slopes.at[:, left : left + images.shape[0]], images))
-            left += images.shape[0]
-    step = 3 * lanes
-    for left in range(0, width, step):
-        total = None
-        for slopes, images in terms:
-            part = jnp.dot(slopes[...], images[:, left : left + step], preferred_element_type=f32)
-            total = part if total is None else total + part
+    own_slopes = jnp.concatenate([near_slopes_ref[...], far_slopes_ref[...]], axis=1)
+    other_slopes = jnp.concatenate([other_slopes_ref[...], slopes_ref[...]], axis=1)
+    for left, step in column_cuts(width):
+        cut = slice(left, left + step)
+        total = jnp.dot(
+            own_slopes,
+            joined([ref.at[:, cut] for ref in (images_ref, *far_refs)]),
+            preferred_element_type=f32,
+        ) + jnp.dot(
+            other_slopes,
+            joined([ref.at[:, cut] for ref in (images_swapped_ref, *far_swapped_refs)]),
+            preferred_element_type=f32,
+        )
         for k, out in enumerate(outs):
-            out[:, left : left + step] = total[k * rows : (k + 1) * rows, :].astype(out.dtype)
+            out[:, cut] = total[k * rows : (k + 1) * rows, :].astype(out.dtype)
 
 
 def late_image_kernel(zs, ys, *refs):

time: 57.9 us -> 57.1 us (0.986)
  waiting for transfers between devices: 21 us -> 22.7 us
  starting transfers between devices: 20.6 us -> 19.3 us
  Pallas kernels: 12.1 us -> 10.8 us
    pallas_call x18, Pallas kernels: 12.1 us -> 10.8 us  [call(): pl.pallas_call(lambda *refs: kernel(*refs[:first], *refs[last:]), out_sha...]
    ppermute x17, starting transfers between devices: 20.3 us -> 19.1 us  [swapped(): lax.ppermute(value, axis, [(place, place ^ step) for place in range(lax.a...]
    ppermute x17, waiting for transfers between devices: 13.6 us -> 14.8 us  [swapped(): lax.ppermute(value, axis, [(place, place ^ step) for place in range(lax.a...]
  transfers between devices with their start and end apart: 18 -> 18, of which waited for: 7 -> 7; matrix products, arithmetic and copies ran while one was open for 2% -> 2% of each run, Pallas kernels for 18% -> 16%
where the time goes in v13:
time: 57.1 us; the launch traced here: 56.9 us
  waiting for transfers between devices  22.7 us (40%)
  starting transfers between devices  19.3 us (34%)
  Pallas kernels  10.8 us (19%)
  between operations  2.14 us (4%)
  local copies, waits for them, and re-layouts  1.92 us (3%)
    ppermute x17, starting transfers between devices, swapped(): lax.ppermute(value, axis, [(place, place ^ step) for place in range(lax.a...  19.1 us
    ppermute x17, waiting for transfers between devices, swapped(): lax.ppermute(value, axis, [(place, place ^ step) for place in range(lax.a...  14.8 us
    pallas_call x18, Pallas kernels, call(): pl.pallas_call(lambda *refs: kernel(*refs[:first], *refs[last:]), out_sha...  10.8 us
    ppermute x1, waiting for transfers between devices, swapped_both(): return lax.ppermute(value, ('dp', 'inner'), pairs)  7.87 us
  transfers between devices with their start and end apart: 18, of which 7 were waited for; matrix products, arithmetic and copies ran while one was open for 2% of the time, Pallas kernels for 16%

profile of v13, /device:TPU:0, one launch (start us, length us, event | category | flops | bytes accessed | tf_op | source)
XLA Modules:
  0.0 56.9 jit_solution(16885951922538923733)
XLA Ops:
  0.6 3.1 %collective-permute-start.1 = (bf16[128,1152]{1,0:T(8,128)(2,1)}, bf16[128,1152]{1,0:T(8,128)(2,1)S(1)}, u32[]{:S(2)}, u32[]{:S(2)}) collective-permute-start(bf16[128,1152]{1,0:T(8,128)(2,1)} %refs_2_.1), channel_id=1, source_target_pairs={{0,1},{1,0},{2,3},{3,2},{4,5},{5,4},{6,7},{7,6},{8,9},{9,8},{10,11... | collective-permute-start | bytes 884744 | tf_op jit(solution)/shard_map/ppermute | solution.py:21
  3.7 1.5 %collective-permute-start = (bf16[128,1152]{1,0:T(8,128)(2,1)}, bf16[128,1152]{1,0:T(8,128)(2,1)S(1)}, u32[]{:S(2)}, u32[]{:S(2)}) collective-permute-start(bf16[128,1152]{1,0:T(8,128)(2,1)} %refs_2_.1), channel_id=1, source_target_pairs={{0,8},{4,12},{8,0},{12,4},{16,24},{20,28},{24,16},{28,20},{1,9},{5... | collective-permute-start | bytes 884744 | tf_op jit(solution)/shard_map/ppermute | solution.py:21
  5.2 1.5 %collective-permute-start.5 = (bf16[128,1152]{1,0:T(8,128)(2,1)}, bf16[128,1152]{1,0:T(8,128)(2,1)S(1)}, u32[]{:S(2)}, u32[]{:S(2)}) collective-permute-start(bf16[128,1152]{1,0:T(8,128)(2,1)} %refs_3_.1), channel_id=1, source_target_pairs={{0,16},{4,20},{8,24},{12,28},{16,0},{20,4},{24,8},{28,12},{1,17},{... | collective-permute-start | bytes 884744 | tf_op jit(solution)/shard_map/ppermute | solution.py:21
  6.7 1.0 %slice.3 = bf16[64,1152]{1,0:T(8,128)(2,1)S(1)} slice(bf16[128,1152]{1,0:T(8,128)(2,1)} %refs_3_.1), slice={[0:64], [0:1152]} | slice | bytes 294912 | tf_op jit(solution)/shard_map/slice | solution.py:318
  7.7 2.7 %collective-permute-start.4 = (bf16[64,1152]{1,0:T(8,128)(2,1)S(1)}, bf16[64,1152]{1,0:T(8,128)(2,1)S(1)}, u32[]{:S(2)}, u32[]{:S(2)}) collective-permute-start(bf16[64,1152]{1,0:T(8,128)(2,1)S(1)} %slice.3), channel_id=1, source_target_pairs={{0,2},{1,3},{2,0},{3,1},{4,6},{5,7},{6,4},{7,5},{8,10},{9,11},{10,... | collective-permute-start | bytes 442376 | tf_op jit(solution)/shard_map/ppermute | solution.py:21
  11.7 1.0 %copy-done.1 = bf16[128,1152]{1,0:T(8,128)(2,1)S(1)} copy-done((bf16[128,1152]{1,0:T(8,128)(2,1)S(1)}, bf16[128,1152]{1,0:T(8,128)(2,1)}, u32[]{:S(2)}) %copy-start.1) | copy-done | bytes 294936
  13.5 2.6 %collective-permute-start.2 = (bf16[128,1152]{1,0:T(8,128)(2,1)S(1)}, bf16[128,1152]{1,0:T(8,128)(2,1)S(1)}, u32[]{:S(2)}, u32[]{:S(2)}) collective-permute-start(bf16[128,1152]{1,0:T(8,128)(2,1)S(1)} %shard_map.68.refs_2_.refs_1_), channel_id=1, source_target_pairs={{0,8},{4,12},{8,0},{12,4},{16,24},{20,28},{24,16},{28,20},{1,9},{5... | collective-permute-start | bytes 884744 | tf_op jit(solution)/shard_map/ppermute | solution.py:21
  16.3 4.1 %collective-permute-done.4.refs_0_ = bf16[64,1152]{1,0:T(8,128)(2,1)S(1)} collective-permute-done((bf16[64,1152]{1,0:T(8,128)(2,1)S(1)}, bf16[64,1152]{1,0:T(8,128)(2,1)S(1)}, u32[]{:S(2)}, u32[]{:S(2)}) %collective-permute-start.4) | collective-permute-done | bytes 147488 | tf_op jit(solution)/shard_map/ppermute | solution.py:21
  20.6 2.6 %collective-permute-done.3.refs_0_ = bf16[64,1152]{1,0:T(8,128)(2,1)S(1)} collective-permute-done((bf16[64,1152]{1,0:T(8,128)(2,1)S(1)}, bf16[64,1152]{1,0:T(8,128)(2,1)S(1)}, u32[]{:S(2)}, u32[]{:S(2)}) %collective-permute-start.3) | collective-permute-done | bytes 147488 | tf_op jit(solution)/shard_map/ppermute | solution.py:21
  23.2 1.0 %collective-permute-start.10 = (bf16[64,1152]{1,0:T(8,128)(2,1)S(1)}, bf16[64,1152]{1,0:T(8,128)(2,1)S(1)}, u32[]{:S(2)}, u32[]{:S(2)}) collective-permute-start(bf16[64,1152]{1,0:T(8,128)(2,1)S(1)} %shard_map.71.refs_1_.refs_3_), channel_id=1, source_target_pairs={{0,16},{4,20},{8,24},{12,28},{16,0},{20,4},{24,8},{28,12},{1,17},{... | collective-permute-start | bytes 442376 | tf_op jit(solution)/shard_map/ppermute | solution.py:21
  25.8 1.3 %shard_map.74 = (bf16[512,384]{1,0:T(8,128)(2,1)S(1)}, f32[1,384]{1,0:T(1,128)S(1)}) custom-call(f32[1]{0:T(128)S(6)} %exp.3.refs_0_, f32[1]{0:T(128)S(6)} %copy.8.refs_1_, bf16[384,1152]{1,0:T(8,128)(2,1)S(1)} %shard_map.69.refs_2_, bf16[128,1152]{1,0:T(8,128)(2,1)S(1)} %shard_map.72.refs_3_.refs_1_, bf16[384,1152]{1,0:T(8,128)(2,1)S(1)} %shard_map.73.refs_4_), custom_call_target="tpu_custom_call" | custom-call | flops 452984832 | bytes 2459144 | tf_op jit(solution)/shard_map/pallas_call | solution.py:38
  27.2 1.0 %shard_map.76.refs_2_.refs_7_.refs_8_ = bf16[512,384]{1,0:T(8,128)(2,1)S(1)} custom-call(f32[1]{0:T(128)S(6)} %exp.3.refs_0_, f32[1]{0:T(128)S(6)} %copy.8.refs_1_, bf16[384,1152]{1,0:T(8,128)(2,1)S(1)} %shard_map.69.refs_2_, bf16[128,1152]{1,0:T(8,128)(2,1)S(1)} %shard_map.72.refs_3_.refs_1_, bf16[384,1152]{1,0:T(8,128)(2,1)S(1)} %collective-permute-done.8.refs_4_.refs_5_, ...), custom_call_target="tpu_custom_call" | custom-call | flops 452984832 | bytes 2457608 | tf_op jit(solution)/shard_map/pallas_call | solution.py:38
  29.0 1.5 %shard_map.78 = (bf16[512,128]{1,0:T(8,128)(2,1)S(1)}, bf16[1168,128]{1,0:T(8,128)(2,1)S(1)}) custom-call(f32[1]{0:T(128)S(6)} %exp.3.refs_0_, f32[1]{0:T(128)S(6)} %copy.8.refs_1_, bf16[384,1152]{1,0:T(8,128)(2,1)S(1)} %shard_map.69.refs_2_, bf16[128,1152]{1,0:T(8,128)(2,1)S(1)} %shard_map.72.refs_3_.refs_1_, ...), custom_call_target="tpu_custom_call" | custom-call | flops 603979776 | bytes 3084296 | tf_op jit(solution)/shard_map/pallas_call | solution.py:38
  30.5 1.1 %collective-permute-start.12 = (bf16[1168,128]{1,0:T(8,128)(2,1)S(1)}, bf16[1168,128]{1,0:T(8,128)(2,1)S(1)}, u32[]{:S(2)}, u32[]{:S(2)}) collective-permute-start(bf16[1168,128]{1,0:T(8,128)(2,1)S(1)} %get-tuple-element.36.refs_11_), channel_id=1, source_target_pairs={{0,16},{4,20},{8,24},{12,28},{16,0},{20,4},{24,8},{28,12},{1,17},{... | collective-permute-start | bytes 897032 | tf_op jit(solution)/shard_map/ppermute | solution.py:21
  31.6 1.8 %shard_map.79 = (f32[128,1152]{1,0:T(8,128)S(1)}, bf16[128,1152]{1,0:T(8,128)(2,1)S(1)}, bf16[128,1152]{1,0:T(8,128)(2,1)S(1)}, bf16[128,1152]{1,0:T(8,128)(2,1)S(1)}) custom-call(f32[1]{0:T(128)S(6)} %exp.3.refs_0_, f32[1]{0:T(128)S(6)} %copy.8.refs_1_, bf16[384,1152]{1,0:T(8,128)(2,1)S(1)} %shard_map.69.refs_2_, ...), custom_call_target="tpu_custom_call" | custom-call | flops 1811939328 | bytes 5931016 | tf_op jit(solution)/shard_map/pallas_call | solution.py:38
  33.7 1.8 %collective-permute-start.16 = (bf16[128,1152]{1,0:T(8,128)(2,1)S(1)}, bf16[128,1152]{1,0:T(8,128)(2,1)S(1)}, u32[]{:S(2)}, u32[]{:S(2)}) collective-permute-start(bf16[128,1152]{1,0:T(8,128)(2,1)S(1)} %get-tuple-element.49), channel_id=1, source_target_pairs={{0,1},{1,0},{2,3},{3,2},{4,5},{5,4},{6,7},{7,6},{8,9},{9,8},{10,11... | collective-permute-start | bytes 884744 | tf_op jit(solution)/shard_map/ppermute | solution.py:21
  35.6 1.3 %shard_map.80 = (bf16[512,384]{1,0:T(8,128)(2,1)S(1)}, f32[1,384]{1,0:T(1,128)S(1)}) custom-call(f32[1]{0:T(128)S(6)} %exp.3.refs_0_, f32[1]{0:T(128)S(6)} %copy.8.refs_1_, bf16[384,1152]{1,0:T(8,128)(2,1)S(1)} %collective-permute-done.6.refs_2_.refs_4_, bf16[128,1152]{1,0:T(8,128)(2,1)S(1)} %collective-permute-done.7.refs_5_.refs_3_, ...), custom_call_target="tpu_custom_call" | custom-call | flops 452984832 | bytes 2460680 | tf_op jit(solution)/shard_map/pallas_call | solution.py:38
  36.9 1.2 %shard_map.81 = (f32[128,1152]{1,0:T(8,128)S(1)}, f32[1,128]{1,0:T(1,128)S(1)}, bf16[1168,128]{1,0:T(8,128)(2,1)S(1)}, f32[1152,128]{1,0:T(8,128)S(1)}, f32[1,128]{1,0:T(1,128)S(1)}) custom-call(bf16[512,384]{1,0:T(8,128)(2,1)S(1)} %get-tuple-element.33.refs_5_.refs_6_.refs_0_, bf16[512,384]{1,0:T(8,128)(2,1)S(1)} %get-tuple-element.38.refs_1_, ...), custom_call_target="tpu_custom_call" | custom-call | flops 905969664 | bytes 4626944 | tf_op jit(solution)/shard_map/pallas_call | solution.py:38
  38.1 2.0 %collective-permute-done.12.refs_2_ = bf16[1168,128]{1,0:T(8,128)(2,1)S(1)} collective-permute-done((bf16[1168,128]{1,0:T(8,128)(2,1)S(1)}, bf16[1168,128]{1,0:T(8,128)(2,1)S(1)}, u32[]{:S(2)}, u32[]{:S(2)}) %collective-permute-start.12) | collective-permute-done | bytes 299040 | tf_op jit(solution)/shard_map/ppermute | solution.py:21
  40.2 1.3 %collective-permute-start.14 = (bf16[1168,128]{1,0:T(8,128)(2,1)S(1)}, bf16[1168,128]{1,0:T(8,128)(2,1)S(1)}, u32[]{:S(2)}, u32[]{:S(2)}) collective-permute-start(bf16[1168,128]{1,0:T(8,128)(2,1)S(1)} %get-tuple-element.47), channel_id=1, source_target_pairs={{0,16},{4,20},{8,24},{12,28},{16,0},{20,4},{24,8},{28,12},{1,17},{... | collective-permute-start | bytes 897032 | tf_op jit(solution)/shard_map/ppermute | solution.py:21
  41.5 1.3 %collective-permute-start.17 = (bf16[128,1152]{1,0:T(8,128)(2,1)S(1)}, bf16[128,1152]{1,0:T(8,128)(2,1)S(1)}, u32[]{:S(2)}, u32[]{:S(2)}) collective-permute-start(bf16[128,1152]{1,0:T(8,128)(2,1)S(1)} %get-tuple-element.37.refs_6_.refs_7_), channel_id=1, source_target_pairs={{0,8},{4,12},{8,0},{12,4},{16,24},{20,28},{24,16},{28,20},{1,9},{5... | collective-permute-start | bytes 884744 | tf_op jit(solution)/shard_map/ppermute | solution.py:21
  42.8 7.9 %collective-permute-done.15.refs_0_.refs_8_ = bf16[128,1152]{1,0:T(8,128)(2,1)S(1)} collective-permute-done((bf16[128,1152]{1,0:T(8,128)(2,1)S(1)}, bf16[128,1152]{1,0:T(8,128)(2,1)S(1)}, u32[]{:S(2)}, u32[]{:S(2)}) %collective-permute-start.15) | collective-permute-done | bytes 294944 | tf_op jit(solution)/shard_map/ppermute | solution.py:31
  50.7 4.6 %collective-permute-done.16.refs_1_.refs_9_ = bf16[128,1152]{1,0:T(8,128)(2,1)S(1)} collective-permute-done((bf16[128,1152]{1,0:T(8,128)(2,1)S(1)}, bf16[128,1152]{1,0:T(8,128)(2,1)S(1)}, u32[]{:S(2)}, u32[]{:S(2)}) %collective-permute-start.16) | collective-permute-done | bytes 294944 | tf_op jit(solution)/shard_map/ppermute | solution.py:21
  55.3 1.6 %shard_map.84 = (f32[128,1152]{1,0:T(8,128)}, f32[128,1152]{1,0:T(8,128)}, f32[1,128]{1,0:T(1,128)}) custom-call(f32[1]{0:T(128)S(6)} %exp.3.refs_0_, bf16[128,1152]{1,0:T(8,128)(2,1)S(1)} %get-tuple-element.28.refs_1_, bf16[128,1152]{1,0:T(8,128)(2,1)S(1)} %get-tuple-element.29.refs_2_, f32[128,1152]{1,0:T(8,128)S(1)} %get-tuple-element.40.refs_3_, ...), custom_call_target="tpu_custom_call" | custom-call | bytes 4432900 | tf_op jit(solution)/shard_map/pallas_call | solution.py:38
  (35 shorter events, 4.1 us)
Async XLA Ops:
  0.6 11.1 %copy-start = (bf16[128,1152]{1,0:T(8,128)(2,1)S(1)}, bf16[128,1152]{1,0:T(8,128)(2,1)}, u32[]{:S(2)}) copy-start(bf16[128,1152]{1,0:T(8,128)(2,1)} %refs_3_.1) | copy-start | bytes 884740
  0.6 12.7 %collective-permute-start.1 = (bf16[128,1152]{1,0:T(8,128)(2,1)}, bf16[128,1152]{1,0:T(8,128)(2,1)S(1)}, u32[]{:S(2)}, u32[]{:S(2)}) collective-permute-start(bf16[128,1152]{1,0:T(8,128)(2,1)} %refs_2_.1), channel_id=1, source_target_pairs={{0,1},{1,0},{2,3},{3,2},{4,5},{5,4},{6,7},{7,6},{8,9},{9,8},{10,11... | collective-permute-start | bytes 884744 | tf_op jit(solution)/shard_map/ppermute | solution.py:21
  3.7 9.6 %collective-permute-start = (bf16[128,1152]{1,0:T(8,128)(2,1)}, bf16[128,1152]{1,0:T(8,128)(2,1)S(1)}, u32[]{:S(2)}, u32[]{:S(2)}) collective-permute-start(bf16[128,1152]{1,0:T(8,128)(2,1)} %refs_2_.1), channel_id=1, source_target_pairs={{0,8},{4,12},{8,0},{12,4},{16,24},{20,28},{24,16},{28,20},{1,9},{5... | collective-permute-start | bytes 884744 | tf_op jit(solution)/shard_map/ppermute | solution.py:21
  5.2 15.2 %collective-permute-start.5 = (bf16[128,1152]{1,0:T(8,128)(2,1)}, bf16[128,1152]{1,0:T(8,128)(2,1)S(1)}, u32[]{:S(2)}, u32[]{:S(2)}) collective-permute-start(bf16[128,1152]{1,0:T(8,128)(2,1)} %refs_3_.1), channel_id=1, source_target_pairs={{0,16},{4,20},{8,24},{12,28},{16,0},{20,4},{24,8},{28,12},{1,17},{... | collective-permute-start | bytes 884744 | tf_op jit(solution)/shard_map/ppermute | solution.py:21
  7.7 12.7 %collective-permute-start.4 = (bf16[64,1152]{1,0:T(8,128)(2,1)S(1)}, bf16[64,1152]{1,0:T(8,128)(2,1)S(1)}, u32[]{:S(2)}, u32[]{:S(2)}) collective-permute-start(bf16[64,1152]{1,0:T(8,128)(2,1)S(1)} %slice.3), channel_id=1, source_target_pairs={{0,2},{1,3},{2,0},{3,1},{4,6},{5,7},{6,4},{7,5},{8,10},{9,11},{10,... | collective-permute-start | bytes 442376 | tf_op jit(solution)/shard_map/ppermute | solution.py:21
  11.7 1.0 %copy-start.1 = (bf16[128,1152]{1,0:T(8,128)(2,1)S(1)}, bf16[128,1152]{1,0:T(8,128)(2,1)}, u32[]{:S(2)}) copy-start(bf16[128,1152]{1,0:T(8,128)(2,1)} %refs_2_.1) | copy-start | bytes 884740
  12.9 10.3 %collective-permute-start.3 = (bf16[64,1152]{1,0:T(8,128)(2,1)S(1)}, bf16[64,1152]{1,0:T(8,128)(2,1)S(1)}, u32[]{:S(2)}, u32[]{:S(2)}) collective-permute-start(bf16[64,1152]{1,0:T(8,128)(2,1)S(1)} %get-tuple-element.31.refs_2_), channel_id=1, source_target_pairs={{0,2},{1,3},{2,0},{3,1},{4,6},{5,7},{6,4},{7,5},{8,10},{9,11},{10,... | collective-permute-start | bytes 442376 | tf_op jit(solution)/shard_map/ppermute | solution.py:21
  13.5 10.7 %collective-permute-start.2 = (bf16[128,1152]{1,0:T(8,128)(2,1)S(1)}, bf16[128,1152]{1,0:T(8,128)(2,1)S(1)}, u32[]{:S(2)}, u32[]{:S(2)}) collective-permute-start(bf16[128,1152]{1,0:T(8,128)(2,1)S(1)} %shard_map.68.refs_2_.refs_1_), channel_id=1, source_target_pairs={{0,8},{4,12},{8,0},{12,4},{16,24},{20,28},{24,16},{28,20},{1,9},{5... | collective-permute-start | bytes 884744 | tf_op jit(solution)/shard_map/ppermute | solution.py:21
  16.2 7.0 %collective-permute-start.6 = (bf16[384,1152]{1,0:T(8,128)(2,1)S(1)}, bf16[384,1152]{1,0:T(8,128)(2,1)S(1)}, u32[]{:S(2)}, u32[]{:S(2)}) collective-permute-start(bf16[384,1152]{1,0:T(8,128)(2,1)S(1)} %shard_map.69.refs_2_), channel_id=1, source_target_pairs={{0,4},{4,0},{8,12},{12,8},{16,20},{20,16},{24,28},{28,24},{1,5},{5... | collective-permute-start | bytes 2654216 | tf_op jit(solution)/shard_map/ppermute | solution.py:21
  20.5 5.3 %collective-permute-start.9 = (bf16[64,1152]{1,0:T(8,128)(2,1)S(1)}, bf16[64,1152]{1,0:T(8,128)(2,1)S(1)}, u32[]{:S(2)}, u32[]{:S(2)}) collective-permute-start(bf16[64,1152]{1,0:T(8,128)(2,1)S(1)} %shard_map.70.refs_1_.refs_2_), channel_id=1, source_target_pairs={{0,16},{4,20},{8,24},{12,28},{16,0},{20,4},{24,8},{28,12},{1,17},{... | collective-permute-start | bytes 442376 | tf_op jit(solution)/shard_map/ppermute | solution.py:21
  23.2 5.7 %collective-permute-start.10 = (bf16[64,1152]{1,0:T(8,128)(2,1)S(1)}, bf16[64,1152]{1,0:T(8,128)(2,1)S(1)}, u32[]{:S(2)}, u32[]{:S(2)}) collective-permute-start(bf16[64,1152]{1,0:T(8,128)(2,1)S(1)} %shard_map.71.refs_1_.refs_3_), channel_id=1, source_target_pairs={{0,16},{4,20},{8,24},{12,28},{16,0},{20,4},{24,8},{28,12},{1,17},{... | collective-permute-start | bytes 442376 | tf_op jit(solution)/shard_map/ppermute | solution.py:21
  24.2 4.8 %collective-permute-start.7 = (bf16[128,1152]{1,0:T(8,128)(2,1)S(1)}, bf16[128,1152]{1,0:T(8,128)(2,1)S(1)}, u32[]{:S(2)}, u32[]{:S(2)}) collective-permute-start(bf16[128,1152]{1,0:T(8,128)(2,1)S(1)} %shard_map.72.refs_3_.refs_1_), channel_id=1, source_target_pairs={{0,4},{4,0},{8,12},{12,8},{16,20},{20,16},{24,28},{28,24},{1,5},{5... | collective-permute-start | bytes 884744 | tf_op jit(solution)/shard_map/ppermute | solution.py:21
  24.4 2.7 %collective-permute-start.8 = (bf16[384,1152]{1,0:T(8,128)(2,1)S(1)}, bf16[384,1152]{1,0:T(8,128)(2,1)S(1)}, u32[]{:S(2)}, u32[]{:S(2)}) collective-permute-start(bf16[384,1152]{1,0:T(8,128)(2,1)S(1)} %shard_map.73.refs_4_), channel_id=1, source_target_pairs={{0,4},{4,0},{8,12},{12,8},{16,20},{20,16},{24,28},{28,24},{1,5},{5... | collective-permute-start | bytes 2654216 | tf_op jit(solution)/shard_map/ppermute | solution.py:21
  28.9 2.7 %collective-permute-start.11 = (bf16[128,1152]{1,0:T(8,128)(2,1)S(1)}, bf16[128,1152]{1,0:T(8,128)(2,1)S(1)}, u32[]{:S(2)}, u32[]{:S(2)}) collective-permute-start(bf16[128,1152]{1,0:T(8,128)(2,1)S(1)} %shard_map.77.refs_6_.refs_9_), channel_id=1, source_target_pairs={{0,4},{4,0},{8,12},{12,8},{16,20},{20,16},{24,28},{28,24},{1,5},{5... | collective-permute-start | bytes 884744 | tf_op jit(solution)/shard_map/ppermute | solution.py:21
  30.5 9.6 %collective-permute-start.12 = (bf16[1168,128]{1,0:T(8,128)(2,1)S(1)}, bf16[1168,128]{1,0:T(8,128)(2,1)S(1)}, u32[]{:S(2)}, u32[]{:S(2)}) collective-permute-start(bf16[1168,128]{1,0:T(8,128)(2,1)S(1)} %get-tuple-element.36.refs_11_), channel_id=1, source_target_pairs={{0,16},{4,20},{8,24},{12,28},{16,0},{20,4},{24,8},{28,12},{1,17},{... | collective-permute-start | bytes 897032 | tf_op jit(solution)/shard_map/ppermute | solution.py:21
  33.5 17.2 %collective-permute-start.15 = (bf16[128,1152]{1,0:T(8,128)(2,1)S(1)}, bf16[128,1152]{1,0:T(8,128)(2,1)S(1)}, u32[]{:S(2)}, u32[]{:S(2)}) collective-permute-start(bf16[128,1152]{1,0:T(8,128)(2,1)S(1)} %get-tuple-element.48), channel_id=1, source_target_pairs={{0,9},{1,8},{2,11},{3,10},{4,13},{5,12},{6,15},{7,14},{8,1},{9,0},... | collective-permute-start | bytes 884744 | tf_op jit(solution)/shard_map/ppermute | solution.py:31
  33.7 21.5 %collective-permute-start.16 = (bf16[128,1152]{1,0:T(8,128)(2,1)S(1)}, bf16[128,1152]{1,0:T(8,128)(2,1)S(1)}, u32[]{:S(2)}, u32[]{:S(2)}) collective-permute-start(bf16[128,1152]{1,0:T(8,128)(2,1)S(1)} %get-tuple-element.49), channel_id=1, source_target_pairs={{0,1},{1,0},{2,3},{3,2},{4,5},{5,4},{6,7},{7,6},{8,9},{9,8},{10,11... | collective-permute-start | bytes 884744 | tf_op jit(solution)/shard_map/ppermute | solution.py:21
  40.2 15.1 %collective-permute-start.13 = (bf16[1168,128]{1,0:T(8,128)(2,1)S(1)}, bf16[1168,128]{1,0:T(8,128)(2,1)S(1)}, u32[]{:S(2)}, u32[]{:S(2)}) collective-permute-start(bf16[1168,128]{1,0:T(8,128)(2,1)S(1)} %get-tuple-element.46), channel_id=1, source_target_pairs={{0,2},{1,3},{2,0},{3,1},{4,6},{5,7},{6,4},{7,5},{8,10},{9,11},{10,... | collective-permute-start | bytes 897032 | tf_op jit(solution)/shard_map/ppermute | solution.py:21
  40.2 15.0 %collective-permute-start.14 = (bf16[1168,128]{1,0:T(8,128)(2,1)S(1)}, bf16[1168,128]{1,0:T(8,128)(2,1)S(1)}, u32[]{:S(2)}, u32[]{:S(2)}) collective-permute-start(bf16[1168,128]{1,0:T(8,128)(2,1)S(1)} %get-tuple-element.47), channel_id=1, source_target_pairs={{0,16},{4,20},{8,24},{12,28},{16,0},{20,4},{24,8},{28,12},{1,17},{... | collective-permute-start | bytes 897032 | tf_op jit(solution)/shard_map/ppermute | solution.py:21
  41.5 13.8 %collective-permute-start.17 = (bf16[128,1152]{1,0:T(8,128)(2,1)S(1)}, bf16[128,1152]{1,0:T(8,128)(2,1)S(1)}, u32[]{:S(2)}, u32[]{:S(2)}) collective-permute-start(bf16[128,1152]{1,0:T(8,128)(2,1)S(1)} %get-tuple-element.37.refs_6_.refs_7_), channel_id=1, source_target_pairs={{0,8},{4,12},{8,0},{12,4},{16,24},{20,28},{24,16},{28,20},{1,9},{5... | collective-permute-start | bytes 884744 | tf_op jit(solution)/shard_map/ppermute | solution.py:21

commit v14 on v13

--- a/solution.py
+++ b/solution.py
@@ -324,7 +324,10 @@
     second_z = [swapped(second_half, "inner", q) for q in image_inner]
     zs, ys = len(first_z), len(images_y)
 
-    (text_z_emb,) = call(unit_kernel, [block], text_z, weight=weights["x"], after=[text_x, second_half])
+    first_z = call(
+        unit_kernel, [half_block] * zs, *first_z, weight=weights["a"]
+    )
+    (text_z_emb,) = call(unit_kernel, [block], text_z, weight=weights["x"], after=[text_x, second_half, *images_y, *first_z])
     near_texts = call(
         functools.partial(near_kernel, frozenset({1})),
         shape((3 * rows, width), bf16),
@@ -334,12 +337,9 @@
     )
     texts_swapped = swapped(near_texts, "dp", 1)
     far_places = [(p, q) for q in image_inner for p in image_dp]
-    first_z = call(
-        unit_kernel, [half_block] * zs, *first_z, weight=weights["a"], after=[text_z_emb, *images_y]
-    )
     first_far = [swapped(emb, "dp", p) for emb in first_z for p in image_dp]
-    second_z = call(copies_kernel, [half_block] * zs, *second_z, weight=weights["b"], after=[*first_z, texts_swapped])
-    (far_text,) = call(copies_kernel, [block], swapped(text_z_emb, "dp", 2), weight=weights["x far"], after=second_z)
+    second_z = call(copies_kernel, [half_block] * zs, *second_z, weight=weights["b"], after=first_z)
+    (far_text,) = call(copies_kernel, [block], swapped(text_z_emb, "dp", 2), weight=weights["x far"], after=[*second_z, texts_swapped])
     first_far = call(
         copies_kernel, [half_block] * (zs * ys), *first_far, weight=weights["y far"], after=[far_text]
     )

time: 57.1 us -> 59.8 us (1.047)
  starting transfers between devices: 19.3 us -> 21.4 us
  waiting for transfers between devices: 22.7 us -> 23.4 us
    ppermute x17, starting transfers between devices: 19.1 us -> 20.8 us  [swapped(): lax.ppermute(value, axis, [(place, place ^ step) for place in range(lax.a...]
    ppermute x17, waiting for transfers between devices: 14.8 us -> 16 us  [swapped(): lax.ppermute(value, axis, [(place, place ^ step) for place in range(lax.a...]
  transfers between devices with their start and end apart: 18 -> 18, of which waited for: 7 -> 5; matrix products, arithmetic and copies ran while one was open for 2% -> 0% of each run, Pallas kernels for 16% -> 15%
where the time goes in v14:
time: 59.8 us; the launch traced here: 59.6 us
  waiting for transfers between devices  23.4 us (39%)
  starting transfers between devices  21.4 us (36%)
  Pallas kernels  10.8 us (18%)
  between operations  2.14 us (4%)
  local copies, waits for them, and re-layouts  1.95 us (3%)
    ppermute x17, starting transfers between devices, swapped(): lax.ppermute(value, axis, [(place, place ^ step) for place in range(lax.a...  20.8 us
    ppermute x17, waiting for transfers between devices, swapped(): lax.ppermute(value, axis, [(place, place ^ step) for place in range(lax.a...  16 us
    pallas_call x18, Pallas kernels, call(): pl.pallas_call(lambda *refs: kernel(*refs[:first], *refs[last:]), out_sha...  10.8 us
    ppermute x1, waiting for transfers between devices, swapped_both(): return lax.ppermute(value, ('dp', 'inner'), pairs)  7.32 us
  transfers between devices with their start and end apart: 18, of which 5 were waited for; matrix products, arithmetic and copies ran while one was open for 0% of the time, Pallas kernels for 15%

profile of v14, /device:TPU:0, one launch (start us, length us, event | category | flops | bytes accessed | tf_op | source)
XLA Modules:
  0.0 59.6 jit_solution(4102073434207474996)
XLA Ops:
  0.6 1.0 %slice.3 = bf16[64,1152]{1,0:T(8,128)(2,1)S(1)} slice(bf16[128,1152]{1,0:T(8,128)(2,1)} %refs_3_.1), slice={[0:64], [0:1152]} | slice | bytes 294912 | tf_op jit(solution)/shard_map/slice | solution.py:318
  1.6 4.1 %collective-permute-start.3 = (bf16[64,1152]{1,0:T(8,128)(2,1)S(1)}, bf16[64,1152]{1,0:T(8,128)(2,1)S(1)}, u32[]{:S(2)}, u32[]{:S(2)}) collective-permute-start(bf16[64,1152]{1,0:T(8,128)(2,1)S(1)} %slice.3), channel_id=1, source_target_pairs={{0,2},{1,3},{2,0},{3,1},{4,6},{5,7},{6,4},{7,5},{8,10},{9,11},{10,... | collective-permute-start | bytes 442376 | tf_op jit(solution)/shard_map/ppermute | solution.py:21
  5.7 1.5 %collective-permute-start.2 = (bf16[128,1152]{1,0:T(8,128)(2,1)S(1)}, bf16[128,1152]{1,0:T(8,128)(2,1)S(1)}, u32[]{:S(2)}, u32[]{:S(2)}) collective-permute-start(bf16[128,1152]{1,0:T(8,128)(2,1)S(1)} %copy-done), channel_id=1, source_target_pairs={{0,16},{4,20},{8,24},{12,28},{16,0},{20,4},{24,8},{28,12},{1,17},{... | collective-permute-start | bytes 884744 | tf_op jit(solution)/shard_map/ppermute | solution.py:21
  7.3 1.6 %collective-permute-start.1 = (bf16[128,1152]{1,0:T(8,128)(2,1)}, bf16[128,1152]{1,0:T(8,128)(2,1)S(1)}, u32[]{:S(2)}, u32[]{:S(2)}) collective-permute-start(bf16[128,1152]{1,0:T(8,128)(2,1)} %refs_2_.1), channel_id=1, source_target_pairs={{0,1},{1,0},{2,3},{3,2},{4,5},{5,4},{6,7},{7,6},{8,9},{9,8},{10,11... | collective-permute-start | bytes 884744 | tf_op jit(solution)/shard_map/ppermute | solution.py:21
  8.8 1.5 %collective-permute-start = (bf16[128,1152]{1,0:T(8,128)(2,1)}, bf16[128,1152]{1,0:T(8,128)(2,1)S(1)}, u32[]{:S(2)}, u32[]{:S(2)}) collective-permute-start(bf16[128,1152]{1,0:T(8,128)(2,1)} %refs_2_.1), channel_id=1, source_target_pairs={{0,8},{4,12},{8,0},{12,4},{16,24},{20,28},{24,16},{28,20},{1,9},{5... | collective-permute-start | bytes 884744 | tf_op jit(solution)/shard_map/ppermute | solution.py:21
  11.7 1.0 %copy-done.1 = bf16[128,1152]{1,0:T(8,128)(2,1)S(1)} copy-done((bf16[128,1152]{1,0:T(8,128)(2,1)S(1)}, bf16[128,1152]{1,0:T(8,128)(2,1)}, u32[]{:S(2)}) %copy-start.1) | copy-done | bytes 294936
  13.4 1.2 %collective-permute-start.9 = (bf16[64,1152]{1,0:T(8,128)(2,1)S(1)}, bf16[64,1152]{1,0:T(8,128)(2,1)S(1)}, u32[]{:S(2)}, u32[]{:S(2)}) collective-permute-start(bf16[64,1152]{1,0:T(8,128)(2,1)S(1)} %shard_map.68.refs_4_.refs_1_.refs_2_), channel_id=1, source_target_pairs={{0,16},{4,20},{8,24},{12,28},{16,0},{20,4},{24,8},{28,12},{1,17},{... | collective-permute-start | bytes 442376 | tf_op jit(solution)/shard_map/ppermute | solution.py:21
  14.6 5.0 %collective-permute-done.1.refs_0_ = bf16[128,1152]{1,0:T(8,128)(2,1)S(1)} collective-permute-done((bf16[128,1152]{1,0:T(8,128)(2,1)}, bf16[128,1152]{1,0:T(8,128)(2,1)S(1)}, u32[]{:S(2)}, u32[]{:S(2)}) %collective-permute-start.1) | collective-permute-done | bytes 294944 | tf_op jit(solution)/shard_map/ppermute | solution.py:21
  19.8 2.2 %collective-permute-start.4 = (bf16[128,1152]{1,0:T(8,128)(2,1)S(1)}, bf16[128,1152]{1,0:T(8,128)(2,1)S(1)}, u32[]{:S(2)}, u32[]{:S(2)}) collective-permute-start(bf16[128,1152]{1,0:T(8,128)(2,1)S(1)} %shard_map.69.refs_2_), channel_id=1, source_target_pairs={{0,8},{4,12},{8,0},{12,4},{16,24},{20,28},{24,16},{28,20},{1,9},{5... | collective-permute-start | bytes 884744 | tf_op jit(solution)/shard_map/ppermute | solution.py:21
  22.2 1.2 %collective-permute-start.10 = (bf16[64,1152]{1,0:T(8,128)(2,1)S(1)}, bf16[64,1152]{1,0:T(8,128)(2,1)S(1)}, u32[]{:S(2)}, u32[]{:S(2)}) collective-permute-start(bf16[64,1152]{1,0:T(8,128)(2,1)S(1)} %shard_map.71.refs_1_.refs_3_), channel_id=1, source_target_pairs={{0,16},{4,20},{8,24},{12,28},{16,0},{20,4},{24,8},{28,12},{1,17},{... | collective-permute-start | bytes 442376 | tf_op jit(solution)/shard_map/ppermute | solution.py:21
  23.8 4.3 %collective-permute-done.4.refs_0_ = bf16[128,1152]{1,0:T(8,128)(2,1)S(1)} collective-permute-done((bf16[128,1152]{1,0:T(8,128)(2,1)S(1)}, bf16[128,1152]{1,0:T(8,128)(2,1)S(1)}, u32[]{:S(2)}, u32[]{:S(2)}) %collective-permute-start.4) | collective-permute-done | bytes 294944 | tf_op jit(solution)/shard_map/ppermute | solution.py:21
  28.3 1.3 %shard_map.74 = (bf16[512,384]{1,0:T(8,128)(2,1)S(1)}, f32[1,384]{1,0:T(1,128)S(1)}) custom-call(f32[1]{0:T(128)S(6)} %exp.3.refs_0_, f32[1]{0:T(128)S(6)} %copy.8.refs_1_, bf16[384,1152]{1,0:T(8,128)(2,1)S(1)} %shard_map.70.refs_2_, bf16[128,1152]{1,0:T(8,128)(2,1)S(1)} %shard_map.72.refs_3_.refs_1_, bf16[384,1152]{1,0:T(8,128)(2,1)S(1)} %shard_map.73.refs_4_), custom_call_target="tpu_custom_call" | custom-call | flops 452984832 | bytes 2459144 | tf_op jit(solution)/shard_map/pallas_call | solution.py:38
  29.6 1.0 %shard_map.76.refs_2_.refs_7_.refs_8_ = bf16[512,384]{1,0:T(8,128)(2,1)S(1)} custom-call(f32[1]{0:T(128)S(6)} %exp.3.refs_0_, f32[1]{0:T(128)S(6)} %copy.8.refs_1_, bf16[384,1152]{1,0:T(8,128)(2,1)S(1)} %shard_map.70.refs_2_, bf16[128,1152]{1,0:T(8,128)(2,1)S(1)} %shard_map.72.refs_3_.refs_1_, bf16[384,1152]{1,0:T(8,128)(2,1)S(1)} %collective-permute-done.8.refs_4_.refs_5_, ...), custom_call_target="tpu_custom_call" | custom-call | flops 452984832 | bytes 2457608 | tf_op jit(solution)/shard_map/pallas_call | solution.py:38
  31.2 1.5 %shard_map.78 = (bf16[512,128]{1,0:T(8,128)(2,1)S(1)}, bf16[1168,128]{1,0:T(8,128)(2,1)S(1)}) custom-call(f32[1]{0:T(128)S(6)} %exp.3.refs_0_, f32[1]{0:T(128)S(6)} %copy.8.refs_1_, bf16[384,1152]{1,0:T(8,128)(2,1)S(1)} %shard_map.70.refs_2_, bf16[128,1152]{1,0:T(8,128)(2,1)S(1)} %shard_map.72.refs_3_.refs_1_, ...), custom_call_target="tpu_custom_call" | custom-call | flops 603979776 | bytes 3084296 | tf_op jit(solution)/shard_map/pallas_call | solution.py:38
  33.5 1.8 %shard_map.79 = (f32[128,1152]{1,0:T(8,128)S(1)}, bf16[128,1152]{1,0:T(8,128)(2,1)S(1)}, bf16[128,1152]{1,0:T(8,128)(2,1)S(1)}, bf16[128,1152]{1,0:T(8,128)(2,1)S(1)}) custom-call(f32[1]{0:T(128)S(6)} %exp.3.refs_0_, f32[1]{0:T(128)S(6)} %copy.8.refs_1_, bf16[384,1152]{1,0:T(8,128)(2,1)S(1)} %shard_map.70.refs_2_, ...), custom_call_target="tpu_custom_call" | custom-call | flops 1811939328 | bytes 5931016 | tf_op jit(solution)/shard_map/pallas_call | solution.py:38
  35.9 2.7 %collective-permute-start.16 = (bf16[128,1152]{1,0:T(8,128)(2,1)S(1)}, bf16[128,1152]{1,0:T(8,128)(2,1)S(1)}, u32[]{:S(2)}, u32[]{:S(2)}) collective-permute-start(bf16[128,1152]{1,0:T(8,128)(2,1)S(1)} %get-tuple-element.49), channel_id=1, source_target_pairs={{0,1},{1,0},{2,3},{3,2},{4,5},{5,4},{6,7},{7,6},{8,9},{9,8},{10,11... | collective-permute-start | bytes 884744 | tf_op jit(solution)/shard_map/ppermute | solution.py:21
  38.6 1.3 %shard_map.80 = (bf16[512,384]{1,0:T(8,128)(2,1)S(1)}, f32[1,384]{1,0:T(1,128)S(1)}) custom-call(f32[1]{0:T(128)S(6)} %exp.3.refs_0_, f32[1]{0:T(128)S(6)} %copy.8.refs_1_, bf16[384,1152]{1,0:T(8,128)(2,1)S(1)} %collective-permute-done.6.refs_2_.refs_4_, bf16[128,1152]{1,0:T(8,128)(2,1)S(1)} %collective-permute-done.7.refs_5_.refs_3_, ...), custom_call_target="tpu_custom_call" | custom-call | flops 452984832 | bytes 2460680 | tf_op jit(solution)/shard_map/pallas_call | solution.py:38
  39.9 1.2 %shard_map.81 = (f32[128,1152]{1,0:T(8,128)S(1)}, f32[1,128]{1,0:T(1,128)S(1)}, bf16[1168,128]{1,0:T(8,128)(2,1)S(1)}, f32[1152,128]{1,0:T(8,128)S(1)}, f32[1,128]{1,0:T(1,128)S(1)}) custom-call(bf16[512,384]{1,0:T(8,128)(2,1)S(1)} %get-tuple-element.33.refs_5_.refs_6_.refs_0_, bf16[512,384]{1,0:T(8,128)(2,1)S(1)} %get-tuple-element.38.refs_1_, ...), custom_call_target="tpu_custom_call" | custom-call | flops 905969664 | bytes 4626944 | tf_op jit(solution)/shard_map/pallas_call | solution.py:38
  41.9 1.0 %collective-permute-start.13 = (bf16[1168,128]{1,0:T(8,128)(2,1)S(1)}, bf16[1168,128]{1,0:T(8,128)(2,1)S(1)}, u32[]{:S(2)}, u32[]{:S(2)}) collective-permute-start(bf16[1168,128]{1,0:T(8,128)(2,1)S(1)} %get-tuple-element.46), channel_id=1, source_target_pairs={{0,2},{1,3},{2,0},{3,1},{4,6},{5,7},{6,4},{7,5},{8,10},{9,11},{10,... | collective-permute-start | bytes 897032 | tf_op jit(solution)/shard_map/ppermute | solution.py:21
  42.9 0.8 %collective-permute-start.14 = (bf16[1168,128]{1,0:T(8,128)(2,1)S(1)}, bf16[1168,128]{1,0:T(8,128)(2,1)S(1)}, u32[]{:S(2)}, u32[]{:S(2)}) collective-permute-start(bf16[1168,128]{1,0:T(8,128)(2,1)S(1)} %get-tuple-element.47), channel_id=1, source_target_pairs={{0,16},{4,20},{8,24},{12,28},{16,0},{20,4},{24,8},{28,12},{1,17},{... | collective-permute-start | bytes 897032 | tf_op jit(solution)/shard_map/ppermute | solution.py:21
  43.7 1.0 %collective-permute-start.17 = (bf16[128,1152]{1,0:T(8,128)(2,1)S(1)}, bf16[128,1152]{1,0:T(8,128)(2,1)S(1)}, u32[]{:S(2)}, u32[]{:S(2)}) collective-permute-start(bf16[128,1152]{1,0:T(8,128)(2,1)S(1)} %get-tuple-element.37.refs_6_.refs_7_), channel_id=1, source_target_pairs={{0,8},{4,12},{8,0},{12,4},{16,24},{20,28},{24,16},{28,20},{1,9},{5... | collective-permute-start | bytes 884744 | tf_op jit(solution)/shard_map/ppermute | solution.py:21
  44.7 7.3 %collective-permute-done.15.refs_0_.refs_8_ = bf16[128,1152]{1,0:T(8,128)(2,1)S(1)} collective-permute-done((bf16[128,1152]{1,0:T(8,128)(2,1)S(1)}, bf16[128,1152]{1,0:T(8,128)(2,1)S(1)}, u32[]{:S(2)}, u32[]{:S(2)}) %collective-permute-start.15) | collective-permute-done | bytes 294944 | tf_op jit(solution)/shard_map/ppermute | solution.py:31
  52.0 6.0 %collective-permute-done.16.refs_1_.refs_9_ = bf16[128,1152]{1,0:T(8,128)(2,1)S(1)} collective-permute-done((bf16[128,1152]{1,0:T(8,128)(2,1)S(1)}, bf16[128,1152]{1,0:T(8,128)(2,1)S(1)}, u32[]{:S(2)}, u32[]{:S(2)}) %collective-permute-start.16) | collective-permute-done | bytes 294944 | tf_op jit(solution)/shard_map/ppermute | solution.py:21
  58.0 1.6 %shard_map.84 = (f32[128,1152]{1,0:T(8,128)}, f32[128,1152]{1,0:T(8,128)}, f32[1,128]{1,0:T(1,128)}) custom-call(f32[1]{0:T(128)S(6)} %exp.3.refs_0_, bf16[128,1152]{1,0:T(8,128)(2,1)S(1)} %get-tuple-element.28.refs_1_, bf16[128,1152]{1,0:T(8,128)(2,1)S(1)} %get-tuple-element.29.refs_2_, f32[128,1152]{1,0:T(8,128)S(1)} %get-tuple-element.40.refs_3_, ...), custom_call_target="tpu_custom_call" | custom-call | bytes 4432900 | tf_op jit(solution)/shard_map/pallas_call | solution.py:38
  (35 shorter events, 4.3 us)
Async XLA Ops:
  0.6 5.1 %copy-start = (bf16[128,1152]{1,0:T(8,128)(2,1)S(1)}, bf16[128,1152]{1,0:T(8,128)(2,1)}, u32[]{:S(2)}) copy-start(bf16[128,1152]{1,0:T(8,128)(2,1)} %refs_3_.1) | copy-start | bytes 884740
  1.6 11.6 %collective-permute-start.3 = (bf16[64,1152]{1,0:T(8,128)(2,1)S(1)}, bf16[64,1152]{1,0:T(8,128)(2,1)S(1)}, u32[]{:S(2)}, u32[]{:S(2)}) collective-permute-start(bf16[64,1152]{1,0:T(8,128)(2,1)S(1)} %slice.3), channel_id=1, source_target_pairs={{0,2},{1,3},{2,0},{3,1},{4,6},{5,7},{6,4},{7,5},{8,10},{9,11},{10,... | collective-permute-start | bytes 442376 | tf_op jit(solution)/shard_map/ppermute | solution.py:21
  5.7 8.9 %collective-permute-start.2 = (bf16[128,1152]{1,0:T(8,128)(2,1)S(1)}, bf16[128,1152]{1,0:T(8,128)(2,1)S(1)}, u32[]{:S(2)}, u32[]{:S(2)}) collective-permute-start(bf16[128,1152]{1,0:T(8,128)(2,1)S(1)} %copy-done), channel_id=1, source_target_pairs={{0,16},{4,20},{8,24},{12,28},{16,0},{20,4},{24,8},{28,12},{1,17},{... | collective-permute-start | bytes 884744 | tf_op jit(solution)/shard_map/ppermute | solution.py:21
  7.3 12.4 %collective-permute-start.1 = (bf16[128,1152]{1,0:T(8,128)(2,1)}, bf16[128,1152]{1,0:T(8,128)(2,1)S(1)}, u32[]{:S(2)}, u32[]{:S(2)}) collective-permute-start(bf16[128,1152]{1,0:T(8,128)(2,1)} %refs_2_.1), channel_id=1, source_target_pairs={{0,1},{1,0},{2,3},{3,2},{4,5},{5,4},{6,7},{7,6},{8,9},{9,8},{10,11... | collective-permute-start | bytes 884744 | tf_op jit(solution)/shard_map/ppermute | solution.py:21
  8.8 10.8 %collective-permute-start = (bf16[128,1152]{1,0:T(8,128)(2,1)}, bf16[128,1152]{1,0:T(8,128)(2,1)S(1)}, u32[]{:S(2)}, u32[]{:S(2)}) collective-permute-start(bf16[128,1152]{1,0:T(8,128)(2,1)} %refs_2_.1), channel_id=1, source_target_pairs={{0,8},{4,12},{8,0},{12,4},{16,24},{20,28},{24,16},{28,20},{1,9},{5... | collective-permute-start | bytes 884744 | tf_op jit(solution)/shard_map/ppermute | solution.py:21
  11.7 1.0 %copy-start.1 = (bf16[128,1152]{1,0:T(8,128)(2,1)S(1)}, bf16[128,1152]{1,0:T(8,128)(2,1)}, u32[]{:S(2)}) copy-start(bf16[128,1152]{1,0:T(8,128)(2,1)} %refs_2_.1) | copy-start | bytes 884740
  12.9 9.3 %collective-permute-start.5 = (bf16[64,1152]{1,0:T(8,128)(2,1)S(1)}, bf16[64,1152]{1,0:T(8,128)(2,1)S(1)}, u32[]{:S(2)}, u32[]{:S(2)}) collective-permute-start(bf16[64,1152]{1,0:T(8,128)(2,1)S(1)} %get-tuple-element.31.refs_2_), channel_id=1, source_target_pairs={{0,2},{1,3},{2,0},{3,1},{4,6},{5,7},{6,4},{7,5},{8,10},{9,11},{10,... | collective-permute-start | bytes 442376 | tf_op jit(solution)/shard_map/ppermute | solution.py:21
  13.4 14.8 %collective-permute-start.9 = (bf16[64,1152]{1,0:T(8,128)(2,1)S(1)}, bf16[64,1152]{1,0:T(8,128)(2,1)S(1)}, u32[]{:S(2)}, u32[]{:S(2)}) collective-permute-start(bf16[64,1152]{1,0:T(8,128)(2,1)S(1)} %shard_map.68.refs_4_.refs_1_.refs_2_), channel_id=1, source_target_pairs={{0,16},{4,20},{8,24},{12,28},{16,0},{20,4},{24,8},{28,12},{1,17},{... | collective-permute-start | bytes 442376 | tf_op jit(solution)/shard_map/ppermute | solution.py:21
  19.8 8.3 %collective-permute-start.4 = (bf16[128,1152]{1,0:T(8,128)(2,1)S(1)}, bf16[128,1152]{1,0:T(8,128)(2,1)S(1)}, u32[]{:S(2)}, u32[]{:S(2)}) collective-permute-start(bf16[128,1152]{1,0:T(8,128)(2,1)S(1)} %shard_map.69.refs_2_), channel_id=1, source_target_pairs={{0,8},{4,12},{8,0},{12,4},{16,24},{20,28},{24,16},{28,20},{1,9},{5... | collective-permute-start | bytes 884744 | tf_op jit(solution)/shard_map/ppermute | solution.py:21
  22.1 6.0 %collective-permute-start.6 = (bf16[384,1152]{1,0:T(8,128)(2,1)S(1)}, bf16[384,1152]{1,0:T(8,128)(2,1)S(1)}, u32[]{:S(2)}, u32[]{:S(2)}) collective-permute-start(bf16[384,1152]{1,0:T(8,128)(2,1)S(1)} %shard_map.70.refs_2_), channel_id=1, source_target_pairs={{0,4},{4,0},{8,12},{12,8},{16,20},{20,16},{24,28},{28,24},{1,5},{5... | collective-permute-start | bytes 2654216 | tf_op jit(solution)/shard_map/ppermute | solution.py:21
  22.2 8.4 %collective-permute-start.10 = (bf16[64,1152]{1,0:T(8,128)(2,1)S(1)}, bf16[64,1152]{1,0:T(8,128)(2,1)S(1)}, u32[]{:S(2)}, u32[]{:S(2)}) collective-permute-start(bf16[64,1152]{1,0:T(8,128)(2,1)S(1)} %shard_map.71.refs_1_.refs_3_), channel_id=1, source_target_pairs={{0,16},{4,20},{8,24},{12,28},{16,0},{20,4},{24,8},{28,12},{1,17},{... | collective-permute-start | bytes 442376 | tf_op jit(solution)/shard_map/ppermute | solution.py:21
  23.6 6.0 %collective-permute-start.8 = (bf16[384,1152]{1,0:T(8,128)(2,1)S(1)}, bf16[384,1152]{1,0:T(8,128)(2,1)S(1)}, u32[]{:S(2)}, u32[]{:S(2)}) collective-permute-start(bf16[384,1152]{1,0:T(8,128)(2,1)S(1)} %shard_map.73.refs_4_), channel_id=1, source_target_pairs={{0,4},{4,0},{8,12},{12,8},{16,20},{20,16},{24,28},{28,24},{1,5},{5... | collective-permute-start | bytes 2654216 | tf_op jit(solution)/shard_map/ppermute | solution.py:21
  28.1 3.1 %collective-permute-start.7 = (bf16[128,1152]{1,0:T(8,128)(2,1)S(1)}, bf16[128,1152]{1,0:T(8,128)(2,1)S(1)}, u32[]{:S(2)}, u32[]{:S(2)}) collective-permute-start(bf16[128,1152]{1,0:T(8,128)(2,1)S(1)} %shard_map.72.refs_3_.refs_1_), channel_id=1, source_target_pairs={{0,4},{4,0},{8,12},{12,8},{16,20},{20,16},{24,28},{28,24},{1,5},{5... | collective-permute-start | bytes 884744 | tf_op jit(solution)/shard_map/ppermute | solution.py:21
  30.7 2.8 %collective-permute-start.11 = (bf16[128,1152]{1,0:T(8,128)(2,1)S(1)}, bf16[128,1152]{1,0:T(8,128)(2,1)S(1)}, u32[]{:S(2)}, u32[]{:S(2)}) collective-permute-start(bf16[128,1152]{1,0:T(8,128)(2,1)S(1)} %shard_map.77.refs_6_.refs_9_), channel_id=1, source_target_pairs={{0,4},{4,0},{8,12},{12,8},{16,20},{20,16},{24,28},{28,24},{1,5},{5... | collective-permute-start | bytes 884744 | tf_op jit(solution)/shard_map/ppermute | solution.py:21
  32.8 9.1 %collective-permute-start.12 = (bf16[1168,128]{1,0:T(8,128)(2,1)S(1)}, bf16[1168,128]{1,0:T(8,128)(2,1)S(1)}, u32[]{:S(2)}, u32[]{:S(2)}) collective-permute-start(bf16[1168,128]{1,0:T(8,128)(2,1)S(1)} %get-tuple-element.36.refs_11_), channel_id=1, source_target_pairs={{0,16},{4,20},{8,24},{12,28},{16,0},{20,4},{24,8},{28,12},{1,17},{... | collective-permute-start | bytes 897032 | tf_op jit(solution)/shard_map/ppermute | solution.py:21
  35.3 16.7 %collective-permute-start.15 = (bf16[128,1152]{1,0:T(8,128)(2,1)S(1)}, bf16[128,1152]{1,0:T(8,128)(2,1)S(1)}, u32[]{:S(2)}, u32[]{:S(2)}) collective-permute-start(bf16[128,1152]{1,0:T(8,128)(2,1)S(1)} %get-tuple-element.48), channel_id=1, source_target_pairs={{0,9},{1,8},{2,11},{3,10},{4,13},{5,12},{6,15},{7,14},{8,1},{9,0},... | collective-permute-start | bytes 884744 | tf_op jit(solution)/shard_map/ppermute | solution.py:31
  35.9 22.1 %collective-permute-start.16 = (bf16[128,1152]{1,0:T(8,128)(2,1)S(1)}, bf16[128,1152]{1,0:T(8,128)(2,1)S(1)}, u32[]{:S(2)}, u32[]{:S(2)}) collective-permute-start(bf16[128,1152]{1,0:T(8,128)(2,1)S(1)} %get-tuple-element.49), channel_id=1, source_target_pairs={{0,1},{1,0},{2,3},{3,2},{4,5},{5,4},{6,7},{7,6},{8,9},{9,8},{10,11... | collective-permute-start | bytes 884744 | tf_op jit(solution)/shard_map/ppermute | solution.py:21
  41.9 16.0 %collective-permute-start.13 = (bf16[1168,128]{1,0:T(8,128)(2,1)S(1)}, bf16[1168,128]{1,0:T(8,128)(2,1)S(1)}, u32[]{:S(2)}, u32[]{:S(2)}) collective-permute-start(bf16[1168,128]{1,0:T(8,128)(2,1)S(1)} %get-tuple-element.46), channel_id=1, source_target_pairs={{0,2},{1,3},{2,0},{3,1},{4,6},{5,7},{6,4},{7,5},{8,10},{9,11},{10,... | collective-permute-start | bytes 897032 | tf_op jit(solution)/shard_map/ppermute | solution.py:21
  42.9 15.1 %collective-permute-start.14 = (bf16[1168,128]{1,0:T(8,128)(2,1)S(1)}, bf16[1168,128]{1,0:T(8,128)(2,1)S(1)}, u32[]{:S(2)}, u32[]{:S(2)}) collective-permute-start(bf16[1168,128]{1,0:T(8,128)(2,1)S(1)} %get-tuple-element.47), channel_id=1, source_target_pairs={{0,16},{4,20},{8,24},{12,28},{16,0},{20,4},{24,8},{28,12},{1,17},{... | collective-permute-start | bytes 897032 | tf_op jit(solution)/shard_map/ppermute | solution.py:21
  43.7 14.3 %collective-permute-start.17 = (bf16[128,1152]{1,0:T(8,128)(2,1)S(1)}, bf16[128,1152]{1,0:T(8,128)(2,1)S(1)}, u32[]{:S(2)}, u32[]{:S(2)}) collective-permute-start(bf16[128,1152]{1,0:T(8,128)(2,1)S(1)} %get-tuple-element.37.refs_6_.refs_7_), channel_id=1, source_target_pairs={{0,8},{4,12},{8,0},{12,4},{16,24},{20,28},{24,16},{28,20},{1,9},{5... | collective-permute-start | bytes 884744 | tf_op jit(solution)/shard_map/ppermute | solution.py:21

commit v15 on v13

--- a/solution.py
+++ b/solution.py
@@ -324,7 +324,7 @@
     second_z = [swapped(second_half, "inner", q) for q in image_inner]
     zs, ys = len(first_z), len(images_y)
 
-    (text_z_emb,) = call(unit_kernel, [block], text_z, weight=weights["x"], after=[text_x, second_half])
+    (text_z_emb,) = call(unit_kernel, [block], text_z, weight=weights["x"], after=[second_half])
     near_texts = call(
         functools.partial(near_kernel, frozenset({1})),
         shape((3 * rows, width), bf16),
@@ -335,10 +335,10 @@
     texts_swapped = swapped(near_texts, "dp", 1)
     far_places = [(p, q) for q in image_inner for p in image_dp]
     first_z = call(
-        unit_kernel, [half_block] * zs, *first_z, weight=weights["a"], after=[text_z_emb, *images_y]
+        unit_kernel, [half_block] * zs, *first_z, weight=weights["a"], after=[text_z_emb]
     )
     first_far = [swapped(emb, "dp", p) for emb in first_z for p in image_dp]
-    second_z = call(copies_kernel, [half_block] * zs, *second_z, weight=weights["b"], after=[*first_z, texts_swapped])
+    second_z = call(copies_kernel, [half_block] * zs, *second_z, weight=weights["b"], after=[*first_z, texts_swapped, *images_y])
     (far_text,) = call(copies_kernel, [block], swapped(text_z_emb, "dp", 2), weight=weights["x far"], after=second_z)
     first_far = call(
         copies_kernel, [half_block] * (zs * ys), *first_far, weight=weights["y far"], after=[far_text]

time: 57.1 us -> 57 us (level)
  starting transfers between devices: 19.3 us -> 22.5 us
  waiting for transfers between devices: 22.7 us -> 19.5 us
    ppermute x17, starting transfers between devices: 19.1 us -> 22.5 us  [swapped(): lax.ppermute(value, axis, [(place, place ^ step) for place in range(lax.a...]
    ppermute x17, waiting for transfers between devices: 14.8 us -> 12.4 us  [swapped(): lax.ppermute(value, axis, [(place, place ^ step) for place in range(lax.a...]
    ppermute x1, waiting for transfers between devices: 7.87 us -> 7.16 us  [swapped_both(): return lax.ppermute(value, ('dp', 'inner'), pairs)]
where the time goes in v15:
time: 57 us; the launch traced here: 56.8 us
  starting transfers between devices  22.5 us (39%)
  waiting for transfers between devices  19.5 us (34%)
  Pallas kernels  10.8 us (19%)
  between operations  2.13 us (4%)
  local copies, waits for them, and re-layouts  1.88 us (3%)
    ppermute x17, starting transfers between devices, swapped(): lax.ppermute(value, axis, [(place, place ^ step) for place in range(lax.a...  22.5 us
    ppermute x17, waiting for transfers between devices, swapped(): lax.ppermute(value, axis, [(place, place ^ step) for place in range(lax.a...  12.4 us
    pallas_call x18, Pallas kernels, call(): pl.pallas_call(lambda *refs: kernel(*refs[:first], *refs[last:]), out_sha...  10.8 us
    ppermute x1, waiting for transfers between devices, swapped_both(): return lax.ppermute(value, ('dp', 'inner'), pairs)  7.16 us
  transfers between devices with their start and end apart: 18, of which 7 were waited for; matrix products, arithmetic and copies ran while one was open for 2% of the time, Pallas kernels for 16%

profile of v15, /device:TPU:0, one launch (start us, length us, event | category | flops | bytes accessed | tf_op | source)
XLA Modules:
  0.0 56.8 jit_solution(8426527426203389029)
XLA Ops:
  0.6 3.1 %collective-permute-start.1 = (bf16[128,1152]{1,0:T(8,128)(2,1)}, bf16[128,1152]{1,0:T(8,128)(2,1)S(1)}, u32[]{:S(2)}, u32[]{:S(2)}) collective-permute-start(bf16[128,1152]{1,0:T(8,128)(2,1)} %refs_2_.1), channel_id=1, source_target_pairs={{0,1},{1,0},{2,3},{3,2},{4,5},{5,4},{6,7},{7,6},{8,9},{9,8},{10,11... | collective-permute-start | bytes 884744 | tf_op jit(solution)/shard_map/ppermute | solution.py:21
  3.7 1.5 %collective-permute-start = (bf16[128,1152]{1,0:T(8,128)(2,1)}, bf16[128,1152]{1,0:T(8,128)(2,1)S(1)}, u32[]{:S(2)}, u32[]{:S(2)}) collective-permute-start(bf16[128,1152]{1,0:T(8,128)(2,1)} %refs_2_.1), channel_id=1, source_target_pairs={{0,8},{4,12},{8,0},{12,4},{16,24},{20,28},{24,16},{28,20},{1,9},{5... | collective-permute-start | bytes 884744 | tf_op jit(solution)/shard_map/ppermute | solution.py:21
  5.2 0.9 %slice.3 = bf16[64,1152]{1,0:T(8,128)(2,1)S(1)} slice(bf16[128,1152]{1,0:T(8,128)(2,1)} %refs_3_.1), slice={[0:64], [0:1152]} | slice | bytes 294912 | tf_op jit(solution)/shard_map/slice | solution.py:318
  6.1 2.7 %collective-permute-start.4 = (bf16[64,1152]{1,0:T(8,128)(2,1)S(1)}, bf16[64,1152]{1,0:T(8,128)(2,1)S(1)}, u32[]{:S(2)}, u32[]{:S(2)}) collective-permute-start(bf16[64,1152]{1,0:T(8,128)(2,1)S(1)} %slice.3), channel_id=1, source_target_pairs={{0,2},{1,3},{2,0},{3,1},{4,6},{5,7},{6,4},{7,5},{8,10},{9,11},{10,... | collective-permute-start | bytes 442376 | tf_op jit(solution)/shard_map/ppermute | solution.py:21
  8.8 1.5 %collective-permute-start.6 = (bf16[128,1152]{1,0:T(8,128)(2,1)S(1)}, bf16[128,1152]{1,0:T(8,128)(2,1)S(1)}, u32[]{:S(2)}, u32[]{:S(2)}) collective-permute-start(bf16[128,1152]{1,0:T(8,128)(2,1)S(1)} %copy-done), channel_id=1, source_target_pairs={{0,16},{4,20},{8,24},{12,28},{16,0},{20,4},{24,8},{28,12},{1,17},{... | collective-permute-start | bytes 884744 | tf_op jit(solution)/shard_map/ppermute | solution.py:21
  11.7 1.0 %copy-done.1 = bf16[128,1152]{1,0:T(8,128)(2,1)S(1)} copy-done((bf16[128,1152]{1,0:T(8,128)(2,1)S(1)}, bf16[128,1152]{1,0:T(8,128)(2,1)}, u32[]{:S(2)}) %copy-start.1) | copy-done | bytes 294936
  14.3 1.8 %collective-permute-start.2 = (bf16[128,1152]{1,0:T(8,128)(2,1)S(1)}, bf16[128,1152]{1,0:T(8,128)(2,1)S(1)}, u32[]{:S(2)}, u32[]{:S(2)}) collective-permute-start(bf16[128,1152]{1,0:T(8,128)(2,1)S(1)} %shard_map.68.refs_2_.refs_1_), channel_id=1, source_target_pairs={{0,8},{4,12},{8,0},{12,4},{16,24},{20,28},{24,16},{28,20},{1,9},{5... | collective-permute-start | bytes 884744 | tf_op jit(solution)/shard_map/ppermute | solution.py:21
  16.4 2.2 %collective-permute-start.9 = (bf16[64,1152]{1,0:T(8,128)(2,1)S(1)}, bf16[64,1152]{1,0:T(8,128)(2,1)S(1)}, u32[]{:S(2)}, u32[]{:S(2)}) collective-permute-start(bf16[64,1152]{1,0:T(8,128)(2,1)S(1)} %shard_map.70.refs_1_.refs_2_), channel_id=1, source_target_pairs={{0,16},{4,20},{8,24},{12,28},{16,0},{20,4},{24,8},{28,12},{1,17},{... | collective-permute-start | bytes 442376 | tf_op jit(solution)/shard_map/ppermute | solution.py:21
  18.6 4.0 %collective-permute-done.3.refs_0_ = bf16[64,1152]{1,0:T(8,128)(2,1)S(1)} collective-permute-done((bf16[64,1152]{1,0:T(8,128)(2,1)S(1)}, bf16[64,1152]{1,0:T(8,128)(2,1)S(1)}, u32[]{:S(2)}, u32[]{:S(2)}) %collective-permute-start.3) | collective-permute-done | bytes 147488 | tf_op jit(solution)/shard_map/ppermute | solution.py:21
  22.6 1.5 %collective-permute-start.10 = (bf16[64,1152]{1,0:T(8,128)(2,1)S(1)}, bf16[64,1152]{1,0:T(8,128)(2,1)S(1)}, u32[]{:S(2)}, u32[]{:S(2)}) collective-permute-start(bf16[64,1152]{1,0:T(8,128)(2,1)S(1)} %shard_map.71.refs_1_.refs_3_), channel_id=1, source_target_pairs={{0,16},{4,20},{8,24},{12,28},{16,0},{20,4},{24,8},{28,12},{1,17},{... | collective-permute-start | bytes 442376 | tf_op jit(solution)/shard_map/ppermute | solution.py:21
  25.0 1.3 %shard_map.74 = (bf16[512,384]{1,0:T(8,128)(2,1)S(1)}, f32[1,384]{1,0:T(1,128)S(1)}) custom-call(f32[1]{0:T(128)S(6)} %exp.3.refs_0_, f32[1]{0:T(128)S(6)} %copy.8.refs_1_, bf16[384,1152]{1,0:T(8,128)(2,1)S(1)} %shard_map.69.refs_2_, bf16[128,1152]{1,0:T(8,128)(2,1)S(1)} %shard_map.72.refs_3_.refs_1_, bf16[384,1152]{1,0:T(8,128)(2,1)S(1)} %shard_map.73.refs_4_), custom_call_target="tpu_custom_call" | custom-call | flops 452984832 | bytes 2459144 | tf_op jit(solution)/shard_map/pallas_call | solution.py:38
  27.1 1.0 %shard_map.76.refs_2_.refs_7_.refs_8_ = bf16[512,384]{1,0:T(8,128)(2,1)S(1)} custom-call(f32[1]{0:T(128)S(6)} %exp.3.refs_0_, f32[1]{0:T(128)S(6)} %copy.8.refs_1_, bf16[384,1152]{1,0:T(8,128)(2,1)S(1)} %shard_map.69.refs_2_, bf16[128,1152]{1,0:T(8,128)(2,1)S(1)} %shard_map.72.refs_3_.refs_1_, bf16[384,1152]{1,0:T(8,128)(2,1)S(1)} %collective-permute-done.8.refs_4_.refs_5_, ...), custom_call_target="tpu_custom_call" | custom-call | flops 452984832 | bytes 2457608 | tf_op jit(solution)/shard_map/pallas_call | solution.py:38
  28.6 1.5 %shard_map.78 = (bf16[512,128]{1,0:T(8,128)(2,1)S(1)}, bf16[1168,128]{1,0:T(8,128)(2,1)S(1)}) custom-call(f32[1]{0:T(128)S(6)} %exp.3.refs_0_, f32[1]{0:T(128)S(6)} %copy.8.refs_1_, bf16[384,1152]{1,0:T(8,128)(2,1)S(1)} %shard_map.69.refs_2_, bf16[128,1152]{1,0:T(8,128)(2,1)S(1)} %shard_map.72.refs_3_.refs_1_, ...), custom_call_target="tpu_custom_call" | custom-call | flops 603979776 | bytes 3084296 | tf_op jit(solution)/shard_map/pallas_call | solution.py:38
  30.1 1.4 %collective-permute-start.12 = (bf16[1168,128]{1,0:T(8,128)(2,1)S(1)}, bf16[1168,128]{1,0:T(8,128)(2,1)S(1)}, u32[]{:S(2)}, u32[]{:S(2)}) collective-permute-start(bf16[1168,128]{1,0:T(8,128)(2,1)S(1)} %get-tuple-element.36.refs_11_), channel_id=1, source_target_pairs={{0,16},{4,20},{8,24},{12,28},{16,0},{20,4},{24,8},{28,12},{1,17},{... | collective-permute-start | bytes 897032 | tf_op jit(solution)/shard_map/ppermute | solution.py:21
  31.6 1.8 %shard_map.79 = (f32[128,1152]{1,0:T(8,128)S(1)}, bf16[128,1152]{1,0:T(8,128)(2,1)S(1)}, bf16[128,1152]{1,0:T(8,128)(2,1)S(1)}, bf16[128,1152]{1,0:T(8,128)(2,1)S(1)}) custom-call(f32[1]{0:T(128)S(6)} %exp.3.refs_0_, f32[1]{0:T(128)S(6)} %copy.8.refs_1_, bf16[384,1152]{1,0:T(8,128)(2,1)S(1)} %shard_map.69.refs_2_, ...), custom_call_target="tpu_custom_call" | custom-call | flops 1811939328 | bytes 5931016 | tf_op jit(solution)/shard_map/pallas_call | solution.py:38
  33.5 2.1 %collective-permute-start.16 = (bf16[128,1152]{1,0:T(8,128)(2,1)S(1)}, bf16[128,1152]{1,0:T(8,128)(2,1)S(1)}, u32[]{:S(2)}, u32[]{:S(2)}) collective-permute-start(bf16[128,1152]{1,0:T(8,128)(2,1)S(1)} %get-tuple-element.49), channel_id=1, source_target_pairs={{0,1},{1,0},{2,3},{3,2},{4,5},{5,4},{6,7},{7,6},{8,9},{9,8},{10,11... | collective-permute-start | bytes 884744 | tf_op jit(solution)/shard_map/ppermute | solution.py:21
  35.6 1.3 %shard_map.80 = (bf16[512,384]{1,0:T(8,128)(2,1)S(1)}, f32[1,384]{1,0:T(1,128)S(1)}) custom-call(f32[1]{0:T(128)S(6)} %exp.3.refs_0_, f32[1]{0:T(128)S(6)} %copy.8.refs_1_, bf16[384,1152]{1,0:T(8,128)(2,1)S(1)} %collective-permute-done.5.refs_2_.refs_4_, bf16[128,1152]{1,0:T(8,128)(2,1)S(1)} %collective-permute-done.7.refs_5_.refs_3_, ...), custom_call_target="tpu_custom_call" | custom-call | flops 452984832 | bytes 2460680 | tf_op jit(solution)/shard_map/pallas_call | solution.py:38
  36.8 1.2 %shard_map.81 = (f32[128,1152]{1,0:T(8,128)S(1)}, f32[1,128]{1,0:T(1,128)S(1)}, bf16[1168,128]{1,0:T(8,128)(2,1)S(1)}, f32[1152,128]{1,0:T(8,128)S(1)}, f32[1,128]{1,0:T(1,128)S(1)}) custom-call(bf16[512,384]{1,0:T(8,128)(2,1)S(1)} %get-tuple-element.33.refs_5_.refs_6_.refs_0_, bf16[512,384]{1,0:T(8,128)(2,1)S(1)} %get-tuple-element.38.refs_1_, ...), custom_call_target="tpu_custom_call" | custom-call | flops 905969664 | bytes 4626944 | tf_op jit(solution)/shard_map/pallas_call | solution.py:38
  38.1 1.6 %collective-permute-done.12.refs_2_ = bf16[1168,128]{1,0:T(8,128)(2,1)S(1)} collective-permute-done((bf16[1168,128]{1,0:T(8,128)(2,1)S(1)}, bf16[1168,128]{1,0:T(8,128)(2,1)S(1)}, u32[]{:S(2)}, u32[]{:S(2)}) %collective-permute-start.12) | collective-permute-done | bytes 299040 | tf_op jit(solution)/shard_map/ppermute | solution.py:21
  40.4 1.2 %collective-permute-start.14 = (bf16[1168,128]{1,0:T(8,128)(2,1)S(1)}, bf16[1168,128]{1,0:T(8,128)(2,1)S(1)}, u32[]{:S(2)}, u32[]{:S(2)}) collective-permute-start(bf16[1168,128]{1,0:T(8,128)(2,1)S(1)} %get-tuple-element.47), channel_id=1, source_target_pairs={{0,16},{4,20},{8,24},{12,28},{16,0},{20,4},{24,8},{28,12},{1,17},{... | collective-permute-start | bytes 897032 | tf_op jit(solution)/shard_map/ppermute | solution.py:21
  41.6 1.7 %collective-permute-start.17 = (bf16[128,1152]{1,0:T(8,128)(2,1)S(1)}, bf16[128,1152]{1,0:T(8,128)(2,1)S(1)}, u32[]{:S(2)}, u32[]{:S(2)}) collective-permute-start(bf16[128,1152]{1,0:T(8,128)(2,1)S(1)} %get-tuple-element.37.refs_6_.refs_7_), channel_id=1, source_target_pairs={{0,8},{4,12},{8,0},{12,4},{16,24},{20,28},{24,16},{28,20},{1,9},{5... | collective-permute-start | bytes 884744 | tf_op jit(solution)/shard_map/ppermute | solution.py:21
  43.3 7.2 %collective-permute-done.15.refs_0_.refs_8_ = bf16[128,1152]{1,0:T(8,128)(2,1)S(1)} collective-permute-done((bf16[128,1152]{1,0:T(8,128)(2,1)S(1)}, bf16[128,1152]{1,0:T(8,128)(2,1)S(1)}, u32[]{:S(2)}, u32[]{:S(2)}) %collective-permute-start.15) | collective-permute-done | bytes 294944 | tf_op jit(solution)/shard_map/ppermute | solution.py:31
  50.5 4.8 %collective-permute-done.16.refs_1_.refs_9_ = bf16[128,1152]{1,0:T(8,128)(2,1)S(1)} collective-permute-done((bf16[128,1152]{1,0:T(8,128)(2,1)S(1)}, bf16[128,1152]{1,0:T(8,128)(2,1)S(1)}, u32[]{:S(2)}, u32[]{:S(2)}) %collective-permute-start.16) | collective-permute-done | bytes 294944 | tf_op jit(solution)/shard_map/ppermute | solution.py:21
  55.3 1.6 %shard_map.84 = (f32[128,1152]{1,0:T(8,128)}, f32[128,1152]{1,0:T(8,128)}, f32[1,128]{1,0:T(1,128)}) custom-call(f32[1]{0:T(128)S(6)} %exp.3.refs_0_, bf16[128,1152]{1,0:T(8,128)(2,1)S(1)} %get-tuple-element.28.refs_1_, bf16[128,1152]{1,0:T(8,128)(2,1)S(1)} %get-tuple-element.29.refs_2_, f32[128,1152]{1,0:T(8,128)S(1)} %get-tuple-element.40.refs_3_, ...), custom_call_target="tpu_custom_call" | custom-call | bytes 4432900 | tf_op jit(solution)/shard_map/pallas_call | solution.py:38
  (35 shorter events, 4.8 us)
Async XLA Ops:
  0.6 8.2 %copy-start = (bf16[128,1152]{1,0:T(8,128)(2,1)S(1)}, bf16[128,1152]{1,0:T(8,128)(2,1)}, u32[]{:S(2)}) copy-start(bf16[128,1152]{1,0:T(8,128)(2,1)} %refs_3_.1) | copy-start | bytes 884740
  0.6 13.5 %collective-permute-start.1 = (bf16[128,1152]{1,0:T(8,128)(2,1)}, bf16[128,1152]{1,0:T(8,128)(2,1)S(1)}, u32[]{:S(2)}, u32[]{:S(2)}) collective-permute-start(bf16[128,1152]{1,0:T(8,128)(2,1)} %refs_2_.1), channel_id=1, source_target_pairs={{0,1},{1,0},{2,3},{3,2},{4,5},{5,4},{6,7},{7,6},{8,9},{9,8},{10,11... | collective-permute-start | bytes 884744 | tf_op jit(solution)/shard_map/ppermute | solution.py:21
  3.7 12.3 %collective-permute-start = (bf16[128,1152]{1,0:T(8,128)(2,1)}, bf16[128,1152]{1,0:T(8,128)(2,1)S(1)}, u32[]{:S(2)}, u32[]{:S(2)}) collective-permute-start(bf16[128,1152]{1,0:T(8,128)(2,1)} %refs_2_.1), channel_id=1, source_target_pairs={{0,8},{4,12},{8,0},{12,4},{16,24},{20,28},{24,16},{28,20},{1,9},{5... | collective-permute-start | bytes 884744 | tf_op jit(solution)/shard_map/ppermute | solution.py:21
  6.1 10.1 %collective-permute-start.4 = (bf16[64,1152]{1,0:T(8,128)(2,1)S(1)}, bf16[64,1152]{1,0:T(8,128)(2,1)S(1)}, u32[]{:S(2)}, u32[]{:S(2)}) collective-permute-start(bf16[64,1152]{1,0:T(8,128)(2,1)S(1)} %slice.3), channel_id=1, source_target_pairs={{0,2},{1,3},{2,0},{3,1},{4,6},{5,7},{6,4},{7,5},{8,10},{9,11},{10,... | collective-permute-start | bytes 442376 | tf_op jit(solution)/shard_map/ppermute | solution.py:21
  8.8 13.8 %collective-permute-start.6 = (bf16[128,1152]{1,0:T(8,128)(2,1)S(1)}, bf16[128,1152]{1,0:T(8,128)(2,1)S(1)}, u32[]{:S(2)}, u32[]{:S(2)}) collective-permute-start(bf16[128,1152]{1,0:T(8,128)(2,1)S(1)} %copy-done), channel_id=1, source_target_pairs={{0,16},{4,20},{8,24},{12,28},{16,0},{20,4},{24,8},{28,12},{1,17},{... | collective-permute-start | bytes 884744 | tf_op jit(solution)/shard_map/ppermute | solution.py:21
  11.7 1.0 %copy-start.1 = (bf16[128,1152]{1,0:T(8,128)(2,1)S(1)}, bf16[128,1152]{1,0:T(8,128)(2,1)}, u32[]{:S(2)}) copy-start(bf16[128,1152]{1,0:T(8,128)(2,1)} %refs_2_.1) | copy-start | bytes 884740
  12.9 9.8 %collective-permute-start.3 = (bf16[64,1152]{1,0:T(8,128)(2,1)S(1)}, bf16[64,1152]{1,0:T(8,128)(2,1)S(1)}, u32[]{:S(2)}, u32[]{:S(2)}) collective-permute-start(bf16[64,1152]{1,0:T(8,128)(2,1)S(1)} %get-tuple-element.31.refs_1_), channel_id=1, source_target_pairs={{0,2},{1,3},{2,0},{3,1},{4,6},{5,7},{6,4},{7,5},{8,10},{9,11},{10,... | collective-permute-start | bytes 442376 | tf_op jit(solution)/shard_map/ppermute | solution.py:21
  14.3 9.9 %collective-permute-start.2 = (bf16[128,1152]{1,0:T(8,128)(2,1)S(1)}, bf16[128,1152]{1,0:T(8,128)(2,1)S(1)}, u32[]{:S(2)}, u32[]{:S(2)}) collective-permute-start(bf16[128,1152]{1,0:T(8,128)(2,1)S(1)} %shard_map.68.refs_2_.refs_1_), channel_id=1, source_target_pairs={{0,8},{4,12},{8,0},{12,4},{16,24},{20,28},{24,16},{28,20},{1,9},{5... | collective-permute-start | bytes 884744 | tf_op jit(solution)/shard_map/ppermute | solution.py:21
  16.2 6.4 %collective-permute-start.5 = (bf16[384,1152]{1,0:T(8,128)(2,1)S(1)}, bf16[384,1152]{1,0:T(8,128)(2,1)S(1)}, u32[]{:S(2)}, u32[]{:S(2)}) collective-permute-start(bf16[384,1152]{1,0:T(8,128)(2,1)S(1)} %shard_map.69.refs_2_), channel_id=1, source_target_pairs={{0,4},{4,0},{8,12},{12,8},{16,20},{20,16},{24,28},{28,24},{1,5},{5... | collective-permute-start | bytes 2654216 | tf_op jit(solution)/shard_map/ppermute | solution.py:21
  16.4 8.6 %collective-permute-start.9 = (bf16[64,1152]{1,0:T(8,128)(2,1)S(1)}, bf16[64,1152]{1,0:T(8,128)(2,1)S(1)}, u32[]{:S(2)}, u32[]{:S(2)}) collective-permute-start(bf16[64,1152]{1,0:T(8,128)(2,1)S(1)} %shard_map.70.refs_1_.refs_2_), channel_id=1, source_target_pairs={{0,16},{4,20},{8,24},{12,28},{16,0},{20,4},{24,8},{28,12},{1,17},{... | collective-permute-start | bytes 442376 | tf_op jit(solution)/shard_map/ppermute | solution.py:21
  22.6 5.8 %collective-permute-start.10 = (bf16[64,1152]{1,0:T(8,128)(2,1)S(1)}, bf16[64,1152]{1,0:T(8,128)(2,1)S(1)}, u32[]{:S(2)}, u32[]{:S(2)}) collective-permute-start(bf16[64,1152]{1,0:T(8,128)(2,1)S(1)} %shard_map.71.refs_1_.refs_3_), channel_id=1, source_target_pairs={{0,16},{4,20},{8,24},{12,28},{16,0},{20,4},{24,8},{28,12},{1,17},{... | collective-permute-start | bytes 442376 | tf_op jit(solution)/shard_map/ppermute | solution.py:21
  24.2 4.4 %collective-permute-start.7 = (bf16[128,1152]{1,0:T(8,128)(2,1)S(1)}, bf16[128,1152]{1,0:T(8,128)(2,1)S(1)}, u32[]{:S(2)}, u32[]{:S(2)}) collective-permute-start(bf16[128,1152]{1,0:T(8,128)(2,1)S(1)} %shard_map.72.refs_3_.refs_1_), channel_id=1, source_target_pairs={{0,4},{4,0},{8,12},{12,8},{16,20},{20,16},{24,28},{28,24},{1,5},{5... | collective-permute-start | bytes 884744 | tf_op jit(solution)/shard_map/ppermute | solution.py:21
  24.4 2.7 %collective-permute-start.8 = (bf16[384,1152]{1,0:T(8,128)(2,1)S(1)}, bf16[384,1152]{1,0:T(8,128)(2,1)S(1)}, u32[]{:S(2)}, u32[]{:S(2)}) collective-permute-start(bf16[384,1152]{1,0:T(8,128)(2,1)S(1)} %shard_map.73.refs_4_), channel_id=1, source_target_pairs={{0,4},{4,0},{8,12},{12,8},{16,20},{20,16},{24,28},{28,24},{1,5},{5... | collective-permute-start | bytes 2654216 | tf_op jit(solution)/shard_map/ppermute | solution.py:21
  28.5 3.1 %collective-permute-start.11 = (bf16[128,1152]{1,0:T(8,128)(2,1)S(1)}, bf16[128,1152]{1,0:T(8,128)(2,1)S(1)}, u32[]{:S(2)}, u32[]{:S(2)}) collective-permute-start(bf16[128,1152]{1,0:T(8,128)(2,1)S(1)} %shard_map.77.refs_6_.refs_9_), channel_id=1, source_target_pairs={{0,4},{4,0},{8,12},{12,8},{16,20},{20,16},{24,28},{28,24},{1,5},{5... | collective-permute-start | bytes 884744 | tf_op jit(solution)/shard_map/ppermute | solution.py:21
  30.1 9.6 %collective-permute-start.12 = (bf16[1168,128]{1,0:T(8,128)(2,1)S(1)}, bf16[1168,128]{1,0:T(8,128)(2,1)S(1)}, u32[]{:S(2)}, u32[]{:S(2)}) collective-permute-start(bf16[1168,128]{1,0:T(8,128)(2,1)S(1)} %get-tuple-element.36.refs_11_), channel_id=1, source_target_pairs={{0,16},{4,20},{8,24},{12,28},{16,0},{20,4},{24,8},{28,12},{1,17},{... | collective-permute-start | bytes 897032 | tf_op jit(solution)/shard_map/ppermute | solution.py:21
  33.4 17.1 %collective-permute-start.15 = (bf16[128,1152]{1,0:T(8,128)(2,1)S(1)}, bf16[128,1152]{1,0:T(8,128)(2,1)S(1)}, u32[]{:S(2)}, u32[]{:S(2)}) collective-permute-start(bf16[128,1152]{1,0:T(8,128)(2,1)S(1)} %get-tuple-element.48), channel_id=1, source_target_pairs={{0,9},{1,8},{2,11},{3,10},{4,13},{5,12},{6,15},{7,14},{8,1},{9,0},... | collective-permute-start | bytes 884744 | tf_op jit(solution)/shard_map/ppermute | solution.py:31
  33.5 21.7 %collective-permute-start.16 = (bf16[128,1152]{1,0:T(8,128)(2,1)S(1)}, bf16[128,1152]{1,0:T(8,128)(2,1)S(1)}, u32[]{:S(2)}, u32[]{:S(2)}) collective-permute-start(bf16[128,1152]{1,0:T(8,128)(2,1)S(1)} %get-tuple-element.49), channel_id=1, source_target_pairs={{0,1},{1,0},{2,3},{3,2},{4,5},{5,4},{6,7},{7,6},{8,9},{9,8},{10,11... | collective-permute-start | bytes 884744 | tf_op jit(solution)/shard_map/ppermute | solution.py:21
  39.8 15.5 %collective-permute-start.13 = (bf16[1168,128]{1,0:T(8,128)(2,1)S(1)}, bf16[1168,128]{1,0:T(8,128)(2,1)S(1)}, u32[]{:S(2)}, u32[]{:S(2)}) collective-permute-start(bf16[1168,128]{1,0:T(8,128)(2,1)S(1)} %get-tuple-element.46), channel_id=1, source_target_pairs={{0,2},{1,3},{2,0},{3,1},{4,6},{5,7},{6,4},{7,5},{8,10},{9,11},{10,... | collective-permute-start | bytes 897032 | tf_op jit(solution)/shard_map/ppermute | solution.py:21
  40.4 14.8 %collective-permute-start.14 = (bf16[1168,128]{1,0:T(8,128)(2,1)S(1)}, bf16[1168,128]{1,0:T(8,128)(2,1)S(1)}, u32[]{:S(2)}, u32[]{:S(2)}) collective-permute-start(bf16[1168,128]{1,0:T(8,128)(2,1)S(1)} %get-tuple-element.47), channel_id=1, source_target_pairs={{0,16},{4,20},{8,24},{12,28},{16,0},{20,4},{24,8},{28,12},{1,17},{... | collective-permute-start | bytes 897032 | tf_op jit(solution)/shard_map/ppermute | solution.py:21
  41.6 13.7 %collective-permute-start.17 = (bf16[128,1152]{1,0:T(8,128)(2,1)S(1)}, bf16[128,1152]{1,0:T(8,128)(2,1)S(1)}, u32[]{:S(2)}, u32[]{:S(2)}) collective-permute-start(bf16[128,1152]{1,0:T(8,128)(2,1)S(1)} %get-tuple-element.37.refs_6_.refs_7_), channel_id=1, source_target_pairs={{0,8},{4,12},{8,0},{12,4},{16,24},{20,28},{24,16},{28,20},{1,9},{5... | collective-permute-start | bytes 884744 | tf_op jit(solution)/shard_map/ppermute | solution.py:21

commit v16 on v15

--- a/solution.py
+++ b/solution.py
@@ -370,18 +370,7 @@
         flops=pair_flops * (1 + ys + zs),
         scalars=2,
     )
-    swapped_slopes = call(
-        swapped_pairs_kernel,
-        near_slopes,
-        scale,
-        bias,
-        *own_texts,
-        images_swapped,
-        flops=pair_flops * (1 + ys + zs),
-        scalars=2,
-        after=[own_slopes],
-    )
-    far = call(join_kernel, [block] * (zs * ys), *first_far, *second_far, after=[swapped_slopes])
+    far = call(join_kernel, [block] * (zs * ys), *first_far, *second_far, after=[own_slopes])
     far_swapped = [swapped(emb, "dp", 1) for emb in far]
     far_slopes, *far_sent = call(
         functools.partial(far_kernel, len(far)),
@@ -394,9 +383,20 @@
         flops=4 * pair_flops * len(far),
         scalars=2,
         scratch=[pltpu.VMEM((half, far_rows), bf16)],
-        after=[swapped_slopes],
+        after=[own_slopes],
     )
     moved = [swapped(part, "dp", p) for part, (p, q) in zip(far_sent, far_places)]
+    swapped_slopes = call(
+        swapped_pairs_kernel,
+        near_slopes,
+        scale,
+        bias,
+        *own_texts,
+        images_swapped,
+        flops=pair_flops * (1 + ys + zs),
+        scalars=2,
+        after=far_sent[:1],
+    )
     text_grad, text_x_sums, text_z_sums, text_xz_sums = call(
         functools.partial(text_kernel, len(far)),
         (wide_block, block, block, block),

time: 57 us -> 58.1 us (1.019)
  waiting for transfers between devices: 19.5 us -> 22.3 us
  starting transfers between devices: 22.5 us -> 20.8 us
    ppermute x1, waiting for transfers between devices: 7.16 us -> 9.93 us  [swapped_both(): return lax.ppermute(value, ('dp', 'inner'), pairs)]
    ppermute x17, starting transfers between devices: 22.5 us -> 20.7 us  [swapped(): lax.ppermute(value, axis, [(place, place ^ step) for place in range(lax.a...]
  transfers between devices with their start and end apart: 18 -> 18, of which waited for: 7 -> 6; matrix products, arithmetic and copies ran while one was open for 2% -> 2% of each run, Pallas kernels for 16% -> 16%
where the time goes in v16:
time: 58.1 us; the launch traced here: 57.9 us
  waiting for transfers between devices  22.3 us (38%)
  starting transfers between devices  20.8 us (36%)
  Pallas kernels  10.8 us (19%)
  between operations  2.13 us (4%)
  local copies, waits for them, and re-layouts  1.88 us (3%)
    ppermute x17, starting transfers between devices, swapped(): lax.ppermute(value, axis, [(place, place ^ step) for place in range(lax.a...  20.7 us
    ppermute x17, waiting for transfers between devices, swapped(): lax.ppermute(value, axis, [(place, place ^ step) for place in range(lax.a...  12.4 us
    pallas_call x18, Pallas kernels, call(): pl.pallas_call(lambda *refs: kernel(*refs[:first], *refs[last:]), out_sha...  10.8 us
    ppermute x1, waiting for transfers between devices, swapped_both(): return lax.ppermute(value, ('dp', 'inner'), pairs)  9.93 us
  transfers between devices with their start and end apart: 18, of which 6 were waited for; matrix products, arithmetic and copies ran while one was open for 2% of the time, Pallas kernels for 16%

profile of v16, /device:TPU:0, one launch (start us, length us, event | category | flops | bytes accessed | tf_op | source)
XLA Modules:
  0.0 57.9 jit_solution(12145493832842936242)
XLA Ops:
  0.6 3.1 %collective-permute-start.1 = (bf16[128,1152]{1,0:T(8,128)(2,1)}, bf16[128,1152]{1,0:T(8,128)(2,1)S(1)}, u32[]{:S(2)}, u32[]{:S(2)}) collective-permute-start(bf16[128,1152]{1,0:T(8,128)(2,1)} %refs_2_.1), channel_id=1, source_target_pairs={{0,1},{1,0},{2,3},{3,2},{4,5},{5,4},{6,7},{7,6},{8,9},{9,8},{10,11... | collective-permute-start | bytes 884744 | tf_op jit(solution)/shard_map/ppermute | solution.py:21
  3.7 1.5 %collective-permute-start = (bf16[128,1152]{1,0:T(8,128)(2,1)}, bf16[128,1152]{1,0:T(8,128)(2,1)S(1)}, u32[]{:S(2)}, u32[]{:S(2)}) collective-permute-start(bf16[128,1152]{1,0:T(8,128)(2,1)} %refs_2_.1), channel_id=1, source_target_pairs={{0,8},{4,12},{8,0},{12,4},{16,24},{20,28},{24,16},{28,20},{1,9},{5... | collective-permute-start | bytes 884744 | tf_op jit(solution)/shard_map/ppermute | solution.py:21
  5.2 0.9 %slice.3 = bf16[64,1152]{1,0:T(8,128)(2,1)S(1)} slice(bf16[128,1152]{1,0:T(8,128)(2,1)} %refs_3_.1), slice={[0:64], [0:1152]} | slice | bytes 294912 | tf_op jit(solution)/shard_map/slice | solution.py:318
  6.1 2.7 %collective-permute-start.4 = (bf16[64,1152]{1,0:T(8,128)(2,1)S(1)}, bf16[64,1152]{1,0:T(8,128)(2,1)S(1)}, u32[]{:S(2)}, u32[]{:S(2)}) collective-permute-start(bf16[64,1152]{1,0:T(8,128)(2,1)S(1)} %slice.3), channel_id=1, source_target_pairs={{0,2},{1,3},{2,0},{3,1},{4,6},{5,7},{6,4},{7,5},{8,10},{9,11},{10,... | collective-permute-start | bytes 442376 | tf_op jit(solution)/shard_map/ppermute | solution.py:21
  8.8 1.5 %collective-permute-start.6 = (bf16[128,1152]{1,0:T(8,128)(2,1)S(1)}, bf16[128,1152]{1,0:T(8,128)(2,1)S(1)}, u32[]{:S(2)}, u32[]{:S(2)}) collective-permute-start(bf16[128,1152]{1,0:T(8,128)(2,1)S(1)} %copy-done), channel_id=1, source_target_pairs={{0,16},{4,20},{8,24},{12,28},{16,0},{20,4},{24,8},{28,12},{1,17},{... | collective-permute-start | bytes 884744 | tf_op jit(solution)/shard_map/ppermute | solution.py:21
  11.7 1.0 %copy-done.1 = bf16[128,1152]{1,0:T(8,128)(2,1)S(1)} copy-done((bf16[128,1152]{1,0:T(8,128)(2,1)S(1)}, bf16[128,1152]{1,0:T(8,128)(2,1)}, u32[]{:S(2)}) %copy-start.1) | copy-done | bytes 294936
  13.3 0.8 %collective-permute-done.1.refs_0_ = bf16[128,1152]{1,0:T(8,128)(2,1)S(1)} collective-permute-done((bf16[128,1152]{1,0:T(8,128)(2,1)}, bf16[128,1152]{1,0:T(8,128)(2,1)S(1)}, u32[]{:S(2)}, u32[]{:S(2)}) %collective-permute-start.1) | collective-permute-done | bytes 294944 | tf_op jit(solution)/shard_map/ppermute | solution.py:21
  14.3 1.8 %collective-permute-start.2 = (bf16[128,1152]{1,0:T(8,128)(2,1)S(1)}, bf16[128,1152]{1,0:T(8,128)(2,1)S(1)}, u32[]{:S(2)}, u32[]{:S(2)}) collective-permute-start(bf16[128,1152]{1,0:T(8,128)(2,1)S(1)} %shard_map.68.refs_2_.refs_1_), channel_id=1, source_target_pairs={{0,8},{4,12},{8,0},{12,4},{16,24},{20,28},{24,16},{28,20},{1,9},{5... | collective-permute-start | bytes 884744 | tf_op jit(solution)/shard_map/ppermute | solution.py:21
  16.4 2.2 %collective-permute-start.9 = (bf16[64,1152]{1,0:T(8,128)(2,1)S(1)}, bf16[64,1152]{1,0:T(8,128)(2,1)S(1)}, u32[]{:S(2)}, u32[]{:S(2)}) collective-permute-start(bf16[64,1152]{1,0:T(8,128)(2,1)S(1)} %shard_map.70.refs_1_.refs_2_), channel_id=1, source_target_pairs={{0,16},{4,20},{8,24},{12,28},{16,0},{20,4},{24,8},{28,12},{1,17},{... | collective-permute-start | bytes 442376 | tf_op jit(solution)/shard_map/ppermute | solution.py:21
  18.6 4.0 %collective-permute-done.3.refs_0_ = bf16[64,1152]{1,0:T(8,128)(2,1)S(1)} collective-permute-done((bf16[64,1152]{1,0:T(8,128)(2,1)S(1)}, bf16[64,1152]{1,0:T(8,128)(2,1)S(1)}, u32[]{:S(2)}, u32[]{:S(2)}) %collective-permute-start.3) | collective-permute-done | bytes 147488 | tf_op jit(solution)/shard_map/ppermute | solution.py:21
  22.6 1.5 %collective-permute-start.10 = (bf16[64,1152]{1,0:T(8,128)(2,1)S(1)}, bf16[64,1152]{1,0:T(8,128)(2,1)S(1)}, u32[]{:S(2)}, u32[]{:S(2)}) collective-permute-start(bf16[64,1152]{1,0:T(8,128)(2,1)S(1)} %shard_map.71.refs_1_.refs_3_), channel_id=1, source_target_pairs={{0,16},{4,20},{8,24},{12,28},{16,0},{20,4},{24,8},{28,12},{1,17},{... | collective-permute-start | bytes 442376 | tf_op jit(solution)/shard_map/ppermute | solution.py:21
  25.0 1.3 %shard_map.74 = (bf16[512,384]{1,0:T(8,128)(2,1)S(1)}, f32[1,384]{1,0:T(1,128)S(1)}) custom-call(f32[1]{0:T(128)S(6)} %exp.3.refs_0_, f32[1]{0:T(128)S(6)} %copy.8.refs_1_, bf16[384,1152]{1,0:T(8,128)(2,1)S(1)} %shard_map.69.refs_2_, bf16[128,1152]{1,0:T(8,128)(2,1)S(1)} %shard_map.72.refs_3_.refs_1_, bf16[384,1152]{1,0:T(8,128)(2,1)S(1)} %shard_map.73.refs_4_), custom_call_target="tpu_custom_call" | custom-call | flops 452984832 | bytes 2459144 | tf_op jit(solution)/shard_map/pallas_call | solution.py:38
  26.3 2.2 %collective-permute-done.10.refs_1_ = bf16[64,1152]{1,0:T(8,128)(2,1)S(1)} collective-permute-done((bf16[64,1152]{1,0:T(8,128)(2,1)S(1)}, bf16[64,1152]{1,0:T(8,128)(2,1)S(1)}, u32[]{:S(2)}, u32[]{:S(2)}) %collective-permute-start.10) | collective-permute-done | bytes 147488 | tf_op jit(solution)/shard_map/ppermute | solution.py:21
  28.6 1.5 %shard_map.77 = (bf16[512,128]{1,0:T(8,128)(2,1)S(1)}, bf16[1168,128]{1,0:T(8,128)(2,1)S(1)}) custom-call(f32[1]{0:T(128)S(6)} %exp.3.refs_0_, f32[1]{0:T(128)S(6)} %copy.8.refs_1_, bf16[384,1152]{1,0:T(8,128)(2,1)S(1)} %shard_map.69.refs_2_, bf16[128,1152]{1,0:T(8,128)(2,1)S(1)} %shard_map.72.refs_3_.refs_1_, ...), custom_call_target="tpu_custom_call" | custom-call | flops 603979776 | bytes 3084296 | tf_op jit(solution)/shard_map/pallas_call | solution.py:38
  30.1 1.4 %collective-permute-start.12 = (bf16[1168,128]{1,0:T(8,128)(2,1)S(1)}, bf16[1168,128]{1,0:T(8,128)(2,1)S(1)}, u32[]{:S(2)}, u32[]{:S(2)}) collective-permute-start(bf16[1168,128]{1,0:T(8,128)(2,1)S(1)} %get-tuple-element.36.refs_5_.refs_11_), channel_id=1, source_target_pairs={{0,16},{4,20},{8,24},{12,28},{16,0},{20,4},{24,8},{28,12},{1,17},{... | collective-permute-start | bytes 897032 | tf_op jit(solution)/shard_map/ppermute | solution.py:21
  31.6 1.0 %shard_map.78.refs_8_ = bf16[512,384]{1,0:T(8,128)(2,1)S(1)} custom-call(f32[1]{0:T(128)S(6)} %exp.3.refs_0_, f32[1]{0:T(128)S(6)} %copy.8.refs_1_, bf16[384,1152]{1,0:T(8,128)(2,1)S(1)} %shard_map.69.refs_2_, bf16[128,1152]{1,0:T(8,128)(2,1)S(1)} %shard_map.72.refs_3_.refs_1_, bf16[384,1152]{1,0:T(8,128)(2,1)S(1)} %collective-permute-done.8.refs_4_.refs_5_, ...), custom_call_target="tpu_custom_call" | custom-call | flops 452984832 | bytes 2457608 | tf_op jit(solution)/shard_map/pallas_call | solution.py:38
  32.6 1.8 %shard_map.79 = (f32[128,1152]{1,0:T(8,128)S(1)}, bf16[128,1152]{1,0:T(8,128)(2,1)S(1)}, bf16[128,1152]{1,0:T(8,128)(2,1)S(1)}, bf16[128,1152]{1,0:T(8,128)(2,1)S(1)}) custom-call(f32[1]{0:T(128)S(6)} %exp.3.refs_0_, f32[1]{0:T(128)S(6)} %copy.8.refs_1_, bf16[384,1152]{1,0:T(8,128)(2,1)S(1)} %shard_map.69.refs_2_, ...), custom_call_target="tpu_custom_call" | custom-call | flops 1811939328 | bytes 5931016 | tf_op jit(solution)/shard_map/pallas_call | solution.py:38
  34.5 1.9 %collective-permute-start.16 = (bf16[128,1152]{1,0:T(8,128)(2,1)S(1)}, bf16[128,1152]{1,0:T(8,128)(2,1)S(1)}, u32[]{:S(2)}, u32[]{:S(2)}) collective-permute-start(bf16[128,1152]{1,0:T(8,128)(2,1)S(1)} %get-tuple-element.49), channel_id=1, source_target_pairs={{0,1},{1,0},{2,3},{3,2},{4,5},{5,4},{6,7},{7,6},{8,9},{9,8},{10,11... | collective-permute-start | bytes 884744 | tf_op jit(solution)/shard_map/ppermute | solution.py:21
  36.5 1.3 %shard_map.80 = (bf16[512,384]{1,0:T(8,128)(2,1)S(1)}, f32[1,384]{1,0:T(1,128)S(1)}) custom-call(f32[1]{0:T(128)S(6)} %exp.3.refs_0_, f32[1]{0:T(128)S(6)} %copy.8.refs_1_, bf16[384,1152]{1,0:T(8,128)(2,1)S(1)} %collective-permute-done.5.refs_2_.refs_4_, bf16[128,1152]{1,0:T(8,128)(2,1)S(1)} %collective-permute-done.7.refs_5_.refs_3_, ...), custom_call_target="tpu_custom_call" | custom-call | flops 452984832 | bytes 2460680 | tf_op jit(solution)/shard_map/pallas_call | solution.py:38
  37.7 1.2 %shard_map.81 = (f32[128,1152]{1,0:T(8,128)S(1)}, f32[1,128]{1,0:T(1,128)S(1)}, bf16[1168,128]{1,0:T(8,128)(2,1)S(1)}, f32[1152,128]{1,0:T(8,128)S(1)}, f32[1,128]{1,0:T(1,128)S(1)}) custom-call(bf16[512,384]{1,0:T(8,128)(2,1)S(1)} %get-tuple-element.33.refs_2_.refs_7_.refs_6_.refs_0_, bf16[512,384]{1,0:T(8,128)(2,1)S(1)} %get-tuple-element.38.refs_1_, ...), custom_call_target="tpu_custom_call" | custom-call | flops 905969664 | bytes 4626944 | tf_op jit(solution)/shard_map/pallas_call | solution.py:38
  39.9 1.4 %collective-permute-start.14 = (bf16[1168,128]{1,0:T(8,128)(2,1)S(1)}, bf16[1168,128]{1,0:T(8,128)(2,1)S(1)}, u32[]{:S(2)}, u32[]{:S(2)}) collective-permute-start(bf16[1168,128]{1,0:T(8,128)(2,1)S(1)} %get-tuple-element.47), channel_id=1, source_target_pairs={{0,16},{4,20},{8,24},{12,28},{16,0},{20,4},{24,8},{28,12},{1,17},{... | collective-permute-start | bytes 897032 | tf_op jit(solution)/shard_map/ppermute | solution.py:21
  41.7 9.9 %collective-permute-done.15.refs_0_.refs_8_ = bf16[128,1152]{1,0:T(8,128)(2,1)S(1)} collective-permute-done((bf16[128,1152]{1,0:T(8,128)(2,1)S(1)}, bf16[128,1152]{1,0:T(8,128)(2,1)S(1)}, u32[]{:S(2)}, u32[]{:S(2)}) %collective-permute-start.15) | collective-permute-done | bytes 294944 | tf_op jit(solution)/shard_map/ppermute | solution.py:31
  51.7 4.6 %collective-permute-done.16.refs_1_.refs_9_ = bf16[128,1152]{1,0:T(8,128)(2,1)S(1)} collective-permute-done((bf16[128,1152]{1,0:T(8,128)(2,1)S(1)}, bf16[128,1152]{1,0:T(8,128)(2,1)S(1)}, u32[]{:S(2)}, u32[]{:S(2)}) %collective-permute-start.16) | collective-permute-done | bytes 294944 | tf_op jit(solution)/shard_map/ppermute | solution.py:21
  56.3 1.6 %shard_map.84 = (f32[128,1152]{1,0:T(8,128)}, f32[128,1152]{1,0:T(8,128)}, f32[1,128]{1,0:T(1,128)}) custom-call(f32[1]{0:T(128)S(6)} %exp.3.refs_0_, bf16[128,1152]{1,0:T(8,128)(2,1)S(1)} %get-tuple-element.28.refs_1_, bf16[128,1152]{1,0:T(8,128)(2,1)S(1)} %get-tuple-element.29.refs_2_, f32[128,1152]{1,0:T(8,128)S(1)} %get-tuple-element.40.refs_3_, ...), custom_call_target="tpu_custom_call" | custom-call | bytes 4432900 | tf_op jit(solution)/shard_map/pallas_call | solution.py:38
  (35 shorter events, 3.5 us)
Async XLA Ops:
  0.6 8.2 %copy-start = (bf16[128,1152]{1,0:T(8,128)(2,1)S(1)}, bf16[128,1152]{1,0:T(8,128)(2,1)}, u32[]{:S(2)}) copy-start(bf16[128,1152]{1,0:T(8,128)(2,1)} %refs_3_.1) | copy-start | bytes 884740
  0.6 13.5 %collective-permute-start.1 = (bf16[128,1152]{1,0:T(8,128)(2,1)}, bf16[128,1152]{1,0:T(8,128)(2,1)S(1)}, u32[]{:S(2)}, u32[]{:S(2)}) collective-permute-start(bf16[128,1152]{1,0:T(8,128)(2,1)} %refs_2_.1), channel_id=1, source_target_pairs={{0,1},{1,0},{2,3},{3,2},{4,5},{5,4},{6,7},{7,6},{8,9},{9,8},{10,11... | collective-permute-start | bytes 884744 | tf_op jit(solution)/shard_map/ppermute | solution.py:21
  3.7 12.3 %collective-permute-start = (bf16[128,1152]{1,0:T(8,128)(2,1)}, bf16[128,1152]{1,0:T(8,128)(2,1)S(1)}, u32[]{:S(2)}, u32[]{:S(2)}) collective-permute-start(bf16[128,1152]{1,0:T(8,128)(2,1)} %refs_2_.1), channel_id=1, source_target_pairs={{0,8},{4,12},{8,0},{12,4},{16,24},{20,28},{24,16},{28,20},{1,9},{5... | collective-permute-start | bytes 884744 | tf_op jit(solution)/shard_map/ppermute | solution.py:21
  6.1 10.1 %collective-permute-start.4 = (bf16[64,1152]{1,0:T(8,128)(2,1)S(1)}, bf16[64,1152]{1,0:T(8,128)(2,1)S(1)}, u32[]{:S(2)}, u32[]{:S(2)}) collective-permute-start(bf16[64,1152]{1,0:T(8,128)(2,1)S(1)} %slice.3), channel_id=1, source_target_pairs={{0,2},{1,3},{2,0},{3,1},{4,6},{5,7},{6,4},{7,5},{8,10},{9,11},{10,... | collective-permute-start | bytes 442376 | tf_op jit(solution)/shard_map/ppermute | solution.py:21
  8.8 13.8 %collective-permute-start.6 = (bf16[128,1152]{1,0:T(8,128)(2,1)S(1)}, bf16[128,1152]{1,0:T(8,128)(2,1)S(1)}, u32[]{:S(2)}, u32[]{:S(2)}) collective-permute-start(bf16[128,1152]{1,0:T(8,128)(2,1)S(1)} %copy-done), channel_id=1, source_target_pairs={{0,16},{4,20},{8,24},{12,28},{16,0},{20,4},{24,8},{28,12},{1,17},{... | collective-permute-start | bytes 884744 | tf_op jit(solution)/shard_map/ppermute | solution.py:21
  11.7 1.0 %copy-start.1 = (bf16[128,1152]{1,0:T(8,128)(2,1)S(1)}, bf16[128,1152]{1,0:T(8,128)(2,1)}, u32[]{:S(2)}) copy-start(bf16[128,1152]{1,0:T(8,128)(2,1)} %refs_2_.1) | copy-start | bytes 884740
  12.9 9.8 %collective-permute-start.3 = (bf16[64,1152]{1,0:T(8,128)(2,1)S(1)}, bf16[64,1152]{1,0:T(8,128)(2,1)S(1)}, u32[]{:S(2)}, u32[]{:S(2)}) collective-permute-start(bf16[64,1152]{1,0:T(8,128)(2,1)S(1)} %get-tuple-element.31.refs_1_), channel_id=1, source_target_pairs={{0,2},{1,3},{2,0},{3,1},{4,6},{5,7},{6,4},{7,5},{8,10},{9,11},{10,... | collective-permute-start | bytes 442376 | tf_op jit(solution)/shard_map/ppermute | solution.py:21
  14.3 9.9 %collective-permute-start.2 = (bf16[128,1152]{1,0:T(8,128)(2,1)S(1)}, bf16[128,1152]{1,0:T(8,128)(2,1)S(1)}, u32[]{:S(2)}, u32[]{:S(2)}) collective-permute-start(bf16[128,1152]{1,0:T(8,128)(2,1)S(1)} %shard_map.68.refs_2_.refs_1_), channel_id=1, source_target_pairs={{0,8},{4,12},{8,0},{12,4},{16,24},{20,28},{24,16},{28,20},{1,9},{5... | collective-permute-start | bytes 884744 | tf_op jit(solution)/shard_map/ppermute | solution.py:21
  16.2 6.4 %collective-permute-start.5 = (bf16[384,1152]{1,0:T(8,128)(2,1)S(1)}, bf16[384,1152]{1,0:T(8,128)(2,1)S(1)}, u32[]{:S(2)}, u32[]{:S(2)}) collective-permute-start(bf16[384,1152]{1,0:T(8,128)(2,1)S(1)} %shard_map.69.refs_2_), channel_id=1, source_target_pairs={{0,4},{4,0},{8,12},{12,8},{16,20},{20,16},{24,28},{28,24},{1,5},{5... | collective-permute-start | bytes 2654216 | tf_op jit(solution)/shard_map/ppermute | solution.py:21
  16.4 8.6 %collective-permute-start.9 = (bf16[64,1152]{1,0:T(8,128)(2,1)S(1)}, bf16[64,1152]{1,0:T(8,128)(2,1)S(1)}, u32[]{:S(2)}, u32[]{:S(2)}) collective-permute-start(bf16[64,1152]{1,0:T(8,128)(2,1)S(1)} %shard_map.70.refs_1_.refs_2_), channel_id=1, source_target_pairs={{0,16},{4,20},{8,24},{12,28},{16,0},{20,4},{24,8},{28,12},{1,17},{... | collective-permute-start | bytes 442376 | tf_op jit(solution)/shard_map/ppermute | solution.py:21
  22.6 5.8 %collective-permute-start.10 = (bf16[64,1152]{1,0:T(8,128)(2,1)S(1)}, bf16[64,1152]{1,0:T(8,128)(2,1)S(1)}, u32[]{:S(2)}, u32[]{:S(2)}) collective-permute-start(bf16[64,1152]{1,0:T(8,128)(2,1)S(1)} %shard_map.71.refs_1_.refs_3_), channel_id=1, source_target_pairs={{0,16},{4,20},{8,24},{12,28},{16,0},{20,4},{24,8},{28,12},{1,17},{... | collective-permute-start | bytes 442376 | tf_op jit(solution)/shard_map/ppermute | solution.py:21
  24.2 4.4 %collective-permute-start.7 = (bf16[128,1152]{1,0:T(8,128)(2,1)S(1)}, bf16[128,1152]{1,0:T(8,128)(2,1)S(1)}, u32[]{:S(2)}, u32[]{:S(2)}) collective-permute-start(bf16[128,1152]{1,0:T(8,128)(2,1)S(1)} %shard_map.72.refs_3_.refs_1_), channel_id=1, source_target_pairs={{0,4},{4,0},{8,12},{12,8},{16,20},{20,16},{24,28},{28,24},{1,5},{5... | collective-permute-start | bytes 884744 | tf_op jit(solution)/shard_map/ppermute | solution.py:21
  24.4 7.1 %collective-permute-start.8 = (bf16[384,1152]{1,0:T(8,128)(2,1)S(1)}, bf16[384,1152]{1,0:T(8,128)(2,1)S(1)}, u32[]{:S(2)}, u32[]{:S(2)}) collective-permute-start(bf16[384,1152]{1,0:T(8,128)(2,1)S(1)} %shard_map.73.refs_4_), channel_id=1, source_target_pairs={{0,4},{4,0},{8,12},{12,8},{16,20},{20,16},{24,28},{28,24},{1,5},{5... | collective-permute-start | bytes 2654216 | tf_op jit(solution)/shard_map/ppermute | solution.py:21
  28.5 4.1 %collective-permute-start.11 = (bf16[128,1152]{1,0:T(8,128)(2,1)S(1)}, bf16[128,1152]{1,0:T(8,128)(2,1)S(1)}, u32[]{:S(2)}, u32[]{:S(2)}) collective-permute-start(bf16[128,1152]{1,0:T(8,128)(2,1)S(1)} %shard_map.76.refs_6_.refs_9_), channel_id=1, source_target_pairs={{0,4},{4,0},{8,12},{12,8},{16,20},{20,16},{24,28},{28,24},{1,5},{5... | collective-permute-start | bytes 884744 | tf_op jit(solution)/shard_map/ppermute | solution.py:21
  30.1 9.6 %collective-permute-start.12 = (bf16[1168,128]{1,0:T(8,128)(2,1)S(1)}, bf16[1168,128]{1,0:T(8,128)(2,1)S(1)}, u32[]{:S(2)}, u32[]{:S(2)}) collective-permute-start(bf16[1168,128]{1,0:T(8,128)(2,1)S(1)} %get-tuple-element.36.refs_5_.refs_11_), channel_id=1, source_target_pairs={{0,16},{4,20},{8,24},{12,28},{16,0},{20,4},{24,8},{28,12},{1,17},{... | collective-permute-start | bytes 897032 | tf_op jit(solution)/shard_map/ppermute | solution.py:21
  34.5 17.2 %collective-permute-start.15 = (bf16[128,1152]{1,0:T(8,128)(2,1)S(1)}, bf16[128,1152]{1,0:T(8,128)(2,1)S(1)}, u32[]{:S(2)}, u32[]{:S(2)}) collective-permute-start(bf16[128,1152]{1,0:T(8,128)(2,1)S(1)} %get-tuple-element.48), channel_id=1, source_target_pairs={{0,9},{1,8},{2,11},{3,10},{4,13},{5,12},{6,15},{7,14},{8,1},{9,0},... | collective-permute-start | bytes 884744 | tf_op jit(solution)/shard_map/ppermute | solution.py:31
  34.5 21.7 %collective-permute-start.16 = (bf16[128,1152]{1,0:T(8,128)(2,1)S(1)}, bf16[128,1152]{1,0:T(8,128)(2,1)S(1)}, u32[]{:S(2)}, u32[]{:S(2)}) collective-permute-start(bf16[128,1152]{1,0:T(8,128)(2,1)S(1)} %get-tuple-element.49), channel_id=1, source_target_pairs={{0,1},{1,0},{2,3},{3,2},{4,5},{5,4},{6,7},{7,6},{8,9},{9,8},{10,11... | collective-permute-start | bytes 884744 | tf_op jit(solution)/shard_map/ppermute | solution.py:21
  39.8 16.5 %collective-permute-start.13 = (bf16[1168,128]{1,0:T(8,128)(2,1)S(1)}, bf16[1168,128]{1,0:T(8,128)(2,1)S(1)}, u32[]{:S(2)}, u32[]{:S(2)}) collective-permute-start(bf16[1168,128]{1,0:T(8,128)(2,1)S(1)} %get-tuple-element.46), channel_id=1, source_target_pairs={{0,2},{1,3},{2,0},{3,1},{4,6},{5,7},{6,4},{7,5},{8,10},{9,11},{10,... | collective-permute-start | bytes 897032 | tf_op jit(solution)/shard_map/ppermute | solution.py:21
  39.9 16.4 %collective-permute-start.14 = (bf16[1168,128]{1,0:T(8,128)(2,1)S(1)}, bf16[1168,128]{1,0:T(8,128)(2,1)S(1)}, u32[]{:S(2)}, u32[]{:S(2)}) collective-permute-start(bf16[1168,128]{1,0:T(8,128)(2,1)S(1)} %get-tuple-element.47), channel_id=1, source_target_pairs={{0,16},{4,20},{8,24},{12,28},{16,0},{20,4},{24,8},{28,12},{1,17},{... | collective-permute-start | bytes 897032 | tf_op jit(solution)/shard_map/ppermute | solution.py:21
  41.3 15.0 %collective-permute-start.17 = (bf16[128,1152]{1,0:T(8,128)(2,1)S(1)}, bf16[128,1152]{1,0:T(8,128)(2,1)S(1)}, u32[]{:S(2)}, u32[]{:S(2)}) collective-permute-start(bf16[128,1152]{1,0:T(8,128)(2,1)S(1)} %get-tuple-element.37.refs_6_.refs_7_), channel_id=1, source_target_pairs={{0,8},{4,12},{8,0},{12,4},{16,24},{20,28},{24,16},{28,20},{1,9},{5... | collective-permute-start | bytes 884744 | tf_op jit(solution)/shard_map/ppermute | solution.py:21

commit v17 on v15

--- a/solution.py
+++ b/solution.py
@@ -31,7 +31,7 @@
     return lax.ppermute(value, ("dp", "inner"), pairs)
 
 
-def call(kernel, out_shape, *operands, flops=0, weight=0, scalars=0, scratch=(), after=()):
+def call(kernel, out_shape, *operands, flops=0, weight=0, scalars=0, scratch=(), after=(), out_specs=None):
     moved = sum(o.size * o.dtype.itemsize for o in operands)
     moved += sum(o.size * o.dtype.itemsize for o in jax.tree.leaves(out_shape))
     first, last = len(operands), len(operands) + len(after)
@@ -39,7 +39,7 @@
         lambda *refs: kernel(*refs[:first], *refs[last:]),
         out_shape=out_shape,
         in_specs=[SMEM] * scalars + [VMEM] * (len(operands) - scalars) + [ANY] * len(after),
-        out_specs=jax.tree.map(lambda _: VMEM, out_shape),
+        out_specs=out_specs or jax.tree.map(lambda _: VMEM, out_shape),
         scratch_shapes=scratch,
         compiler_params=pltpu.CompilerParams(vmem_limit_bytes=40 * 1024 * 1024),
         cost_estimate=pl.CostEstimate(
@@ -282,7 +282,8 @@
 
 
 def end_kernel(batch, images, scale_ref, image_ref, text_ref, grad_ref, loss_ref, text_grad_ref, *refs):
-    parts, text_parts, (out_ref, text_out_ref, out_loss_ref, sums_ref) = refs[:images], refs[images:-4], refs[-4:]
+    parts, text_parts, outs = refs[:images], refs[images:-7], refs[-7:]
+    out_ref, text_out_ref, out_loss_ref, sums_ref, rows_ref, text_rows_ref, done = outs
     rows, width = image_ref.shape
     loss = loss_ref[...]
     for part in parts:
@@ -295,11 +296,17 @@
         for part in parts:
             sums = sums + part[panel * rows : (panel + 1) * rows, :].astype(f32)
         sums_ref[:, cut] = sums
-    row_gradient(image_ref[...], sums_ref[...], scale_ref[0], out_ref)
+    row_gradient(image_ref[...], sums_ref[...], scale_ref[0], rows_ref)
+    image_copy = pltpu.make_async_copy(rows_ref, out_ref, done.at[0])
+    image_copy.start()
     sums = text_grad_ref[...]
     for part in text_parts:
         sums = sums + part[...].astype(f32)
-    row_gradient(text_ref[...], sums, scale_ref[0], text_out_ref)
+    row_gradient(text_ref[...], sums, scale_ref[0], text_rows_ref)
+    text_copy = pltpu.make_async_copy(text_rows_ref, text_out_ref, done.at[1])
+    text_copy.start()
+    image_copy.wait()
+    text_copy.wait()
 
 
 def body(image, text, logarithm_scale, bias):
@@ -470,7 +477,8 @@
         *image_parts,
         *text_parts,
         scalars=1,
-        scratch=[pltpu.VMEM((rows, width), f32)],
+        scratch=[pltpu.VMEM((rows, width), f32)] * 3 + [pltpu.SemaphoreType.DMA((2,))],
+        out_specs=(ANY, ANY, VMEM),
         after=[gate],
     )
     return (image_gradient, text_gradient, image_loss.reshape(rows))

time: 57 us -> 57.5 us (level)
  no operation moved by 1% of the time
where the time goes in v17:
time: 57.5 us; the launch traced here: 57.4 us
  starting transfers between devices  22.5 us (39%)
  waiting for transfers between devices  19.5 us (34%)
  Pallas kernels  11.3 us (20%)
  between operations  2.13 us (4%)
  local copies, waits for them, and re-layouts  1.88 us (3%)
    ppermute x17, starting transfers between devices, swapped(): lax.ppermute(value, axis, [(place, place ^ step) for place in range(lax.a...  22.5 us
    ppermute x17, waiting for transfers between devices, swapped(): lax.ppermute(value, axis, [(place, place ^ step) for place in range(lax.a...  12.4 us
    pallas_call x18, Pallas kernels, call(): pl.pallas_call(lambda *refs: kernel(*refs[:first], *refs[last:]), out_sha...  11.3 us
    ppermute x1, waiting for transfers between devices, swapped_both(): return lax.ppermute(value, ('dp', 'inner'), pairs)  7.16 us
  transfers between devices with their start and end apart: 18, of which 7 were waited for; matrix products, arithmetic and copies ran while one was open for 2% of the time, Pallas kernels for 16%

profile of v17, /device:TPU:0, one launch (start us, length us, event | category | flops | bytes accessed | tf_op | source)
XLA Modules:
  0.0 57.4 jit_solution(13654475024885151612)
XLA Ops:
  0.6 3.1 %collective-permute-start.1 = (bf16[128,1152]{1,0:T(8,128)(2,1)}, bf16[128,1152]{1,0:T(8,128)(2,1)S(1)}, u32[]{:S(2)}, u32[]{:S(2)}) collective-permute-start(bf16[128,1152]{1,0:T(8,128)(2,1)} %refs_2_.1), channel_id=1, source_target_pairs={{0,1},{1,0},{2,3},{3,2},{4,5},{5,4},{6,7},{7,6},{8,9},{9,8},{10,11... | collective-permute-start | bytes 884744 | tf_op jit(solution)/shard_map/ppermute | solution.py:21
  3.7 1.5 %collective-permute-start = (bf16[128,1152]{1,0:T(8,128)(2,1)}, bf16[128,1152]{1,0:T(8,128)(2,1)S(1)}, u32[]{:S(2)}, u32[]{:S(2)}) collective-permute-start(bf16[128,1152]{1,0:T(8,128)(2,1)} %refs_2_.1), channel_id=1, source_target_pairs={{0,8},{4,12},{8,0},{12,4},{16,24},{20,28},{24,16},{28,20},{1,9},{5... | collective-permute-start | bytes 884744 | tf_op jit(solution)/shard_map/ppermute | solution.py:21
  5.2 0.9 %slice.3 = bf16[64,1152]{1,0:T(8,128)(2,1)S(1)} slice(bf16[128,1152]{1,0:T(8,128)(2,1)} %refs_3_.1), slice={[0:64], [0:1152]} | slice | bytes 294912 | tf_op jit(solution)/shard_map/slice | solution.py:325
  6.1 2.7 %collective-permute-start.4 = (bf16[64,1152]{1,0:T(8,128)(2,1)S(1)}, bf16[64,1152]{1,0:T(8,128)(2,1)S(1)}, u32[]{:S(2)}, u32[]{:S(2)}) collective-permute-start(bf16[64,1152]{1,0:T(8,128)(2,1)S(1)} %slice.3), channel_id=1, source_target_pairs={{0,2},{1,3},{2,0},{3,1},{4,6},{5,7},{6,4},{7,5},{8,10},{9,11},{10,... | collective-permute-start | bytes 442376 | tf_op jit(solution)/shard_map/ppermute | solution.py:21
  8.8 1.5 %collective-permute-start.6 = (bf16[128,1152]{1,0:T(8,128)(2,1)S(1)}, bf16[128,1152]{1,0:T(8,128)(2,1)S(1)}, u32[]{:S(2)}, u32[]{:S(2)}) collective-permute-start(bf16[128,1152]{1,0:T(8,128)(2,1)S(1)} %copy-done), channel_id=1, source_target_pairs={{0,16},{4,20},{8,24},{12,28},{16,0},{20,4},{24,8},{28,12},{1,17},{... | collective-permute-start | bytes 884744 | tf_op jit(solution)/shard_map/ppermute | solution.py:21
  11.7 1.0 %copy-done.1 = bf16[128,1152]{1,0:T(8,128)(2,1)S(1)} copy-done((bf16[128,1152]{1,0:T(8,128)(2,1)S(1)}, bf16[128,1152]{1,0:T(8,128)(2,1)}, u32[]{:S(2)}) %copy-start.1) | copy-done | bytes 294936
  14.3 1.8 %collective-permute-start.2 = (bf16[128,1152]{1,0:T(8,128)(2,1)S(1)}, bf16[128,1152]{1,0:T(8,128)(2,1)S(1)}, u32[]{:S(2)}, u32[]{:S(2)}) collective-permute-start(bf16[128,1152]{1,0:T(8,128)(2,1)S(1)} %shard_map.68.refs_2_.refs_1_), channel_id=1, source_target_pairs={{0,8},{4,12},{8,0},{12,4},{16,24},{20,28},{24,16},{28,20},{1,9},{5... | collective-permute-start | bytes 884744 | tf_op jit(solution)/shard_map/ppermute | solution.py:21
  16.4 2.2 %collective-permute-start.9 = (bf16[64,1152]{1,0:T(8,128)(2,1)S(1)}, bf16[64,1152]{1,0:T(8,128)(2,1)S(1)}, u32[]{:S(2)}, u32[]{:S(2)}) collective-permute-start(bf16[64,1152]{1,0:T(8,128)(2,1)S(1)} %shard_map.70.refs_1_.refs_2_), channel_id=1, source_target_pairs={{0,16},{4,20},{8,24},{12,28},{16,0},{20,4},{24,8},{28,12},{1,17},{... | collective-permute-start | bytes 442376 | tf_op jit(solution)/shard_map/ppermute | solution.py:21
  18.6 4.0 %collective-permute-done.3.refs_0_ = bf16[64,1152]{1,0:T(8,128)(2,1)S(1)} collective-permute-done((bf16[64,1152]{1,0:T(8,128)(2,1)S(1)}, bf16[64,1152]{1,0:T(8,128)(2,1)S(1)}, u32[]{:S(2)}, u32[]{:S(2)}) %collective-permute-start.3) | collective-permute-done | bytes 147488 | tf_op jit(solution)/shard_map/ppermute | solution.py:21
  22.6 1.5 %collective-permute-start.10 = (bf16[64,1152]{1,0:T(8,128)(2,1)S(1)}, bf16[64,1152]{1,0:T(8,128)(2,1)S(1)}, u32[]{:S(2)}, u32[]{:S(2)}) collective-permute-start(bf16[64,1152]{1,0:T(8,128)(2,1)S(1)} %shard_map.71.refs_1_.refs_3_), channel_id=1, source_target_pairs={{0,16},{4,20},{8,24},{12,28},{16,0},{20,4},{24,8},{28,12},{1,17},{... | collective-permute-start | bytes 442376 | tf_op jit(solution)/shard_map/ppermute | solution.py:21
  25.0 1.3 %shard_map.74 = (bf16[512,384]{1,0:T(8,128)(2,1)S(1)}, f32[1,384]{1,0:T(1,128)S(1)}) custom-call(f32[1]{0:T(128)S(6)} %exp.3.refs_0_, f32[1]{0:T(128)S(6)} %copy.8.refs_1_, bf16[384,1152]{1,0:T(8,128)(2,1)S(1)} %shard_map.69.refs_2_, bf16[128,1152]{1,0:T(8,128)(2,1)S(1)} %shard_map.72.refs_3_.refs_1_, bf16[384,1152]{1,0:T(8,128)(2,1)S(1)} %shard_map.73.refs_4_), custom_call_target="tpu_custom_call" | custom-call | flops 452984832 | bytes 2459144 | tf_op jit(solution)/shard_map/pallas_call | solution.py:38
  27.1 1.0 %shard_map.76.refs_2_.refs_7_.refs_8_ = bf16[512,384]{1,0:T(8,128)(2,1)S(1)} custom-call(f32[1]{0:T(128)S(6)} %exp.3.refs_0_, f32[1]{0:T(128)S(6)} %copy.8.refs_1_, bf16[384,1152]{1,0:T(8,128)(2,1)S(1)} %shard_map.69.refs_2_, bf16[128,1152]{1,0:T(8,128)(2,1)S(1)} %shard_map.72.refs_3_.refs_1_, bf16[384,1152]{1,0:T(8,128)(2,1)S(1)} %collective-permute-done.8.refs_4_.refs_5_, ...), custom_call_target="tpu_custom_call" | custom-call | flops 452984832 | bytes 2457608 | tf_op jit(solution)/shard_map/pallas_call | solution.py:38
  28.6 1.5 %shard_map.78 = (bf16[512,128]{1,0:T(8,128)(2,1)S(1)}, bf16[1168,128]{1,0:T(8,128)(2,1)S(1)}) custom-call(f32[1]{0:T(128)S(6)} %exp.3.refs_0_, f32[1]{0:T(128)S(6)} %copy.8.refs_1_, bf16[384,1152]{1,0:T(8,128)(2,1)S(1)} %shard_map.69.refs_2_, bf16[128,1152]{1,0:T(8,128)(2,1)S(1)} %shard_map.72.refs_3_.refs_1_, ...), custom_call_target="tpu_custom_call" | custom-call | flops 603979776 | bytes 3084296 | tf_op jit(solution)/shard_map/pallas_call | solution.py:38
  30.1 1.4 %collective-permute-start.12 = (bf16[1168,128]{1,0:T(8,128)(2,1)S(1)}, bf16[1168,128]{1,0:T(8,128)(2,1)S(1)}, u32[]{:S(2)}, u32[]{:S(2)}) collective-permute-start(bf16[1168,128]{1,0:T(8,128)(2,1)S(1)} %get-tuple-element.36.refs_11_), channel_id=1, source_target_pairs={{0,16},{4,20},{8,24},{12,28},{16,0},{20,4},{24,8},{28,12},{1,17},{... | collective-permute-start | bytes 897032 | tf_op jit(solution)/shard_map/ppermute | solution.py:21
  31.6 1.8 %shard_map.79 = (f32[128,1152]{1,0:T(8,128)S(1)}, bf16[128,1152]{1,0:T(8,128)(2,1)S(1)}, bf16[128,1152]{1,0:T(8,128)(2,1)S(1)}, bf16[128,1152]{1,0:T(8,128)(2,1)S(1)}) custom-call(f32[1]{0:T(128)S(6)} %exp.3.refs_0_, f32[1]{0:T(128)S(6)} %copy.8.refs_1_, bf16[384,1152]{1,0:T(8,128)(2,1)S(1)} %shard_map.69.refs_2_, ...), custom_call_target="tpu_custom_call" | custom-call | flops 1811939328 | bytes 5931016 | tf_op jit(solution)/shard_map/pallas_call | solution.py:38
  33.5 2.1 %collective-permute-start.16 = (bf16[128,1152]{1,0:T(8,128)(2,1)S(1)}, bf16[128,1152]{1,0:T(8,128)(2,1)S(1)}, u32[]{:S(2)}, u32[]{:S(2)}) collective-permute-start(bf16[128,1152]{1,0:T(8,128)(2,1)S(1)} %get-tuple-element.49), channel_id=1, source_target_pairs={{0,1},{1,0},{2,3},{3,2},{4,5},{5,4},{6,7},{7,6},{8,9},{9,8},{10,11... | collective-permute-start | bytes 884744 | tf_op jit(solution)/shard_map/ppermute | solution.py:21
  35.6 1.3 %shard_map.80 = (bf16[512,384]{1,0:T(8,128)(2,1)S(1)}, f32[1,384]{1,0:T(1,128)S(1)}) custom-call(f32[1]{0:T(128)S(6)} %exp.3.refs_0_, f32[1]{0:T(128)S(6)} %copy.8.refs_1_, bf16[384,1152]{1,0:T(8,128)(2,1)S(1)} %collective-permute-done.5.refs_2_.refs_4_, bf16[128,1152]{1,0:T(8,128)(2,1)S(1)} %collective-permute-done.7.refs_5_.refs_3_, ...), custom_call_target="tpu_custom_call" | custom-call | flops 452984832 | bytes 2460680 | tf_op jit(solution)/shard_map/pallas_call | solution.py:38
  36.8 1.2 %shard_map.81 = (f32[128,1152]{1,0:T(8,128)S(1)}, f32[1,128]{1,0:T(1,128)S(1)}, bf16[1168,128]{1,0:T(8,128)(2,1)S(1)}, f32[1152,128]{1,0:T(8,128)S(1)}, f32[1,128]{1,0:T(1,128)S(1)}) custom-call(bf16[512,384]{1,0:T(8,128)(2,1)S(1)} %get-tuple-element.33.refs_5_.refs_6_.refs_0_, bf16[512,384]{1,0:T(8,128)(2,1)S(1)} %get-tuple-element.38.refs_1_, ...), custom_call_target="tpu_custom_call" | custom-call | flops 905969664 | bytes 4626944 | tf_op jit(solution)/shard_map/pallas_call | solution.py:38
  38.1 1.6 %collective-permute-done.12.refs_2_ = bf16[1168,128]{1,0:T(8,128)(2,1)S(1)} collective-permute-done((bf16[1168,128]{1,0:T(8,128)(2,1)S(1)}, bf16[1168,128]{1,0:T(8,128)(2,1)S(1)}, u32[]{:S(2)}, u32[]{:S(2)}) %collective-permute-start.12) | collective-permute-done | bytes 299040 | tf_op jit(solution)/shard_map/ppermute | solution.py:21
  40.4 1.2 %collective-permute-start.14 = (bf16[1168,128]{1,0:T(8,128)(2,1)S(1)}, bf16[1168,128]{1,0:T(8,128)(2,1)S(1)}, u32[]{:S(2)}, u32[]{:S(2)}) collective-permute-start(bf16[1168,128]{1,0:T(8,128)(2,1)S(1)} %get-tuple-element.47), channel_id=1, source_target_pairs={{0,16},{4,20},{8,24},{12,28},{16,0},{20,4},{24,8},{28,12},{1,17},{... | collective-permute-start | bytes 897032 | tf_op jit(solution)/shard_map/ppermute | solution.py:21
  41.6 1.7 %collective-permute-start.17 = (bf16[128,1152]{1,0:T(8,128)(2,1)S(1)}, bf16[128,1152]{1,0:T(8,128)(2,1)S(1)}, u32[]{:S(2)}, u32[]{:S(2)}) collective-permute-start(bf16[128,1152]{1,0:T(8,128)(2,1)S(1)} %get-tuple-element.37.refs_6_.refs_7_), channel_id=1, source_target_pairs={{0,8},{4,12},{8,0},{12,4},{16,24},{20,28},{24,16},{28,20},{1,9},{5... | collective-permute-start | bytes 884744 | tf_op jit(solution)/shard_map/ppermute | solution.py:21
  43.3 7.2 %collective-permute-done.15.refs_0_.refs_8_ = bf16[128,1152]{1,0:T(8,128)(2,1)S(1)} collective-permute-done((bf16[128,1152]{1,0:T(8,128)(2,1)S(1)}, bf16[128,1152]{1,0:T(8,128)(2,1)S(1)}, u32[]{:S(2)}, u32[]{:S(2)}) %collective-permute-start.15) | collective-permute-done | bytes 294944 | tf_op jit(solution)/shard_map/ppermute | solution.py:31
  50.5 4.8 %collective-permute-done.16.refs_1_.refs_9_ = bf16[128,1152]{1,0:T(8,128)(2,1)S(1)} collective-permute-done((bf16[128,1152]{1,0:T(8,128)(2,1)S(1)}, bf16[128,1152]{1,0:T(8,128)(2,1)S(1)}, u32[]{:S(2)}, u32[]{:S(2)}) %collective-permute-start.16) | collective-permute-done | bytes 294944 | tf_op jit(solution)/shard_map/ppermute | solution.py:21
  55.3 2.1 %shard_map.84 = (f32[128,1152]{1,0:T(8,128)}, f32[128,1152]{1,0:T(8,128)}, f32[1,128]{1,0:T(1,128)}) custom-call(f32[1]{0:T(128)S(6)} %exp.3.refs_0_, bf16[128,1152]{1,0:T(8,128)(2,1)S(1)} %get-tuple-element.28.refs_1_, bf16[128,1152]{1,0:T(8,128)(2,1)S(1)} %get-tuple-element.29.refs_2_, f32[128,1152]{1,0:T(8,128)S(1)} %get-tuple-element.40.refs_3_, ...), custom_call_target="tpu_custom_call" | custom-call | bytes 4432900 | tf_op jit(solution)/shard_map/pallas_call | solution.py:38
  (35 shorter events, 4.8 us)
Async XLA Ops:
  0.6 8.2 %copy-start = (bf16[128,1152]{1,0:T(8,128)(2,1)S(1)}, bf16[128,1152]{1,0:T(8,128)(2,1)}, u32[]{:S(2)}) copy-start(bf16[128,1152]{1,0:T(8,128)(2,1)} %refs_3_.1) | copy-start | bytes 884740
  0.6 13.5 %collective-permute-start.1 = (bf16[128,1152]{1,0:T(8,128)(2,1)}, bf16[128,1152]{1,0:T(8,128)(2,1)S(1)}, u32[]{:S(2)}, u32[]{:S(2)}) collective-permute-start(bf16[128,1152]{1,0:T(8,128)(2,1)} %refs_2_.1), channel_id=1, source_target_pairs={{0,1},{1,0},{2,3},{3,2},{4,5},{5,4},{6,7},{7,6},{8,9},{9,8},{10,11... | collective-permute-start | bytes 884744 | tf_op jit(solution)/shard_map/ppermute | solution.py:21
  3.7 12.3 %collective-permute-start = (bf16[128,1152]{1,0:T(8,128)(2,1)}, bf16[128,1152]{1,0:T(8,128)(2,1)S(1)}, u32[]{:S(2)}, u32[]{:S(2)}) collective-permute-start(bf16[128,1152]{1,0:T(8,128)(2,1)} %refs_2_.1), channel_id=1, source_target_pairs={{0,8},{4,12},{8,0},{12,4},{16,24},{20,28},{24,16},{28,20},{1,9},{5... | collective-permute-start | bytes 884744 | tf_op jit(solution)/shard_map/ppermute | solution.py:21
  6.1 10.1 %collective-permute-start.4 = (bf16[64,1152]{1,0:T(8,128)(2,1)S(1)}, bf16[64,1152]{1,0:T(8,128)(2,1)S(1)}, u32[]{:S(2)}, u32[]{:S(2)}) collective-permute-start(bf16[64,1152]{1,0:T(8,128)(2,1)S(1)} %slice.3), channel_id=1, source_target_pairs={{0,2},{1,3},{2,0},{3,1},{4,6},{5,7},{6,4},{7,5},{8,10},{9,11},{10,... | collective-permute-start | bytes 442376 | tf_op jit(solution)/shard_map/ppermute | solution.py:21
  8.8 13.8 %collective-permute-start.6 = (bf16[128,1152]{1,0:T(8,128)(2,1)S(1)}, bf16[128,1152]{1,0:T(8,128)(2,1)S(1)}, u32[]{:S(2)}, u32[]{:S(2)}) collective-permute-start(bf16[128,1152]{1,0:T(8,128)(2,1)S(1)} %copy-done), channel_id=1, source_target_pairs={{0,16},{4,20},{8,24},{12,28},{16,0},{20,4},{24,8},{28,12},{1,17},{... | collective-permute-start | bytes 884744 | tf_op jit(solution)/shard_map/ppermute | solution.py:21
  11.7 1.0 %copy-start.1 = (bf16[128,1152]{1,0:T(8,128)(2,1)S(1)}, bf16[128,1152]{1,0:T(8,128)(2,1)}, u32[]{:S(2)}) copy-start(bf16[128,1152]{1,0:T(8,128)(2,1)} %refs_2_.1) | copy-start | bytes 884740
  12.9 9.8 %collective-permute-start.3 = (bf16[64,1152]{1,0:T(8,128)(2,1)S(1)}, bf16[64,1152]{1,0:T(8,128)(2,1)S(1)}, u32[]{:S(2)}, u32[]{:S(2)}) collective-permute-start(bf16[64,1152]{1,0:T(8,128)(2,1)S(1)} %get-tuple-element.31.refs_1_), channel_id=1, source_target_pairs={{0,2},{1,3},{2,0},{3,1},{4,6},{5,7},{6,4},{7,5},{8,10},{9,11},{10,... | collective-permute-start | bytes 442376 | tf_op jit(solution)/shard_map/ppermute | solution.py:21
  14.3 9.9 %collective-permute-start.2 = (bf16[128,1152]{1,0:T(8,128)(2,1)S(1)}, bf16[128,1152]{1,0:T(8,128)(2,1)S(1)}, u32[]{:S(2)}, u32[]{:S(2)}) collective-permute-start(bf16[128,1152]{1,0:T(8,128)(2,1)S(1)} %shard_map.68.refs_2_.refs_1_), channel_id=1, source_target_pairs={{0,8},{4,12},{8,0},{12,4},{16,24},{20,28},{24,16},{28,20},{1,9},{5... | collective-permute-start | bytes 884744 | tf_op jit(solution)/shard_map/ppermute | solution.py:21
  16.2 6.4 %collective-permute-start.5 = (bf16[384,1152]{1,0:T(8,128)(2,1)S(1)}, bf16[384,1152]{1,0:T(8,128)(2,1)S(1)}, u32[]{:S(2)}, u32[]{:S(2)}) collective-permute-start(bf16[384,1152]{1,0:T(8,128)(2,1)S(1)} %shard_map.69.refs_2_), channel_id=1, source_target_pairs={{0,4},{4,0},{8,12},{12,8},{16,20},{20,16},{24,28},{28,24},{1,5},{5... | collective-permute-start | bytes 2654216 | tf_op jit(solution)/shard_map/ppermute | solution.py:21
  16.4 8.6 %collective-permute-start.9 = (bf16[64,1152]{1,0:T(8,128)(2,1)S(1)}, bf16[64,1152]{1,0:T(8,128)(2,1)S(1)}, u32[]{:S(2)}, u32[]{:S(2)}) collective-permute-start(bf16[64,1152]{1,0:T(8,128)(2,1)S(1)} %shard_map.70.refs_1_.refs_2_), channel_id=1, source_target_pairs={{0,16},{4,20},{8,24},{12,28},{16,0},{20,4},{24,8},{28,12},{1,17},{... | collective-permute-start | bytes 442376 | tf_op jit(solution)/shard_map/ppermute | solution.py:21
  22.6 5.8 %collective-permute-start.10 = (bf16[64,1152]{1,0:T(8,128)(2,1)S(1)}, bf16[64,1152]{1,0:T(8,128)(2,1)S(1)}, u32[]{:S(2)}, u32[]{:S(2)}) collective-permute-start(bf16[64,1152]{1,0:T(8,128)(2,1)S(1)} %shard_map.71.refs_1_.refs_3_), channel_id=1, source_target_pairs={{0,16},{4,20},{8,24},{12,28},{16,0},{20,4},{24,8},{28,12},{1,17},{... | collective-permute-start | bytes 442376 | tf_op jit(solution)/shard_map/ppermute | solution.py:21
  24.2 4.4 %collective-permute-start.7 = (bf16[128,1152]{1,0:T(8,128)(2,1)S(1)}, bf16[128,1152]{1,0:T(8,128)(2,1)S(1)}, u32[]{:S(2)}, u32[]{:S(2)}) collective-permute-start(bf16[128,1152]{1,0:T(8,128)(2,1)S(1)} %shard_map.72.refs_3_.refs_1_), channel_id=1, source_target_pairs={{0,4},{4,0},{8,12},{12,8},{16,20},{20,16},{24,28},{28,24},{1,5},{5... | collective-permute-start | bytes 884744 | tf_op jit(solution)/shard_map/ppermute | solution.py:21
  24.4 2.7 %collective-permute-start.8 = (bf16[384,1152]{1,0:T(8,128)(2,1)S(1)}, bf16[384,1152]{1,0:T(8,128)(2,1)S(1)}, u32[]{:S(2)}, u32[]{:S(2)}) collective-permute-start(bf16[384,1152]{1,0:T(8,128)(2,1)S(1)} %shard_map.73.refs_4_), channel_id=1, source_target_pairs={{0,4},{4,0},{8,12},{12,8},{16,20},{20,16},{24,28},{28,24},{1,5},{5... | collective-permute-start | bytes 2654216 | tf_op jit(solution)/shard_map/ppermute | solution.py:21
  28.5 3.1 %collective-permute-start.11 = (bf16[128,1152]{1,0:T(8,128)(2,1)S(1)}, bf16[128,1152]{1,0:T(8,128)(2,1)S(1)}, u32[]{:S(2)}, u32[]{:S(2)}) collective-permute-start(bf16[128,1152]{1,0:T(8,128)(2,1)S(1)} %shard_map.77.refs_6_.refs_9_), channel_id=1, source_target_pairs={{0,4},{4,0},{8,12},{12,8},{16,20},{20,16},{24,28},{28,24},{1,5},{5... | collective-permute-start | bytes 884744 | tf_op jit(solution)/shard_map/ppermute | solution.py:21
  30.1 9.6 %collective-permute-start.12 = (bf16[1168,128]{1,0:T(8,128)(2,1)S(1)}, bf16[1168,128]{1,0:T(8,128)(2,1)S(1)}, u32[]{:S(2)}, u32[]{:S(2)}) collective-permute-start(bf16[1168,128]{1,0:T(8,128)(2,1)S(1)} %get-tuple-element.36.refs_11_), channel_id=1, source_target_pairs={{0,16},{4,20},{8,24},{12,28},{16,0},{20,4},{24,8},{28,12},{1,17},{... | collective-permute-start | bytes 897032 | tf_op jit(solution)/shard_map/ppermute | solution.py:21
  33.4 17.1 %collective-permute-start.15 = (bf16[128,1152]{1,0:T(8,128)(2,1)S(1)}, bf16[128,1152]{1,0:T(8,128)(2,1)S(1)}, u32[]{:S(2)}, u32[]{:S(2)}) collective-permute-start(bf16[128,1152]{1,0:T(8,128)(2,1)S(1)} %get-tuple-element.48), channel_id=1, source_target_pairs={{0,9},{1,8},{2,11},{3,10},{4,13},{5,12},{6,15},{7,14},{8,1},{9,0},... | collective-permute-start | bytes 884744 | tf_op jit(solution)/shard_map/ppermute | solution.py:31
  33.5 21.7 %collective-permute-start.16 = (bf16[128,1152]{1,0:T(8,128)(2,1)S(1)}, bf16[128,1152]{1,0:T(8,128)(2,1)S(1)}, u32[]{:S(2)}, u32[]{:S(2)}) collective-permute-start(bf16[128,1152]{1,0:T(8,128)(2,1)S(1)} %get-tuple-element.49), channel_id=1, source_target_pairs={{0,1},{1,0},{2,3},{3,2},{4,5},{5,4},{6,7},{7,6},{8,9},{9,8},{10,11... | collective-permute-start | bytes 884744 | tf_op jit(solution)/shard_map/ppermute | solution.py:21
  39.8 15.5 %collective-permute-start.13 = (bf16[1168,128]{1,0:T(8,128)(2,1)S(1)}, bf16[1168,128]{1,0:T(8,128)(2,1)S(1)}, u32[]{:S(2)}, u32[]{:S(2)}) collective-permute-start(bf16[1168,128]{1,0:T(8,128)(2,1)S(1)} %get-tuple-element.46), channel_id=1, source_target_pairs={{0,2},{1,3},{2,0},{3,1},{4,6},{5,7},{6,4},{7,5},{8,10},{9,11},{10,... | collective-permute-start | bytes 897032 | tf_op jit(solution)/shard_map/ppermute | solution.py:21
  40.4 14.8 %collective-permute-start.14 = (bf16[1168,128]{1,0:T(8,128)(2,1)S(1)}, bf16[1168,128]{1,0:T(8,128)(2,1)S(1)}, u32[]{:S(2)}, u32[]{:S(2)}) collective-permute-start(bf16[1168,128]{1,0:T(8,128)(2,1)S(1)} %get-tuple-element.47), channel_id=1, source_target_pairs={{0,16},{4,20},{8,24},{12,28},{16,0},{20,4},{24,8},{28,12},{1,17},{... | collective-permute-start | bytes 897032 | tf_op jit(solution)/shard_map/ppermute | solution.py:21
  41.6 13.7 %collective-permute-start.17 = (bf16[128,1152]{1,0:T(8,128)(2,1)S(1)}, bf16[128,1152]{1,0:T(8,128)(2,1)S(1)}, u32[]{:S(2)}, u32[]{:S(2)}) collective-permute-start(bf16[128,1152]{1,0:T(8,128)(2,1)S(1)} %get-tuple-element.37.refs_6_.refs_7_), channel_id=1, source_target_pairs={{0,8},{4,12},{8,0},{12,4},{16,24},{20,28},{24,16},{28,20},{1,9},{5... | collective-permute-start | bytes 884744 | tf_op jit(solution)/shard_map/ppermute | solution.py:21

commit v18 on v15

--- a/solution.py
+++ b/solution.py
@@ -221,6 +221,7 @@
 
 def text_kernel(
     count,
+    first,
     scale_ref,
     bias_ref,
     near_ref,
@@ -232,12 +233,15 @@
     other_slopes_ref,
     *refs,
 ):
-    far_refs, far_swapped_refs, outs, slopes_ref = refs[:count], refs[count : 2 * count], refs[2 * count : -1], refs[-1]
+    far_refs, far_swapped_refs, rest = refs[:count], refs[count : 2 * count], refs[2 * count :]
+    outs, slopes_ref = (rest[:2], rest[2]) if first else (rest[1:], rest[0])
     rows, width = far_ref.shape
     own_texts = (near_ref, far_ref)
-    pair_terms(scale_ref[0], bias_ref[0], own_texts, far_swapped_refs, slopes_ref, losses=False)
-    own_slopes = jnp.concatenate([near_slopes_ref[...], far_slopes_ref[...]], axis=1)
-    other_slopes = jnp.concatenate([other_slopes_ref[...], slopes_ref[...]], axis=1)
+    if first:
+        pair_terms(scale_ref[0], bias_ref[0], own_texts, far_swapped_refs, slopes_ref, losses=False)
+    held = slice(first * rows, (first + 2) * rows)
+    own_slopes = jnp.concatenate([near_slopes_ref[held, :], far_slopes_ref[held, :]], axis=1)
+    other_slopes = jnp.concatenate([other_slopes_ref[held, :], slopes_ref[held, :]], axis=1)
     for left, step in column_cuts(width):
         cut = slice(left, left + step)
         total = jnp.dot(
@@ -397,9 +401,9 @@
         after=[swapped_slopes],
     )
     moved = [swapped(part, "dp", p) for part, (p, q) in zip(far_sent, far_places)]
-    text_grad, text_x_sums, text_z_sums, text_xz_sums = call(
-        functools.partial(text_kernel, len(far)),
-        (wide_block, block, block, block),
+    text_z_sums, text_xz_sums, swapped_far_slopes = call(
+        functools.partial(text_kernel, len(far), 2),
+        (block, block, shape((half, far_rows), bf16)),
         scale,
         bias,
         *own_texts,
@@ -410,10 +414,27 @@
         swapped_slopes,
         *far,
         *far_swapped,
-        flops=3 * pair_flops * (1 + ys + zs + len(far)),
+        flops=2 * pair_flops * (1 + ys + zs + len(far)),
         scalars=2,
-        scratch=[pltpu.VMEM((half, far_rows), bf16)],
         after=far_sent[:1],
+    )
+    text_grad, text_x_sums = call(
+        functools.partial(text_kernel, len(far), 0),
+        (wide_block, block),
+        scale,
+        bias,
+        *own_texts,
+        near_images,
+        images_swapped,
+        own_slopes,
+        far_slopes,
+        swapped_slopes,
+        *far,
+        *far_swapped,
+        swapped_far_slopes,
+        flops=pair_flops * (1 + ys + zs + len(far)),
+        scalars=2,
+        after=[text_z_sums],
     )
     text_parts = [
         swapped_both(text_xz_sums, 2, 1),

time: 57 us -> 57.7 us (1.012)
    ppermute x17, waiting for transfers between devices: 12.4 us -> 19.6 us  [swapped(): lax.ppermute(value, axis, [(place, place ^ step) for place in range(lax.a...]
    ppermute x1, waiting for transfers between devices: 7.16 us -> 0.28 us  [swapped_both(): return lax.ppermute(value, ('dp', 'inner'), pairs)]
    pallas_call x18 -> x19, Pallas kernels: 10.8 us -> 11 us  [call(): pl.pallas_call(lambda *refs: kernel(*refs[:first], *refs[last:]), out_sha...]
  transfers between devices with their start and end apart: 18 -> 18, of which waited for: 7 -> 8; matrix products, arithmetic and copies ran while one was open for 2% -> 2% of each run, Pallas kernels for 16% -> 16%
where the time goes in v18:
time: 57.7 us; the launch traced here: 57.5 us
  starting transfers between devices  22.5 us (39%)
  waiting for transfers between devices  19.9 us (34%)
  Pallas kernels  11 us (19%)
  between operations  2.12 us (4%)
  local copies, waits for them, and re-layouts  1.88 us (3%)
    ppermute x17, starting transfers between devices, swapped(): lax.ppermute(value, axis, [(place, place ^ step) for place in range(lax.a...  22.5 us
    ppermute x17, waiting for transfers between devices, swapped(): lax.ppermute(value, axis, [(place, place ^ step) for place in range(lax.a...  19.6 us
    pallas_call x19, Pallas kernels, call(): pl.pallas_call(lambda *refs: kernel(*refs[:first], *refs[last:]), out_sha...  11 us
  transfers between devices with their start and end apart: 18, of which 8 were waited for; matrix products, arithmetic and copies ran while one was open for 2% of the time, Pallas kernels for 16%

profile of v18, /device:TPU:0, one launch (start us, length us, event | category | flops | bytes accessed | tf_op | source)
XLA Modules:
  0.0 57.5 jit_solution(7546007509298984665)
XLA Ops:
  0.6 3.1 %collective-permute-start.1 = (bf16[128,1152]{1,0:T(8,128)(2,1)}, bf16[128,1152]{1,0:T(8,128)(2,1)S(1)}, u32[]{:S(2)}, u32[]{:S(2)}) collective-permute-start(bf16[128,1152]{1,0:T(8,128)(2,1)} %refs_2_.1), channel_id=1, source_target_pairs={{0,1},{1,0},{2,3},{3,2},{4,5},{5,4},{6,7},{7,6},{8,9},{9,8},{10,11... | collective-permute-start | bytes 884744 | tf_op jit(solution)/shard_map/ppermute | solution.py:21
  3.7 1.5 %collective-permute-start = (bf16[128,1152]{1,0:T(8,128)(2,1)}, bf16[128,1152]{1,0:T(8,128)(2,1)S(1)}, u32[]{:S(2)}, u32[]{:S(2)}) collective-permute-start(bf16[128,1152]{1,0:T(8,128)(2,1)} %refs_2_.1), channel_id=1, source_target_pairs={{0,8},{4,12},{8,0},{12,4},{16,24},{20,28},{24,16},{28,20},{1,9},{5... | collective-permute-start | bytes 884744 | tf_op jit(solution)/shard_map/ppermute | solution.py:21
  5.2 0.9 %slice.3 = bf16[64,1152]{1,0:T(8,128)(2,1)S(1)} slice(bf16[128,1152]{1,0:T(8,128)(2,1)} %refs_3_.1), slice={[0:64], [0:1152]} | slice | bytes 294912 | tf_op jit(solution)/shard_map/slice | solution.py:322
  6.1 2.7 %collective-permute-start.4 = (bf16[64,1152]{1,0:T(8,128)(2,1)S(1)}, bf16[64,1152]{1,0:T(8,128)(2,1)S(1)}, u32[]{:S(2)}, u32[]{:S(2)}) collective-permute-start(bf16[64,1152]{1,0:T(8,128)(2,1)S(1)} %slice.3), channel_id=1, source_target_pairs={{0,2},{1,3},{2,0},{3,1},{4,6},{5,7},{6,4},{7,5},{8,10},{9,11},{10,... | collective-permute-start | bytes 442376 | tf_op jit(solution)/shard_map/ppermute | solution.py:21
  8.8 1.5 %collective-permute-start.6 = (bf16[128,1152]{1,0:T(8,128)(2,1)S(1)}, bf16[128,1152]{1,0:T(8,128)(2,1)S(1)}, u32[]{:S(2)}, u32[]{:S(2)}) collective-permute-start(bf16[128,1152]{1,0:T(8,128)(2,1)S(1)} %copy-done), channel_id=1, source_target_pairs={{0,16},{4,20},{8,24},{12,28},{16,0},{20,4},{24,8},{28,12},{1,17},{... | collective-permute-start | bytes 884744 | tf_op jit(solution)/shard_map/ppermute | solution.py:21
  11.7 1.0 %copy-done.1 = bf16[128,1152]{1,0:T(8,128)(2,1)S(1)} copy-done((bf16[128,1152]{1,0:T(8,128)(2,1)S(1)}, bf16[128,1152]{1,0:T(8,128)(2,1)}, u32[]{:S(2)}) %copy-start.1) | copy-done | bytes 294936
  14.3 1.8 %collective-permute-start.2 = (bf16[128,1152]{1,0:T(8,128)(2,1)S(1)}, bf16[128,1152]{1,0:T(8,128)(2,1)S(1)}, u32[]{:S(2)}, u32[]{:S(2)}) collective-permute-start(bf16[128,1152]{1,0:T(8,128)(2,1)S(1)} %shard_map.68.refs_2_.refs_1_), channel_id=1, source_target_pairs={{0,8},{4,12},{8,0},{12,4},{16,24},{20,28},{24,16},{28,20},{1,9},{5... | collective-permute-start | bytes 884744 | tf_op jit(solution)/shard_map/ppermute | solution.py:21
  16.4 2.2 %collective-permute-start.9 = (bf16[64,1152]{1,0:T(8,128)(2,1)S(1)}, bf16[64,1152]{1,0:T(8,128)(2,1)S(1)}, u32[]{:S(2)}, u32[]{:S(2)}) collective-permute-start(bf16[64,1152]{1,0:T(8,128)(2,1)S(1)} %shard_map.70.refs_1_.refs_2_), channel_id=1, source_target_pairs={{0,16},{4,20},{8,24},{12,28},{16,0},{20,4},{24,8},{28,12},{1,17},{... | collective-permute-start | bytes 442376 | tf_op jit(solution)/shard_map/ppermute | solution.py:21
  18.6 4.0 %collective-permute-done.3.refs_0_ = bf16[64,1152]{1,0:T(8,128)(2,1)S(1)} collective-permute-done((bf16[64,1152]{1,0:T(8,128)(2,1)S(1)}, bf16[64,1152]{1,0:T(8,128)(2,1)S(1)}, u32[]{:S(2)}, u32[]{:S(2)}) %collective-permute-start.3) | collective-permute-done | bytes 147488 | tf_op jit(solution)/shard_map/ppermute | solution.py:21
  22.6 1.5 %collective-permute-start.10 = (bf16[64,1152]{1,0:T(8,128)(2,1)S(1)}, bf16[64,1152]{1,0:T(8,128)(2,1)S(1)}, u32[]{:S(2)}, u32[]{:S(2)}) collective-permute-start(bf16[64,1152]{1,0:T(8,128)(2,1)S(1)} %shard_map.71.refs_1_.refs_3_), channel_id=1, source_target_pairs={{0,16},{4,20},{8,24},{12,28},{16,0},{20,4},{24,8},{28,12},{1,17},{... | collective-permute-start | bytes 442376 | tf_op jit(solution)/shard_map/ppermute | solution.py:21
  25.0 1.3 %shard_map.74 = (bf16[512,384]{1,0:T(8,128)(2,1)S(1)}, f32[1,384]{1,0:T(1,128)S(1)}) custom-call(f32[1]{0:T(128)S(6)} %exp.3.refs_0_, f32[1]{0:T(128)S(6)} %copy.8.refs_1_, bf16[384,1152]{1,0:T(8,128)(2,1)S(1)} %shard_map.69.refs_2_, bf16[128,1152]{1,0:T(8,128)(2,1)S(1)} %shard_map.72.refs_3_.refs_1_, bf16[384,1152]{1,0:T(8,128)(2,1)S(1)} %shard_map.73.refs_4_), custom_call_target="tpu_custom_call" | custom-call | flops 452984832 | bytes 2459144 | tf_op jit(solution)/shard_map/pallas_call | solution.py:38
  27.1 1.0 %shard_map.76.refs_2_.refs_7_.refs_8_ = bf16[512,384]{1,0:T(8,128)(2,1)S(1)} custom-call(f32[1]{0:T(128)S(6)} %exp.3.refs_0_, f32[1]{0:T(128)S(6)} %copy.8.refs_1_, bf16[384,1152]{1,0:T(8,128)(2,1)S(1)} %shard_map.69.refs_2_, bf16[128,1152]{1,0:T(8,128)(2,1)S(1)} %shard_map.72.refs_3_.refs_1_, bf16[384,1152]{1,0:T(8,128)(2,1)S(1)} %collective-permute-done.8.refs_4_.refs_5_, ...), custom_call_target="tpu_custom_call" | custom-call | flops 452984832 | bytes 2457608 | tf_op jit(solution)/shard_map/pallas_call | solution.py:38
  28.6 1.5 %shard_map.78 = (bf16[512,128]{1,0:T(8,128)(2,1)S(1)}, bf16[1168,128]{1,0:T(8,128)(2,1)S(1)}) custom-call(f32[1]{0:T(128)S(6)} %exp.3.refs_0_, f32[1]{0:T(128)S(6)} %copy.8.refs_1_, bf16[384,1152]{1,0:T(8,128)(2,1)S(1)} %shard_map.69.refs_2_, bf16[128,1152]{1,0:T(8,128)(2,1)S(1)} %shard_map.72.refs_3_.refs_1_, ...), custom_call_target="tpu_custom_call" | custom-call | flops 603979776 | bytes 3084296 | tf_op jit(solution)/shard_map/pallas_call | solution.py:38
  30.1 1.4 %collective-permute-start.12 = (bf16[1168,128]{1,0:T(8,128)(2,1)S(1)}, bf16[1168,128]{1,0:T(8,128)(2,1)S(1)}, u32[]{:S(2)}, u32[]{:S(2)}) collective-permute-start(bf16[1168,128]{1,0:T(8,128)(2,1)S(1)} %get-tuple-element.37.refs_11_), channel_id=1, source_target_pairs={{0,16},{4,20},{8,24},{12,28},{16,0},{20,4},{24,8},{28,12},{1,17},{... | collective-permute-start | bytes 897032 | tf_op jit(solution)/shard_map/ppermute | solution.py:21
  31.5 1.2 %shard_map.79 = (bf16[128,1152]{1,0:T(8,128)(2,1)S(1)}, bf16[128,1152]{1,0:T(8,128)(2,1)S(1)}, bf16[512,128]{1,0:T(8,128)(2,1)S(1)}) custom-call(f32[1]{0:T(128)S(6)} %exp.3.refs_0_, f32[1]{0:T(128)S(6)} %copy.8.refs_1_, bf16[384,1152]{1,0:T(8,128)(2,1)S(1)} %shard_map.69.refs_2_, bf16[128,1152]{1,0:T(8,128)(2,1)S(1)} %shard_map.72.refs_3_.refs_1_, ...), custom_call_target="tpu_custom_call" | custom-call | flops 1207959552 | bytes 5177352 | tf_op jit(solution)/shard_map/pallas_call | solution.py:38
  32.9 2.1 %collective-permute-start.16 = (bf16[128,1152]{1,0:T(8,128)(2,1)S(1)}, bf16[128,1152]{1,0:T(8,128)(2,1)S(1)}, u32[]{:S(2)}, u32[]{:S(2)}) collective-permute-start(bf16[128,1152]{1,0:T(8,128)(2,1)S(1)} %get-tuple-element.39.refs_12_), channel_id=1, source_target_pairs={{0,1},{1,0},{2,3},{3,2},{4,5},{5,4},{6,7},{7,6},{8,9},{9,8},{10,11... | collective-permute-start | bytes 884744 | tf_op jit(solution)/shard_map/ppermute | solution.py:21
  35.8 1.3 %shard_map.81 = (bf16[512,384]{1,0:T(8,128)(2,1)S(1)}, f32[1,384]{1,0:T(1,128)S(1)}) custom-call(f32[1]{0:T(128)S(6)} %exp.3.refs_0_, f32[1]{0:T(128)S(6)} %copy.8.refs_1_, bf16[384,1152]{1,0:T(8,128)(2,1)S(1)} %collective-permute-done.5.refs_2_.refs_4_, bf16[128,1152]{1,0:T(8,128)(2,1)S(1)} %collective-permute-done.7.refs_5_.refs_3_, ...), custom_call_target="tpu_custom_call" | custom-call | flops 452984832 | bytes 2460680 | tf_op jit(solution)/shard_map/pallas_call | solution.py:38
  37.1 1.2 %shard_map.82 = (f32[128,1152]{1,0:T(8,128)S(1)}, f32[1,128]{1,0:T(1,128)S(1)}, bf16[1168,128]{1,0:T(8,128)(2,1)S(1)}, f32[1152,128]{1,0:T(8,128)S(1)}, f32[1,128]{1,0:T(1,128)S(1)}) custom-call(bf16[512,384]{1,0:T(8,128)(2,1)S(1)} %get-tuple-element.34.refs_5_.refs_6_.refs_0_, bf16[512,384]{1,0:T(8,128)(2,1)S(1)} %get-tuple-element.41.refs_1_, ...), custom_call_target="tpu_custom_call" | custom-call | flops 905969664 | bytes 4626944 | tf_op jit(solution)/shard_map/pallas_call | solution.py:38
  38.3 1.3 %collective-permute-done.12.refs_2_ = bf16[1168,128]{1,0:T(8,128)(2,1)S(1)} collective-permute-done((bf16[1168,128]{1,0:T(8,128)(2,1)S(1)}, bf16[1168,128]{1,0:T(8,128)(2,1)S(1)}, u32[]{:S(2)}, u32[]{:S(2)}) %collective-permute-start.12) | collective-permute-done | bytes 299040 | tf_op jit(solution)/shard_map/ppermute | solution.py:21
  40.7 0.9 %collective-permute-start.14 = (bf16[1168,128]{1,0:T(8,128)(2,1)S(1)}, bf16[1168,128]{1,0:T(8,128)(2,1)S(1)}, u32[]{:S(2)}, u32[]{:S(2)}) collective-permute-start(bf16[1168,128]{1,0:T(8,128)(2,1)S(1)} %get-tuple-element.50), channel_id=1, source_target_pairs={{0,16},{4,20},{8,24},{12,28},{16,0},{20,4},{24,8},{28,12},{1,17},{... | collective-permute-start | bytes 897032 | tf_op jit(solution)/shard_map/ppermute | solution.py:21
  41.6 1.7 %collective-permute-start.17 = (bf16[128,1152]{1,0:T(8,128)(2,1)S(1)}, bf16[128,1152]{1,0:T(8,128)(2,1)S(1)}, u32[]{:S(2)}, u32[]{:S(2)}) collective-permute-start(bf16[128,1152]{1,0:T(8,128)(2,1)S(1)} %get-tuple-element.40.refs_6_.refs_7_), channel_id=1, source_target_pairs={{0,8},{4,12},{8,0},{12,4},{16,24},{20,28},{24,16},{28,20},{1,9},{5... | collective-permute-start | bytes 884744 | tf_op jit(solution)/shard_map/ppermute | solution.py:21
  43.6 10.9 %collective-permute-done.16.refs_1_.refs_9_ = bf16[128,1152]{1,0:T(8,128)(2,1)S(1)} collective-permute-done((bf16[128,1152]{1,0:T(8,128)(2,1)S(1)}, bf16[128,1152]{1,0:T(8,128)(2,1)S(1)}, u32[]{:S(2)}, u32[]{:S(2)}) %collective-permute-start.16) | collective-permute-done | bytes 294944 | tf_op jit(solution)/shard_map/ppermute | solution.py:21
  54.6 1.3 %collective-permute-done.13.refs_6_ = bf16[1168,128]{1,0:T(8,128)(2,1)S(1)} collective-permute-done((bf16[1168,128]{1,0:T(8,128)(2,1)S(1)}, bf16[1168,128]{1,0:T(8,128)(2,1)S(1)}, u32[]{:S(2)}, u32[]{:S(2)}) %collective-permute-start.13) | collective-permute-done | bytes 299040 | tf_op jit(solution)/shard_map/ppermute | solution.py:21
  55.9 1.6 %shard_map.85 = (f32[128,1152]{1,0:T(8,128)}, f32[128,1152]{1,0:T(8,128)}, f32[1,128]{1,0:T(1,128)}) custom-call(f32[1]{0:T(128)S(6)} %exp.3.refs_0_, bf16[128,1152]{1,0:T(8,128)(2,1)S(1)} %get-tuple-element.29.refs_1_, bf16[128,1152]{1,0:T(8,128)(2,1)S(1)} %get-tuple-element.30.refs_2_, f32[128,1152]{1,0:T(8,128)S(1)} %get-tuple-element.43.refs_3_, ...), custom_call_target="tpu_custom_call" | custom-call | bytes 4432900 | tf_op jit(solution)/shard_map/pallas_call | solution.py:38
  (36 shorter events, 6.2 us)
Async XLA Ops:
  0.6 8.2 %copy-start = (bf16[128,1152]{1,0:T(8,128)(2,1)S(1)}, bf16[128,1152]{1,0:T(8,128)(2,1)}, u32[]{:S(2)}) copy-start(bf16[128,1152]{1,0:T(8,128)(2,1)} %refs_3_.1) | copy-start | bytes 884740
  0.6 13.5 %collective-permute-start.1 = (bf16[128,1152]{1,0:T(8,128)(2,1)}, bf16[128,1152]{1,0:T(8,128)(2,1)S(1)}, u32[]{:S(2)}, u32[]{:S(2)}) collective-permute-start(bf16[128,1152]{1,0:T(8,128)(2,1)} %refs_2_.1), channel_id=1, source_target_pairs={{0,1},{1,0},{2,3},{3,2},{4,5},{5,4},{6,7},{7,6},{8,9},{9,8},{10,11... | collective-permute-start | bytes 884744 | tf_op jit(solution)/shard_map/ppermute | solution.py:21
  3.7 12.3 %collective-permute-start = (bf16[128,1152]{1,0:T(8,128)(2,1)}, bf16[128,1152]{1,0:T(8,128)(2,1)S(1)}, u32[]{:S(2)}, u32[]{:S(2)}) collective-permute-start(bf16[128,1152]{1,0:T(8,128)(2,1)} %refs_2_.1), channel_id=1, source_target_pairs={{0,8},{4,12},{8,0},{12,4},{16,24},{20,28},{24,16},{28,20},{1,9},{5... | collective-permute-start | bytes 884744 | tf_op jit(solution)/shard_map/ppermute | solution.py:21
  6.1 10.1 %collective-permute-start.4 = (bf16[64,1152]{1,0:T(8,128)(2,1)S(1)}, bf16[64,1152]{1,0:T(8,128)(2,1)S(1)}, u32[]{:S(2)}, u32[]{:S(2)}) collective-permute-start(bf16[64,1152]{1,0:T(8,128)(2,1)S(1)} %slice.3), channel_id=1, source_target_pairs={{0,2},{1,3},{2,0},{3,1},{4,6},{5,7},{6,4},{7,5},{8,10},{9,11},{10,... | collective-permute-start | bytes 442376 | tf_op jit(solution)/shard_map/ppermute | solution.py:21
  8.8 13.8 %collective-permute-start.6 = (bf16[128,1152]{1,0:T(8,128)(2,1)S(1)}, bf16[128,1152]{1,0:T(8,128)(2,1)S(1)}, u32[]{:S(2)}, u32[]{:S(2)}) collective-permute-start(bf16[128,1152]{1,0:T(8,128)(2,1)S(1)} %copy-done), channel_id=1, source_target_pairs={{0,16},{4,20},{8,24},{12,28},{16,0},{20,4},{24,8},{28,12},{1,17},{... | collective-permute-start | bytes 884744 | tf_op jit(solution)/shard_map/ppermute | solution.py:21
  11.7 1.0 %copy-start.1 = (bf16[128,1152]{1,0:T(8,128)(2,1)S(1)}, bf16[128,1152]{1,0:T(8,128)(2,1)}, u32[]{:S(2)}) copy-start(bf16[128,1152]{1,0:T(8,128)(2,1)} %refs_2_.1) | copy-start | bytes 884740
  12.9 9.8 %collective-permute-start.3 = (bf16[64,1152]{1,0:T(8,128)(2,1)S(1)}, bf16[64,1152]{1,0:T(8,128)(2,1)S(1)}, u32[]{:S(2)}, u32[]{:S(2)}) collective-permute-start(bf16[64,1152]{1,0:T(8,128)(2,1)S(1)} %get-tuple-element.32.refs_1_), channel_id=1, source_target_pairs={{0,2},{1,3},{2,0},{3,1},{4,6},{5,7},{6,4},{7,5},{8,10},{9,11},{10,... | collective-permute-start | bytes 442376 | tf_op jit(solution)/shard_map/ppermute | solution.py:21
  14.3 9.9 %collective-permute-start.2 = (bf16[128,1152]{1,0:T(8,128)(2,1)S(1)}, bf16[128,1152]{1,0:T(8,128)(2,1)S(1)}, u32[]{:S(2)}, u32[]{:S(2)}) collective-permute-start(bf16[128,1152]{1,0:T(8,128)(2,1)S(1)} %shard_map.68.refs_2_.refs_1_), channel_id=1, source_target_pairs={{0,8},{4,12},{8,0},{12,4},{16,24},{20,28},{24,16},{28,20},{1,9},{5... | collective-permute-start | bytes 884744 | tf_op jit(solution)/shard_map/ppermute | solution.py:21
  16.2 6.4 %collective-permute-start.5 = (bf16[384,1152]{1,0:T(8,128)(2,1)S(1)}, bf16[384,1152]{1,0:T(8,128)(2,1)S(1)}, u32[]{:S(2)}, u32[]{:S(2)}) collective-permute-start(bf16[384,1152]{1,0:T(8,128)(2,1)S(1)} %shard_map.69.refs_2_), channel_id=1, source_target_pairs={{0,4},{4,0},{8,12},{12,8},{16,20},{20,16},{24,28},{28,24},{1,5},{5... | collective-permute-start | bytes 2654216 | tf_op jit(solution)/shard_map/ppermute | solution.py:21
  16.4 8.6 %collective-permute-start.9 = (bf16[64,1152]{1,0:T(8,128)(2,1)S(1)}, bf16[64,1152]{1,0:T(8,128)(2,1)S(1)}, u32[]{:S(2)}, u32[]{:S(2)}) collective-permute-start(bf16[64,1152]{1,0:T(8,128)(2,1)S(1)} %shard_map.70.refs_1_.refs_2_), channel_id=1, source_target_pairs={{0,16},{4,20},{8,24},{12,28},{16,0},{20,4},{24,8},{28,12},{1,17},{... | collective-permute-start | bytes 442376 | tf_op jit(solution)/shard_map/ppermute | solution.py:21
  22.6 5.8 %collective-permute-start.10 = (bf16[64,1152]{1,0:T(8,128)(2,1)S(1)}, bf16[64,1152]{1,0:T(8,128)(2,1)S(1)}, u32[]{:S(2)}, u32[]{:S(2)}) collective-permute-start(bf16[64,1152]{1,0:T(8,128)(2,1)S(1)} %shard_map.71.refs_1_.refs_3_), channel_id=1, source_target_pairs={{0,16},{4,20},{8,24},{12,28},{16,0},{20,4},{24,8},{28,12},{1,17},{... | collective-permute-start | bytes 442376 | tf_op jit(solution)/shard_map/ppermute | solution.py:21
  24.2 4.4 %collective-permute-start.7 = (bf16[128,1152]{1,0:T(8,128)(2,1)S(1)}, bf16[128,1152]{1,0:T(8,128)(2,1)S(1)}, u32[]{:S(2)}, u32[]{:S(2)}) collective-permute-start(bf16[128,1152]{1,0:T(8,128)(2,1)S(1)} %shard_map.72.refs_3_.refs_1_), channel_id=1, source_target_pairs={{0,4},{4,0},{8,12},{12,8},{16,20},{20,16},{24,28},{28,24},{1,5},{5... | collective-permute-start | bytes 884744 | tf_op jit(solution)/shard_map/ppermute | solution.py:21
  24.4 2.7 %collective-permute-start.8 = (bf16[384,1152]{1,0:T(8,128)(2,1)S(1)}, bf16[384,1152]{1,0:T(8,128)(2,1)S(1)}, u32[]{:S(2)}, u32[]{:S(2)}) collective-permute-start(bf16[384,1152]{1,0:T(8,128)(2,1)S(1)} %shard_map.73.refs_4_), channel_id=1, source_target_pairs={{0,4},{4,0},{8,12},{12,8},{16,20},{20,16},{24,28},{28,24},{1,5},{5... | collective-permute-start | bytes 2654216 | tf_op jit(solution)/shard_map/ppermute | solution.py:21
  28.5 3.0 %collective-permute-start.11 = (bf16[128,1152]{1,0:T(8,128)(2,1)S(1)}, bf16[128,1152]{1,0:T(8,128)(2,1)S(1)}, u32[]{:S(2)}, u32[]{:S(2)}) collective-permute-start(bf16[128,1152]{1,0:T(8,128)(2,1)S(1)} %shard_map.77.refs_6_.refs_9_), channel_id=1, source_target_pairs={{0,4},{4,0},{8,12},{12,8},{16,20},{20,16},{24,28},{28,24},{1,5},{5... | collective-permute-start | bytes 884744 | tf_op jit(solution)/shard_map/ppermute | solution.py:21
  30.1 9.6 %collective-permute-start.12 = (bf16[1168,128]{1,0:T(8,128)(2,1)S(1)}, bf16[1168,128]{1,0:T(8,128)(2,1)S(1)}, u32[]{:S(2)}, u32[]{:S(2)}) collective-permute-start(bf16[1168,128]{1,0:T(8,128)(2,1)S(1)} %get-tuple-element.37.refs_11_), channel_id=1, source_target_pairs={{0,16},{4,20},{8,24},{12,28},{16,0},{20,4},{24,8},{28,12},{1,17},{... | collective-permute-start | bytes 897032 | tf_op jit(solution)/shard_map/ppermute | solution.py:21
  32.8 10.8 %collective-permute-start.15 = (bf16[128,1152]{1,0:T(8,128)(2,1)S(1)}, bf16[128,1152]{1,0:T(8,128)(2,1)S(1)}, u32[]{:S(2)}, u32[]{:S(2)}) collective-permute-start(bf16[128,1152]{1,0:T(8,128)(2,1)S(1)} %get-tuple-element.51), channel_id=1, source_target_pairs={{0,9},{1,8},{2,11},{3,10},{4,13},{5,12},{6,15},{7,14},{8,1},{9,0},... | collective-permute-start | bytes 884744 | tf_op jit(solution)/shard_map/ppermute | solution.py:31
  32.9 21.7 %collective-permute-start.16 = (bf16[128,1152]{1,0:T(8,128)(2,1)S(1)}, bf16[128,1152]{1,0:T(8,128)(2,1)S(1)}, u32[]{:S(2)}, u32[]{:S(2)}) collective-permute-start(bf16[128,1152]{1,0:T(8,128)(2,1)S(1)} %get-tuple-element.39.refs_12_), channel_id=1, source_target_pairs={{0,1},{1,0},{2,3},{3,2},{4,5},{5,4},{6,7},{7,6},{8,9},{9,8},{10,11... | collective-permute-start | bytes 884744 | tf_op jit(solution)/shard_map/ppermute | solution.py:21
  39.8 16.1 %collective-permute-start.13 = (bf16[1168,128]{1,0:T(8,128)(2,1)S(1)}, bf16[1168,128]{1,0:T(8,128)(2,1)S(1)}, u32[]{:S(2)}, u32[]{:S(2)}) collective-permute-start(bf16[1168,128]{1,0:T(8,128)(2,1)S(1)} %get-tuple-element.49), channel_id=1, source_target_pairs={{0,2},{1,3},{2,0},{3,1},{4,6},{5,7},{6,4},{7,5},{8,10},{9,11},{10,... | collective-permute-start | bytes 897032 | tf_op jit(solution)/shard_map/ppermute | solution.py:21
  40.7 15.2 %collective-permute-start.14 = (bf16[1168,128]{1,0:T(8,128)(2,1)S(1)}, bf16[1168,128]{1,0:T(8,128)(2,1)S(1)}, u32[]{:S(2)}, u32[]{:S(2)}) collective-permute-start(bf16[1168,128]{1,0:T(8,128)(2,1)S(1)} %get-tuple-element.50), channel_id=1, source_target_pairs={{0,16},{4,20},{8,24},{12,28},{16,0},{20,4},{24,8},{28,12},{1,17},{... | collective-permute-start | bytes 897032 | tf_op jit(solution)/shard_map/ppermute | solution.py:21
  41.6 13.0 %collective-permute-start.17 = (bf16[128,1152]{1,0:T(8,128)(2,1)S(1)}, bf16[128,1152]{1,0:T(8,128)(2,1)S(1)}, u32[]{:S(2)}, u32[]{:S(2)}) collective-permute-start(bf16[128,1152]{1,0:T(8,128)(2,1)S(1)} %get-tuple-element.40.refs_6_.refs_7_), channel_id=1, source_target_pairs={{0,8},{4,12},{8,0},{12,4},{16,24},{20,28},{24,16},{28,20},{1,9},{5... | collective-permute-start | bytes 884744 | tf_op jit(solution)/shard_map/ppermute | solution.py:21
